TPU v7x, 256 devices: a whole 4x4x8 slice. The times are simulated.
256 devices in a mesh: dp: 32 (over z, x_hi, core), tensor: 8 (over x_lo, y).
Axes of the slice: x: 4 (x_hi: 2, x_lo: 2; x = x_hi * 2 + x_lo), y: 4, z: 8, core: 2. Of those that a mesh axis runs over, the one named last changes fastest.
Arguments:
- tokens: bfloat16 [32768, 4096], P(('dp', 'tensor')), may hold values from -6 to 6
- norm_gain: float32 [4096], replicated, may hold values from 0.25 to 1.75
- norm_bias: float32 [4096], replicated, may hold values from -3 to 3
- qkv_weight: bfloat16 [4096, 6144], P('dp', 'tensor'), may hold values from -8 to 8
- out_weight: bfloat16 [2048, 4096], P('tensor', 'dp'), may hold values from -0.125 to 0.125
- match_weight: bfloat16 [4096, 512], P('dp'), may hold values from -0.09375 to 0.09375
- matcher_qkv: bfloat16 [512, 1536], replicated, may hold values from -12 to 12
- matcher_out: bfloat16 [512, 512], replicated, may hold values from -0.25 to 0.25
Outputs:
- features: bfloat16 [32768, 4096], P(('dp', 'tensor'))
- matched: bfloat16 [32768, 512], P(('dp', 'tensor'))
All inputs are finite; a program needn't handle non-finite values.
Results may differ from a plain program's by a relative error of at most 0.014.
Values may be sent and summed in bfloat16 or wider, within the bound.
No kernel may reach another device: no remote copies, remote signals or barrier semaphores. Data moves between devices by JAX's collectives and lax.ppermute only.
A program may use at most 128 MiB of HBM per device.

v0:
```python
import functools
import itertools
import math

import jax
import jax.numpy as jnp
from jax import lax
from jax.experimental import pallas as pl
from jax.experimental.pallas import tpu as pltpu
from jax.sharding import Mesh
from jax.sharding import PartitionSpec as P

HEAD_DIM = 128
MATCH_HEADS = 8
DISTANCES = (1, -1, 2)
WAIT = 23_000_000_000
LOG2_E = math.log2(math.e)
AXES = ("z", "xh", "core", "xl", "y")
SIZES = (8, 2, 2, 2, 4)


def moved(block, target):
    def index(place):
        at = 0
        for axis, size in zip(AXES, SIZES):
            at = at * size + place[axis]
        return at

    route = []
    for values in itertools.product(*[range(size) for size in SIZES]):
        place = dict(zip(AXES, values))
        route.append((index(place), index({**place, **target(place)})))
    return lax.ppermute(block, AXES, route)


def along_y(k):
    return lambda p: {"y": (p["y"] + k) % 4}


def along_z(k):
    return lambda p: {"z": (p["z"] + k) % 8}


def two_along_z(p):
    return {"z": (p["z"] + 2 - 4 * (p["z"] % 2)) % 8}


def along_x(k):
    def target(p):
        x = (p["xh"] * 2 + p["xl"] + k) % 4
        return {"xh": x // 2, "xl": x % 2}

    return target


def other_core(p):
    return {"core": 1 - p["core"]}


def swapped_roles(block):
    return moved(block, lambda p: {"core": p["xl"], "xl": p["core"]})


def gathered_z(block, z, *wait_for):
    pair = after(jnp.stack([block, moved(block, along_z(4))]), *wait_for)
    pairs = [pair, moved(pair, along_z(1)), moved(pair, along_z(-1)), moved(pair, two_along_z)]
    sign = 1 - 2 * (z % 2)
    whole = jnp.zeros((2, 4) + block.shape, block.dtype)
    rest = (0,) * block.ndim
    for k, pair in zip((0, 1, -1, 2 * sign), pairs):
        owner = (z - k) % 8
        low = jnp.where(owner < 4, pair, pair[::-1])
        whole = lax.dynamic_update_slice(whole, low[:, None], (0, owner % 4) + rest)
    return whole.reshape((8,) + block.shape)


def along_x_parts(block):
    return [block] + [moved(block, along_x(k)) for k in DISTANCES]


def gathered_x(block, x, axis):
    whole = jnp.zeros(block.shape[:axis] + (4,) + block.shape[axis:], block.dtype)
    for k, part in zip((0,) + DISTANCES, along_x_parts(block)):
        at = [0] * whole.ndim
        at[axis] = (x - k) % 4
        whole = lax.dynamic_update_slice(whole, jnp.expand_dims(part, axis), at)
    return whole


def layer_norm(rows_in, norm_gain, norm_bias):
    values = rows_in.astype(jnp.float32)
    center = jnp.mean(values, axis=-1, keepdims=True)
    spread = jnp.mean((values - center) ** 2, axis=-1, keepdims=True)
    return ((values - center) * lax.rsqrt(spread + 1e-06) * norm_gain + norm_bias).astype(
        jnp.bfloat16
    )


def local(kernel, out_shape, mebibytes, flops=0, moved_bytes=0, **kwargs):
    return pl.pallas_call(
        kernel,
        out_shape=out_shape,
        compiler_params=pltpu.CompilerParams(vmem_limit_bytes=mebibytes << 20),
        cost_estimate=pl.CostEstimate(flops=flops, bytes_accessed=moved_bytes, transcendentals=0),
        **kwargs,
    )


def together(*values, flops=0):
    def kernel(*refs):
        pass

    held = pl.BlockSpec(memory_space=pltpu.HBM)
    count = len(values)
    return local(
        kernel,
        tuple(jax.ShapeDtypeStruct(value.shape, value.dtype) for value in values),
        1,
        flops=flops,
        in_specs=[held] * count,
        out_specs=(held,) * count,
        input_output_aliases={i: i for i in range(count)},
    )(*values)


def after(value, *earlier):
    def kernel(*refs):
        pass

    held = pl.BlockSpec(memory_space=pltpu.HBM)
    return local(
        kernel,
        jax.ShapeDtypeStruct(value.shape, value.dtype),
        1,
        in_specs=[held] * (1 + len(earlier)),
        out_specs=held,
        input_output_aliases={0: 0},
    )(value, *earlier)


def attend(queries, keys, values, scale):
    scores = dot_transposed(queries, keys)
    raised = jnp.exp2((scores - jnp.max(scores, axis=-1, keepdims=True)) * (scale * LOG2_E))
    mixed = dot(raised.astype(jnp.bfloat16), values)
    return mixed * (1.0 / jnp.sum(raised, axis=-1, keepdims=True))


def dot(left, right):
    return jnp.dot(left, right, preferred_element_type=jnp.float32)


def dot_transposed(left, right):
    return lax.dot_general(
        left, right, (((1,), (1,)), ((), ())), preferred_element_type=jnp.float32
    )


PARTS = 4


def attention_kernel(*refs):
    place, *pieces, first = refs[:10]
    seconds = refs[10:14]
    own, other, held, held_weight, total, projected, sems = refs[14:]
    depth = held.shape[1] // PARTS
    x = place[0]
    block = first.shape[3]
    copies = []
    for part in range(PARTS):
        span = pl.ds(part * depth, depth)
        planes = pl.ds(part * 8 // PARTS, 8 // PARTS)
        moves = []
        for column in range(first.shape[2]):
            there = held_weight.at[planes, :, :, pl.ds(column * block, block)]
            moves.append((first.at[planes, :, column], there))
        for k, second in zip((0,) + DISTANCES, seconds):
            at = first.shape[2] * block
            there = held_weight.at[planes, (x - k + 4) % 4, :, pl.ds(at, block)]
            moves.append((second.at[planes, 0], there))
        at = 0
        for piece in pieces:
            count = piece.shape[0]
            moves.append((piece.at[:, span], held.at[pl.ds(at, count), span]))
            at += count
        starting = [
            pltpu.make_async_copy(source, there, sems.at[part, i])
            for i, (source, there) in enumerate(moves)
        ]
        for copy in starting:
            copy.start()
        copies.append(starting)
    step = 512
    for part in range(PARTS):
        for copy in copies[part]:
            copy.wait()
        span = pl.ds(part * depth, depth)
        planes = pl.ds(part * 8 // PARTS, 8 // PARTS)

        @pl.loop(0, held.shape[0], step=step)
        def _(row, part=part, span=span, planes=planes):
            rows = pl.ds(pl.multiple_of(row, step), step)
            term = dot(held[rows, span], held_weight[planes].reshape(depth, -1))
            if part:
                term = total[rows, :] + term
            if part < PARTS - 1:
                total[rows, :] = term
            else:
                projected[rows, :] = term.astype(jnp.bfloat16)

    step = 256
    for head in range(2):
        at = head * 3 * HEAD_DIM
        for half, out in enumerate((own, other)):

            @pl.loop(0, out.shape[0], step=step)
            def _(row, at=at, half=half, out=out, head=head):
                rows = pl.ds(pl.multiple_of(half * out.shape[0] + row, step), step)
                mixed = attend(
                    projected[rows, at : at + HEAD_DIM],
                    projected[:, at + HEAD_DIM : at + 2 * HEAD_DIM],
                    projected[:, at + 2 * HEAD_DIM : at + 3 * HEAD_DIM],
                    1.0 / math.sqrt(HEAD_DIM),
                )
                out[pl.ds(pl.multiple_of(row, step), step), pl.ds(head * HEAD_DIM, HEAD_DIM)] = (
                    mixed.astype(jnp.bfloat16)
                )


def attention(x, pieces, first, seconds):
    count = sum(piece.shape[0] for piece in pieces)
    depth = pieces[0].shape[1]
    block = first.shape[3]
    columns = (first.shape[2] + 1) * block
    result = jax.ShapeDtypeStruct((count // 2, columns // 3), jnp.bfloat16)
    copies = len(pieces) + first.shape[2] + 4
    return local(
        attention_kernel,
        (result, result),
        44,
        flops=2 * count * depth * columns,
        moved_bytes=2 * depth * (count + columns),
        in_specs=[pl.BlockSpec(memory_space=pltpu.SMEM)]
        + [pl.BlockSpec(memory_space=pltpu.HBM)] * (len(pieces) + 5),
        out_specs=(pl.BlockSpec(memory_space=pltpu.VMEM),) * 2,
        scratch_shapes=[
            pltpu.VMEM((count, depth), jnp.bfloat16),
            pltpu.VMEM((8, 4, block, columns), jnp.bfloat16),
            pltpu.VMEM((count, columns), jnp.float32),
            pltpu.VMEM((count, columns), jnp.bfloat16),
            pltpu.SemaphoreType.DMA((PARTS, copies)),
        ],
    )(x.astype(jnp.int32).reshape(1), *pieces, first, *seconds)


def out_kernel(skipped, picked, place, mine, theirs, *refs):
    parts, outs, matrix = refs[:16], refs[16 + skipped : -1], refs[-1]
    planes, _, block, wide = parts[0].shape
    for i in range(16):
        k, at = ((0,) + DISTANCES)[i // 2 % 4], (i // 8 * 2 + i % 2) * block
        for plane in range(planes):
            column = (plane * 4 + (place[0] - k + 4) % 4) * wide
            matrix[at : at + block, pl.ds(pl.multiple_of(column, wide), wide)] = parts[i][plane, 0]
    rows = [range(at, at + many) for spans in picked for at, many in spans]
    both = [
        jnp.concatenate([mine[r.start : r.stop, :], theirs[r.start : r.stop, :]], axis=1)
        for r in rows
    ]
    terms = dot(jnp.concatenate(both, axis=0), matrix[...])
    at = 0
    for out in outs:
        out[...] = terms[at : at + out.shape[0]].astype(out.dtype)
        at += out.shape[0]


def out_projection(x, mine, theirs, weights, picked, dtype, earlier=()):
    earlier = list(earlier)
    planes, _, block, wide = weights[0].shape
    at_once = 2
    columns = at_once * 4 * wide
    counts = [sum(many for _, many in spans) for spans in picked]
    whole = pl.BlockSpec(mine.shape, lambda i: (0, 0))
    halves = [pl.BlockSpec((at_once, 1, block, wide), lambda i, h=h: (i, h, 0, 0)) for h in (1, 2)]
    return local(
        functools.partial(out_kernel, len(earlier), picked),
        tuple(jax.ShapeDtypeStruct((many, planes * 4 * wide), dtype) for many in counts),
        24,
        flops=4 * sum(counts) * block * planes * 16 * wide,
        moved_bytes=16 * planes * block * wide,
        grid=(planes // at_once,),
        in_specs=[pl.BlockSpec(memory_space=pltpu.SMEM), whole, whole]
        + halves * 8
        + [pl.BlockSpec(memory_space=pltpu.HBM)] * len(earlier),
        out_specs=tuple(pl.BlockSpec((many, columns), lambda i: (0, i)) for many in counts),
        scratch_shapes=[pltpu.VMEM((4 * block, columns), jnp.bfloat16)],
    )(
        x.astype(jnp.int32).reshape(1),
        mine,
        theirs,
        *[weight for weight in weights for _ in range(2)],
        *earlier,
    )


def added_kernel(a, b, c, d, first, second):
    first[...] = (a[...] + b[...].astype(jnp.float32)).astype(first.dtype)
    second[...] = (c[...] + d[...].astype(jnp.float32)).astype(second.dtype)


def added(a, b, b_half, c, d, d_half):
    whole = pl.BlockSpec(a.shape, lambda i: (0, 0))
    return local(
        added_kernel,
        (jax.ShapeDtypeStruct(a.shape, b.dtype),) * 2,
        20,
        grid=(1,),
        in_specs=[
            whole,
            pl.BlockSpec(a.shape, lambda i: (b_half, 0)),
            whole,
            pl.BlockSpec(a.shape, lambda i: (d_half, 0)),
        ],
        out_specs=(whole, whole),
    )(a, b, c, d)


def features_kernel(
    tokens, own, low_a, high_a, low_b, high_b, weight, features, descriptor, total
):
    step = pl.program_id(0)
    summed = own[...]
    summed = summed + jnp.concatenate([low_a[...], high_a[...]], axis=0).astype(jnp.float32)
    summed = summed + jnp.concatenate([low_b[...], high_b[...]], axis=0).astype(jnp.float32)
    rounded = (tokens[...].astype(jnp.float32) + summed).astype(jnp.bfloat16)
    features[...] = rounded
    planes, cores, highs = weight.shape[:3]
    blocks = [weight[p, c, h] for p in range(planes) for h in range(highs) for c in range(cores)]
    term = dot(rounded, jnp.concatenate(blocks, axis=0))

    @pl.when(step == 0)
    def _():
        total[...] = term

    @pl.when(step > 0)
    def _():
        total[...] += term

    @pl.when(step == pl.num_programs(0) - 1)
    def _():
        descriptor[...] = total[...].astype(jnp.bfloat16)


def features_and_descriptor(tokens, own, halves, weight):
    rows, depth = tokens.shape
    width = weight.shape[-1]
    wide = 1024
    whole = pl.BlockSpec((rows, wide), lambda i: (0, i))
    half = pl.BlockSpec((rows // 2, wide), lambda i: (0, i))
    second_half = pl.BlockSpec((rows // 2, wide), lambda i: (1, i))
    return local(
        features_kernel,
        (
            jax.ShapeDtypeStruct((rows, depth), jnp.bfloat16),
            jax.ShapeDtypeStruct((rows, width), jnp.bfloat16),
        ),
        20,
        grid=(depth // wide,),
        in_specs=[whole, whole, half, half, second_half, half]
        + [pl.BlockSpec((2,) + weight.shape[1:], lambda i: (i, 0, 0, 0, 0))],
        out_specs=(whole, pl.BlockSpec((rows, width), lambda i: (0, 0))),
        scratch_shapes=[pltpu.VMEM((rows, width), jnp.float32)],
    )(tokens, own, *halves, weight)


def matcher_kernel(*refs):
    descriptor, qkv, out_weight, *pieces, matched, keys, values, mixed = refs
    rows, width = descriptor.shape
    bf16 = jnp.bfloat16
    queries = dot(descriptor[...], qkv[:, :width]).astype(bf16)
    at = 0
    for piece in pieces:
        count = piece.shape[0]
        keys[at : at + count, :] = dot(piece[...], qkv[:, width : 2 * width]).astype(bf16)
        values[at : at + count, :] = dot(piece[...], qkv[:, 2 * width :]).astype(bf16)
        at += count
    head_width = width // MATCH_HEADS
    pair = 2 * head_width
    low = lax.broadcasted_iota(jnp.int32, (rows, pair), 1) < head_width
    for first in range(0, width, pair):
        span = slice(first, first + pair)
        two = queries[:, span]
        results = []
        for chosen in (low, jnp.logical_not(low)):
            asked = jnp.where(chosen, two, jnp.zeros_like(two))
            scale = 1.0 / math.sqrt(head_width)
            results.append(attend(asked, keys[:, span], values[:, span], scale))
        mixed[:, span] = jnp.where(low, results[0], results[1]).astype(bf16)
    matched[...] = (descriptor[...].astype(jnp.float32) + dot(mixed[...], out_weight[...])).astype(
        bf16
    )


def match(descriptor, pieces, qkv, out_weight):
    count = sum(piece.shape[0] for piece in pieces)
    width = descriptor.shape[1]
    return local(
        matcher_kernel,
        jax.ShapeDtypeStruct(descriptor.shape, jnp.bfloat16),
        24,
        scratch_shapes=[
            pltpu.VMEM((count, width), jnp.bfloat16),
            pltpu.VMEM((count, width), jnp.bfloat16),
            pltpu.VMEM(descriptor.shape, jnp.bfloat16),
        ],
    )(descriptor, qkv, out_weight, *pieces)


def per_device(
    tokens, norm_gain, norm_bias, qkv_weight, out_weight, match_weight, matcher_qkv, matcher_out
):
    bf16, f32 = jnp.bfloat16, jnp.float32
    z, core = lax.axis_index("z"), lax.axis_index("core")
    x = lax.axis_index("xh") * 2 + lax.axis_index("xl")
    width = matcher_out.shape[0]
    rows, features_width = tokens.shape
    mid = rows // 2

    block, wide = qkv_weight.shape[0], out_weight.shape[1]
    packed = qkv_weight.reshape(block, -1, wide).transpose(1, 0, 2).reshape(-1, wide)
    packed = swapped_roles(jnp.concatenate([packed, out_weight], axis=0))
    tokens = swapped_roles(tokens)
    early = 5 * block
    early_ones = gathered_x(packed[:early], x, 0)
    first = lax.all_gather(early_ones, "z", axis=0, tiled=True)
    first = first.reshape(8, 4, 5, block, wide)

    normed = layer_norm(tokens, norm_gain, norm_bias)
    pieces = [normed] + [moved(normed, along_y(k)) for k in DISTANCES]
    pieces = list(together(*pieces, flops=WAIT))
    pieces += [moved(piece, other_core) for piece in pieces]
    later = gathered_z(packed[early:], z, early_ones).reshape(8, 3, block, wide)
    parts = along_x_parts(later)
    parts += [moved(part, other_core) for part in parts]
    together_now = together(*pieces, *parts)
    pieces, parts = together_now[:8], together_now[8:]
    mine, theirs = attention(x, pieces, first, parts[:4])

    match_weight = after(match_weight, parts[0])
    other_half = moved(match_weight, lambda p: {"xh": 1 - p["xh"], "xl": 1 - p["xl"]})
    match_pair = jnp.where(
        lax.axis_index("xh") == 0,
        jnp.concatenate([match_weight, other_half], axis=0),
        jnp.concatenate([other_half, match_weight], axis=0),
    )
    match_all = lax.all_gather(match_pair, ("z", "core"), axis=0, tiled=True)
    match_all = match_all.reshape(8, 2, 2, match_weight.shape[0], width)

    both = (x, mine, moved(theirs, other_core), parts)
    up, down = out_projection(
        *both, [[(2 * rows + mid, rows)], [(3 * rows + mid, mid), (rows, mid)]], bf16
    )
    own, down_high, up_low = out_projection(
        *both, [[(0, rows)], [(rows + mid, mid)], [(2 * rows, mid)]], f32, [up, down]
    )
    up, down = moved(up, along_y(1)), moved(down, along_y(-1))
    up_low, down_high = added(up_low, up, 1, down_high, down, 0)
    up_low, down_high = moved(up_low, along_y(1)), moved(down_high, along_y(-1))

    features, descriptor = features_and_descriptor(
        tokens, own, (up_low, up, down, down_high), match_all
    )
    partner = moved(descriptor, along_z(4))
    quarter = jnp.concatenate([partner] + [moved(partner, along_y(k)) for k in DISTANCES], axis=0)
    pieces = [quarter, moved(quarter, other_core)]
    matched = match(descriptor, pieces, matcher_qkv, matcher_out)
    return (swapped_roles(features), swapped_roles(matched))


def solution(mesh):
    fine = Mesh(mesh.devices.reshape(SIZES), AXES)
    dp, tensor = ("z", "xh", "core"), ("xl", "y")
    return jax.shard_map(
        per_device,
        mesh=fine,
        in_specs=(
            P(AXES, None),
            P(),
            P(),
            P(dp, tensor),
            P(tensor, dp),
            P(dp, None),
            P(),
            P(),
        ),
        out_specs=(P(AXES, None), P(AXES, None)),
        check_vma=False,
    )
```

profile of v0, /device:TPU:1, one launch (start us, length us, event | category | flops | bytes accessed | tf_op | source)
XLA Modules:
  0.0 260.2 jit_solution(15371882003317268061)
XLA Ops:
  8.1 1.1 copy.43
  10.4 4.5 %collective-permute-start.8 = (bf16[1024,128]{1,0:T(8,128)(2,1)S(1)}, bf16[1024,128]{1,0:T(8,128)(2,1)S(1)}, u32[]{:S(2)}, u32[]{:S(2)}) collective-permute-start(bf16[1024,128]{1,0:T(8,128)(2,1)S(1)} %pad_maximum_fusion), channel_id=1, source_target_pairs={{0,0},{1,1},{2,2},{3,3},{4,8},{5,9},{6,10},{7,11},{8,4},{9,5},{10,... | collective-permute-start | bytes 786440 | tf_op jit(solution)/shard_map/ppermute | solution.py:33
  14.9 4.0 %collective-permute-done.8 = bf16[1024,128]{1,0:T(8,128)(2,1)S(1)} collective-permute-done((bf16[1024,128]{1,0:T(8,128)(2,1)S(1)}, bf16[1024,128]{1,0:T(8,128)(2,1)S(1)}, u32[]{:S(2)}, u32[]{:S(2)}) %collective-permute-start.8) | collective-permute-done | bytes 262176 | tf_op jit(solution)/shard_map/ppermute | solution.py:33
  19.0 2.7 %collective-permute-start.11 = (bf16[640,128]{1,0:T(8,128)(2,1)S(1)}, bf16[640,128]{1,0:T(8,128)(2,1)S(1)}, u32[]{:S(2)}, u32[]{:S(2)}) collective-permute-start(bf16[640,128]{1,0:T(8,128)(2,1)S(1)} %slice.9), channel_id=1, source_target_pairs={{0,20},{1,21},{2,22},{3,23},{4,0},{5,1},{6,2},{7,3},{8,28},{9,29},... | collective-permute-start | bytes 491528 | tf_op jit(solution)/shard_map/ppermute | solution.py:33
  21.7 1.5 collective-permute-start.12
  23.3 2.6 collective-permute-done.10
  25.9 3.5 %collective-permute-done.12 = bf16[640,128]{1,0:T(8,128)(2,1)S(1)} collective-permute-done((bf16[640,128]{1,0:T(8,128)(2,1)S(1)}, bf16[640,128]{1,0:T(8,128)(2,1)S(1)}, u32[]{:S(2)}, u32[]{:S(2)}) %collective-permute-start.12) | collective-permute-done | bytes 163872 | tf_op jit(solution)/shard_map/ppermute | solution.py:33
  30.4 4.0 %collective-permute-start = (bf16[128,4096]{1,0:T(8,128)(2,1)S(1)}, bf16[128,4096]{1,0:T(8,128)(2,1)S(1)}, u32[]{:S(2)}, u32[]{:S(2)}) collective-permute-start(bf16[128,4096]{1,0:T(8,128)(2,1)S(1)} %copy-done.37), channel_id=1, source_target_pairs={{0,0},{1,1},{2,2},{3,3},{4,8},{5,9},{6,10},{7,11},{8,4},{9,5},{10,... | collective-permute-start | bytes 3145736 | tf_op jit(solution)/shard_map/ppermute | solution.py:33
  34.4 7.0 %collective-permute-start.9 = (bf16[384,128]{1,0:T(8,128)(2,1)S(1)}, bf16[384,128]{1,0:T(8,128)(2,1)S(1)}, u32[]{:S(2)}, u32[]{:S(2)}) collective-permute-start(bf16[384,128]{1,0:T(8,128)(2,1)S(1)} %get-tuple-element.65), channel_id=1, source_target_pairs={{0,128},{1,129},{2,130},{3,131},{4,132},{5,133},{6,134},{7,135},{8... | collective-permute-start | bytes 294920 | tf_op jit(solution)/shard_map/ppermute | solution.py:33
  41.4 2.8 %collective-permute-done.9 = bf16[384,128]{1,0:T(8,128)(2,1)S(1)} collective-permute-done((bf16[384,128]{1,0:T(8,128)(2,1)S(1)}, bf16[384,128]{1,0:T(8,128)(2,1)S(1)}, u32[]{:S(2)}, u32[]{:S(2)}) %collective-permute-start.9) | collective-permute-done | bytes 98336 | tf_op jit(solution)/shard_map/ppermute | solution.py:33
  44.2 1.1 copy-done.11
  45.2 2.1 collective-permute-start.13
  47.4 1.9 collective-permute-start.14
  49.5 9.1 %collective-permute-done.13 = bf16[2,384,128]{2,1,0:T(8,128)(2,1)S(1)} collective-permute-done((bf16[2,384,128]{2,1,0:T(8,128)(2,1)S(1)}, bf16[2,384,128]{2,1,0:T(8,128)(2,1)S(1)}, u32[]{:S(2)}, u32[]{:S(2)}) %collective-permute-start.13) | collective-permute-done | bytes 196640 | tf_op jit(solution)/shard_map/ppermute | solution.py:33
  59.9 1.4 collective-permute-start.1
  61.3 1.6 collective-permute-start.2
  62.9 1.6 collective-permute-start.3
  64.5 3.7 %collective-permute-done.15 = bf16[2,384,128]{2,1,0:T(8,128)(2,1)S(1)} collective-permute-done((bf16[2,384,128]{2,1,0:T(8,128)(2,1)S(1)}, bf16[2,384,128]{2,1,0:T(8,128)(2,1)S(1)}, u32[]{:S(2)}, u32[]{:S(2)}) %collective-permute-start.15) | collective-permute-done | bytes 196640 | tf_op jit(solution)/shard_map/ppermute | solution.py:33
  68.4 2.7 %collective-permute-start.17 = (bf16[8,3,128,128]{3,2,1,0:T(8,128)(2,1)S(1)}, bf16[8,3,128,128]{3,2,1,0:T(8,128)(2,1)S(1)}, u32[]{:S(2)}, u32[]{:S(2)}) collective-permute-start(bf16[8,3,128,128]{3,2,1,0:T(8,128)(2,1)S(1)} %bitcast.44), channel_id=1, source_target_pairs={{0,20},{1,21},{2,22},{3,23},{4,0},{5,1},{6,2},{7,3},{8,28},{9,29},... | collective-permute-start | bytes 2359304 | tf_op jit(solution)/shard_map/ppermute | solution.py:33
  71.1 17.4 %collective-permute-done.16.refs_9_ = bf16[8,3,128,128]{3,2,1,0:T(8,128)(2,1)S(1)} collective-permute-done((bf16[8,3,128,128]{3,2,1,0:T(8,128)(2,1)S(1)}, bf16[8,3,128,128]{3,2,1,0:T(8,128)(2,1)S(1)}, u32[]{:S(2)}, u32[]{:S(2)}) %collective-permute-start.16) | collective-permute-done | bytes 786464 | tf_op jit(solution)/shard_map/ppermute | solution.py:33
  88.4 1.1 collective-permute-start.19
  89.7 19.1 %collective-permute-start.21 = (bf16[8,3,128,128]{3,2,1,0:T(8,128)(2,1)S(1)}, bf16[8,3,128,128]{3,2,1,0:T(8,128)(2,1)S(1)}, u32[]{:S(2)}, u32[]{:S(2)}) collective-permute-start(bf16[8,3,128,128]{3,2,1,0:T(8,128)(2,1)S(1)} %collective-permute-done.17.refs_10_), channel_id=1, source_target_pairs={{0,8},{1,9},{2,10},{3,11},{4,12},{5,13},{6,14},{7,15},{8,0},{9,1},... | collective-permute-start | bytes 2359304 | tf_op jit(solution)/shard_map/ppermute | solution.py:33
  108.8 1.1 collective-permute-done.3.refs_3_
  111.6 6.9 %collective-permute-done.22.refs_15_ = bf16[8,3,128,128]{3,2,1,0:T(8,128)(2,1)S(1)} collective-permute-done((bf16[8,3,128,128]{3,2,1,0:T(8,128)(2,1)S(1)}, bf16[8,3,128,128]{3,2,1,0:T(8,128)(2,1)S(1)}, u32[]{:S(2)}, u32[]{:S(2)}) %collective-permute-start.22) | collective-permute-done | bytes 786464 | tf_op jit(solution)/shard_map/ppermute | solution.py:33
  122.1 1.0 copy-done.12
  123.1 1.0 copy-done.24
  125.1 1.0 copy-done.28
  126.0 1.0 copy-done.30
  127.0 1.0 copy-done.32
  128.0 1.0 copy-done.33
  129.0 1.0 copy-done.22
  130.0 5.9 %collective-permute-done.28 = bf16[128,512]{1,0:T(8,128)(2,1)S(1)} collective-permute-done((bf16[128,512]{1,0:T(8,128)(2,1)S(1)}, bf16[128,512]{1,0:T(8,128)(2,1)S(1)}, u32[]{:S(2)}, u32[]{:S(2)}) %collective-permute-start.28) | collective-permute-done | bytes 131104 | tf_op jit(solution)/shard_map/ppermute | solution.py:33
  136.7 1.2 copy-done.13
  138.0 1.2 copy-done.23
  139.2 1.2 copy-done.25
  140.4 1.2 copy-done.27
  141.6 1.2 copy-done.29
  142.9 1.2 copy-done.31
  144.1 15.4 %shard_map.98 = (bf16[512,256]{1,0:T(8,128)(2,1)S(1)}, bf16[512,256]{1,0:T(8,128)(2,1)S(1)}) custom-call(s32[1]{0:T(128)} %bitcast.refs_0_.place, bf16[128,4096]{1,0:T(8,128)(2,1)S(1)} %copy-done.13, bf16[128,4096]{1,0:T(8,128)(2,1)S(1)} %copy-done.25, bf16[128,4096]{1,0:T(8,128)(2,1)S(1)} %copy-done.27, bf16[128,4096]{1,0:T(8,128)(2,1)S(1)} %copy-done.31, ...), custom_call_target="tpu_custom_call" | custom-call | flops 6442450944 | bytes 14680064 | tf_op jit(solution)/shard_map/pallas_call | solution.py:236
  159.5 1.3 collective-permute-start.23
  160.8 1.2 collective-permute-done.23.theirs
  162.0 3.5 %shard_map.99 = (bf16[128,4096]{1,0:T(8,128)(2,1)S(1)}, bf16[128,4096]{1,0:T(8,128)(2,1)S(1)}) custom-call(s32[1]{0:T(128)} %bitcast.refs_0_.place, bf16[512,256]{1,0:T(8,128)(2,1)S(1)} %get-tuple-element.49.mine, bf16[512,256]{1,0:T(8,128)(2,1)S(1)} %collective-permute-done.23.theirs, ...), custom_call_target="tpu_custom_call" | custom-call | flops 2147483648 | bytes 2097152 | tf_op jit(solution)/shard_map/pallas_call | solution.py:283
  165.5 1.2 collective-permute-start.24
  166.7 1.9 collective-permute-start.25
  168.6 3.6 %shard_map.100 = (f32[128,4096]{1,0:T(8,128)S(1)}, f32[64,4096]{1,0:T(8,128)S(1)}, f32[64,4096]{1,0:T(8,128)S(1)}) custom-call(s32[1]{0:T(128)} %bitcast.refs_0_.place, bf16[512,256]{1,0:T(8,128)(2,1)S(1)} %get-tuple-element.49.mine, bf16[512,256]{1,0:T(8,128)(2,1)S(1)} %collective-permute-done.23.theirs, ...), custom_call_target="tpu_custom_call" | custom-call | flops 2147483648 | bytes 2097152 | tf_op jit(solution)/shard_map/pallas_call | solution.py:283
  172.2 19.2 %collective-permute-done.24.b.high_a = bf16[128,4096]{1,0:T(8,128)(2,1)S(1)} collective-permute-done((bf16[128,4096]{1,0:T(8,128)(2,1)S(1)}, bf16[128,4096]{1,0:T(8,128)(2,1)S(1)}, u32[]{:S(2)}, u32[]{:S(2)}) %collective-permute-start.24) | collective-permute-done | bytes 1048608 | tf_op jit(solution)/shard_map/ppermute | solution.py:33
  193.2 2.3 collective-permute-start.27
  195.5 10.8 %collective-permute-done.26.low_a = bf16[64,4096]{1,0:T(8,128)(2,1)S(1)} collective-permute-done((bf16[64,4096]{1,0:T(8,128)(2,1)S(1)}, bf16[64,4096]{1,0:T(8,128)(2,1)S(1)}, u32[]{:S(2)}, u32[]{:S(2)}) %collective-permute-start.26) | collective-permute-done | bytes 524320 | tf_op jit(solution)/shard_map/ppermute | solution.py:33
  206.3 2.2 copy-done.14
  208.5 1.2 copy-done.16
  209.7 1.2 copy-done.18
  210.9 1.6 copy-done.20
  212.5 1.9 shard_map.103
  214.4 7.4 %collective-permute-start.30 = (bf16[128,512]{1,0:T(8,128)(2,1)S(1)}, bf16[128,512]{1,0:T(8,128)(2,1)S(1)}, u32[]{:S(2)}, u32[]{:S(2)}) collective-permute-start(bf16[128,512]{1,0:T(8,128)(2,1)S(1)} %get-tuple-element.63.refs_0_), channel_id=1, source_target_pairs={{0,128},{1,129},{2,130},{3,131},{4,132},{5,133},{6,134},{7,135},{8... | collective-permute-start | bytes 393224 | tf_op jit(solution)/shard_map/ppermute | solution.py:33
  221.9 5.5 %collective-permute-done.30 = bf16[128,512]{1,0:T(8,128)(2,1)S(1)} collective-permute-done((bf16[128,512]{1,0:T(8,128)(2,1)S(1)}, bf16[128,512]{1,0:T(8,128)(2,1)S(1)}, u32[]{:S(2)}, u32[]{:S(2)}) %collective-permute-start.30) | collective-permute-done | bytes 131104 | tf_op jit(solution)/shard_map/ppermute | solution.py:33
  227.4 1.9 collective-permute-start.29
  229.3 2.8 %collective-permute-start.32 = (bf16[128,512]{1,0:T(8,128)(2,1)S(1)}, bf16[128,512]{1,0:T(8,128)(2,1)S(1)}, u32[]{:S(2)}, u32[]{:S(2)}) collective-permute-start(bf16[128,512]{1,0:T(8,128)(2,1)S(1)} %collective-permute-done.30), channel_id=1, source_target_pairs={{0,3},{1,0},{2,1},{3,2},{4,7},{5,4},{6,5},{7,6},{8,11},{9,8},{10,9... | collective-permute-start | bytes 393224 | tf_op jit(solution)/shard_map/ppermute | solution.py:33
  232.8 3.0 %collective-permute-done.32 = bf16[128,512]{1,0:T(8,128)(2,1)S(1)} collective-permute-done((bf16[128,512]{1,0:T(8,128)(2,1)S(1)}, bf16[128,512]{1,0:T(8,128)(2,1)S(1)}, u32[]{:S(2)}, u32[]{:S(2)}) %collective-permute-start.32) | collective-permute-done | bytes 131104 | tf_op jit(solution)/shard_map/ppermute | solution.py:33
  235.8 2.0 collective-permute-done.33
  237.9 1.8 collective-permute-start.34
  239.7 1.5 collective-permute-done.34.refs_4_
  241.2 4.2 %shard_map.104 = bf16[128,512]{1,0:T(8,128)(2,1)S(1)} custom-call(bf16[128,512]{1,0:T(8,128)(2,1)S(1)} %get-tuple-element.63.refs_0_, bf16[512,1536]{1,0:T(8,128)(2,1)S(1)} %copy-done.21, bf16[512,512]{1,0:T(8,128)(2,1)S(1)} %copy-done.34, bf16[512,512]{1,0:T(8,128)(2,1)S(1)} %constant_dynamic-update-slice_fusion.refs_3_, ...), custom_call_target="tpu_custom_call" | custom-call | tf_op jit(solution)/shard_map/pallas_call | solution.py:405
  245.4 3.3 %collective-permute-start.35 = (bf16[128,512]{1,0:T(8,128)(2,1)S(1)}, bf16[128,512]{1,0:T(8,128)(2,1)S(1)}, u32[]{:S(2)}, u32[]{:S(2)}) collective-permute-start(bf16[128,512]{1,0:T(8,128)(2,1)S(1)} %shard_map.104), channel_id=1, source_target_pairs={{0,0},{1,1},{2,2},{3,3},{4,8},{5,9},{6,10},{7,11},{8,4},{9,5},{10,... | collective-permute-start | bytes 393224 | tf_op jit(solution)/shard_map/ppermute | solution.py:33
  248.8 2.9 %collective-permute-done.35 = bf16[128,512]{1,0:T(8,128)(2,1)S(1)} collective-permute-done((bf16[128,512]{1,0:T(8,128)(2,1)S(1)}, bf16[128,512]{1,0:T(8,128)(2,1)S(1)}, u32[]{:S(2)}, u32[]{:S(2)}) %collective-permute-start.35) | collective-permute-done | bytes 131104 | tf_op jit(solution)/shard_map/ppermute | solution.py:33
  (129 shorter events, 16.3 us)
Async XLA Ops:
  7.2 129.6 %all-gather.3.cloned.1.call-start = ((), (), s32[]{:S(2)}) async-start(), calls=%async_computation | async-start | bytes 5898240 | tf_op jit(solution)/shard_map/all_gather | solution.py:433
  9.2 21.2 %copy-start.37 = (bf16[128,4096]{1,0:T(8,128)(2,1)S(1)}, bf16[128,4096]{1,0:T(8,128)(2,1)}, u32[]{:S(2)}) copy-start(bf16[128,4096]{1,0:T(8,128)(2,1)} %param.8) | copy-start | bytes 3145732
  10.4 8.6 %collective-permute-start.8 = (bf16[1024,128]{1,0:T(8,128)(2,1)S(1)}, bf16[1024,128]{1,0:T(8,128)(2,1)S(1)}, u32[]{:S(2)}, u32[]{:S(2)}) collective-permute-start(bf16[1024,128]{1,0:T(8,128)(2,1)S(1)} %pad_maximum_fusion), channel_id=1, source_target_pairs={{0,0},{1,1},{2,2},{3,3},{4,8},{5,9},{6,10},{7,11},{8,4},{9,5},{10,... | collective-permute-start | bytes 786440 | tf_op jit(solution)/shard_map/ppermute | solution.py:33
  18.9 6.9 %collective-permute-start.10 = (bf16[640,128]{1,0:T(8,128)(2,1)S(1)}, bf16[640,128]{1,0:T(8,128)(2,1)S(1)}, u32[]{:S(2)}, u32[]{:S(2)}) collective-permute-start(bf16[640,128]{1,0:T(8,128)(2,1)S(1)} %slice.9), channel_id=1, source_target_pairs={{0,4},{1,5},{2,6},{3,7},{4,16},{5,17},{6,18},{7,19},{8,12},{9,13},... | collective-permute-start | bytes 491528 | tf_op jit(solution)/shard_map/ppermute | solution.py:33
  19.0 6.9 %collective-permute-start.11 = (bf16[640,128]{1,0:T(8,128)(2,1)S(1)}, bf16[640,128]{1,0:T(8,128)(2,1)S(1)}, u32[]{:S(2)}, u32[]{:S(2)}) collective-permute-start(bf16[640,128]{1,0:T(8,128)(2,1)S(1)} %slice.9), channel_id=1, source_target_pairs={{0,20},{1,21},{2,22},{3,23},{4,0},{5,1},{6,2},{7,3},{8,28},{9,29},... | collective-permute-start | bytes 491528 | tf_op jit(solution)/shard_map/ppermute | solution.py:33
  21.7 7.7 %collective-permute-start.12 = (bf16[640,128]{1,0:T(8,128)(2,1)S(1)}, bf16[640,128]{1,0:T(8,128)(2,1)S(1)}, u32[]{:S(2)}, u32[]{:S(2)}) collective-permute-start(bf16[640,128]{1,0:T(8,128)(2,1)S(1)} %slice.9), channel_id=1, source_target_pairs={{0,16},{1,17},{2,18},{3,19},{4,20},{5,21},{6,22},{7,23},{8,24},{9,... | collective-permute-start | bytes 491528 | tf_op jit(solution)/shard_map/ppermute | solution.py:33
  30.3 165.2 %all-gather.5.cloned.1.call-start = ((), (), s32[]{:S(2)}) async-start(), calls=%async_computation.1 | async-start | bytes 4456448 | tf_op jit(solution)/shard_map/all_gather | solution.py:454
  30.4 28.3 %collective-permute-start = (bf16[128,4096]{1,0:T(8,128)(2,1)S(1)}, bf16[128,4096]{1,0:T(8,128)(2,1)S(1)}, u32[]{:S(2)}, u32[]{:S(2)}) collective-permute-start(bf16[128,4096]{1,0:T(8,128)(2,1)S(1)} %copy-done.37), channel_id=1, source_target_pairs={{0,0},{1,1},{2,2},{3,3},{4,8},{5,9},{6,10},{7,11},{8,4},{9,5},{10,... | collective-permute-start | bytes 3145736 | tf_op jit(solution)/shard_map/ppermute | solution.py:33
  34.4 9.8 %collective-permute-start.9 = (bf16[384,128]{1,0:T(8,128)(2,1)S(1)}, bf16[384,128]{1,0:T(8,128)(2,1)S(1)}, u32[]{:S(2)}, u32[]{:S(2)}) collective-permute-start(bf16[384,128]{1,0:T(8,128)(2,1)S(1)} %get-tuple-element.65), channel_id=1, source_target_pairs={{0,128},{1,129},{2,130},{3,131},{4,132},{5,133},{6,134},{7,135},{8... | collective-permute-start | bytes 294920 | tf_op jit(solution)/shard_map/ppermute | solution.py:33
  44.2 1.1 copy-start.11
  45.2 14.1 %copy-start.35 = (f32[4096]{0:T(1024)S(1)}, f32[4096]{0:T(1024)}, u32[]{:S(2)}) copy-start(f32[4096]{0:T(1024)} %param.10) | copy-start | bytes 49156
  45.2 14.1 %copy-start.36 = (f32[4096]{0:T(1024)S(1)}, f32[4096]{0:T(1024)}, u32[]{:S(2)}) copy-start(f32[4096]{0:T(1024)} %param.9) | copy-start | bytes 49156
  45.2 13.3 %collective-permute-start.13 = (bf16[2,384,128]{2,1,0:T(8,128)(2,1)S(1)}, bf16[2,384,128]{2,1,0:T(8,128)(2,1)S(1)}, u32[]{:S(2)}, u32[]{:S(2)}) collective-permute-start(bf16[2,384,128]{2,1,0:T(8,128)(2,1)S(1)} %shard_map.96), channel_id=1, source_target_pairs={{0,32},{1,33},{2,34},{3,35},{4,36},{5,37},{6,38},{7,39},{8,40},{9,... | collective-permute-start | bytes 589832 | tf_op jit(solution)/shard_map/ppermute | solution.py:33
  47.4 17.0 %collective-permute-start.14 = (bf16[2,384,128]{2,1,0:T(8,128)(2,1)S(1)}, bf16[2,384,128]{2,1,0:T(8,128)(2,1)S(1)}, u32[]{:S(2)}, u32[]{:S(2)}) collective-permute-start(bf16[2,384,128]{2,1,0:T(8,128)(2,1)S(1)} %shard_map.96), channel_id=1, source_target_pairs={{0,224},{1,225},{2,226},{3,227},{4,228},{5,229},{6,230},{7,231},{8... | collective-permute-start | bytes 589832 | tf_op jit(solution)/shard_map/ppermute | solution.py:33
  49.3 19.0 %collective-permute-start.15 = (bf16[2,384,128]{2,1,0:T(8,128)(2,1)S(1)}, bf16[2,384,128]{2,1,0:T(8,128)(2,1)S(1)}, u32[]{:S(2)}, u32[]{:S(2)}) collective-permute-start(bf16[2,384,128]{2,1,0:T(8,128)(2,1)S(1)} %shard_map.96), channel_id=1, source_target_pairs={{0,64},{1,65},{2,66},{3,67},{4,68},{5,69},{6,70},{7,71},{8,72},{9,... | collective-permute-start | bytes 589832 | tf_op jit(solution)/shard_map/ppermute | solution.py:33
  58.7 1.2 copy-start.8
  59.9 29.7 %collective-permute-start.1 = (bf16[128,4096]{1,0:T(8,128)(2,1)S(1)}, bf16[128,4096]{1,0:T(8,128)(2,1)S(1)}, u32[]{:S(2)}, u32[]{:S(2)}) collective-permute-start(bf16[128,4096]{1,0:T(8,128)(2,1)S(1)} %fusion.5.refs_0_), channel_id=1, source_target_pairs={{0,1},{1,2},{2,3},{3,0},{4,5},{5,6},{6,7},{7,4},{8,9},{9,10},{10,1... | collective-permute-start | bytes 3145736 | tf_op jit(solution)/shard_map/ppermute | solution.py:33
  61.3 28.4 %collective-permute-start.2 = (bf16[128,4096]{1,0:T(8,128)(2,1)S(1)}, bf16[128,4096]{1,0:T(8,128)(2,1)S(1)}, u32[]{:S(2)}, u32[]{:S(2)}) collective-permute-start(bf16[128,4096]{1,0:T(8,128)(2,1)S(1)} %fusion.5.refs_0_), channel_id=1, source_target_pairs={{0,3},{1,0},{2,1},{3,2},{4,7},{5,4},{6,5},{7,6},{8,11},{9,8},{10,9... | collective-permute-start | bytes 3145736 | tf_op jit(solution)/shard_map/ppermute | solution.py:33
  62.9 47.0 %collective-permute-start.3 = (bf16[128,4096]{1,0:T(8,128)(2,1)S(1)}, bf16[128,4096]{1,0:T(8,128)(2,1)S(1)}, u32[]{:S(2)}, u32[]{:S(2)}) collective-permute-start(bf16[128,4096]{1,0:T(8,128)(2,1)S(1)} %fusion.5.refs_0_), channel_id=1, source_target_pairs={{0,2},{1,3},{2,0},{3,1},{4,6},{5,7},{6,4},{7,5},{8,10},{9,11},{10,... | collective-permute-start | bytes 3145736 | tf_op jit(solution)/shard_map/ppermute | solution.py:33
  68.3 20.1 %collective-permute-start.16 = (bf16[8,3,128,128]{3,2,1,0:T(8,128)(2,1)S(1)}, bf16[8,3,128,128]{3,2,1,0:T(8,128)(2,1)S(1)}, u32[]{:S(2)}, u32[]{:S(2)}) collective-permute-start(bf16[8,3,128,128]{3,2,1,0:T(8,128)(2,1)S(1)} %bitcast.43), channel_id=1, source_target_pairs={{0,4},{1,5},{2,6},{3,7},{4,16},{5,17},{6,18},{7,19},{8,12},{9,13},... | collective-permute-start | bytes 2359304 | tf_op jit(solution)/shard_map/ppermute | solution.py:33
  68.4 20.0 %collective-permute-start.17 = (bf16[8,3,128,128]{3,2,1,0:T(8,128)(2,1)S(1)}, bf16[8,3,128,128]{3,2,1,0:T(8,128)(2,1)S(1)}, u32[]{:S(2)}, u32[]{:S(2)}) collective-permute-start(bf16[8,3,128,128]{3,2,1,0:T(8,128)(2,1)S(1)} %bitcast.44), channel_id=1, source_target_pairs={{0,20},{1,21},{2,22},{3,23},{4,0},{5,1},{6,2},{7,3},{8,28},{9,29},... | collective-permute-start | bytes 2359304 | tf_op jit(solution)/shard_map/ppermute | solution.py:33
  88.4 22.1 %collective-permute-start.18 = (bf16[8,3,128,128]{3,2,1,0:T(8,128)(2,1)S(1)}, bf16[8,3,128,128]{3,2,1,0:T(8,128)(2,1)S(1)}, u32[]{:S(2)}, u32[]{:S(2)}) collective-permute-start(bf16[8,3,128,128]{3,2,1,0:T(8,128)(2,1)S(1)} %bitcast.45), channel_id=1, source_target_pairs={{0,16},{1,17},{2,18},{3,19},{4,20},{5,21},{6,22},{7,23},{8,24},{9,... | collective-permute-start | bytes 2359304 | tf_op jit(solution)/shard_map/ppermute | solution.py:33
  88.4 22.2 %collective-permute-start.19 = (bf16[8,3,128,128]{3,2,1,0:T(8,128)(2,1)S(1)}, bf16[8,3,128,128]{3,2,1,0:T(8,128)(2,1)S(1)}, u32[]{:S(2)}, u32[]{:S(2)}) collective-permute-start(bf16[8,3,128,128]{3,2,1,0:T(8,128)(2,1)S(1)} %bitcast.46), channel_id=1, source_target_pairs={{0,8},{1,9},{2,10},{3,11},{4,12},{5,13},{6,14},{7,15},{8,0},{9,1},... | collective-permute-start | bytes 2359304 | tf_op jit(solution)/shard_map/ppermute | solution.py:33
  89.6 21.5 %collective-permute-start.20 = (bf16[8,3,128,128]{3,2,1,0:T(8,128)(2,1)S(1)}, bf16[8,3,128,128]{3,2,1,0:T(8,128)(2,1)S(1)}, u32[]{:S(2)}, u32[]{:S(2)}) collective-permute-start(bf16[8,3,128,128]{3,2,1,0:T(8,128)(2,1)S(1)} %collective-permute-done.16.refs_9_), channel_id=1, source_target_pairs={{0,8},{1,9},{2,10},{3,11},{4,12},{5,13},{6,14},{7,15},{8,0},{9,1},... | collective-permute-start | bytes 2359304 | tf_op jit(solution)/shard_map/ppermute | solution.py:33
  89.7 21.5 %collective-permute-start.21 = (bf16[8,3,128,128]{3,2,1,0:T(8,128)(2,1)S(1)}, bf16[8,3,128,128]{3,2,1,0:T(8,128)(2,1)S(1)}, u32[]{:S(2)}, u32[]{:S(2)}) collective-permute-start(bf16[8,3,128,128]{3,2,1,0:T(8,128)(2,1)S(1)} %collective-permute-done.17.refs_10_), channel_id=1, source_target_pairs={{0,8},{1,9},{2,10},{3,11},{4,12},{5,13},{6,14},{7,15},{8,0},{9,1},... | collective-permute-start | bytes 2359304 | tf_op jit(solution)/shard_map/ppermute | solution.py:33
  109.8 8.6 %collective-permute-start.4 = (bf16[128,4096]{1,0:T(8,128)(2,1)S(1)}, bf16[128,4096]{1,0:T(8,128)(2,1)S(1)}, u32[]{:S(2)}, u32[]{:S(2)}) collective-permute-start(bf16[128,4096]{1,0:T(8,128)(2,1)S(1)} %get-tuple-element.33.refs_0_), channel_id=1, source_target_pairs={{0,8},{1,9},{2,10},{3,11},{4,12},{5,13},{6,14},{7,15},{8,0},{9,1},... | collective-permute-start | bytes 3145736 | tf_op jit(solution)/shard_map/ppermute | solution.py:33
  110.6 7.9 %collective-permute-start.5 = (bf16[128,4096]{1,0:T(8,128)(2,1)S(1)}, bf16[128,4096]{1,0:T(8,128)(2,1)S(1)}, u32[]{:S(2)}, u32[]{:S(2)}) collective-permute-start(bf16[128,4096]{1,0:T(8,128)(2,1)S(1)} %get-tuple-element.34.refs_1_), channel_id=1, source_target_pairs={{0,8},{1,9},{2,10},{3,11},{4,12},{5,13},{6,14},{7,15},{8,0},{9,1},... | collective-permute-start | bytes 3145736 | tf_op jit(solution)/shard_map/ppermute | solution.py:33
  110.7 7.8 %collective-permute-start.6 = (bf16[128,4096]{1,0:T(8,128)(2,1)S(1)}, bf16[128,4096]{1,0:T(8,128)(2,1)S(1)}, u32[]{:S(2)}, u32[]{:S(2)}) collective-permute-start(bf16[128,4096]{1,0:T(8,128)(2,1)S(1)} %get-tuple-element.35.refs_2_), channel_id=1, source_target_pairs={{0,8},{1,9},{2,10},{3,11},{4,12},{5,13},{6,14},{7,15},{8,0},{9,1},... | collective-permute-start | bytes 3145736 | tf_op jit(solution)/shard_map/ppermute | solution.py:33
  111.1 7.4 %collective-permute-start.7 = (bf16[128,4096]{1,0:T(8,128)(2,1)S(1)}, bf16[128,4096]{1,0:T(8,128)(2,1)S(1)}, u32[]{:S(2)}, u32[]{:S(2)}) collective-permute-start(bf16[128,4096]{1,0:T(8,128)(2,1)S(1)} %get-tuple-element.36.refs_3_), channel_id=1, source_target_pairs={{0,8},{1,9},{2,10},{3,11},{4,12},{5,13},{6,14},{7,15},{8,0},{9,1},... | collective-permute-start | bytes 3145736 | tf_op jit(solution)/shard_map/ppermute | solution.py:33
  111.2 7.3 %collective-permute-start.22 = (bf16[8,3,128,128]{3,2,1,0:T(8,128)(2,1)S(1)}, bf16[8,3,128,128]{3,2,1,0:T(8,128)(2,1)S(1)}, u32[]{:S(2)}, u32[]{:S(2)}) collective-permute-start(bf16[8,3,128,128]{3,2,1,0:T(8,128)(2,1)S(1)} %collective-permute-done.18.refs_11_), channel_id=1, source_target_pairs={{0,8},{1,9},{2,10},{3,11},{4,12},{5,13},{6,14},{7,15},{8,0},{9,1},... | collective-permute-start | bytes 2359304 | tf_op jit(solution)/shard_map/ppermute | solution.py:33
  123.1 1.0 copy-start.24
  129.0 1.0 copy-start.22
  130.0 5.9 %collective-permute-start.28 = (bf16[128,512]{1,0:T(8,128)(2,1)S(1)}, bf16[128,512]{1,0:T(8,128)(2,1)S(1)}, u32[]{:S(2)}, u32[]{:S(2)}) collective-permute-start(bf16[128,512]{1,0:T(8,128)(2,1)S(1)} %shard_map.102), channel_id=1, source_target_pairs={{0,20},{1,21},{2,22},{3,23},{4,16},{5,17},{6,18},{7,19},{8,28},{9,... | collective-permute-start | bytes 393224 | tf_op jit(solution)/shard_map/ppermute | solution.py:33
  136.7 1.2 copy-start.13
  138.0 1.2 copy-start.23
  139.2 1.2 copy-start.25
  140.4 1.2 copy-start.27
  141.6 1.2 copy-start.29
  142.9 1.2 copy-start.31
  144.1 17.9 %copy-start.1 = (bf16[8,3,128,128]{3,2,1,0:T(8,128)(2,1)S(1)}, bf16[8,3,128,128]{3,2,1,0:T(8,128)(2,1)}, u32[]{:S(2)}) copy-start(bf16[8,3,128,128]{3,2,1,0:T(8,128)(2,1)} %copy-done) | copy-start | bytes 2359300
  144.1 17.9 %copy-start.3 = (bf16[8,3,128,128]{3,2,1,0:T(8,128)(2,1)S(1)}, bf16[8,3,128,128]{3,2,1,0:T(8,128)(2,1)}, u32[]{:S(2)}) copy-start(bf16[8,3,128,128]{3,2,1,0:T(8,128)(2,1)} %copy-done.2) | copy-start | bytes 2359300
  144.1 17.9 %copy-start.5 = (bf16[8,3,128,128]{3,2,1,0:T(8,128)(2,1)S(1)}, bf16[8,3,128,128]{3,2,1,0:T(8,128)(2,1)}, u32[]{:S(2)}) copy-start(bf16[8,3,128,128]{3,2,1,0:T(8,128)(2,1)} %copy-done.4) | copy-start | bytes 2359300
  144.1 17.9 %copy-start.7 = (bf16[8,3,128,128]{3,2,1,0:T(8,128)(2,1)S(1)}, bf16[8,3,128,128]{3,2,1,0:T(8,128)(2,1)}, u32[]{:S(2)}) copy-start(bf16[8,3,128,128]{3,2,1,0:T(8,128)(2,1)} %copy-done.6) | copy-start | bytes 2359300
  159.5 2.4 collective-permute-start.23
  165.5 25.9 %collective-permute-start.24 = (bf16[128,4096]{1,0:T(8,128)(2,1)S(1)}, bf16[128,4096]{1,0:T(8,128)(2,1)S(1)}, u32[]{:S(2)}, u32[]{:S(2)}) collective-permute-start(bf16[128,4096]{1,0:T(8,128)(2,1)S(1)} %get-tuple-element.55.refs_16_), channel_id=1, source_target_pairs={{0,1},{1,2},{2,3},{3,0},{4,5},{5,6},{6,7},{7,4},{8,9},{9,10},{10,1... | collective-permute-start | bytes 3145736 | tf_op jit(solution)/shard_map/ppermute | solution.py:33
  166.7 24.7 %collective-permute-start.25 = (bf16[128,4096]{1,0:T(8,128)(2,1)S(1)}, bf16[128,4096]{1,0:T(8,128)(2,1)S(1)}, u32[]{:S(2)}, u32[]{:S(2)}) collective-permute-start(bf16[128,4096]{1,0:T(8,128)(2,1)S(1)} %get-tuple-element.56.refs_17_), channel_id=1, source_target_pairs={{0,3},{1,0},{2,1},{3,2},{4,7},{5,4},{6,5},{7,6},{8,11},{9,8},{10,9... | collective-permute-start | bytes 3145736 | tf_op jit(solution)/shard_map/ppermute | solution.py:33
  172.2 19.4 %copy-start.19 = (f32[128,4096]{1,0:T(8,128)}, f32[128,4096]{1,0:T(8,128)S(1)}, u32[]{:S(2)}) copy-start(f32[128,4096]{1,0:T(8,128)S(1)} %get-tuple-element.57.own) | copy-start | bytes 6291460
  191.5 1.4 copy-start.17
  191.5 14.8 %copy-start.9 = (bf16[128,4096]{1,0:T(8,128)(2,1)S(1)}, bf16[128,4096]{1,0:T(8,128)(2,1)}, u32[]{:S(2)}) copy-start(bf16[128,4096]{1,0:T(8,128)(2,1)} %copy-done.8) | copy-start | bytes 3145732
  192.8 13.5 %collective-permute-start.26 = (bf16[64,4096]{1,0:T(8,128)(2,1)S(1)}, bf16[64,4096]{1,0:T(8,128)(2,1)S(1)}, u32[]{:S(2)}, u32[]{:S(2)}) collective-permute-start(bf16[64,4096]{1,0:T(8,128)(2,1)S(1)} %get-tuple-element.60), channel_id=1, source_target_pairs={{0,1},{1,2},{2,3},{3,0},{4,5},{5,6},{6,7},{7,4},{8,9},{9,10},{10,1... | collective-permute-start | bytes 1572872 | tf_op jit(solution)/shard_map/ppermute | solution.py:33
  193.2 13.1 %collective-permute-start.27 = (bf16[64,4096]{1,0:T(8,128)(2,1)S(1)}, bf16[64,4096]{1,0:T(8,128)(2,1)S(1)}, u32[]{:S(2)}, u32[]{:S(2)}) collective-permute-start(bf16[64,4096]{1,0:T(8,128)(2,1)S(1)} %get-tuple-element.61), channel_id=1, source_target_pairs={{0,3},{1,0},{2,1},{3,2},{4,7},{5,4},{6,5},{7,6},{8,11},{9,8},{10,9... | collective-permute-start | bytes 1572872 | tf_op jit(solution)/shard_map/ppermute | solution.py:33
  206.3 2.2 copy-start.14
  208.5 1.2 copy-start.16
  209.7 1.2 copy-start.18
  210.9 1.6 copy-start.20
  212.5 28.7 %copy-start.21 = (bf16[512,1536]{1,0:T(8,128)(2,1)S(1)}, bf16[512,1536]{1,0:T(8,128)(2,1)}, u32[]{:S(2)}) copy-start(bf16[512,1536]{1,0:T(8,128)(2,1)} %refs_1_.1) | copy-start | bytes 4718596
  212.5 28.7 %copy-start.34 = (bf16[512,512]{1,0:T(8,128)(2,1)S(1)}, bf16[512,512]{1,0:T(8,128)(2,1)}, u32[]{:S(2)}) copy-start(bf16[512,512]{1,0:T(8,128)(2,1)} %refs_2_.1) | copy-start | bytes 1572868
  214.4 12.9 %collective-permute-start.30 = (bf16[128,512]{1,0:T(8,128)(2,1)S(1)}, bf16[128,512]{1,0:T(8,128)(2,1)S(1)}, u32[]{:S(2)}, u32[]{:S(2)}) collective-permute-start(bf16[128,512]{1,0:T(8,128)(2,1)S(1)} %get-tuple-element.63.refs_0_), channel_id=1, source_target_pairs={{0,128},{1,129},{2,130},{3,131},{4,132},{5,133},{6,134},{7,135},{8... | collective-permute-start | bytes 393224 | tf_op jit(solution)/shard_map/ppermute | solution.py:33
  227.4 5.4 %collective-permute-start.31 = (bf16[128,512]{1,0:T(8,128)(2,1)S(1)}, bf16[128,512]{1,0:T(8,128)(2,1)S(1)}, u32[]{:S(2)}, u32[]{:S(2)}) collective-permute-start(bf16[128,512]{1,0:T(8,128)(2,1)S(1)} %collective-permute-done.30), channel_id=1, source_target_pairs={{0,1},{1,2},{2,3},{3,0},{4,5},{5,6},{6,7},{7,4},{8,9},{9,10},{10,1... | collective-permute-start | bytes 393224 | tf_op jit(solution)/shard_map/ppermute | solution.py:33
  227.4 24.3 %collective-permute-start.29 = (bf16[128,4096]{1,0:T(8,128)(2,1)S(1)}, bf16[128,4096]{1,0:T(8,128)(2,1)S(1)}, u32[]{:S(2)}, u32[]{:S(2)}) collective-permute-start(bf16[128,4096]{1,0:T(8,128)(2,1)S(1)} %get-tuple-element.62), channel_id=1, source_target_pairs={{0,0},{1,1},{2,2},{3,3},{4,8},{5,9},{6,10},{7,11},{8,4},{9,5},{10,... | collective-permute-start | bytes 3145736 | tf_op jit(solution)/shard_map/ppermute | solution.py:33
  229.3 6.5 %collective-permute-start.32 = (bf16[128,512]{1,0:T(8,128)(2,1)S(1)}, bf16[128,512]{1,0:T(8,128)(2,1)S(1)}, u32[]{:S(2)}, u32[]{:S(2)}) collective-permute-start(bf16[128,512]{1,0:T(8,128)(2,1)S(1)} %collective-permute-done.30), channel_id=1, source_target_pairs={{0,3},{1,0},{2,1},{3,2},{4,7},{5,4},{6,5},{7,6},{8,11},{9,8},{10,9... | collective-permute-start | bytes 393224 | tf_op jit(solution)/shard_map/ppermute | solution.py:33
  232.1 5.8 %collective-permute-start.33 = (bf16[128,512]{1,0:T(8,128)(2,1)S(1)}, bf16[128,512]{1,0:T(8,128)(2,1)S(1)}, u32[]{:S(2)}, u32[]{:S(2)}) collective-permute-start(bf16[128,512]{1,0:T(8,128)(2,1)S(1)} %collective-permute-done.30), channel_id=1, source_target_pairs={{0,2},{1,3},{2,0},{3,1},{4,6},{5,7},{6,4},{7,5},{8,10},{9,11},{10,... | collective-permute-start | bytes 393224 | tf_op jit(solution)/shard_map/ppermute | solution.py:33
  237.9 3.3 %collective-permute-start.34 = (bf16[512,512]{1,0:T(8,128)(2,1)S(1)}, bf16[512,512]{1,0:T(8,128)(2,1)S(1)}, u32[]{:S(2)}, u32[]{:S(2)}) collective-permute-start(bf16[512,512]{1,0:T(8,128)(2,1)S(1)} %constant_dynamic-update-slice_fusion.refs_3_), channel_id=1, source_target_pairs={{0,8},{1,9},{2,10},{3,11},{4,12},{5,13},{6,14},{7,15},{8,0},{9,1},... | collective-permute-start | bytes 1572872 | tf_op jit(solution)/shard_map/ppermute | solution.py:33
  245.4 6.3 %collective-permute-start.35 = (bf16[128,512]{1,0:T(8,128)(2,1)S(1)}, bf16[128,512]{1,0:T(8,128)(2,1)S(1)}, u32[]{:S(2)}, u32[]{:S(2)}) collective-permute-start(bf16[128,512]{1,0:T(8,128)(2,1)S(1)} %shard_map.104), channel_id=1, source_target_pairs={{0,0},{1,1},{2,2},{3,3},{4,8},{5,9},{6,10},{7,11},{8,4},{9,5},{10,... | collective-permute-start | bytes 393224 | tf_op jit(solution)/shard_map/ppermute | solution.py:33
  (12 other events, 11.3 us)
Sparse Core Ops, SparseCore 0:
  30.4 76.2 all-gather.2
  136.8 43.2 all-gather.4
where the time goes:
time: 261 us; the launch traced here: 260 us
  waiting for transfers between devices  103 us (39%)
  starting transfers between devices  78.2 us (30%)
  local copies, waits for them, and re-layouts  32.3 us (12%)
  Pallas kernels  28.9 us (11%)
  between operations  14.5 us (6%)
  other arithmetic  3.16 us (1%)
    ppermute x36, waiting for transfers between devices, moved(): return lax.ppermute(block, AXES, route)  103 us
    ppermute x36, starting transfers between devices, moved(): return lax.ppermute(block, AXES, route)  78.1 us
    unnamed x83, local copies, waits for them, and re-layouts  31.8 us
    pallas_call x1, Pallas kernels, attention(): local(attention_kernel, (result, result), 44, flops=2 * count * depth * c...  15.4 us
    pallas_call x2, Pallas kernels, out_projection(): local(functools.partial(out_kernel, len(earlier), picked), tuple((jax.Sha...  7.12 us
  transfers between devices with their start and end apart: 38, of which 18 were waited for; matrix products, arithmetic and copies ran while one was open for 1% of the time, Pallas kernels for 10%

commit v1 on v0

v1 whole, which is shorter than its diff:
```python
import functools
import itertools
import math

import jax
import jax.numpy as jnp
from jax import lax
from jax.experimental import pallas as pl
from jax.experimental.pallas import tpu as pltpu
from jax.sharding import Mesh
from jax.sharding import PartitionSpec as P

HEAD_DIM = 128
MATCH_HEADS = 8
DISTANCES = (1, -1, 2)
WAIT = 23_000_000_000
LOG2_E = math.log2(math.e)
AXES = ("z", "xh", "core", "xl", "y")
SIZES = (8, 2, 2, 2, 4)


def moved(block, target):
    def index(place):
        at = 0
        for axis, size in zip(AXES, SIZES):
            at = at * size + place[axis]
        return at

    route = []
    for values in itertools.product(*[range(size) for size in SIZES]):
        place = dict(zip(AXES, values))
        route.append((index(place), index({**place, **target(place)})))
    return lax.ppermute(block, AXES, route)


def along_y(k):
    return lambda p: {"y": (p["y"] + k) % 4}


def along_z(k):
    return lambda p: {"z": (p["z"] + k) % 8}


def other_core(p):
    return {"core": 1 - p["core"]}


def swapped_roles(block):
    return moved(block, lambda p: {"core": p["xl"], "xl": p["core"]})


def layer_norm(rows_in, norm_gain, norm_bias):
    values = rows_in.astype(jnp.float32)
    center = jnp.mean(values, axis=-1, keepdims=True)
    spread = jnp.mean((values - center) ** 2, axis=-1, keepdims=True)
    return ((values - center) * lax.rsqrt(spread + 1e-06) * norm_gain + norm_bias).astype(
        jnp.bfloat16
    )


def local(kernel, out_shape, mebibytes, flops=0, moved_bytes=0, **kwargs):
    return pl.pallas_call(
        kernel,
        out_shape=out_shape,
        compiler_params=pltpu.CompilerParams(vmem_limit_bytes=mebibytes << 20),
        cost_estimate=pl.CostEstimate(flops=flops, bytes_accessed=moved_bytes, transcendentals=0),
        **kwargs,
    )


def together(*values, flops=0):
    def kernel(*refs):
        pass

    held = pl.BlockSpec(memory_space=pltpu.HBM)
    count = len(values)
    return local(
        kernel,
        tuple(jax.ShapeDtypeStruct(value.shape, value.dtype) for value in values),
        1,
        flops=flops,
        in_specs=[held] * count,
        out_specs=(held,) * count,
        input_output_aliases={i: i for i in range(count)},
    )(*values)


def after(value, *earlier):
    def kernel(*refs):
        pass

    held = pl.BlockSpec(memory_space=pltpu.HBM)
    return local(
        kernel,
        jax.ShapeDtypeStruct(value.shape, value.dtype),
        1,
        in_specs=[held] * (1 + len(earlier)),
        out_specs=held,
        input_output_aliases={0: 0},
    )(value, *earlier)


def attend(queries, keys, values, scale):
    scores = dot_transposed(queries, keys)
    raised = jnp.exp2((scores - jnp.max(scores, axis=-1, keepdims=True)) * (scale * LOG2_E))
    mixed = dot(raised.astype(jnp.bfloat16), values)
    return mixed * (1.0 / jnp.sum(raised, axis=-1, keepdims=True))


def dot(left, right):
    return jnp.dot(left, right, preferred_element_type=jnp.float32)


def dot_transposed(left, right):
    return lax.dot_general(
        left, right, (((1,), (1,)), ((), ())), preferred_element_type=jnp.float32
    )


PARTS = 4


def attention_kernel(*refs):
    *pieces, weight, own, other, held, held_weight, total, projected, sems = refs
    depth = held.shape[1] // PARTS
    block = weight.shape[3]
    copies = []
    for part in range(PARTS):
        span = pl.ds(part * depth, depth)
        planes = pl.ds(part * 8 // PARTS, 8 // PARTS)
        moves = []
        for column in range(held_weight.shape[3] // block):
            there = held_weight.at[planes, :, :, pl.ds(column * block, block)]
            moves.append((weight.at[planes, :, column], there))
        at = 0
        for piece in pieces:
            count = piece.shape[0]
            moves.append((piece.at[:, span], held.at[pl.ds(at, count), span]))
            at += count
        starting = [
            pltpu.make_async_copy(source, there, sems.at[part, i])
            for i, (source, there) in enumerate(moves)
        ]
        for copy in starting:
            copy.start()
        copies.append(starting)
    step = 512
    for part in range(PARTS):
        for copy in copies[part]:
            copy.wait()
        span = pl.ds(part * depth, depth)
        planes = pl.ds(part * 8 // PARTS, 8 // PARTS)

        @pl.loop(0, held.shape[0], step=step)
        def _(row, part=part, span=span, planes=planes):
            rows = pl.ds(pl.multiple_of(row, step), step)
            term = dot(held[rows, span], held_weight[planes].reshape(depth, -1))
            if part:
                term = total[rows, :] + term
            if part < PARTS - 1:
                total[rows, :] = term
            else:
                projected[rows, :] = term.astype(jnp.bfloat16)

    step = 256
    for head in range(2):
        at = head * 3 * HEAD_DIM
        for half, out in enumerate((own, other)):

            @pl.loop(0, out.shape[0], step=step)
            def _(row, at=at, half=half, out=out, head=head):
                rows = pl.ds(pl.multiple_of(half * out.shape[0] + row, step), step)
                mixed = attend(
                    projected[rows, at : at + HEAD_DIM],
                    projected[:, at + HEAD_DIM : at + 2 * HEAD_DIM],
                    projected[:, at + 2 * HEAD_DIM : at + 3 * HEAD_DIM],
                    1.0 / math.sqrt(HEAD_DIM),
                )
                out[pl.ds(pl.multiple_of(row, step), step), pl.ds(head * HEAD_DIM, HEAD_DIM)] = (
                    mixed.astype(jnp.bfloat16)
                )


def attention(pieces, weight):
    count = sum(piece.shape[0] for piece in pieces)
    depth = pieces[0].shape[1]
    block = weight.shape[3]
    columns = 6 * block
    result = jax.ShapeDtypeStruct((count // 2, columns // 3), jnp.bfloat16)
    return local(
        attention_kernel,
        (result, result),
        60,
        flops=2 * count * depth * columns,
        moved_bytes=2 * depth * (count + columns),
        in_specs=[pl.BlockSpec(memory_space=pltpu.HBM)] * (len(pieces) + 1),
        out_specs=(pl.BlockSpec(memory_space=pltpu.VMEM),) * 2,
        scratch_shapes=[
            pltpu.VMEM((count, depth), jnp.bfloat16),
            pltpu.VMEM((8, 4, block, columns), jnp.bfloat16),
            pltpu.VMEM((count, columns), jnp.float32),
            pltpu.VMEM((count, columns), jnp.bfloat16),
            pltpu.SemaphoreType.DMA((PARTS, len(pieces) + 6)),
        ],
    )(*pieces, weight)


def out_kernel(skipped, picked, mine, theirs, weight, other_weight, *refs):
    outs = refs[skipped:]
    planes, xs, halves = weight.shape[:3]
    matrix = jnp.concatenate(
        [
            jnp.concatenate([w[p, x, h] for p in range(planes) for x in range(xs)], axis=1)
            for w in (weight, other_weight)
            for h in range(halves)
        ],
        axis=0,
    )
    both = [
        jnp.concatenate([mine[at : at + many, :], theirs[at : at + many, :]], axis=1)
        for at, many in picked
    ]
    terms = dot(jnp.concatenate(both, axis=0), matrix)
    at = 0
    for out in outs:
        out[...] = terms[at : at + out.shape[0]].astype(out.dtype)
        at += out.shape[0]


def out_projection(mine, theirs, weight, other_weight, picked, dtype, earlier=()):
    earlier = list(earlier)
    planes, xs, _, block, wide = weight.shape
    at_once = 2
    columns = at_once * xs * wide
    rows = sum(many for _, many in picked)
    whole = pl.BlockSpec(mine.shape, lambda i: (0, 0))
    part = (at_once, xs, 2, block, wide)
    return local(
        functools.partial(out_kernel, len(earlier), picked),
        tuple(jax.ShapeDtypeStruct((many, planes * xs * wide), dtype) for _, many in picked),
        52,
        flops=8 * rows * block * planes * xs * wide,
        moved_bytes=8 * planes * xs * block * wide,
        grid=(planes // at_once,),
        in_specs=[
            whole,
            whole,
            pl.BlockSpec(part, lambda i: (i, 0, 3, 0, 0)),
            pl.BlockSpec(part, lambda i: (i, 0, 0, 0, 0)),
        ]
        + [pl.BlockSpec(memory_space=pltpu.HBM)] * len(earlier),
        out_specs=tuple(pl.BlockSpec((many, columns), lambda i: (0, i)) for _, many in picked),
    )(mine, theirs, weight, other_weight, *earlier)


def added_kernel(a, b, c, d, first, second):
    first[...] = (a[...] + b[...].astype(jnp.float32)).astype(first.dtype)
    second[...] = (c[...] + d[...].astype(jnp.float32)).astype(second.dtype)


def added(a, b, c, d):
    return local(added_kernel, (jax.ShapeDtypeStruct(a.shape, b.dtype),) * 2, 20)(a, b, c, d)


def features_kernel(
    place, tokens, own, low_a, high_a, low_b, high_b, mine, theirs, features, descriptor, total
):
    step = pl.program_id(0)
    summed = own[...]
    summed = summed + jnp.concatenate([low_a[...], high_a[...]], axis=0).astype(jnp.float32)
    summed = summed + jnp.concatenate([low_b[...], high_b[...]], axis=0).astype(jnp.float32)
    rounded = (tokens[...].astype(jnp.float32) + summed).astype(jnp.bfloat16)
    features[...] = rounded
    planes, xs, parts, block, _ = mine.shape
    half = block // 2
    first = place[0] == 0
    blocks = []
    for plane in range(planes):
        for x in range(xs):
            halves = [
                jnp.concatenate(
                    [w[plane, x, i, at : at + half] for i in range(parts) for at in (0, half)],
                    axis=1,
                )
                for w in (mine, theirs)
            ]
            blocks += [jnp.where(first, *halves), jnp.where(first, *halves[::-1])]
    term = dot(rounded, jnp.concatenate(blocks, axis=0))

    @pl.when(step == 0)
    def _():
        total[...] = term

    @pl.when(step > 0)
    def _():
        total[...] += term

    @pl.when(step == pl.num_programs(0) - 1)
    def _():
        descriptor[...] = total[...].astype(jnp.bfloat16)


def features_and_descriptor(core, tokens, own, halves, weights, other_weights):
    rows, depth = tokens.shape
    _, xs, _, block, wide = weights.shape
    parts = 2
    width = 2 * parts * wide
    at_once = 2
    columns = at_once * xs * block
    whole = pl.BlockSpec((rows, columns), lambda i: (0, i))
    half = pl.BlockSpec((rows // 2, columns), lambda i: (0, i))
    part = (at_once, xs, parts, block, wide)
    return local(
        features_kernel,
        (
            jax.ShapeDtypeStruct((rows, depth), jnp.bfloat16),
            jax.ShapeDtypeStruct((rows, width), jnp.bfloat16),
        ),
        52,
        grid=(depth // columns,),
        in_specs=[pl.BlockSpec(memory_space=pltpu.SMEM), whole, whole]
        + [half] * 4
        + [
            pl.BlockSpec(part, lambda i: (i, 0, 4, 0, 0)),
            pl.BlockSpec(part, lambda i: (i, 0, 1, 0, 0)),
        ],
        out_specs=(whole, pl.BlockSpec((rows, width), lambda i: (0, 0))),
        scratch_shapes=[pltpu.VMEM((rows, width), jnp.float32)],
    )(core.astype(jnp.int32).reshape(1), tokens, own, *halves, weights, other_weights)


def matcher_kernel(*refs):
    descriptor, qkv, out_weight, *pieces, matched, keys, values, mixed = refs
    rows, width = descriptor.shape
    bf16 = jnp.bfloat16
    queries = dot(descriptor[...], qkv[:, :width]).astype(bf16)
    at = 0
    for piece in pieces:
        count = piece.shape[0]
        keys[at : at + count, :] = dot(piece[...], qkv[:, width : 2 * width]).astype(bf16)
        values[at : at + count, :] = dot(piece[...], qkv[:, 2 * width :]).astype(bf16)
        at += count
    head_width = width // MATCH_HEADS
    pair = 2 * head_width
    low = lax.broadcasted_iota(jnp.int32, (rows, pair), 1) < head_width
    for first in range(0, width, pair):
        span = slice(first, first + pair)
        two = queries[:, span]
        results = []
        for chosen in (low, jnp.logical_not(low)):
            asked = jnp.where(chosen, two, jnp.zeros_like(two))
            scale = 1.0 / math.sqrt(head_width)
            results.append(attend(asked, keys[:, span], values[:, span], scale))
        mixed[:, span] = jnp.where(low, results[0], results[1]).astype(bf16)
    matched[...] = (descriptor[...].astype(jnp.float32) + dot(mixed[...], out_weight[...])).astype(
        bf16
    )


def match(descriptor, pieces, qkv, out_weight):
    count = sum(piece.shape[0] for piece in pieces)
    width = descriptor.shape[1]
    return local(
        matcher_kernel,
        jax.ShapeDtypeStruct(descriptor.shape, jnp.bfloat16),
        24,
        scratch_shapes=[
            pltpu.VMEM((count, width), jnp.bfloat16),
            pltpu.VMEM((count, width), jnp.bfloat16),
            pltpu.VMEM(descriptor.shape, jnp.bfloat16),
        ],
    )(descriptor, qkv, out_weight, *pieces)


def per_device(
    tokens, norm_gain, norm_bias, qkv_weight, out_weight, match_weight, matcher_qkv, matcher_out
):
    bf16, f32 = jnp.bfloat16, jnp.float32
    width = matcher_out.shape[0]
    rows, features_width = tokens.shape
    mid = rows // 2

    block, wide = qkv_weight.shape[0], out_weight.shape[1]

    def in_blocks(weight):
        return weight.reshape(weight.shape[0], -1, wide).transpose(1, 0, 2).reshape(-1, wide)

    part = match_weight.shape[0] // 2
    match_low = in_blocks(match_weight[:part])
    match_high = in_blocks(match_weight[part:])
    match_half = jnp.where(lax.axis_index("xl") == 0, match_low, match_high)
    packed = swapped_roles(
        jnp.concatenate([in_blocks(qkv_weight), out_weight, match_half], axis=0)
    )
    weights = lax.all_gather(packed, ("z", "xh", "xl"), axis=0, tiled=True)
    weights = weights.reshape(8, 4, 10, block, wide)

    tokens = swapped_roles(tokens)
    normed = layer_norm(tokens, norm_gain, norm_bias)
    pieces = [normed] + [moved(normed, along_y(k)) for k in DISTANCES]
    pieces += [moved(piece, other_core) for piece in pieces]
    pieces = together(*pieces, flops=WAIT)
    other_weights = moved(after(weights[:, :, 6:], pieces[0]), other_core)
    mine, theirs = attention(pieces, weights)

    both = (mine, moved(theirs, other_core), weights, other_weights)
    far_low, far_high, up_high, down_low = out_projection(
        *both,
        [(3 * rows, mid), (3 * rows + mid, mid), (2 * rows + mid, mid), (rows, mid)],
        bf16,
    )
    own, down_high, up_low = out_projection(
        *both, [(0, rows), (rows + mid, mid), (2 * rows, mid)], f32, [far_low]
    )
    far_low, far_high = moved(far_low, along_y(1)), moved(far_high, along_y(-1))
    up_high, down_low = moved(up_high, along_y(1)), moved(down_low, along_y(-1))
    up_low, down_high = added(up_low, far_low, down_high, far_high)
    up_low, down_high = moved(up_low, along_y(1)), moved(down_high, along_y(-1))

    features, descriptor = features_and_descriptor(
        lax.axis_index("core"),
        tokens,
        own,
        (up_low, up_high, down_low, down_high),
        weights,
        other_weights,
    )
    partner = moved(descriptor, along_z(4))
    quarter = jnp.concatenate([partner] + [moved(partner, along_y(k)) for k in DISTANCES], axis=0)
    pieces = [quarter, moved(quarter, other_core)]
    matched = match(descriptor, pieces, matcher_qkv, matcher_out)
    return (swapped_roles(features), swapped_roles(matched))


def solution(mesh):
    fine = Mesh(mesh.devices.reshape(SIZES), AXES)
    dp, tensor = ("z", "xh", "core"), ("xl", "y")
    return jax.shard_map(
        per_device,
        mesh=fine,
        in_specs=(
            P(AXES, None),
            P(),
            P(),
            P(dp, tensor),
            P(tensor, dp),
            P(dp, None),
            P(),
            P(),
        ),
        out_specs=(P(AXES, None), P(AXES, None)),
        check_vma=False,
    )
```

time: 261 us -> 252 us (0.966)
  starting transfers between devices: 78.2 us -> 39.4 us
  waiting for transfers between devices: 103 us -> 140 us
  local copies, waits for them, and re-layouts: 32.3 us -> 17.6 us
  Pallas kernels: 28.9 us -> 36.6 us
    all_gather x2 -> x1, waiting for transfers between devices: 0.02 us -> 54.3 us  [per_device(): weights = lax.all_gather(packed, ('z', 'xh', 'xl'), axis=0, tiled=True)]
    ppermute x36 -> x24, starting transfers between devices: 78.1 us -> 39.4 us  [moved(): return lax.ppermute(block, AXES, route)]
    unnamed x83 -> x42, local copies, waits for them, and re-layouts: 31.8 us -> 12.7 us
    ppermute x36 -> x24, waiting for transfers between devices: 103 us -> 86 us  [moved(): return lax.ppermute(block, AXES, route)]
    slice x1, local copies, waits for them, and re-layouts: 0.01 us -> 4.75 us  [per_device(): other_weights = moved(after(weights[:, :, 6:], pieces[0]), other_core)]
    pallas_call x1, Pallas kernels: 1.9 us -> 5.56 us  [features_and_descriptor(): local(features_kernel, (jax.ShapeDtypeStruct((rows, depth), jnp.bfloat16)...]
    pallas_call x2, Pallas kernels: 7.12 us -> 10.3 us  [out_projection(): local(functools.partial(out_kernel, len(earlier), picked), tuple((jax.Sha...]
  transfers between devices with their start and end apart: 38 -> 25, of which waited for: 18 -> 16; matrix products, arithmetic and copies ran while one was open for 1% -> 0% of each run, Pallas kernels for 10% -> 10%
where the time goes in v1:
time: 252 us; the launch traced here: 251 us
  waiting for transfers between devices  140 us (56%)
  starting transfers between devices  39.4 us (16%)
  Pallas kernels  36.6 us (15%)
  local copies, waits for them, and re-layouts  17.6 us (7%)
  between operations  14.2 us (6%)
  other arithmetic  2.91 us (1%)
    ppermute x24, waiting for transfers between devices, moved(): return lax.ppermute(block, AXES, route)  86 us
    all_gather x1, waiting for transfers between devices, per_device(): weights = lax.all_gather(packed, ('z', 'xh', 'xl'), axis=0, tiled=True)  54.3 us
    ppermute x24, starting transfers between devices, moved(): return lax.ppermute(block, AXES, route)  39.4 us
    pallas_call x1, Pallas kernels, attention(): local(attention_kernel, (result, result), 60, flops=2 * count * depth * c...  16.4 us
    unnamed x42, local copies, waits for them, and re-layouts  12.7 us
    pallas_call x2, Pallas kernels, out_projection(): local(functools.partial(out_kernel, len(earlier), picked), tuple((jax.Sha...  10.3 us
    pallas_call x1, Pallas kernels, features_and_descriptor(): local(features_kernel, (jax.ShapeDtypeStruct((rows, depth), jnp.bfloat16)...  5.56 us
  transfers between devices with their start and end apart: 25, of which 16 were waited for; matrix products, arithmetic and copies ran while one was open for 0% of the time, Pallas kernels for 10%

profile of v1, /device:TPU:1, one launch (start us, length us, event | category | flops | bytes accessed | tf_op | source)
XLA Modules:
  0.0 251.2 jit_solution(14164523727282382382)
XLA Ops:
  7.2 0.0 all-gather.2.cloned.1.call-start
  7.2 1.1 copy.23
  8.3 0.2 copy.24
  8.5 0.9 copy_bitcast_fusion
  9.4 0.9 pad_maximum_fusion
  10.3 4.5 %collective-permute-start.8 = (bf16[1280,128]{1,0:T(8,128)(2,1)S(1)}, bf16[1280,128]{1,0:T(8,128)(2,1)S(1)}, u32[]{:S(2)}, u32[]{:S(2)}) collective-permute-start(bf16[1280,128]{1,0:T(8,128)(2,1)S(1)} %pad_maximum_fusion), channel_id=1, source_target_pairs={{0,0},{1,1},{2,2},{3,3},{4,8},{5,9},{6,10},{7,11},{8,4},{9,5},{10,... | collective-permute-start | bytes 983048 | tf_op jit(solution)/shard_map/ppermute | solution.py:33
  14.8 4.7 %collective-permute-done.8 = bf16[1280,128]{1,0:T(8,128)(2,1)S(1)} collective-permute-done((bf16[1280,128]{1,0:T(8,128)(2,1)S(1)}, bf16[1280,128]{1,0:T(8,128)(2,1)S(1)}, u32[]{:S(2)}, u32[]{:S(2)}) %collective-permute-start.8) | collective-permute-done | bytes 327712 | tf_op jit(solution)/shard_map/ppermute | solution.py:33
  19.5 0.7 copy-done.15
  20.3 3.6 %collective-permute-start = (bf16[128,4096]{1,0:T(8,128)(2,1)}, bf16[128,4096]{1,0:T(8,128)(2,1)S(1)}, u32[]{:S(2)}, u32[]{:S(2)}) collective-permute-start(bf16[128,4096]{1,0:T(8,128)(2,1)} %param.8), channel_id=1, source_target_pairs={{0,0},{1,1},{2,2},{3,3},{4,8},{5,9},{6,10},{7,11},{8,4},{9,5},{10,... | collective-permute-start | bytes 3145736 | tf_op jit(solution)/shard_map/ppermute | solution.py:33
  23.9 13.0 %collective-permute-done.tokens = bf16[128,4096]{1,0:T(8,128)(2,1)S(1)} collective-permute-done((bf16[128,4096]{1,0:T(8,128)(2,1)}, bf16[128,4096]{1,0:T(8,128)(2,1)S(1)}, u32[]{:S(2)}, u32[]{:S(2)}) %collective-permute-start) | collective-permute-done | bytes 1048608 | tf_op jit(solution)/shard_map/ppermute | solution.py:33
  36.9 0.2 convert_reduce_fusion
  37.1 0.4 fusion.2
  37.6 0.5 fusion.5.refs_0_
  38.1 1.7 collective-permute-start.1
  39.8 1.5 collective-permute-start.2
  41.3 1.6 collective-permute-start.3
  42.9 24.3 %collective-permute-done.1.refs_1_ = bf16[128,4096]{1,0:T(8,128)(2,1)S(1)} collective-permute-done((bf16[128,4096]{1,0:T(8,128)(2,1)S(1)}, bf16[128,4096]{1,0:T(8,128)(2,1)S(1)}, u32[]{:S(2)}, u32[]{:S(2)}) %collective-permute-start.1) | collective-permute-done | bytes 1048608 | tf_op jit(solution)/shard_map/ppermute | solution.py:33
  67.1 0.5 collective-permute-start.6
  67.7 0.1 collective-permute-start.7
  67.8 2.0 collective-permute-done.5.refs_5_
  69.8 1.5 collective-permute-done.6.refs_6_
  71.3 1.5 collective-permute-done.7.refs_7_
  72.8 1.0 copy-done.8
  73.8 1.0 copy-done.9
  74.8 1.0 copy-done.10
  75.8 1.0 copy-done.11
  76.8 1.0 copy-done.12
  77.8 54.3 %all-gather.2.cloned.1.call-done = bf16[40960,128]{1,0:T(8,128)(2,1)} async-done(((bf16[1280,128]{1,0:T(8,128)(2,1)}), bf16[40960,128]{1,0:T(8,128)(2,1)}) %all-gather.2.cloned.1.call-update) | async-done | bytes 10485776 | tf_op jit(solution)/shard_map/all_gather | solution.py:395
  132.1 4.8 %slice.12.refs_0_ = bf16[8,4,4,128,128]{4,3,2,1,0:T(8,128)(2,1)} slice(bf16[8,4,10,128,128]{4,3,2,1,0:T(8,128)(2,1)} %bitcast.14), slice={[0:8], [0:4], [6:10], [0:128], [0:128]} | slice | bytes 8388608 | tf_op jit(solution)/shard_map/slice | solution.py:403
  136.9 1.3 collective-permute-start.10
  138.2 16.4 %shard_map.96 = (bf16[512,256]{1,0:T(8,128)(2,1)}, bf16[512,256]{1,0:T(8,128)(2,1)}) custom-call(bf16[128,4096]{1,0:T(8,128)(2,1)} %copy-done, bf16[128,4096]{1,0:T(8,128)(2,1)} %copy-done.6, bf16[128,4096]{1,0:T(8,128)(2,1)} %copy-done.7, bf16[128,4096]{1,0:T(8,128)(2,1)} %copy-done.8, bf16[128,4096]{1,0:T(8,128)(2,1)} %copy-done.9, ...), custom_call_target="tpu_custom_call" | custom-call | flops 6442450944 | bytes 14680064 | tf_op jit(solution)/shard_map/pallas_call | solution.py:190
  154.6 0.1 collective-permute-start.9
  154.7 1.7 collective-permute-done.9.theirs
  156.4 0.9 copy-done.4
  157.4 4.8 %shard_map.98 = (bf16[64,4096]{1,0:T(8,128)(2,1)S(1)}, bf16[64,4096]{1,0:T(8,128)(2,1)S(1)}, bf16[64,4096]{1,0:T(8,128)(2,1)}, bf16[64,4096]{1,0:T(8,128)(2,1)}) custom-call(bf16[512,256]{1,0:T(8,128)(2,1)S(1)} %copy-done.4, bf16[512,256]{1,0:T(8,128)(2,1)S(1)} %collective-permute-done.9.theirs, bf16[8,4,10,128,128]{4,3,2,1,0:T(8,128)(2,1)} %bitcast.16, ...), custom_call_target="tpu_custom_call" | custom-call | flops 1073741824 | bytes 4194304 | tf_op jit(solution)/shard_map/pallas_call | solution.py:238
  162.2 1.2 collective-permute-start.11
  163.5 1.5 collective-permute-start.12
  164.9 2.7 %collective-permute-start.15 = (bf16[64,4096]{1,0:T(8,128)(2,1)}, bf16[64,4096]{1,0:T(8,128)(2,1)S(1)}, u32[]{:S(2)}, u32[]{:S(2)}) collective-permute-start(bf16[64,4096]{1,0:T(8,128)(2,1)} %get-tuple-element.40), channel_id=1, source_target_pairs={{0,3},{1,0},{2,1},{3,2},{4,7},{5,4},{6,5},{7,6},{8,11},{9,8},{10,9... | collective-permute-start | bytes 1572872 | tf_op jit(solution)/shard_map/ppermute | solution.py:33
  167.6 5.4 %shard_map.99 = (f32[128,4096]{1,0:T(8,128)}, f32[64,4096]{1,0:T(8,128)}, f32[64,4096]{1,0:T(8,128)}) custom-call(bf16[512,256]{1,0:T(8,128)(2,1)S(1)} %copy-done.4, bf16[512,256]{1,0:T(8,128)(2,1)S(1)} %collective-permute-done.9.theirs, bf16[8,4,10,128,128]{4,3,2,1,0:T(8,128)(2,1)} %bitcast.17, ...), custom_call_target="tpu_custom_call" | custom-call | flops 1073741824 | bytes 4194304 | tf_op jit(solution)/shard_map/pallas_call | solution.py:238
  173.0 3.8 %collective-permute-done.11.b = bf16[64,4096]{1,0:T(8,128)(2,1)S(1)} collective-permute-done((bf16[64,4096]{1,0:T(8,128)(2,1)S(1)}, bf16[64,4096]{1,0:T(8,128)(2,1)S(1)}, u32[]{:S(2)}, u32[]{:S(2)}) %collective-permute-start.11) | collective-permute-done | bytes 524320 | tf_op jit(solution)/shard_map/ppermute | solution.py:33
  176.8 1.2 copy-done.2
  178.1 1.2 copy-done.3
  179.3 0.2 shard_map.100
  179.5 1.0 collective-permute-start.13
  180.4 1.8 collective-permute-start.16
  182.2 5.8 %collective-permute-done.14.high_a = bf16[64,4096]{1,0:T(8,128)(2,1)S(1)} collective-permute-done((bf16[64,4096]{1,0:T(8,128)(2,1)}, bf16[64,4096]{1,0:T(8,128)(2,1)S(1)}, u32[]{:S(2)}, u32[]{:S(2)}) %collective-permute-start.14) | collective-permute-done | bytes 524320 | tf_op jit(solution)/shard_map/ppermute | solution.py:33
  188.1 11.2 %collective-permute-done.13.low_a = bf16[64,4096]{1,0:T(8,128)(2,1)S(1)} collective-permute-done((bf16[64,4096]{1,0:T(8,128)(2,1)S(1)}, bf16[64,4096]{1,0:T(8,128)(2,1)S(1)}, u32[]{:S(2)}, u32[]{:S(2)}) %collective-permute-start.13) | collective-permute-done | bytes 524320 | tf_op jit(solution)/shard_map/ppermute | solution.py:33
  199.3 0.8 copy-done.14
  200.1 5.6 %shard_map.101 = (bf16[128,4096]{1,0:T(8,128)(2,1)}, bf16[128,512]{1,0:T(8,128)(2,1)S(1)}) custom-call(s32[1]{0:T(128)} %bitcast.place, bf16[128,4096]{1,0:T(8,128)(2,1)} %copy-done.13, f32[128,4096]{1,0:T(8,128)} %get-tuple-element.34.own, bf16[64,4096]{1,0:T(8,128)(2,1)S(1)} %collective-permute-done.13.low_a, ...), custom_call_target="tpu_custom_call" | custom-call | tf_op jit(solution)/shard_map/pallas_call | solution.py:313
  205.7 2.8 %collective-permute-start.18 = (bf16[128,512]{1,0:T(8,128)(2,1)S(1)}, bf16[128,512]{1,0:T(8,128)(2,1)S(1)}, u32[]{:S(2)}, u32[]{:S(2)}) collective-permute-start(bf16[128,512]{1,0:T(8,128)(2,1)S(1)} %get-tuple-element.43.refs_0_), channel_id=1, source_target_pairs={{0,128},{1,129},{2,130},{3,131},{4,132},{5,133},{6,134},{7,135},{8... | collective-permute-start | bytes 393224 | tf_op jit(solution)/shard_map/ppermute | solution.py:33
  208.5 5.0 %collective-permute-done.18 = bf16[128,512]{1,0:T(8,128)(2,1)S(1)} collective-permute-done((bf16[128,512]{1,0:T(8,128)(2,1)S(1)}, bf16[128,512]{1,0:T(8,128)(2,1)S(1)}, u32[]{:S(2)}, u32[]{:S(2)}) %collective-permute-start.18) | collective-permute-done | bytes 131104 | tf_op jit(solution)/shard_map/ppermute | solution.py:33
  213.5 0.9 collective-permute-start.19
  214.4 6.6 %collective-permute-start.17 = (bf16[128,4096]{1,0:T(8,128)(2,1)}, bf16[128,4096]{1,0:T(8,128)(2,1)S(1)}, u32[]{:S(2)}, u32[]{:S(2)}) collective-permute-start(bf16[128,4096]{1,0:T(8,128)(2,1)} %get-tuple-element.42), channel_id=1, source_target_pairs={{0,0},{1,1},{2,2},{3,3},{4,8},{5,9},{6,10},{7,11},{8,4},{9,5},{10,... | collective-permute-start | bytes 3145736 | tf_op jit(solution)/shard_map/ppermute | solution.py:33
  221.0 2.0 collective-permute-start.20
  223.0 0.9 collective-permute-start.21
  223.9 2.3 collective-permute-done.20
  226.2 3.2 %collective-permute-done.21 = bf16[128,512]{1,0:T(8,128)(2,1)S(1)} collective-permute-done((bf16[128,512]{1,0:T(8,128)(2,1)S(1)}, bf16[128,512]{1,0:T(8,128)(2,1)S(1)}, u32[]{:S(2)}, u32[]{:S(2)}) %collective-permute-start.21) | collective-permute-done | bytes 131104 | tf_op jit(solution)/shard_map/ppermute | solution.py:33
  229.4 1.2 collective-permute-start.22
  230.6 1.5 collective-permute-done.22.refs_4_
  232.2 4.2 %shard_map.102 = bf16[128,512]{1,0:T(8,128)(2,1)S(1)} custom-call(bf16[128,512]{1,0:T(8,128)(2,1)S(1)} %get-tuple-element.43.refs_0_, bf16[512,1536]{1,0:T(8,128)(2,1)S(1)} %copy-done.1, bf16[512,512]{1,0:T(8,128)(2,1)S(1)} %copy-done.5, bf16[512,512]{1,0:T(8,128)(2,1)S(1)} %constant_dynamic-update-slice_fusion.refs_3_, ...), custom_call_target="tpu_custom_call" | custom-call | tf_op jit(solution)/shard_map/pallas_call | solution.py:363
  236.4 1.9 collective-permute-start.23
  238.3 4.4 %collective-permute-done.23 = bf16[128,512]{1,0:T(8,128)(2,1)S(1)} collective-permute-done((bf16[128,512]{1,0:T(8,128)(2,1)S(1)}, bf16[128,512]{1,0:T(8,128)(2,1)S(1)}, u32[]{:S(2)}, u32[]{:S(2)}) %collective-permute-start.23) | collective-permute-done | bytes 131104 | tf_op jit(solution)/shard_map/ppermute | solution.py:33
  242.7 1.0 copy.42
  243.7 0.7 copy.43
  (47 shorter events, 0.1 us)
Async XLA Ops:
  7.2 30.4 %copy-start.16 = (f32[4096]{0:T(1024)S(1)}, f32[4096]{0:T(1024)}, u32[]{:S(2)}) copy-start(f32[4096]{0:T(1024)} %param.10) | copy-start | bytes 49156
  7.2 30.4 %copy-start.17 = (f32[4096]{0:T(1024)S(1)}, f32[4096]{0:T(1024)}, u32[]{:S(2)}) copy-start(f32[4096]{0:T(1024)} %param.9) | copy-start | bytes 49156
  7.2 124.9 %all-gather.2.cloned.1.call-start = ((), (), s32[]{:S(2)}) async-start(), calls=%async_computation | async-start | bytes 10813440 | tf_op jit(solution)/shard_map/all_gather | solution.py:395
  10.3 9.3 %collective-permute-start.8 = (bf16[1280,128]{1,0:T(8,128)(2,1)S(1)}, bf16[1280,128]{1,0:T(8,128)(2,1)S(1)}, u32[]{:S(2)}, u32[]{:S(2)}) collective-permute-start(bf16[1280,128]{1,0:T(8,128)(2,1)S(1)} %pad_maximum_fusion), channel_id=1, source_target_pairs={{0,0},{1,1},{2,2},{3,3},{4,8},{5,9},{6,10},{7,11},{8,4},{9,5},{10,... | collective-permute-start | bytes 983048 | tf_op jit(solution)/shard_map/ppermute | solution.py:33
  19.5 0.7 copy-start.15
  20.3 16.6 %collective-permute-start = (bf16[128,4096]{1,0:T(8,128)(2,1)}, bf16[128,4096]{1,0:T(8,128)(2,1)S(1)}, u32[]{:S(2)}, u32[]{:S(2)}) collective-permute-start(bf16[128,4096]{1,0:T(8,128)(2,1)} %param.8), channel_id=1, source_target_pairs={{0,0},{1,1},{2,2},{3,3},{4,8},{5,9},{6,10},{7,11},{8,4},{9,5},{10,... | collective-permute-start | bytes 3145736 | tf_op jit(solution)/shard_map/ppermute | solution.py:33
  36.9 1.2 copy-start.13
  38.1 29.0 %collective-permute-start.1 = (bf16[128,4096]{1,0:T(8,128)(2,1)S(1)}, bf16[128,4096]{1,0:T(8,128)(2,1)S(1)}, u32[]{:S(2)}, u32[]{:S(2)}) collective-permute-start(bf16[128,4096]{1,0:T(8,128)(2,1)S(1)} %fusion.5.refs_0_), channel_id=1, source_target_pairs={{0,1},{1,2},{2,3},{3,0},{4,5},{5,6},{6,7},{7,4},{8,9},{9,10},{10,1... | collective-permute-start | bytes 3145736 | tf_op jit(solution)/shard_map/ppermute | solution.py:33
  39.8 27.4 %collective-permute-start.2 = (bf16[128,4096]{1,0:T(8,128)(2,1)S(1)}, bf16[128,4096]{1,0:T(8,128)(2,1)S(1)}, u32[]{:S(2)}, u32[]{:S(2)}) collective-permute-start(bf16[128,4096]{1,0:T(8,128)(2,1)S(1)} %fusion.5.refs_0_), channel_id=1, source_target_pairs={{0,3},{1,0},{2,1},{3,2},{4,7},{5,4},{6,5},{7,6},{8,11},{9,8},{10,9... | collective-permute-start | bytes 3145736 | tf_op jit(solution)/shard_map/ppermute | solution.py:33
  41.3 26.4 %collective-permute-start.3 = (bf16[128,4096]{1,0:T(8,128)(2,1)S(1)}, bf16[128,4096]{1,0:T(8,128)(2,1)S(1)}, u32[]{:S(2)}, u32[]{:S(2)}) collective-permute-start(bf16[128,4096]{1,0:T(8,128)(2,1)S(1)} %fusion.5.refs_0_), channel_id=1, source_target_pairs={{0,2},{1,3},{2,0},{3,1},{4,6},{5,7},{6,4},{7,5},{8,10},{9,11},{10,... | collective-permute-start | bytes 3145736 | tf_op jit(solution)/shard_map/ppermute | solution.py:33
  42.8 24.9 %collective-permute-start.4 = (bf16[128,4096]{1,0:T(8,128)(2,1)S(1)}, bf16[128,4096]{1,0:T(8,128)(2,1)S(1)}, u32[]{:S(2)}, u32[]{:S(2)}) collective-permute-start(bf16[128,4096]{1,0:T(8,128)(2,1)S(1)} %fusion.5.refs_0_), channel_id=1, source_target_pairs={{0,8},{1,9},{2,10},{3,11},{4,12},{5,13},{6,14},{7,15},{8,0},{9,1},... | collective-permute-start | bytes 3145736 | tf_op jit(solution)/shard_map/ppermute | solution.py:33
  67.1 2.7 %collective-permute-start.5 = (bf16[128,4096]{1,0:T(8,128)(2,1)S(1)}, bf16[128,4096]{1,0:T(8,128)(2,1)S(1)}, u32[]{:S(2)}, u32[]{:S(2)}) collective-permute-start(bf16[128,4096]{1,0:T(8,128)(2,1)S(1)} %collective-permute-done.1.refs_1_), channel_id=1, source_target_pairs={{0,8},{1,9},{2,10},{3,11},{4,12},{5,13},{6,14},{7,15},{8,0},{9,1},... | collective-permute-start | bytes 3145736 | tf_op jit(solution)/shard_map/ppermute | solution.py:33
  67.1 4.2 %collective-permute-start.6 = (bf16[128,4096]{1,0:T(8,128)(2,1)S(1)}, bf16[128,4096]{1,0:T(8,128)(2,1)S(1)}, u32[]{:S(2)}, u32[]{:S(2)}) collective-permute-start(bf16[128,4096]{1,0:T(8,128)(2,1)S(1)} %collective-permute-done.2.refs_2_), channel_id=1, source_target_pairs={{0,8},{1,9},{2,10},{3,11},{4,12},{5,13},{6,14},{7,15},{8,0},{9,1},... | collective-permute-start | bytes 3145736 | tf_op jit(solution)/shard_map/ppermute | solution.py:33
  67.7 5.1 %collective-permute-start.7 = (bf16[128,4096]{1,0:T(8,128)(2,1)S(1)}, bf16[128,4096]{1,0:T(8,128)(2,1)S(1)}, u32[]{:S(2)}, u32[]{:S(2)}) collective-permute-start(bf16[128,4096]{1,0:T(8,128)(2,1)S(1)} %collective-permute-done.3.refs_3_), channel_id=1, source_target_pairs={{0,8},{1,9},{2,10},{3,11},{4,12},{5,13},{6,14},{7,15},{8,0},{9,1},... | collective-permute-start | bytes 3145736 | tf_op jit(solution)/shard_map/ppermute | solution.py:33
  72.8 1.0 copy-start.8
  73.8 1.0 copy-start.9
  74.8 1.0 copy-start.10
  75.8 1.0 copy-start.11
  76.8 1.0 copy-start.12
  77.8 59.1 %copy-start.6 = (bf16[128,4096]{1,0:T(8,128)(2,1)}, bf16[128,4096]{1,0:T(8,128)(2,1)S(1)}, u32[]{:S(2)}) copy-start(bf16[128,4096]{1,0:T(8,128)(2,1)S(1)} %get-tuple-element.24.refs_1_) | copy-start | bytes 3145732
  77.8 59.1 %copy-start.7 = (bf16[128,4096]{1,0:T(8,128)(2,1)}, bf16[128,4096]{1,0:T(8,128)(2,1)S(1)}, u32[]{:S(2)}) copy-start(bf16[128,4096]{1,0:T(8,128)(2,1)S(1)} %get-tuple-element.25.refs_2_) | copy-start | bytes 3145732
  77.8 59.1 %copy-start = (bf16[128,4096]{1,0:T(8,128)(2,1)}, bf16[128,4096]{1,0:T(8,128)(2,1)S(1)}, u32[]{:S(2)}) copy-start(bf16[128,4096]{1,0:T(8,128)(2,1)S(1)} %get-tuple-element.23.refs_0_.refs_1_) | copy-start | bytes 3145732
  136.9 19.5 %collective-permute-start.10 = (bf16[8,4,4,128,128]{4,3,2,1,0:T(8,128)(2,1)}, bf16[8,4,4,128,128]{4,3,2,1,0:T(8,128)(2,1)}, u32[]{:S(2)}, u32[]{:S(2)}) collective-permute-start(bf16[8,4,4,128,128]{4,3,2,1,0:T(8,128)(2,1)} %shard_map.97), channel_id=1, source_target_pairs={{0,8},{1,9},{2,10},{3,11},{4,12},{5,13},{6,14},{7,15},{8,0},{9,1},... | collective-permute-start | bytes 12582920 | tf_op jit(solution)/shard_map/ppermute | solution.py:33
  154.6 1.8 collective-permute-start.9
  156.4 1.0 copy-start.4
  162.2 14.6 %collective-permute-start.11 = (bf16[64,4096]{1,0:T(8,128)(2,1)S(1)}, bf16[64,4096]{1,0:T(8,128)(2,1)S(1)}, u32[]{:S(2)}, u32[]{:S(2)}) collective-permute-start(bf16[64,4096]{1,0:T(8,128)(2,1)S(1)} %get-tuple-element.33.refs_0_), channel_id=1, source_target_pairs={{0,1},{1,2},{2,3},{3,0},{4,5},{5,6},{6,7},{7,4},{8,9},{9,10},{10,1... | collective-permute-start | bytes 1572872 | tf_op jit(solution)/shard_map/ppermute | solution.py:33
  163.5 13.4 %collective-permute-start.12 = (bf16[64,4096]{1,0:T(8,128)(2,1)S(1)}, bf16[64,4096]{1,0:T(8,128)(2,1)S(1)}, u32[]{:S(2)}, u32[]{:S(2)}) collective-permute-start(bf16[64,4096]{1,0:T(8,128)(2,1)S(1)} %get-tuple-element.37), channel_id=1, source_target_pairs={{0,3},{1,0},{2,1},{3,2},{4,7},{5,4},{6,5},{7,6},{8,11},{9,8},{10,9... | collective-permute-start | bytes 1572872 | tf_op jit(solution)/shard_map/ppermute | solution.py:33
  164.9 23.2 %collective-permute-start.14 = (bf16[64,4096]{1,0:T(8,128)(2,1)}, bf16[64,4096]{1,0:T(8,128)(2,1)S(1)}, u32[]{:S(2)}, u32[]{:S(2)}) collective-permute-start(bf16[64,4096]{1,0:T(8,128)(2,1)} %get-tuple-element.39), channel_id=1, source_target_pairs={{0,1},{1,2},{2,3},{3,0},{4,5},{5,6},{6,7},{7,4},{8,9},{9,10},{10,1... | collective-permute-start | bytes 1572872 | tf_op jit(solution)/shard_map/ppermute | solution.py:33
  164.9 23.2 %collective-permute-start.15 = (bf16[64,4096]{1,0:T(8,128)(2,1)}, bf16[64,4096]{1,0:T(8,128)(2,1)S(1)}, u32[]{:S(2)}, u32[]{:S(2)}) collective-permute-start(bf16[64,4096]{1,0:T(8,128)(2,1)} %get-tuple-element.40), channel_id=1, source_target_pairs={{0,3},{1,0},{2,1},{3,2},{4,7},{5,4},{6,5},{7,6},{8,11},{9,8},{10,9... | collective-permute-start | bytes 1572872 | tf_op jit(solution)/shard_map/ppermute | solution.py:33
  176.8 1.2 copy-start.2
  178.1 1.2 copy-start.3
  179.5 19.8 %collective-permute-start.13 = (bf16[64,4096]{1,0:T(8,128)(2,1)S(1)}, bf16[64,4096]{1,0:T(8,128)(2,1)S(1)}, u32[]{:S(2)}, u32[]{:S(2)}) collective-permute-start(bf16[64,4096]{1,0:T(8,128)(2,1)S(1)} %get-tuple-element.38), channel_id=1, source_target_pairs={{0,1},{1,2},{2,3},{3,0},{4,5},{5,6},{6,7},{7,4},{8,9},{9,10},{10,1... | collective-permute-start | bytes 1572872 | tf_op jit(solution)/shard_map/ppermute | solution.py:33
  180.4 18.9 %collective-permute-start.16 = (bf16[64,4096]{1,0:T(8,128)(2,1)S(1)}, bf16[64,4096]{1,0:T(8,128)(2,1)S(1)}, u32[]{:S(2)}, u32[]{:S(2)}) collective-permute-start(bf16[64,4096]{1,0:T(8,128)(2,1)S(1)} %get-tuple-element.41), channel_id=1, source_target_pairs={{0,3},{1,0},{2,1},{3,2},{4,7},{5,4},{6,5},{7,6},{8,11},{9,8},{10,9... | collective-permute-start | bytes 1572872 | tf_op jit(solution)/shard_map/ppermute | solution.py:33
  199.3 0.8 copy-start.14
  200.1 32.0 %copy-start.1 = (bf16[512,1536]{1,0:T(8,128)(2,1)S(1)}, bf16[512,1536]{1,0:T(8,128)(2,1)}, u32[]{:S(2)}) copy-start(bf16[512,1536]{1,0:T(8,128)(2,1)} %refs_1_.1) | copy-start | bytes 4718596
  200.1 32.0 %copy-start.5 = (bf16[512,512]{1,0:T(8,128)(2,1)S(1)}, bf16[512,512]{1,0:T(8,128)(2,1)}, u32[]{:S(2)}) copy-start(bf16[512,512]{1,0:T(8,128)(2,1)} %refs_2_.1) | copy-start | bytes 1572868
  205.7 7.8 %collective-permute-start.18 = (bf16[128,512]{1,0:T(8,128)(2,1)S(1)}, bf16[128,512]{1,0:T(8,128)(2,1)S(1)}, u32[]{:S(2)}, u32[]{:S(2)}) collective-permute-start(bf16[128,512]{1,0:T(8,128)(2,1)S(1)} %get-tuple-element.43.refs_0_), channel_id=1, source_target_pairs={{0,128},{1,129},{2,130},{3,131},{4,132},{5,133},{6,134},{7,135},{8... | collective-permute-start | bytes 393224 | tf_op jit(solution)/shard_map/ppermute | solution.py:33
  213.5 10.4 %collective-permute-start.19 = (bf16[128,512]{1,0:T(8,128)(2,1)S(1)}, bf16[128,512]{1,0:T(8,128)(2,1)S(1)}, u32[]{:S(2)}, u32[]{:S(2)}) collective-permute-start(bf16[128,512]{1,0:T(8,128)(2,1)S(1)} %collective-permute-done.18), channel_id=1, source_target_pairs={{0,1},{1,2},{2,3},{3,0},{4,5},{5,6},{6,7},{7,4},{8,9},{9,10},{10,1... | collective-permute-start | bytes 393224 | tf_op jit(solution)/shard_map/ppermute | solution.py:33
  214.4 28.3 %collective-permute-start.17 = (bf16[128,4096]{1,0:T(8,128)(2,1)}, bf16[128,4096]{1,0:T(8,128)(2,1)S(1)}, u32[]{:S(2)}, u32[]{:S(2)}) collective-permute-start(bf16[128,4096]{1,0:T(8,128)(2,1)} %get-tuple-element.42), channel_id=1, source_target_pairs={{0,0},{1,1},{2,2},{3,3},{4,8},{5,9},{6,10},{7,11},{8,4},{9,5},{10,... | collective-permute-start | bytes 3145736 | tf_op jit(solution)/shard_map/ppermute | solution.py:33
  221.0 5.2 %collective-permute-start.20 = (bf16[128,512]{1,0:T(8,128)(2,1)S(1)}, bf16[128,512]{1,0:T(8,128)(2,1)S(1)}, u32[]{:S(2)}, u32[]{:S(2)}) collective-permute-start(bf16[128,512]{1,0:T(8,128)(2,1)S(1)} %collective-permute-done.18), channel_id=1, source_target_pairs={{0,3},{1,0},{2,1},{3,2},{4,7},{5,4},{6,5},{7,6},{8,11},{9,8},{10,9... | collective-permute-start | bytes 393224 | tf_op jit(solution)/shard_map/ppermute | solution.py:33
  223.0 6.3 %collective-permute-start.21 = (bf16[128,512]{1,0:T(8,128)(2,1)S(1)}, bf16[128,512]{1,0:T(8,128)(2,1)S(1)}, u32[]{:S(2)}, u32[]{:S(2)}) collective-permute-start(bf16[128,512]{1,0:T(8,128)(2,1)S(1)} %collective-permute-done.18), channel_id=1, source_target_pairs={{0,2},{1,3},{2,0},{3,1},{4,6},{5,7},{6,4},{7,5},{8,10},{9,11},{10,... | collective-permute-start | bytes 393224 | tf_op jit(solution)/shard_map/ppermute | solution.py:33
  229.4 2.8 %collective-permute-start.22 = (bf16[512,512]{1,0:T(8,128)(2,1)S(1)}, bf16[512,512]{1,0:T(8,128)(2,1)S(1)}, u32[]{:S(2)}, u32[]{:S(2)}) collective-permute-start(bf16[512,512]{1,0:T(8,128)(2,1)S(1)} %constant_dynamic-update-slice_fusion.refs_3_), channel_id=1, source_target_pairs={{0,8},{1,9},{2,10},{3,11},{4,12},{5,13},{6,14},{7,15},{8,0},{9,1},... | collective-permute-start | bytes 1572872 | tf_op jit(solution)/shard_map/ppermute | solution.py:33
  236.4 6.3 %collective-permute-start.23 = (bf16[128,512]{1,0:T(8,128)(2,1)S(1)}, bf16[128,512]{1,0:T(8,128)(2,1)S(1)}, u32[]{:S(2)}, u32[]{:S(2)}) collective-permute-start(bf16[128,512]{1,0:T(8,128)(2,1)S(1)} %shard_map.102), channel_id=1, source_target_pairs={{0,0},{1,1},{2,2},{3,3},{4,8},{5,9},{6,10},{7,11},{8,4},{9,5},{10,... | collective-permute-start | bytes 393224 | tf_op jit(solution)/shard_map/ppermute | solution.py:33
Sparse Core Ops, SparseCore 0:
  20.4 111.6 all-gather.1

commit v2 on v1

--- a/solution.py
+++ b/solution.py
@@ -205,10 +205,9 @@
     )(*pieces, weight)
 
 
-def out_kernel(skipped, picked, mine, theirs, weight, other_weight, *refs):
-    outs = refs[skipped:]
+def out_matrix(weight, other_weight):
     planes, xs, halves = weight.shape[:3]
-    matrix = jnp.concatenate(
+    return jnp.concatenate(
         [
             jnp.concatenate([w[p, x, h] for p in range(planes) for x in range(xs)], axis=1)
             for w in (weight, other_weight)
@@ -216,61 +215,9 @@
         ],
         axis=0,
     )
-    both = [
-        jnp.concatenate([mine[at : at + many, :], theirs[at : at + many, :]], axis=1)
-        for at, many in picked
-    ]
-    terms = dot(jnp.concatenate(both, axis=0), matrix)
-    at = 0
-    for out in outs:
-        out[...] = terms[at : at + out.shape[0]].astype(out.dtype)
-        at += out.shape[0]
-
-
-def out_projection(mine, theirs, weight, other_weight, picked, dtype, earlier=()):
-    earlier = list(earlier)
-    planes, xs, _, block, wide = weight.shape
-    at_once = 2
-    columns = at_once * xs * wide
-    rows = sum(many for _, many in picked)
-    whole = pl.BlockSpec(mine.shape, lambda i: (0, 0))
-    part = (at_once, xs, 2, block, wide)
-    return local(
-        functools.partial(out_kernel, len(earlier), picked),
-        tuple(jax.ShapeDtypeStruct((many, planes * xs * wide), dtype) for _, many in picked),
-        52,
-        flops=8 * rows * block * planes * xs * wide,
-        moved_bytes=8 * planes * xs * block * wide,
-        grid=(planes // at_once,),
-        in_specs=[
-            whole,
-            whole,
-            pl.BlockSpec(part, lambda i: (i, 0, 3, 0, 0)),
-            pl.BlockSpec(part, lambda i: (i, 0, 0, 0, 0)),
-        ]
-        + [pl.BlockSpec(memory_space=pltpu.HBM)] * len(earlier),
-        out_specs=tuple(pl.BlockSpec((many, columns), lambda i: (0, i)) for _, many in picked),
-    )(mine, theirs, weight, other_weight, *earlier)
-
-
-def added_kernel(a, b, c, d, first, second):
-    first[...] = (a[...] + b[...].astype(jnp.float32)).astype(first.dtype)
-    second[...] = (c[...] + d[...].astype(jnp.float32)).astype(second.dtype)
-
-
-def added(a, b, c, d):
-    return local(added_kernel, (jax.ShapeDtypeStruct(a.shape, b.dtype),) * 2, 20)(a, b, c, d)
-
-
-def features_kernel(
-    place, tokens, own, low_a, high_a, low_b, high_b, mine, theirs, features, descriptor, total
-):
-    step = pl.program_id(0)
-    summed = own[...]
-    summed = summed + jnp.concatenate([low_a[...], high_a[...]], axis=0).astype(jnp.float32)
-    summed = summed + jnp.concatenate([low_b[...], high_b[...]], axis=0).astype(jnp.float32)
-    rounded = (tokens[...].astype(jnp.float32) + summed).astype(jnp.bfloat16)
-    features[...] = rounded
+
+
+def match_matrix(place, mine, theirs):
     planes, xs, parts, block, _ = mine.shape
     half = block // 2
     first = place[0] == 0
@@ -285,48 +232,147 @@
                 for w in (mine, theirs)
             ]
             blocks += [jnp.where(first, *halves), jnp.where(first, *halves[::-1])]
-    term = dot(rounded, jnp.concatenate(blocks, axis=0))
+    return jnp.concatenate(blocks, axis=0)
+
+
+def send_kernel(picked, mine, theirs, weight, other_weight, *outs):
+    both = [
+        jnp.concatenate([mine[at : at + many, :], theirs[at : at + many, :]], axis=1)
+        for at, many in picked
+    ]
+    terms = dot(jnp.concatenate(both, axis=0), out_matrix(weight, other_weight))
+    at = 0
+    for out in outs:
+        out[...] = terms[at : at + out.shape[0]].astype(out.dtype)
+        at += out.shape[0]
+
+
+def weight_part(weights, blocks):
+    _, xs, _, block, wide = weights.shape
+    return pl.BlockSpec((2, xs, 2, block, wide), lambda i: (i, 0, blocks // 2, 0, 0))
+
+
+def terms_to_send(mine, theirs, weights, other_weights, picked):
+    planes, xs, _, _, wide = weights.shape
+    columns = 2 * xs * wide
+    whole = pl.BlockSpec(mine.shape, lambda i: (0, 0))
+    return local(
+        functools.partial(send_kernel, picked),
+        tuple(jax.ShapeDtypeStruct((many, planes * xs * wide), jnp.bfloat16) for _, many in picked),
+        52,
+        flops=2_000_000_000,
+        moved_bytes=8_000_000,
+        grid=(planes // 2,),
+        in_specs=[whole, whole, weight_part(weights, 6), weight_part(other_weights, 0)],
+        out_specs=tuple(pl.BlockSpec((many, columns), lambda i: (0, i)) for _, many in picked),
+    )(mine, theirs, weights, other_weights)
+
+
+def keep_kernel(
+    place, tokens, mine, theirs, weight, other_weight, match_mine, match_theirs, _, own, down, up, *rest
+):
+    *sums, total = rest
+    step = pl.program_id(0)
+    terms = dot(
+        jnp.concatenate([mine[...], theirs[...]], axis=1), out_matrix(weight, other_weight)
+    )
+    rows, mid = own.shape[0], down.shape[0]
+    own[...] = terms[:rows]
+    down[...] = terms[2 * rows - mid : 2 * rows]
+    up[...] = terms[2 * rows : 2 * rows + mid]
+    with_tokens = terms[:rows] + tokens[...].astype(jnp.float32)
+    rounded = jnp.concatenate([with_tokens, terms[rows:]], axis=0).astype(jnp.bfloat16)
+    product = dot(rounded, match_matrix(place, match_mine, match_theirs))
 
     @pl.when(step == 0)
     def _():
-        total[...] = term
+        total[...] = product
 
     @pl.when(step > 0)
     def _():
-        total[...] += term
+        total[...] += product
 
     @pl.when(step == pl.num_programs(0) - 1)
     def _():
-        descriptor[...] = total[...].astype(jnp.bfloat16)
-
-
-def features_and_descriptor(core, tokens, own, halves, weights, other_weights):
+        for i, out in enumerate(sums):
+            out[...] = total[i * rows : (i + 1) * rows].astype(out.dtype)
+
+
+def terms_to_keep(core, tokens, mine, theirs, weights, other_weights, earlier):
+    planes, xs, _, block, wide = weights.shape
     rows, depth = tokens.shape
-    _, xs, _, block, wide = weights.shape
-    parts = 2
-    width = 2 * parts * wide
-    at_once = 2
-    columns = at_once * xs * block
+    width = 4 * wide
+    columns = 2 * xs * wide
+    whole = pl.BlockSpec(mine.shape, lambda i: (0, 0))
+    full = pl.BlockSpec((rows, columns), lambda i: (0, i))
+    half = pl.BlockSpec((rows // 2, columns), lambda i: (0, i))
+    square = pl.BlockSpec((rows, width), lambda i: (0, 0))
+    f32, bf16 = jnp.float32, jnp.bfloat16
+    return local(
+        keep_kernel,
+        (jax.ShapeDtypeStruct((rows, depth), f32),)
+        + (jax.ShapeDtypeStruct((rows // 2, depth), f32),) * 2
+        + (jax.ShapeDtypeStruct((rows, width), f32),)
+        + (jax.ShapeDtypeStruct((rows, width), bf16),) * 3,
+        52,
+        flops=4_000_000_000,
+        moved_bytes=16_000_000,
+        grid=(planes // 2,),
+        in_specs=[
+            pl.BlockSpec(memory_space=pltpu.SMEM),
+            full,
+            whole,
+            whole,
+            weight_part(weights, 6),
+            weight_part(other_weights, 0),
+            weight_part(weights, 8),
+            weight_part(other_weights, 2),
+            pl.BlockSpec(memory_space=pltpu.HBM),
+        ],
+        out_specs=(full, half, half) + (square,) * 4,
+        scratch_shapes=[pltpu.VMEM((4 * rows, width), f32)],
+    )(
+        core.astype(jnp.int32).reshape(1),
+        tokens,
+        mine,
+        theirs,
+        weights,
+        other_weights,
+        weights,
+        other_weights,
+        earlier,
+    )
+
+
+def added_kernel(a, b, c, d, first, second):
+    first[...] = (a[...] + b[...].astype(jnp.float32)).astype(first.dtype)
+    second[...] = (c[...] + d[...].astype(jnp.float32)).astype(second.dtype)
+
+
+def added(a, b, c, d):
+    return local(added_kernel, (jax.ShapeDtypeStruct(a.shape, b.dtype),) * 2, 20)(a, b, c, d)
+
+
+def features_kernel(tokens, own, low_a, high_a, low_b, high_b, features):
+    summed = own[...]
+    summed = summed + jnp.concatenate([low_a[...], high_a[...]], axis=0).astype(jnp.float32)
+    summed = summed + jnp.concatenate([low_b[...], high_b[...]], axis=0).astype(jnp.float32)
+    features[...] = (tokens[...].astype(jnp.float32) + summed).astype(jnp.bfloat16)
+
+
+def features_of(tokens, own, halves):
+    rows, depth = tokens.shape
+    columns = 1024
     whole = pl.BlockSpec((rows, columns), lambda i: (0, i))
     half = pl.BlockSpec((rows // 2, columns), lambda i: (0, i))
-    part = (at_once, xs, parts, block, wide)
     return local(
         features_kernel,
-        (
-            jax.ShapeDtypeStruct((rows, depth), jnp.bfloat16),
-            jax.ShapeDtypeStruct((rows, width), jnp.bfloat16),
-        ),
-        52,
+        jax.ShapeDtypeStruct((rows, depth), jnp.bfloat16),
+        20,
         grid=(depth // columns,),
-        in_specs=[pl.BlockSpec(memory_space=pltpu.SMEM), whole, whole]
-        + [half] * 4
-        + [
-            pl.BlockSpec(part, lambda i: (i, 0, 4, 0, 0)),
-            pl.BlockSpec(part, lambda i: (i, 0, 1, 0, 0)),
-        ],
-        out_specs=(whole, pl.BlockSpec((rows, width), lambda i: (0, 0))),
-        scratch_shapes=[pltpu.VMEM((rows, width), jnp.float32)],
-    )(core.astype(jnp.int32).reshape(1), tokens, own, *halves, weights, other_weights)
+        in_specs=[whole, whole] + [half] * 4,
+        out_specs=whole,
+    )(tokens, own, *halves)
 
 
 def matcher_kernel(*refs):
@@ -404,27 +450,23 @@
     mine, theirs = attention(pieces, weights)
 
     both = (mine, moved(theirs, other_core), weights, other_weights)
-    far_low, far_high, up_high, down_low = out_projection(
-        *both,
-        [(3 * rows, mid), (3 * rows + mid, mid), (2 * rows + mid, mid), (rows, mid)],
-        bf16,
-    )
-    own, down_high, up_low = out_projection(
-        *both, [(0, rows), (rows + mid, mid), (2 * rows, mid)], f32, [far_low]
+    far_low, far_high, up_high, down_low = terms_to_send(
+        *both, [(3 * rows, mid), (3 * rows + mid, mid), (2 * rows + mid, mid), (rows, mid)]
+    )
+    own, down_high, up_low, *sums = terms_to_keep(
+        lax.axis_index("core"), tokens, *both, far_low
     )
     far_low, far_high = moved(far_low, along_y(1)), moved(far_high, along_y(-1))
     up_high, down_low = moved(up_high, along_y(1)), moved(down_low, along_y(-1))
+
+    received = [moved(part, along_y(k)) for part, k in zip(sums[1:], (-1, 1, 2))]
+    descriptor = sums[0] + sum(part.astype(f32) for part in received)
+    descriptor = descriptor.astype(bf16)
+
     up_low, down_high = added(up_low, far_low, down_high, far_high)
     up_low, down_high = moved(up_low, along_y(1)), moved(down_high, along_y(-1))
-
-    features, descriptor = features_and_descriptor(
-        lax.axis_index("core"),
-        tokens,
-        own,
-        (up_low, up_high, down_low, down_high),
-        weights,
-        other_weights,
-    )
+    features = features_of(tokens, own, (up_low, up_high, down_low, down_high))
+
     partner = moved(descriptor, along_z(4))
     quarter = jnp.concatenate([partner] + [moved(partner, along_y(k)) for k in DISTANCES], axis=0)
     pieces = [quarter, moved(quarter, other_core)]

time: 252 us -> 251 us (level)
    ppermute x24 -> x27, starting transfers between devices: 39.4 us -> 41.8 us  [moved(): return lax.ppermute(block, AXES, route)]
    ppermute x24 -> x27, waiting for transfers between devices: 86 us -> 84.4 us  [moved(): return lax.ppermute(block, AXES, route)]
    unnamed x42 -> x50, local copies, waits for them, and re-layouts: 12.7 us -> 11.8 us
  transfers between devices with their start and end apart: 25 -> 28, of which waited for: 16 -> 14; matrix products, arithmetic and copies ran while one was open for 0% -> 1% of each run, Pallas kernels for 10% -> 12%
where the time goes in v2:
time: 251 us; the launch traced here: 250 us
  waiting for transfers between devices  139 us (55%)
  starting transfers between devices  41.8 us (17%)
  Pallas kernels  35.6 us (14%)
  local copies, waits for them, and re-layouts  16.8 us (7%)
  between operations  14.3 us (6%)
  other arithmetic  2.98 us (1%)
    ppermute x27, waiting for transfers between devices, moved(): return lax.ppermute(block, AXES, route)  84.4 us
    all_gather x1, waiting for transfers between devices, per_device(): weights = lax.all_gather(packed, ('z', 'xh', 'xl'), axis=0, tiled=True)  54.4 us
    ppermute x27, starting transfers between devices, moved(): return lax.ppermute(block, AXES, route)  41.8 us
    pallas_call x1, Pallas kernels, attention(): local(attention_kernel, (result, result), 60, flops=2 * count * depth * c...  16.4 us
    unnamed x50, local copies, waits for them, and re-layouts  11.8 us
    pallas_call x1, Pallas kernels, terms_to_keep(): local(keep_kernel, (jax.ShapeDtypeStruct((rows, depth), f32),) + (jax.Sha...  8.95 us
  transfers between devices with their start and end apart: 28, of which 14 were waited for; matrix products, arithmetic and copies ran while one was open for 1% of the time, Pallas kernels for 12%

profile of v2, /device:TPU:1, one launch (start us, length us, event | category | flops | bytes accessed | tf_op | source)
XLA Modules:
  0.0 250.4 jit_solution(15517120077464205436)
XLA Ops:
  7.2 1.1 copy.23
  8.3 0.2 copy.24
  8.5 0.9 copy_bitcast_fusion
  9.4 0.9 pad_maximum_fusion
  10.3 4.5 %collective-permute-start.8 = (bf16[1280,128]{1,0:T(8,128)(2,1)S(1)}, bf16[1280,128]{1,0:T(8,128)(2,1)S(1)}, u32[]{:S(2)}, u32[]{:S(2)}) collective-permute-start(bf16[1280,128]{1,0:T(8,128)(2,1)S(1)} %pad_maximum_fusion), channel_id=1, source_target_pairs={{0,0},{1,1},{2,2},{3,3},{4,8},{5,9},{6,10},{7,11},{8,4},{9,5},{10,... | collective-permute-start | bytes 983048 | tf_op jit(solution)/shard_map/ppermute | solution.py:33
  14.8 4.7 %collective-permute-done.8 = bf16[1280,128]{1,0:T(8,128)(2,1)S(1)} collective-permute-done((bf16[1280,128]{1,0:T(8,128)(2,1)S(1)}, bf16[1280,128]{1,0:T(8,128)(2,1)S(1)}, u32[]{:S(2)}, u32[]{:S(2)}) %collective-permute-start.8) | collective-permute-done | bytes 327712 | tf_op jit(solution)/shard_map/ppermute | solution.py:33
  19.5 0.7 copy-done.17
  20.3 3.6 %collective-permute-start = (bf16[128,4096]{1,0:T(8,128)(2,1)}, bf16[128,4096]{1,0:T(8,128)(2,1)S(1)}, u32[]{:S(2)}, u32[]{:S(2)}) collective-permute-start(bf16[128,4096]{1,0:T(8,128)(2,1)} %param.8), channel_id=1, source_target_pairs={{0,0},{1,1},{2,2},{3,3},{4,8},{5,9},{6,10},{7,11},{8,4},{9,5},{10,... | collective-permute-start | bytes 3145736 | tf_op jit(solution)/shard_map/ppermute | solution.py:33
  23.9 13.0 %collective-permute-done.tokens = bf16[128,4096]{1,0:T(8,128)(2,1)S(1)} collective-permute-done((bf16[128,4096]{1,0:T(8,128)(2,1)}, bf16[128,4096]{1,0:T(8,128)(2,1)S(1)}, u32[]{:S(2)}, u32[]{:S(2)}) %collective-permute-start) | collective-permute-done | bytes 1048608 | tf_op jit(solution)/shard_map/ppermute | solution.py:33
  36.9 0.2 convert_reduce_fusion
  37.2 0.4 fusion.2
  37.6 0.5 fusion.5.refs_0_
  38.1 1.7 collective-permute-start.1
  39.8 1.5 collective-permute-start.2
  41.3 1.6 collective-permute-start.3
  42.9 24.3 %collective-permute-done.1.refs_1_ = bf16[128,4096]{1,0:T(8,128)(2,1)S(1)} collective-permute-done((bf16[128,4096]{1,0:T(8,128)(2,1)S(1)}, bf16[128,4096]{1,0:T(8,128)(2,1)S(1)}, u32[]{:S(2)}, u32[]{:S(2)}) %collective-permute-start.1) | collective-permute-done | bytes 1048608 | tf_op jit(solution)/shard_map/ppermute | solution.py:33
  67.2 0.5 collective-permute-start.6
  67.7 0.1 collective-permute-start.7
  67.8 2.0 collective-permute-done.5.refs_5_
  69.8 1.5 collective-permute-done.6.refs_6_
  71.3 1.5 collective-permute-done.7.refs_7_
  72.8 1.0 copy-done.12
  73.8 1.0 copy-done.13
  74.8 1.0 copy-done.14
  75.8 1.0 copy-done.15
  76.8 1.0 copy-done.16
  77.7 54.4 %all-gather.2.cloned.1.call-done = bf16[40960,128]{1,0:T(8,128)(2,1)} async-done(((bf16[1280,128]{1,0:T(8,128)(2,1)}), bf16[40960,128]{1,0:T(8,128)(2,1)}) %all-gather.2.cloned.1.call-update) | async-done | bytes 10485776 | tf_op jit(solution)/shard_map/all_gather | solution.py:441
  132.1 4.7 %slice.12.refs_0_ = bf16[8,4,4,128,128]{4,3,2,1,0:T(8,128)(2,1)} slice(bf16[8,4,10,128,128]{4,3,2,1,0:T(8,128)(2,1)} %bitcast.14), slice={[0:8], [0:4], [6:10], [0:128], [0:128]} | slice | bytes 8388608 | tf_op jit(solution)/shard_map/slice | solution.py:449
  136.9 1.3 collective-permute-start.10
  138.2 16.4 %shard_map.96 = (bf16[512,256]{1,0:T(8,128)(2,1)}, bf16[512,256]{1,0:T(8,128)(2,1)}) custom-call(bf16[128,4096]{1,0:T(8,128)(2,1)} %copy-done.2, bf16[128,4096]{1,0:T(8,128)(2,1)} %copy-done.10, bf16[128,4096]{1,0:T(8,128)(2,1)} %copy-done.11, bf16[128,4096]{1,0:T(8,128)(2,1)} %copy-done.12, bf16[128,4096]{1,0:T(8,128)(2,1)} %copy-done.13, ...), custom_call_target="tpu_custom_call" | custom-call | flops 6442450944 | bytes 14680064 | tf_op jit(solution)/shard_map/pallas_call | solution.py:190
  154.6 0.1 collective-permute-start.9
  154.7 1.7 collective-permute-done.9.theirs
  156.4 0.9 copy-done.7
  157.4 4.9 %shard_map.98 = (bf16[64,4096]{1,0:T(8,128)(2,1)S(1)}, bf16[64,4096]{1,0:T(8,128)(2,1)S(1)}, bf16[64,4096]{1,0:T(8,128)(2,1)}, bf16[64,4096]{1,0:T(8,128)(2,1)}) custom-call(bf16[512,256]{1,0:T(8,128)(2,1)S(1)} %copy-done.7, bf16[512,256]{1,0:T(8,128)(2,1)S(1)} %collective-permute-done.9.theirs, bf16[8,4,10,128,128]{4,3,2,1,0:T(8,128)(2,1)} %bitcast.16, ...), custom_call_target="tpu_custom_call" | custom-call | flops 2000000000 | bytes 8000000 | tf_op jit(solution)/shard_map/pallas_call | solution.py:259
  162.3 1.2 collective-permute-start.11
  163.5 1.5 collective-permute-start.12
  165.0 9.0 %shard_map.99 = (f32[128,4096]{1,0:T(8,128)}, f32[64,4096]{1,0:T(8,128)}, f32[64,4096]{1,0:T(8,128)}, f32[128,512]{1,0:T(8,128)S(1)}, bf16[128,512]{1,0:T(8,128)...) custom-call(s32[1]{0:T(128)} %bitcast.place, bf16[128,4096]{1,0:T(8,128)(2,1)} %copy-done, ...), custom_call_target="tpu_custom_call" | custom-call | flops 4000000000 | bytes 16000000 | tf_op jit(solution)/shard_map/pallas_call | solution.py:311
  173.9 1.6 collective-permute-start.20
  175.5 0.3 collective-permute-start.19
  175.8 0.8 collective-permute-start.14
  176.7 0.2 collective-permute-done.11.b
  176.9 1.7 collective-permute-start.15
  178.5 1.2 copy-done.5
  179.8 1.2 copy-done.6
  181.0 0.2 shard_map.100
  181.2 0.3 collective-permute-start.13
  181.5 2.7 %collective-permute-start.16 = (bf16[64,4096]{1,0:T(8,128)(2,1)S(1)}, bf16[64,4096]{1,0:T(8,128)(2,1)S(1)}, u32[]{:S(2)}, u32[]{:S(2)}) collective-permute-start(bf16[64,4096]{1,0:T(8,128)(2,1)S(1)} %get-tuple-element.43), channel_id=1, source_target_pairs={{0,3},{1,0},{2,1},{3,2},{4,7},{5,4},{6,5},{7,6},{8,11},{9,8},{10,9... | collective-permute-start | bytes 1572872 | tf_op jit(solution)/shard_map/ppermute | solution.py:33
  184.1 0.1 collective-permute-start.18
  184.2 20.2 %collective-permute-done.18 = bf16[128,512]{1,0:T(8,128)(2,1)S(1)} collective-permute-done((bf16[128,512]{1,0:T(8,128)(2,1)S(1)}, bf16[128,512]{1,0:T(8,128)(2,1)S(1)}, u32[]{:S(2)}, u32[]{:S(2)}) %collective-permute-start.18) | collective-permute-done | bytes 131104 | tf_op jit(solution)/shard_map/ppermute | solution.py:33
  204.4 0.1 add_convert_fusion.refs_0_
  204.5 2.9 %collective-permute-start.21 = (bf16[128,512]{1,0:T(8,128)(2,1)S(1)}, bf16[128,512]{1,0:T(8,128)(2,1)S(1)}, u32[]{:S(2)}, u32[]{:S(2)}) collective-permute-start(bf16[128,512]{1,0:T(8,128)(2,1)S(1)} %add_convert_fusion.refs_0_), channel_id=1, source_target_pairs={{0,128},{1,129},{2,130},{3,131},{4,132},{5,133},{6,134},{7,135},{8... | collective-permute-start | bytes 393224 | tf_op jit(solution)/shard_map/ppermute | solution.py:33
  207.4 5.0 %collective-permute-done.21 = bf16[128,512]{1,0:T(8,128)(2,1)S(1)} collective-permute-done((bf16[128,512]{1,0:T(8,128)(2,1)S(1)}, bf16[128,512]{1,0:T(8,128)(2,1)S(1)}, u32[]{:S(2)}, u32[]{:S(2)}) %collective-permute-start.21) | collective-permute-done | bytes 131104 | tf_op jit(solution)/shard_map/ppermute | solution.py:33
  212.4 3.2 %collective-permute-start.22 = (bf16[128,512]{1,0:T(8,128)(2,1)S(1)}, bf16[128,512]{1,0:T(8,128)(2,1)S(1)}, u32[]{:S(2)}, u32[]{:S(2)}) collective-permute-start(bf16[128,512]{1,0:T(8,128)(2,1)S(1)} %collective-permute-done.21), channel_id=1, source_target_pairs={{0,1},{1,2},{2,3},{3,0},{4,5},{5,6},{6,7},{7,4},{8,9},{9,10},{10,1... | collective-permute-start | bytes 393224 | tf_op jit(solution)/shard_map/ppermute | solution.py:33
  215.7 1.0 shard_map.101
  216.7 6.4 %collective-permute-start.17 = (bf16[128,4096]{1,0:T(8,128)(2,1)S(1)}, bf16[128,4096]{1,0:T(8,128)(2,1)S(1)}, u32[]{:S(2)}, u32[]{:S(2)}) collective-permute-start(bf16[128,4096]{1,0:T(8,128)(2,1)S(1)} %shard_map.101), channel_id=1, source_target_pairs={{0,0},{1,1},{2,2},{3,3},{4,8},{5,9},{6,10},{7,11},{8,4},{9,5},{10,... | collective-permute-start | bytes 3145736 | tf_op jit(solution)/shard_map/ppermute | solution.py:33
  223.1 1.7 collective-permute-start.24
  224.9 4.5 %collective-permute-done.24 = bf16[128,512]{1,0:T(8,128)(2,1)S(1)} collective-permute-done((bf16[128,512]{1,0:T(8,128)(2,1)S(1)}, bf16[128,512]{1,0:T(8,128)(2,1)S(1)}, u32[]{:S(2)}, u32[]{:S(2)}) %collective-permute-start.24) | collective-permute-done | bytes 131104 | tf_op jit(solution)/shard_map/ppermute | solution.py:33
  229.4 0.3 collective-permute-start.25
  229.7 1.7 collective-permute-done.25.refs_4_
  231.4 4.2 %shard_map.102 = bf16[128,512]{1,0:T(8,128)(2,1)S(1)} custom-call(bf16[128,512]{1,0:T(8,128)(2,1)S(1)} %add_convert_fusion.refs_0_, bf16[512,1536]{1,0:T(8,128)(2,1)S(1)} %copy-done.4, bf16[512,512]{1,0:T(8,128)(2,1)S(1)} %copy-done.9, bf16[512,512]{1,0:T(8,128)(2,1)S(1)} %constant_dynamic-update-slice_fusion.refs_3_, ...), custom_call_target="tpu_custom_call" | custom-call | tf_op jit(solution)/shard_map/pallas_call | solution.py:409
  235.6 2.2 collective-permute-start.26
  237.8 4.1 %collective-permute-done.26 = bf16[128,512]{1,0:T(8,128)(2,1)S(1)} collective-permute-done((bf16[128,512]{1,0:T(8,128)(2,1)S(1)}, bf16[128,512]{1,0:T(8,128)(2,1)S(1)}, u32[]{:S(2)}, u32[]{:S(2)}) %collective-permute-start.26) | collective-permute-done | bytes 131104 | tf_op jit(solution)/shard_map/ppermute | solution.py:33
  241.9 1.0 copy.42
  242.9 0.7 copy.43
  (62 shorter events, 0.2 us)
Async XLA Ops:
  7.2 30.4 %copy-start.18 = (f32[4096]{0:T(1024)S(1)}, f32[4096]{0:T(1024)}, u32[]{:S(2)}) copy-start(f32[4096]{0:T(1024)} %param.10) | copy-start | bytes 49156
  7.2 30.4 %copy-start.19 = (f32[4096]{0:T(1024)S(1)}, f32[4096]{0:T(1024)}, u32[]{:S(2)}) copy-start(f32[4096]{0:T(1024)} %param.9) | copy-start | bytes 49156
  7.2 125.0 %all-gather.2.cloned.1.call-start = ((), (), s32[]{:S(2)}) async-start(), calls=%async_computation | async-start | bytes 10813440 | tf_op jit(solution)/shard_map/all_gather | solution.py:441
  10.3 9.3 %collective-permute-start.8 = (bf16[1280,128]{1,0:T(8,128)(2,1)S(1)}, bf16[1280,128]{1,0:T(8,128)(2,1)S(1)}, u32[]{:S(2)}, u32[]{:S(2)}) collective-permute-start(bf16[1280,128]{1,0:T(8,128)(2,1)S(1)} %pad_maximum_fusion), channel_id=1, source_target_pairs={{0,0},{1,1},{2,2},{3,3},{4,8},{5,9},{6,10},{7,11},{8,4},{9,5},{10,... | collective-permute-start | bytes 983048 | tf_op jit(solution)/shard_map/ppermute | solution.py:33
  19.5 0.7 copy-start.17
  20.3 16.6 %collective-permute-start = (bf16[128,4096]{1,0:T(8,128)(2,1)}, bf16[128,4096]{1,0:T(8,128)(2,1)S(1)}, u32[]{:S(2)}, u32[]{:S(2)}) collective-permute-start(bf16[128,4096]{1,0:T(8,128)(2,1)} %param.8), channel_id=1, source_target_pairs={{0,0},{1,1},{2,2},{3,3},{4,8},{5,9},{6,10},{7,11},{8,4},{9,5},{10,... | collective-permute-start | bytes 3145736 | tf_op jit(solution)/shard_map/ppermute | solution.py:33
  36.9 1.2 copy-start
  38.1 29.0 %collective-permute-start.1 = (bf16[128,4096]{1,0:T(8,128)(2,1)S(1)}, bf16[128,4096]{1,0:T(8,128)(2,1)S(1)}, u32[]{:S(2)}, u32[]{:S(2)}) collective-permute-start(bf16[128,4096]{1,0:T(8,128)(2,1)S(1)} %fusion.5.refs_0_), channel_id=1, source_target_pairs={{0,1},{1,2},{2,3},{3,0},{4,5},{5,6},{6,7},{7,4},{8,9},{9,10},{10,1... | collective-permute-start | bytes 3145736 | tf_op jit(solution)/shard_map/ppermute | solution.py:33
  39.8 27.4 %collective-permute-start.2 = (bf16[128,4096]{1,0:T(8,128)(2,1)S(1)}, bf16[128,4096]{1,0:T(8,128)(2,1)S(1)}, u32[]{:S(2)}, u32[]{:S(2)}) collective-permute-start(bf16[128,4096]{1,0:T(8,128)(2,1)S(1)} %fusion.5.refs_0_), channel_id=1, source_target_pairs={{0,3},{1,0},{2,1},{3,2},{4,7},{5,4},{6,5},{7,6},{8,11},{9,8},{10,9... | collective-permute-start | bytes 3145736 | tf_op jit(solution)/shard_map/ppermute | solution.py:33
  41.3 26.4 %collective-permute-start.3 = (bf16[128,4096]{1,0:T(8,128)(2,1)S(1)}, bf16[128,4096]{1,0:T(8,128)(2,1)S(1)}, u32[]{:S(2)}, u32[]{:S(2)}) collective-permute-start(bf16[128,4096]{1,0:T(8,128)(2,1)S(1)} %fusion.5.refs_0_), channel_id=1, source_target_pairs={{0,2},{1,3},{2,0},{3,1},{4,6},{5,7},{6,4},{7,5},{8,10},{9,11},{10,... | collective-permute-start | bytes 3145736 | tf_op jit(solution)/shard_map/ppermute | solution.py:33
  42.9 24.9 %collective-permute-start.4 = (bf16[128,4096]{1,0:T(8,128)(2,1)S(1)}, bf16[128,4096]{1,0:T(8,128)(2,1)S(1)}, u32[]{:S(2)}, u32[]{:S(2)}) collective-permute-start(bf16[128,4096]{1,0:T(8,128)(2,1)S(1)} %fusion.5.refs_0_), channel_id=1, source_target_pairs={{0,8},{1,9},{2,10},{3,11},{4,12},{5,13},{6,14},{7,15},{8,0},{9,1},... | collective-permute-start | bytes 3145736 | tf_op jit(solution)/shard_map/ppermute | solution.py:33
  67.2 2.7 %collective-permute-start.5 = (bf16[128,4096]{1,0:T(8,128)(2,1)S(1)}, bf16[128,4096]{1,0:T(8,128)(2,1)S(1)}, u32[]{:S(2)}, u32[]{:S(2)}) collective-permute-start(bf16[128,4096]{1,0:T(8,128)(2,1)S(1)} %collective-permute-done.1.refs_1_), channel_id=1, source_target_pairs={{0,8},{1,9},{2,10},{3,11},{4,12},{5,13},{6,14},{7,15},{8,0},{9,1},... | collective-permute-start | bytes 3145736 | tf_op jit(solution)/shard_map/ppermute | solution.py:33
  67.2 4.2 %collective-permute-start.6 = (bf16[128,4096]{1,0:T(8,128)(2,1)S(1)}, bf16[128,4096]{1,0:T(8,128)(2,1)S(1)}, u32[]{:S(2)}, u32[]{:S(2)}) collective-permute-start(bf16[128,4096]{1,0:T(8,128)(2,1)S(1)} %collective-permute-done.2.refs_2_), channel_id=1, source_target_pairs={{0,8},{1,9},{2,10},{3,11},{4,12},{5,13},{6,14},{7,15},{8,0},{9,1},... | collective-permute-start | bytes 3145736 | tf_op jit(solution)/shard_map/ppermute | solution.py:33
  67.7 5.1 %collective-permute-start.7 = (bf16[128,4096]{1,0:T(8,128)(2,1)S(1)}, bf16[128,4096]{1,0:T(8,128)(2,1)S(1)}, u32[]{:S(2)}, u32[]{:S(2)}) collective-permute-start(bf16[128,4096]{1,0:T(8,128)(2,1)S(1)} %collective-permute-done.3.refs_3_), channel_id=1, source_target_pairs={{0,8},{1,9},{2,10},{3,11},{4,12},{5,13},{6,14},{7,15},{8,0},{9,1},... | collective-permute-start | bytes 3145736 | tf_op jit(solution)/shard_map/ppermute | solution.py:33
  72.8 1.0 copy-start.12
  73.8 1.0 copy-start.13
  74.8 1.0 copy-start.14
  75.8 1.0 copy-start.15
  76.8 1.0 copy-start.16
  77.7 59.2 %copy-start.10 = (bf16[128,4096]{1,0:T(8,128)(2,1)}, bf16[128,4096]{1,0:T(8,128)(2,1)S(1)}, u32[]{:S(2)}) copy-start(bf16[128,4096]{1,0:T(8,128)(2,1)S(1)} %get-tuple-element.26.refs_1_) | copy-start | bytes 3145732
  77.7 59.2 %copy-start.11 = (bf16[128,4096]{1,0:T(8,128)(2,1)}, bf16[128,4096]{1,0:T(8,128)(2,1)S(1)}, u32[]{:S(2)}) copy-start(bf16[128,4096]{1,0:T(8,128)(2,1)S(1)} %get-tuple-element.27.refs_2_) | copy-start | bytes 3145732
  77.7 59.2 %copy-start.2 = (bf16[128,4096]{1,0:T(8,128)(2,1)}, bf16[128,4096]{1,0:T(8,128)(2,1)S(1)}, u32[]{:S(2)}) copy-start(bf16[128,4096]{1,0:T(8,128)(2,1)S(1)} %get-tuple-element.25.refs_0_.refs_1_) | copy-start | bytes 3145732
  136.9 19.5 %collective-permute-start.10 = (bf16[8,4,4,128,128]{4,3,2,1,0:T(8,128)(2,1)}, bf16[8,4,4,128,128]{4,3,2,1,0:T(8,128)(2,1)}, u32[]{:S(2)}, u32[]{:S(2)}) collective-permute-start(bf16[8,4,4,128,128]{4,3,2,1,0:T(8,128)(2,1)} %shard_map.97), channel_id=1, source_target_pairs={{0,8},{1,9},{2,10},{3,11},{4,12},{5,13},{6,14},{7,15},{8,0},{9,1},... | collective-permute-start | bytes 12582920 | tf_op jit(solution)/shard_map/ppermute | solution.py:33
  154.6 1.8 collective-permute-start.9
  156.4 1.0 copy-start.7
  157.4 7.6 %copy-start.8 = (bf16[512,256]{1,0:T(8,128)(2,1)S(1)}, bf16[512,256]{1,0:T(8,128)(2,1)}, u32[]{:S(2)}) copy-start(bf16[512,256]{1,0:T(8,128)(2,1)} %get-tuple-element.33.mine) | copy-start | bytes 786436
  162.3 14.6 %collective-permute-start.11 = (bf16[64,4096]{1,0:T(8,128)(2,1)S(1)}, bf16[64,4096]{1,0:T(8,128)(2,1)S(1)}, u32[]{:S(2)}, u32[]{:S(2)}) collective-permute-start(bf16[64,4096]{1,0:T(8,128)(2,1)S(1)} %get-tuple-element.35._), channel_id=1, source_target_pairs={{0,1},{1,2},{2,3},{3,0},{4,5},{5,6},{6,7},{7,4},{8,9},{9,10},{10,1... | collective-permute-start | bytes 1572872 | tf_op jit(solution)/shard_map/ppermute | solution.py:33
  163.5 15.0 %collective-permute-start.12 = (bf16[64,4096]{1,0:T(8,128)(2,1)S(1)}, bf16[64,4096]{1,0:T(8,128)(2,1)S(1)}, u32[]{:S(2)}, u32[]{:S(2)}) collective-permute-start(bf16[64,4096]{1,0:T(8,128)(2,1)S(1)} %get-tuple-element.39), channel_id=1, source_target_pairs={{0,3},{1,0},{2,1},{3,2},{4,7},{5,4},{6,5},{7,6},{8,11},{9,8},{10,9... | collective-permute-start | bytes 1572872 | tf_op jit(solution)/shard_map/ppermute | solution.py:33
  165.0 10.9 %copy-start.21 = (bf16[64,4096]{1,0:T(8,128)(2,1)S(1)}, bf16[64,4096]{1,0:T(8,128)(2,1)}, u32[]{:S(2)}) copy-start(bf16[64,4096]{1,0:T(8,128)(2,1)} %get-tuple-element.41) | copy-start | bytes 1572868
  165.0 11.9 %copy-start.20 = (bf16[64,4096]{1,0:T(8,128)(2,1)S(1)}, bf16[64,4096]{1,0:T(8,128)(2,1)}, u32[]{:S(2)}) copy-start(bf16[64,4096]{1,0:T(8,128)(2,1)} %get-tuple-element.42) | copy-start | bytes 1572868
  173.9 41.7 %copy-start.1 = (bf16[128,4096]{1,0:T(8,128)(2,1)S(1)}, bf16[128,4096]{1,0:T(8,128)(2,1)}, u32[]{:S(2)}) copy-start(bf16[128,4096]{1,0:T(8,128)(2,1)} %copy-done) | copy-start | bytes 3145732
  173.9 41.7 %copy-start.3 = (f32[128,4096]{1,0:T(8,128)S(1)}, f32[128,4096]{1,0:T(8,128)}, u32[]{:S(2)}) copy-start(f32[128,4096]{1,0:T(8,128)} %get-tuple-element.36.own) | copy-start | bytes 6291460
  173.9 7.6 %collective-permute-start.20 = (bf16[128,512]{1,0:T(8,128)(2,1)S(1)}, bf16[128,512]{1,0:T(8,128)(2,1)S(1)}, u32[]{:S(2)}, u32[]{:S(2)}) collective-permute-start(bf16[128,512]{1,0:T(8,128)(2,1)S(1)} %get-tuple-element.47), channel_id=1, source_target_pairs={{0,2},{1,3},{2,0},{3,1},{4,6},{5,7},{6,4},{7,5},{8,10},{9,11},{10,... | collective-permute-start | bytes 393224 | tf_op jit(solution)/shard_map/ppermute | solution.py:33
  175.5 8.6 %collective-permute-start.19 = (bf16[128,512]{1,0:T(8,128)(2,1)S(1)}, bf16[128,512]{1,0:T(8,128)(2,1)S(1)}, u32[]{:S(2)}, u32[]{:S(2)}) collective-permute-start(bf16[128,512]{1,0:T(8,128)(2,1)S(1)} %get-tuple-element.46), channel_id=1, source_target_pairs={{0,1},{1,2},{2,3},{3,0},{4,5},{5,6},{6,7},{7,4},{8,9},{9,10},{10,1... | collective-permute-start | bytes 393224 | tf_op jit(solution)/shard_map/ppermute | solution.py:33
  175.8 39.7 %collective-permute-start.14 = (bf16[64,4096]{1,0:T(8,128)(2,1)S(1)}, bf16[64,4096]{1,0:T(8,128)(2,1)S(1)}, u32[]{:S(2)}, u32[]{:S(2)}) collective-permute-start(bf16[64,4096]{1,0:T(8,128)(2,1)S(1)} %copy-done.21), channel_id=1, source_target_pairs={{0,1},{1,2},{2,3},{3,0},{4,5},{5,6},{6,7},{7,4},{8,9},{9,10},{10,1... | collective-permute-start | bytes 1572872 | tf_op jit(solution)/shard_map/ppermute | solution.py:33
  176.9 38.7 %collective-permute-start.15 = (bf16[64,4096]{1,0:T(8,128)(2,1)S(1)}, bf16[64,4096]{1,0:T(8,128)(2,1)S(1)}, u32[]{:S(2)}, u32[]{:S(2)}) collective-permute-start(bf16[64,4096]{1,0:T(8,128)(2,1)S(1)} %copy-done.20), channel_id=1, source_target_pairs={{0,3},{1,0},{2,1},{3,2},{4,7},{5,4},{6,5},{7,6},{8,11},{9,8},{10,9... | collective-permute-start | bytes 1572872 | tf_op jit(solution)/shard_map/ppermute | solution.py:33
  178.5 1.2 copy-start.5
  179.8 1.2 copy-start.6
  181.2 34.4 %collective-permute-start.13 = (bf16[64,4096]{1,0:T(8,128)(2,1)S(1)}, bf16[64,4096]{1,0:T(8,128)(2,1)S(1)}, u32[]{:S(2)}, u32[]{:S(2)}) collective-permute-start(bf16[64,4096]{1,0:T(8,128)(2,1)S(1)} %get-tuple-element.40), channel_id=1, source_target_pairs={{0,1},{1,2},{2,3},{3,0},{4,5},{5,6},{6,7},{7,4},{8,9},{9,10},{10,1... | collective-permute-start | bytes 1572872 | tf_op jit(solution)/shard_map/ppermute | solution.py:33
  181.5 34.1 %collective-permute-start.16 = (bf16[64,4096]{1,0:T(8,128)(2,1)S(1)}, bf16[64,4096]{1,0:T(8,128)(2,1)S(1)}, u32[]{:S(2)}, u32[]{:S(2)}) collective-permute-start(bf16[64,4096]{1,0:T(8,128)(2,1)S(1)} %get-tuple-element.43), channel_id=1, source_target_pairs={{0,3},{1,0},{2,1},{3,2},{4,7},{5,4},{6,5},{7,6},{8,11},{9,8},{10,9... | collective-permute-start | bytes 1572872 | tf_op jit(solution)/shard_map/ppermute | solution.py:33
  184.1 20.2 %collective-permute-start.18 = (bf16[128,512]{1,0:T(8,128)(2,1)S(1)}, bf16[128,512]{1,0:T(8,128)(2,1)S(1)}, u32[]{:S(2)}, u32[]{:S(2)}) collective-permute-start(bf16[128,512]{1,0:T(8,128)(2,1)S(1)} %get-tuple-element.45), channel_id=1, source_target_pairs={{0,3},{1,0},{2,1},{3,2},{4,7},{5,4},{6,5},{7,6},{8,11},{9,8},{10,9... | collective-permute-start | bytes 393224 | tf_op jit(solution)/shard_map/ppermute | solution.py:33
  204.5 7.9 %collective-permute-start.21 = (bf16[128,512]{1,0:T(8,128)(2,1)S(1)}, bf16[128,512]{1,0:T(8,128)(2,1)S(1)}, u32[]{:S(2)}, u32[]{:S(2)}) collective-permute-start(bf16[128,512]{1,0:T(8,128)(2,1)S(1)} %add_convert_fusion.refs_0_), channel_id=1, source_target_pairs={{0,128},{1,129},{2,130},{3,131},{4,132},{5,133},{6,134},{7,135},{8... | collective-permute-start | bytes 393224 | tf_op jit(solution)/shard_map/ppermute | solution.py:33
  212.4 12.5 %collective-permute-start.22 = (bf16[128,512]{1,0:T(8,128)(2,1)S(1)}, bf16[128,512]{1,0:T(8,128)(2,1)S(1)}, u32[]{:S(2)}, u32[]{:S(2)}) collective-permute-start(bf16[128,512]{1,0:T(8,128)(2,1)S(1)} %collective-permute-done.21), channel_id=1, source_target_pairs={{0,1},{1,2},{2,3},{3,0},{4,5},{5,6},{6,7},{7,4},{8,9},{9,10},{10,1... | collective-permute-start | bytes 393224 | tf_op jit(solution)/shard_map/ppermute | solution.py:33
  215.6 9.3 %collective-permute-start.23 = (bf16[128,512]{1,0:T(8,128)(2,1)S(1)}, bf16[128,512]{1,0:T(8,128)(2,1)S(1)}, u32[]{:S(2)}, u32[]{:S(2)}) collective-permute-start(bf16[128,512]{1,0:T(8,128)(2,1)S(1)} %collective-permute-done.21), channel_id=1, source_target_pairs={{0,3},{1,0},{2,1},{3,2},{4,7},{5,4},{6,5},{7,6},{8,11},{9,8},{10,9... | collective-permute-start | bytes 393224 | tf_op jit(solution)/shard_map/ppermute | solution.py:33
  215.6 15.7 %copy-start.4 = (bf16[512,1536]{1,0:T(8,128)(2,1)S(1)}, bf16[512,1536]{1,0:T(8,128)(2,1)}, u32[]{:S(2)}) copy-start(bf16[512,1536]{1,0:T(8,128)(2,1)} %refs_1_.1) | copy-start | bytes 4718596
  215.7 15.7 %copy-start.9 = (bf16[512,512]{1,0:T(8,128)(2,1)S(1)}, bf16[512,512]{1,0:T(8,128)(2,1)}, u32[]{:S(2)}) copy-start(bf16[512,512]{1,0:T(8,128)(2,1)} %refs_2_.1) | copy-start | bytes 1572868
  216.7 25.2 %collective-permute-start.17 = (bf16[128,4096]{1,0:T(8,128)(2,1)S(1)}, bf16[128,4096]{1,0:T(8,128)(2,1)S(1)}, u32[]{:S(2)}, u32[]{:S(2)}) collective-permute-start(bf16[128,4096]{1,0:T(8,128)(2,1)S(1)} %shard_map.101), channel_id=1, source_target_pairs={{0,0},{1,1},{2,2},{3,3},{4,8},{5,9},{6,10},{7,11},{8,4},{9,5},{10,... | collective-permute-start | bytes 3145736 | tf_op jit(solution)/shard_map/ppermute | solution.py:33
  223.1 6.3 %collective-permute-start.24 = (bf16[128,512]{1,0:T(8,128)(2,1)S(1)}, bf16[128,512]{1,0:T(8,128)(2,1)S(1)}, u32[]{:S(2)}, u32[]{:S(2)}) collective-permute-start(bf16[128,512]{1,0:T(8,128)(2,1)S(1)} %collective-permute-done.21), channel_id=1, source_target_pairs={{0,2},{1,3},{2,0},{3,1},{4,6},{5,7},{6,4},{7,5},{8,10},{9,11},{10,... | collective-permute-start | bytes 393224 | tf_op jit(solution)/shard_map/ppermute | solution.py:33
  229.4 2.0 collective-permute-start.25
  235.6 6.3 %collective-permute-start.26 = (bf16[128,512]{1,0:T(8,128)(2,1)S(1)}, bf16[128,512]{1,0:T(8,128)(2,1)S(1)}, u32[]{:S(2)}, u32[]{:S(2)}) collective-permute-start(bf16[128,512]{1,0:T(8,128)(2,1)S(1)} %shard_map.102), channel_id=1, source_target_pairs={{0,0},{1,1},{2,2},{3,3},{4,8},{5,9},{6,10},{7,11},{8,4},{9,5},{10,... | collective-permute-start | bytes 393224 | tf_op jit(solution)/shard_map/ppermute | solution.py:33
Sparse Core Ops, SparseCore 0:
  20.4 111.6 all-gather.1

commit v3 on v2

--- a/solution.py
+++ b/solution.py
@@ -13,7 +13,7 @@
 HEAD_DIM = 128
 MATCH_HEADS = 8
 DISTANCES = (1, -1, 2)
-WAIT = 23_000_000_000
+WAIT = 6_000_000_000
 LOG2_E = math.log2(math.e)
 AXES = ("z", "xh", "core", "xl", "y")
 SIZES = (8, 2, 2, 2, 4)
@@ -41,12 +41,50 @@
     return lambda p: {"z": (p["z"] + k) % 8}
 
 
+def two_along_z(p):
+    return {"z": (p["z"] + 2 - 4 * (p["z"] % 2)) % 8}
+
+
+def along_x(k):
+    def target(p):
+        x = (p["xh"] * 2 + p["xl"] + k) % 4
+        return {"xh": x // 2, "xl": x % 2}
+
+    return target
+
+
 def other_core(p):
     return {"core": 1 - p["core"]}
 
 
 def swapped_roles(block):
     return moved(block, lambda p: {"core": p["xl"], "xl": p["core"]})
+
+
+def gathered_z(block, z):
+    pair = after(jnp.stack([block, moved(block, along_z(4))]))
+    pairs = [pair, moved(pair, along_z(1)), moved(pair, along_z(-1)), moved(pair, two_along_z)]
+    sign = 1 - 2 * (z % 2)
+    whole = jnp.zeros((2, 4) + block.shape, block.dtype)
+    rest = (0,) * block.ndim
+    for k, pair in zip((0, 1, -1, 2 * sign), pairs):
+        owner = (z - k) % 8
+        low = jnp.where(owner < 4, pair, pair[::-1])
+        whole = lax.dynamic_update_slice(whole, low[:, None], (0, owner % 4) + rest)
+    return whole.reshape((8,) + block.shape)
+
+
+def along_x_parts(block):
+    return [block] + [moved(block, along_x(k)) for k in DISTANCES]
+
+
+def gathered_x(block, x, axis):
+    whole = jnp.zeros(block.shape[:axis] + (4,) + block.shape[axis:], block.dtype)
+    for k, part in zip((0,) + DISTANCES, along_x_parts(block)):
+        at = [0] * whole.ndim
+        at[axis] = (x - k) % 4
+        whole = lax.dynamic_update_slice(whole, jnp.expand_dims(part, axis), at)
+    return whole
 
 
 def layer_norm(rows_in, norm_gain, norm_bias):
@@ -121,7 +159,7 @@
 
 
 def attention_kernel(*refs):
-    *pieces, weight, own, other, held, held_weight, total, projected, sems = refs
+    *pieces, weight, _, own, other, held, held_weight, total, projected, sems = refs
     depth = held.shape[1] // PARTS
     block = weight.shape[3]
     copies = []
@@ -181,7 +219,7 @@
                 )
 
 
-def attention(pieces, weight):
+def attention(pieces, weight, earlier):
     count = sum(piece.shape[0] for piece in pieces)
     depth = pieces[0].shape[1]
     block = weight.shape[3]
@@ -193,7 +231,7 @@
         60,
         flops=2 * count * depth * columns,
         moved_bytes=2 * depth * (count + columns),
-        in_specs=[pl.BlockSpec(memory_space=pltpu.HBM)] * (len(pieces) + 1),
+        in_specs=[pl.BlockSpec(memory_space=pltpu.HBM)] * (len(pieces) + 2),
         out_specs=(pl.BlockSpec(memory_space=pltpu.VMEM),) * 2,
         scratch_shapes=[
             pltpu.VMEM((count, depth), jnp.bfloat16),
@@ -202,7 +240,7 @@
             pltpu.VMEM((count, columns), jnp.bfloat16),
             pltpu.SemaphoreType.DMA((PARTS, len(pieces) + 6)),
         ],
-    )(*pieces, weight)
+    )(*pieces, weight, earlier)
 
 
 def out_matrix(weight, other_weight):
@@ -217,72 +255,56 @@
     )
 
 
-def match_matrix(place, mine, theirs):
-    planes, xs, parts, block, _ = mine.shape
-    half = block // 2
-    first = place[0] == 0
-    blocks = []
-    for plane in range(planes):
-        for x in range(xs):
-            halves = [
-                jnp.concatenate(
-                    [w[plane, x, i, at : at + half] for i in range(parts) for at in (0, half)],
-                    axis=1,
-                )
-                for w in (mine, theirs)
-            ]
-            blocks += [jnp.where(first, *halves), jnp.where(first, *halves[::-1])]
+def match_matrix(weight):
+    planes, cores, highs = weight.shape[:3]
+    blocks = [weight[p, c, h] for p in range(planes) for h in range(highs) for c in range(cores)]
     return jnp.concatenate(blocks, axis=0)
 
 
-def send_kernel(picked, mine, theirs, weight, other_weight, *outs):
+def send_kernel(skipped, picked, mine, theirs, weight, other_weight, *refs):
+    outs = refs[skipped:]
     both = [
         jnp.concatenate([mine[at : at + many, :], theirs[at : at + many, :]], axis=1)
         for at, many in picked
     ]
-    terms = dot(jnp.concatenate(both, axis=0), out_matrix(weight, other_weight))
+    products = dot(jnp.concatenate(both, axis=0), out_matrix(weight, other_weight))
     at = 0
     for out in outs:
-        out[...] = terms[at : at + out.shape[0]].astype(out.dtype)
+        out[...] = products[at : at + out.shape[0]].astype(out.dtype)
         at += out.shape[0]
 
 
-def weight_part(weights, blocks):
-    _, xs, _, block, wide = weights.shape
-    return pl.BlockSpec((2, xs, 2, block, wide), lambda i: (i, 0, blocks // 2, 0, 0))
-
-
-def terms_to_send(mine, theirs, weights, other_weights, picked):
-    planes, xs, _, _, wide = weights.shape
+def weight_part(weight):
+    return pl.BlockSpec((2,) + weight.shape[1:], lambda i: (i, 0, 0, 0, 0))
+
+
+def terms(mine, theirs, weight, other_weight, picked, dtype, earlier=()):
+    earlier = list(earlier)
+    planes, xs, _, _, wide = weight.shape
     columns = 2 * xs * wide
     whole = pl.BlockSpec(mine.shape, lambda i: (0, 0))
     return local(
-        functools.partial(send_kernel, picked),
-        tuple(jax.ShapeDtypeStruct((many, planes * xs * wide), jnp.bfloat16) for _, many in picked),
+        functools.partial(send_kernel, len(earlier), picked),
+        tuple(jax.ShapeDtypeStruct((many, planes * xs * wide), dtype) for _, many in picked),
         52,
         flops=2_000_000_000,
         moved_bytes=8_000_000,
         grid=(planes // 2,),
-        in_specs=[whole, whole, weight_part(weights, 6), weight_part(other_weights, 0)],
+        in_specs=[whole, whole, weight_part(weight), weight_part(other_weight)]
+        + [pl.BlockSpec(memory_space=pltpu.HBM)] * len(earlier),
         out_specs=tuple(pl.BlockSpec((many, columns), lambda i: (0, i)) for _, many in picked),
-    )(mine, theirs, weights, other_weights)
-
-
-def keep_kernel(
-    place, tokens, mine, theirs, weight, other_weight, match_mine, match_theirs, _, own, down, up, *rest
-):
+    )(mine, theirs, weight, other_weight, *earlier)
+
+
+def descriptor_kernel(tokens, mine, theirs, weight, other_weight, match_weight, _, __, *rest):
     *sums, total = rest
     step = pl.program_id(0)
-    terms = dot(
-        jnp.concatenate([mine[...], theirs[...]], axis=1), out_matrix(weight, other_weight)
-    )
-    rows, mid = own.shape[0], down.shape[0]
-    own[...] = terms[:rows]
-    down[...] = terms[2 * rows - mid : 2 * rows]
-    up[...] = terms[2 * rows : 2 * rows + mid]
-    with_tokens = terms[:rows] + tokens[...].astype(jnp.float32)
-    rounded = jnp.concatenate([with_tokens, terms[rows:]], axis=0).astype(jnp.bfloat16)
-    product = dot(rounded, match_matrix(place, match_mine, match_theirs))
+    rows = tokens.shape[0]
+    both = jnp.concatenate([mine[...], theirs[...]], axis=1)
+    products = dot(both, out_matrix(weight, other_weight))
+    with_tokens = products[:rows] + tokens[...].astype(jnp.float32)
+    rounded = jnp.concatenate([with_tokens, products[rows:]], axis=0).astype(jnp.bfloat16)
+    product = dot(rounded, match_matrix(match_weight))
 
     @pl.when(step == 0)
     def _():
@@ -298,50 +320,33 @@
             out[...] = total[i * rows : (i + 1) * rows].astype(out.dtype)
 
 
-def terms_to_keep(core, tokens, mine, theirs, weights, other_weights, earlier):
-    planes, xs, _, block, wide = weights.shape
-    rows, depth = tokens.shape
-    width = 4 * wide
-    columns = 2 * xs * wide
+def descriptor_terms(tokens, mine, theirs, weight, other_weight, match_weight, *earlier):
+    planes, xs, _, _, wide = weight.shape
+    rows = tokens.shape[0]
+    width = match_weight.shape[-1]
     whole = pl.BlockSpec(mine.shape, lambda i: (0, 0))
-    full = pl.BlockSpec((rows, columns), lambda i: (0, i))
-    half = pl.BlockSpec((rows // 2, columns), lambda i: (0, i))
     square = pl.BlockSpec((rows, width), lambda i: (0, 0))
     f32, bf16 = jnp.float32, jnp.bfloat16
     return local(
-        keep_kernel,
-        (jax.ShapeDtypeStruct((rows, depth), f32),)
-        + (jax.ShapeDtypeStruct((rows // 2, depth), f32),) * 2
-        + (jax.ShapeDtypeStruct((rows, width), f32),)
+        descriptor_kernel,
+        (jax.ShapeDtypeStruct((rows, width), f32),)
         + (jax.ShapeDtypeStruct((rows, width), bf16),) * 3,
         52,
         flops=4_000_000_000,
-        moved_bytes=16_000_000,
+        moved_bytes=12_000_000,
         grid=(planes // 2,),
         in_specs=[
-            pl.BlockSpec(memory_space=pltpu.SMEM),
-            full,
+            pl.BlockSpec((rows, 2 * xs * wide), lambda i: (0, i)),
             whole,
             whole,
-            weight_part(weights, 6),
-            weight_part(other_weights, 0),
-            weight_part(weights, 8),
-            weight_part(other_weights, 2),
-            pl.BlockSpec(memory_space=pltpu.HBM),
-        ],
-        out_specs=(full, half, half) + (square,) * 4,
+            weight_part(weight),
+            weight_part(other_weight),
+            weight_part(match_weight),
+        ]
+        + [pl.BlockSpec(memory_space=pltpu.HBM)] * len(earlier),
+        out_specs=(square,) * 4,
         scratch_shapes=[pltpu.VMEM((4 * rows, width), f32)],
-    )(
-        core.astype(jnp.int32).reshape(1),
-        tokens,
-        mine,
-        theirs,
-        weights,
-        other_weights,
-        weights,
-        other_weights,
-        earlier,
-    )
+    )(tokens, mine, theirs, weight, other_weight, match_weight, *earlier)
 
 
 def added_kernel(a, b, c, d, first, second):
@@ -422,51 +427,56 @@
     tokens, norm_gain, norm_bias, qkv_weight, out_weight, match_weight, matcher_qkv, matcher_out
 ):
     bf16, f32 = jnp.bfloat16, jnp.float32
+    z = lax.axis_index("z")
+    x = lax.axis_index("xh") * 2 + lax.axis_index("xl")
     width = matcher_out.shape[0]
     rows, features_width = tokens.shape
     mid = rows // 2
 
     block, wide = qkv_weight.shape[0], out_weight.shape[1]
-
-    def in_blocks(weight):
-        return weight.reshape(weight.shape[0], -1, wide).transpose(1, 0, 2).reshape(-1, wide)
-
-    part = match_weight.shape[0] // 2
-    match_low = in_blocks(match_weight[:part])
-    match_high = in_blocks(match_weight[part:])
-    match_half = jnp.where(lax.axis_index("xl") == 0, match_low, match_high)
-    packed = swapped_roles(
-        jnp.concatenate([in_blocks(qkv_weight), out_weight, match_half], axis=0)
-    )
-    weights = lax.all_gather(packed, ("z", "xh", "xl"), axis=0, tiled=True)
-    weights = weights.reshape(8, 4, 10, block, wide)
+    packed = qkv_weight.reshape(block, -1, wide).transpose(1, 0, 2).reshape(-1, wide)
+    packed = swapped_roles(jnp.concatenate([packed, out_weight], axis=0))
+    split = packed.shape[0] - out_weight.shape[0]
+    weights = lax.all_gather(packed[:split], ("z", "xh", "xl"), axis=0, tiled=True)
+    weights = weights.reshape(8, 4, split // block, block, wide)
+
+    match_weight = after(match_weight, packed)
+    other_half = moved(match_weight, lambda p: {"xh": 1 - p["xh"], "xl": 1 - p["xl"]})
+    match_pair = jnp.where(
+        lax.axis_index("xh") == 0,
+        jnp.concatenate([match_weight, other_half], axis=0),
+        jnp.concatenate([other_half, match_weight], axis=0),
+    )
+    match_all = lax.all_gather(match_pair, ("z", "core"), axis=0, tiled=True)
+    match_all = match_all.reshape(8, 2, 2, match_weight.shape[0], width)
 
     tokens = swapped_roles(tokens)
     normed = layer_norm(tokens, norm_gain, norm_bias)
+    out_own = gathered_x(gathered_z(packed[split:], z), x, 1)
+    out_other = moved(out_own, other_core)
     pieces = [normed] + [moved(normed, along_y(k)) for k in DISTANCES]
     pieces += [moved(piece, other_core) for piece in pieces]
     pieces = together(*pieces, flops=WAIT)
-    other_weights = moved(after(weights[:, :, 6:], pieces[0]), other_core)
-    mine, theirs = attention(pieces, weights)
-
-    both = (mine, moved(theirs, other_core), weights, other_weights)
-    far_low, far_high, up_high, down_low = terms_to_send(
-        *both, [(3 * rows, mid), (3 * rows + mid, mid), (2 * rows + mid, mid), (rows, mid)]
-    )
-    own, down_high, up_low, *sums = terms_to_keep(
-        lax.axis_index("core"), tokens, *both, far_low
+    mine, theirs = attention(pieces, weights, out_own)
+
+    shape = (8, 4, 2, block, wide)
+    both = (mine, moved(theirs, other_core), out_own.reshape(shape), out_other.reshape(shape))
+    far_low, far_high, up_high, down_low = terms(
+        *both, [(3 * rows, mid), (3 * rows + mid, mid), (2 * rows + mid, mid), (rows, mid)], bf16
+    )
+    own, down_high, up_low = terms(
+        *both, [(0, rows), (rows + mid, mid), (2 * rows, mid)], f32, [far_low]
     )
     far_low, far_high = moved(far_low, along_y(1)), moved(far_high, along_y(-1))
     up_high, down_low = moved(up_high, along_y(1)), moved(down_low, along_y(-1))
+    up_low, down_high = added(up_low, far_low, down_high, far_high)
+    up_low, down_high = moved(up_low, along_y(1)), moved(down_high, along_y(-1))
+    sums = descriptor_terms(tokens, *both, match_all, up_high, down_low)
+    features = features_of(tokens, own, (up_low, up_high, down_low, down_high))
 
     received = [moved(part, along_y(k)) for part, k in zip(sums[1:], (-1, 1, 2))]
     descriptor = sums[0] + sum(part.astype(f32) for part in received)
     descriptor = descriptor.astype(bf16)
-
-    up_low, down_high = added(up_low, far_low, down_high, far_high)
-    up_low, down_high = moved(up_low, along_y(1)), moved(down_high, along_y(-1))
-    features = features_of(tokens, own, (up_low, up_high, down_low, down_high))
-
     partner = moved(descriptor, along_z(4))
     quarter = jnp.concatenate([partner] + [moved(partner, along_y(k)) for k in DISTANCES], axis=0)
     pieces = [quarter, moved(quarter, other_core)]

time: 251 us -> 237 us (0.944)
  waiting for transfers between devices: 139 us -> 68.5 us
  starting transfers between devices: 41.8 us -> 80.7 us
  local copies, waits for them, and re-layouts: 16.8 us -> 27.1 us
  Pallas kernels: 35.6 us -> 39.7 us
  other arithmetic: 2.98 us -> 5.56 us
    all_gather x1 -> x2, waiting for transfers between devices: 54.4 us -> 9.56 us  [the longest x1 9.55 us: per_device(): lax.all_gather(packed[:split], ('z', 'xh', 'xl'), axis=0, tiled=True)]
    ppermute x27 -> x35, starting transfers between devices: 41.8 us -> 80.7 us  [moved(): return lax.ppermute(block, AXES, route)]
    ppermute x27 -> x35, waiting for transfers between devices: 84.4 us -> 58.9 us  [moved(): return lax.ppermute(block, AXES, route)]
    dynamic_update_slice x0 -> x4, local copies, waits for them, and re-layouts: none -> 6.66 us  [gathered_x(): whole = lax.dynamic_update_slice(whole, jnp.expand_dims(part, axis), at)]
    unnamed x50 -> x49, local copies, waits for them, and re-layouts: 11.8 us -> 16.9 us
    slice x1, local copies, waits for them, and re-layouts: 4.75 us -> 0.68 us  [per_device(): packed[:split]]
    pallas_call x2 -> x3, Pallas kernels: 13.8 us -> 17.9 us  [the longest x2 10.3 us: terms(): local(functools.partial(send_kernel, len(earlier), picked), tuple((jax.Sh...]
    dynamic_update_slice x0 -> x4, other arithmetic: none -> 2.71 us  [gathered_z(): whole = lax.dynamic_update_slice(whole, low[:, None], (0, owner % 4) + rest)]
  transfers between devices with their start and end apart: 28 -> 37, of which waited for: 14 -> 16; matrix products, arithmetic and copies ran while one was open for 1% -> 6% of each run, Pallas kernels for 12% -> 17%
where the time goes in v3:
time: 237 us; the launch traced here: 236 us
  starting transfers between devices  80.7 us (34%)
  waiting for transfers between devices  68.5 us (29%)
  Pallas kernels  39.7 us (17%)
  local copies, waits for them, and re-layouts  27.1 us (11%)
  between operations  14.4 us (6%)
  other arithmetic  5.56 us (2%)
    ppermute x35, starting transfers between devices, moved(): return lax.ppermute(block, AXES, route)  80.7 us
    ppermute x35, waiting for transfers between devices, moved(): return lax.ppermute(block, AXES, route)  58.9 us
    unnamed x49, local copies, waits for them, and re-layouts  16.9 us
    pallas_call x1, Pallas kernels, attention(): local(attention_kernel, (result, result), 60, flops=2 * count * depth * c...  16.4 us
    pallas_call x2, Pallas kernels, terms(): local(functools.partial(send_kernel, len(earlier), picked), tuple((jax.Sh...  10.3 us
    all_gather x1, waiting for transfers between devices, per_device(): lax.all_gather(packed[:split], ('z', 'xh', 'xl'), axis=0, tiled=True)  9.55 us
    pallas_call x1, Pallas kernels, descriptor_terms(): local(descriptor_kernel, (jax.ShapeDtypeStruct((rows, width), f32),) + (j...  7.59 us
    dynamic_update_slice x4, local copies, waits for them, and re-layouts, gathered_x(): whole = lax.dynamic_update_slice(whole, jnp.expand_dims(part, axis), at)  6.66 us
  transfers between devices with their start and end apart: 37, of which 16 were waited for; matrix products, arithmetic and copies ran while one was open for 6% of the time, Pallas kernels for 17%

profile of v3, /device:TPU:1, one launch (start us, length us, event | category | flops | bytes accessed | tf_op | source)
XLA Modules:
  0.0 236.0 jit_solution(12842865132216507)
XLA Ops:
  7.2 1.0 copy.59.refs_0_
  8.2 1.1 copy.27
  10.3 4.5 %collective-permute-start.8 = (bf16[1024,128]{1,0:T(8,128)(2,1)S(1)}, bf16[1024,128]{1,0:T(8,128)(2,1)S(1)}, u32[]{:S(2)}, u32[]{:S(2)}) collective-permute-start(bf16[1024,128]{1,0:T(8,128)(2,1)S(1)} %pad_maximum_fusion), channel_id=1, source_target_pairs={{0,0},{1,1},{2,2},{3,3},{4,8},{5,9},{6,10},{7,11},{8,4},{9,5},{10,... | collective-permute-start | bytes 786440 | tf_op jit(solution)/shard_map/ppermute | solution.py:33
  14.9 4.0 %collective-permute-done.8.refs_1_ = bf16[1024,128]{1,0:T(8,128)(2,1)S(1)} collective-permute-done((bf16[1024,128]{1,0:T(8,128)(2,1)S(1)}, bf16[1024,128]{1,0:T(8,128)(2,1)S(1)}, u32[]{:S(2)}, u32[]{:S(2)}) %collective-permute-start.8) | collective-permute-done | bytes 262176 | tf_op jit(solution)/shard_map/ppermute | solution.py:33
  19.8 6.1 %collective-permute-done.25 = bf16[128,512]{1,0:T(8,128)(2,1)S(1)} collective-permute-done((bf16[128,512]{1,0:T(8,128)(2,1)S(1)}, bf16[128,512]{1,0:T(8,128)(2,1)S(1)}, u32[]{:S(2)}, u32[]{:S(2)}) %collective-permute-start.25) | collective-permute-done | bytes 131104 | tf_op jit(solution)/shard_map/ppermute | solution.py:33
  26.7 2.5 %collective-permute-start = (bf16[128,4096]{1,0:T(8,128)(2,1)S(1)}, bf16[128,4096]{1,0:T(8,128)(2,1)S(1)}, u32[]{:S(2)}, u32[]{:S(2)}) collective-permute-start(bf16[128,4096]{1,0:T(8,128)(2,1)S(1)} %copy-done.20), channel_id=1, source_target_pairs={{0,0},{1,1},{2,2},{3,3},{4,8},{5,9},{6,10},{7,11},{8,4},{9,5},{10,... | collective-permute-start | bytes 3145736 | tf_op jit(solution)/shard_map/ppermute | solution.py:33
  29.2 7.0 %collective-permute-start.9 = (bf16[256,128]{1,0:T(8,128)(2,1)S(1)}, bf16[256,128]{1,0:T(8,128)(2,1)S(1)}, u32[]{:S(2)}, u32[]{:S(2)}) collective-permute-start(bf16[256,128]{1,0:T(8,128)(2,1)S(1)} %get-tuple-element.49), channel_id=1, source_target_pairs={{0,128},{1,129},{2,130},{3,131},{4,132},{5,133},{6,134},{7,135},{8... | collective-permute-start | bytes 196616 | tf_op jit(solution)/shard_map/ppermute | solution.py:33
  36.2 3.2 %collective-permute-done.9 = bf16[256,128]{1,0:T(8,128)(2,1)S(1)} collective-permute-done((bf16[256,128]{1,0:T(8,128)(2,1)S(1)}, bf16[256,128]{1,0:T(8,128)(2,1)S(1)}, u32[]{:S(2)}, u32[]{:S(2)}) %collective-permute-start.9) | collective-permute-done | bytes 65568 | tf_op jit(solution)/shard_map/ppermute | solution.py:33
  39.5 1.7 collective-permute-start.10
  41.2 1.5 collective-permute-start.11
  44.4 3.1 %collective-permute-done.10 = bf16[2,256,128]{2,1,0:T(8,128)(2,1)S(1)} collective-permute-done((bf16[2,256,128]{2,1,0:T(8,128)(2,1)S(1)}, bf16[2,256,128]{2,1,0:T(8,128)(2,1)S(1)}, u32[]{:S(2)}, u32[]{:S(2)}) %collective-permute-start.10) | collective-permute-done | bytes 131104 | tf_op jit(solution)/shard_map/ppermute | solution.py:33
  50.1 2.2 collective-permute-start.1
  52.3 1.8 collective-permute-start.2
  54.1 1.4 collective-permute-start.3
  56.2 2.7 %collective-permute-start.14 = (bf16[8,256,128]{2,1,0:T(8,128)(2,1)}, bf16[8,256,128]{2,1,0:T(8,128)(2,1)}, u32[]{:S(2)}, u32[]{:S(2)}) collective-permute-start(bf16[8,256,128]{2,1,0:T(8,128)(2,1)} %bitcast.15), channel_id=1, source_target_pairs={{0,20},{1,21},{2,22},{3,23},{4,0},{5,1},{6,2},{7,3},{8,28},{9,29},... | collective-permute-start | bytes 1572872 | tf_op jit(solution)/shard_map/ppermute | solution.py:33
  58.9 11.2 %collective-permute-done.13 = bf16[8,256,128]{2,1,0:T(8,128)(2,1)} collective-permute-done((bf16[8,256,128]{2,1,0:T(8,128)(2,1)}, bf16[8,256,128]{2,1,0:T(8,128)(2,1)}, u32[]{:S(2)}, u32[]{:S(2)}) %collective-permute-start.13) | collective-permute-done | bytes 524320 | tf_op jit(solution)/shard_map/ppermute | solution.py:33
  70.1 2.3 collective-permute-start.15
  72.5 1.8 broadcast_in_dim.31
  74.2 1.9 constant_dynamic-update-slice_fusion.4
  76.2 1.9 bitcast_dynamic-update-slice_fusion.1
  78.1 1.1 collective-permute-start.4
  79.3 20.8 %collective-permute-start.6 = (bf16[128,4096]{1,0:T(8,128)(2,1)S(1)}, bf16[128,4096]{1,0:T(8,128)(2,1)S(1)}, u32[]{:S(2)}, u32[]{:S(2)}) collective-permute-start(bf16[128,4096]{1,0:T(8,128)(2,1)S(1)} %collective-permute-done.2.refs_2_), channel_id=1, source_target_pairs={{0,8},{1,9},{2,10},{3,11},{4,12},{5,13},{6,14},{7,15},{8,0},{9,1},... | collective-permute-start | bytes 3145736 | tf_op jit(solution)/shard_map/ppermute | solution.py:33
  100.0 1.1 collective-permute-done.3.refs_3_
  101.9 1.9 bitcast_dynamic-update-slice_fusion
  104.8 1.0 copy-done.6
  105.8 1.0 copy-done.10
  106.8 1.0 copy-done.11
  107.8 1.0 copy-done.12
  108.8 1.0 copy-done.13
  109.7 1.0 copy-done.14
  110.8 1.0 copy-done.15
  111.8 9.6 %all-gather.3.cloned.1.call-done = bf16[24576,128]{1,0:T(8,128)(2,1)} async-done(((bf16[768,128]{1,0:T(8,128)(2,1)}), bf16[24576,128]{1,0:T(8,128)(2,1)}) %all-gather.3.cloned.1.call-update) | async-done | bytes 6291472 | tf_op jit(solution)/shard_map/all_gather | solution.py:440
  121.3 16.4 %shard_map.97 = (bf16[512,256]{1,0:T(8,128)(2,1)}, bf16[512,256]{1,0:T(8,128)(2,1)}) custom-call(bf16[128,4096]{1,0:T(8,128)(2,1)} %copy-done.6, bf16[128,4096]{1,0:T(8,128)(2,1)} %copy-done.10, bf16[128,4096]{1,0:T(8,128)(2,1)} %copy-done.11, bf16[128,4096]{1,0:T(8,128)(2,1)} %get-tuple-element.28.refs_3_, bf16[128,4096]{1,0:T(8,128)(2,1)} %copy-done.12, ...), custom_call_target="tpu_custom_call" | custom-call | flops 6442450944 | bytes 14680064 | tf_op jit(solution)/shard_map/pallas_call | solution.py:228
  137.7 0.9 collective-permute-start.16
  138.6 1.4 collective-permute-done.16.theirs
  140.0 1.0 copy-done.16
  141.0 4.8 %shard_map.98 = (bf16[64,4096]{1,0:T(8,128)(2,1)S(1)}, bf16[64,4096]{1,0:T(8,128)(2,1)S(1)}, bf16[64,4096]{1,0:T(8,128)(2,1)}, bf16[64,4096]{1,0:T(8,128)(2,1)}) custom-call(bf16[512,256]{1,0:T(8,128)(2,1)S(1)} %copy-done.16, bf16[512,256]{1,0:T(8,128)(2,1)S(1)} %collective-permute-done.16.theirs, bf16[8,4,2,128,128]{4,3,2,1,0:T(8,128)(2,1)} %bitcast.21.weight, ...), custom_call_target="tpu_custom_call" | custom-call | flops 2000000000 | bytes 8000000 | tf_op jit(solution)/shard_map/pallas_call | solution.py:286
  146.3 2.2 collective-permute-start.19
  148.5 2.7 %collective-permute-start.22 = (bf16[64,4096]{1,0:T(8,128)(2,1)}, bf16[64,4096]{1,0:T(8,128)(2,1)S(1)}, u32[]{:S(2)}, u32[]{:S(2)}) collective-permute-start(bf16[64,4096]{1,0:T(8,128)(2,1)} %get-tuple-element.42), channel_id=1, source_target_pairs={{0,3},{1,0},{2,1},{3,2},{4,7},{5,4},{6,5},{7,6},{8,11},{9,8},{10,9... | collective-permute-start | bytes 1572872 | tf_op jit(solution)/shard_map/ppermute | solution.py:33
  151.1 5.5 %shard_map.99 = (f32[128,4096]{1,0:T(8,128)}, f32[64,4096]{1,0:T(8,128)}, f32[64,4096]{1,0:T(8,128)}) custom-call(bf16[512,256]{1,0:T(8,128)(2,1)S(1)} %copy-done.16, bf16[512,256]{1,0:T(8,128)(2,1)S(1)} %collective-permute-done.16.theirs, bf16[8,4,2,128,128]{4,3,2,1,0:T(8,128)(2,1)} %bitcast.21.weight, bf16[8,4,2,128,128]{4,3,2,1,0:T(8,128)(2,1)} %bitcast.22.other_weight, ...), custom_call_target="tpu_custom_call" | custom-call | flops 2000000000 | bytes 8000000 | tf_op jit(solution)/shard_map/pallas_call | solution.py:286
  156.6 3.6 %collective-permute-done.18.b = bf16[64,4096]{1,0:T(8,128)(2,1)S(1)} collective-permute-done((bf16[64,4096]{1,0:T(8,128)(2,1)S(1)}, bf16[64,4096]{1,0:T(8,128)(2,1)S(1)}, u32[]{:S(2)}, u32[]{:S(2)}) %collective-permute-start.18) | collective-permute-done | bytes 524320 | tf_op jit(solution)/shard_map/ppermute | solution.py:33
  160.2 1.2 copy-done.4
  161.4 1.2 copy-done.5
  162.9 2.7 %collective-permute-start.23 = (bf16[64,4096]{1,0:T(8,128)(2,1)S(1)}, bf16[64,4096]{1,0:T(8,128)(2,1)S(1)}, u32[]{:S(2)}, u32[]{:S(2)}) collective-permute-start(bf16[64,4096]{1,0:T(8,128)(2,1)S(1)} %get-tuple-element.43), channel_id=1, source_target_pairs={{0,3},{1,0},{2,1},{3,2},{4,7},{5,4},{6,5},{7,6},{8,11},{9,8},{10,9... | collective-permute-start | bytes 1572872 | tf_op jit(solution)/shard_map/ppermute | solution.py:33
  165.6 5.7 %collective-permute-done.21.high_a._ = bf16[64,4096]{1,0:T(8,128)(2,1)S(1)} collective-permute-done((bf16[64,4096]{1,0:T(8,128)(2,1)}, bf16[64,4096]{1,0:T(8,128)(2,1)S(1)}, u32[]{:S(2)}, u32[]{:S(2)}) %collective-permute-start.21) | collective-permute-done | bytes 524320 | tf_op jit(solution)/shard_map/ppermute | solution.py:33
  172.1 0.9 copy-done.17
  173.1 7.6 %shard_map.103 = (f32[128,512]{1,0:T(8,128)S(1)}, bf16[128,512]{1,0:T(8,128)(2,1)S(1)}, bf16[128,512]{1,0:T(8,128)(2,1)S(1)}, bf16[128,512]{1,0:T(8,128)(2,1)S(1)}) custom-call(bf16[128,4096]{1,0:T(8,128)(2,1)} %copy-done, bf16[512,256]{1,0:T(8,128)(2,1)S(1)} %copy-done.17, bf16[512,256]{1,0:T(8,128)(2,1)S(1)} %collective-permute-done.16.theirs, ...), custom_call_target="tpu_custom_call" | custom-call | flops 4000000000 | bytes 12000000 | tf_op jit(solution)/shard_map/pallas_call | solution.py:330
  180.6 1.3 collective-permute-start.28
  181.9 1.7 collective-permute-start.27
  183.7 0.9 collective-permute-start.26
  184.6 1.5 collective-permute-done.28
  186.1 1.8 collective-permute-done.27
  188.0 2.2 collective-permute-start.29
  190.2 5.6 %collective-permute-done.29 = bf16[128,512]{1,0:T(8,128)(2,1)S(1)} collective-permute-done((bf16[128,512]{1,0:T(8,128)(2,1)S(1)}, bf16[128,512]{1,0:T(8,128)(2,1)S(1)}, u32[]{:S(2)}, u32[]{:S(2)}) %collective-permute-start.29) | collective-permute-done | bytes 131104 | tf_op jit(solution)/shard_map/ppermute | solution.py:33
  196.3 2.2 collective-permute-start.31
  198.5 1.0 copy-done.8
  199.5 1.0 shard_map.101
  200.6 9.0 %collective-permute-start.24 = (bf16[128,4096]{1,0:T(8,128)(2,1)S(1)}, bf16[128,4096]{1,0:T(8,128)(2,1)S(1)}, u32[]{:S(2)}, u32[]{:S(2)}) collective-permute-start(bf16[128,4096]{1,0:T(8,128)(2,1)S(1)} %shard_map.101), channel_id=1, source_target_pairs={{0,0},{1,1},{2,2},{3,3},{4,8},{5,9},{6,10},{7,11},{8,4},{9,5},{10,... | collective-permute-start | bytes 3145736 | tf_op jit(solution)/shard_map/ppermute | solution.py:33
  209.8 5.2 %collective-permute-done.32 = bf16[128,512]{1,0:T(8,128)(2,1)S(1)} collective-permute-done((bf16[128,512]{1,0:T(8,128)(2,1)S(1)}, bf16[128,512]{1,0:T(8,128)(2,1)S(1)}, u32[]{:S(2)}, u32[]{:S(2)}) %collective-permute-start.32) | collective-permute-done | bytes 131104 | tf_op jit(solution)/shard_map/ppermute | solution.py:33
  215.1 1.9 collective-permute-done.33.refs_4_
  217.0 4.2 %shard_map.104 = bf16[128,512]{1,0:T(8,128)(2,1)S(1)} custom-call(bf16[128,512]{1,0:T(8,128)(2,1)S(1)} %add_convert_fusion.refs_0_, bf16[512,1536]{1,0:T(8,128)(2,1)S(1)} %copy-done.3, bf16[512,512]{1,0:T(8,128)(2,1)S(1)} %copy-done.9, bf16[512,512]{1,0:T(8,128)(2,1)S(1)} %constant_dynamic-update-slice_fusion.refs_3_, ...), custom_call_target="tpu_custom_call" | custom-call | tf_op jit(solution)/shard_map/pallas_call | solution.py:414
  221.2 3.1 %collective-permute-start.34 = (bf16[128,512]{1,0:T(8,128)(2,1)S(1)}, bf16[128,512]{1,0:T(8,128)(2,1)S(1)}, u32[]{:S(2)}, u32[]{:S(2)}) collective-permute-start(bf16[128,512]{1,0:T(8,128)(2,1)S(1)} %shard_map.104), channel_id=1, source_target_pairs={{0,0},{1,1},{2,2},{3,3},{4,8},{5,9},{6,10},{7,11},{8,4},{9,5},{10,... | collective-permute-start | bytes 393224 | tf_op jit(solution)/shard_map/ppermute | solution.py:33
  224.3 3.2 %collective-permute-done.34 = bf16[128,512]{1,0:T(8,128)(2,1)S(1)} collective-permute-done((bf16[128,512]{1,0:T(8,128)(2,1)S(1)}, bf16[128,512]{1,0:T(8,128)(2,1)S(1)}, u32[]{:S(2)}, u32[]{:S(2)}) %collective-permute-start.34) | collective-permute-done | bytes 131104 | tf_op jit(solution)/shard_map/ppermute | solution.py:33
  227.5 1.0 copy.60
  (94 shorter events, 12.5 us)
Async XLA Ops:
  7.2 19.5 %copy-start.20 = (bf16[128,4096]{1,0:T(8,128)(2,1)S(1)}, bf16[128,4096]{1,0:T(8,128)(2,1)}, u32[]{:S(2)}) copy-start(bf16[128,4096]{1,0:T(8,128)(2,1)} %param.8) | copy-start | bytes 3145732
  7.2 114.1 %all-gather.3.cloned.1.call-start = ((), (), s32[]{:S(2)}) async-start(), calls=%async_computation | async-start | bytes 6488064 | tf_op jit(solution)/shard_map/all_gather | solution.py:440
  10.3 8.6 %collective-permute-start.8 = (bf16[1024,128]{1,0:T(8,128)(2,1)S(1)}, bf16[1024,128]{1,0:T(8,128)(2,1)S(1)}, u32[]{:S(2)}, u32[]{:S(2)}) collective-permute-start(bf16[1024,128]{1,0:T(8,128)(2,1)S(1)} %pad_maximum_fusion), channel_id=1, source_target_pairs={{0,0},{1,1},{2,2},{3,3},{4,8},{5,9},{6,10},{7,11},{8,4},{9,5},{10,... | collective-permute-start | bytes 786440 | tf_op jit(solution)/shard_map/ppermute | solution.py:33
  19.6 146.0 %all-gather.5.cloned.1.call-start = ((), (), s32[]{:S(2)}) async-start(), calls=%async_computation.1 | async-start | bytes 4456448 | tf_op jit(solution)/shard_map/all_gather | solution.py:450
  19.7 6.2 %collective-permute-start.25 = (bf16[128,512]{1,0:T(8,128)(2,1)S(1)}, bf16[128,512]{1,0:T(8,128)(2,1)S(1)}, u32[]{:S(2)}, u32[]{:S(2)}) collective-permute-start(bf16[128,512]{1,0:T(8,128)(2,1)S(1)} %shard_map.102), channel_id=1, source_target_pairs={{0,20},{1,21},{2,22},{3,23},{4,16},{5,17},{6,18},{7,19},{8,28},{9,... | collective-permute-start | bytes 393224 | tf_op jit(solution)/shard_map/ppermute | solution.py:33
  26.7 22.2 %collective-permute-start = (bf16[128,4096]{1,0:T(8,128)(2,1)S(1)}, bf16[128,4096]{1,0:T(8,128)(2,1)S(1)}, u32[]{:S(2)}, u32[]{:S(2)}) collective-permute-start(bf16[128,4096]{1,0:T(8,128)(2,1)S(1)} %copy-done.20), channel_id=1, source_target_pairs={{0,0},{1,1},{2,2},{3,3},{4,8},{5,9},{6,10},{7,11},{8,4},{9,5},{10,... | collective-permute-start | bytes 3145736 | tf_op jit(solution)/shard_map/ppermute | solution.py:33
  29.2 20.4 %copy-start.18 = (f32[4096]{0:T(1024)S(1)}, f32[4096]{0:T(1024)}, u32[]{:S(2)}) copy-start(f32[4096]{0:T(1024)} %param.10) | copy-start | bytes 49156
  29.2 20.4 %copy-start.19 = (f32[4096]{0:T(1024)S(1)}, f32[4096]{0:T(1024)}, u32[]{:S(2)}) copy-start(f32[4096]{0:T(1024)} %param.9) | copy-start | bytes 49156
  29.2 10.2 %collective-permute-start.9 = (bf16[256,128]{1,0:T(8,128)(2,1)S(1)}, bf16[256,128]{1,0:T(8,128)(2,1)S(1)}, u32[]{:S(2)}, u32[]{:S(2)}) collective-permute-start(bf16[256,128]{1,0:T(8,128)(2,1)S(1)} %get-tuple-element.49), channel_id=1, source_target_pairs={{0,128},{1,129},{2,130},{3,131},{4,132},{5,133},{6,134},{7,135},{8... | collective-permute-start | bytes 196616 | tf_op jit(solution)/shard_map/ppermute | solution.py:33
  39.5 8.1 %collective-permute-start.10 = (bf16[2,256,128]{2,1,0:T(8,128)(2,1)S(1)}, bf16[2,256,128]{2,1,0:T(8,128)(2,1)S(1)}, u32[]{:S(2)}, u32[]{:S(2)}) collective-permute-start(bf16[2,256,128]{2,1,0:T(8,128)(2,1)S(1)} %shard_map.96), channel_id=1, source_target_pairs={{0,32},{1,33},{2,34},{3,35},{4,36},{5,37},{6,38},{7,39},{8,40},{9,... | collective-permute-start | bytes 393224 | tf_op jit(solution)/shard_map/ppermute | solution.py:33
  41.2 7.1 %collective-permute-start.11 = (bf16[2,256,128]{2,1,0:T(8,128)(2,1)S(1)}, bf16[2,256,128]{2,1,0:T(8,128)(2,1)S(1)}, u32[]{:S(2)}, u32[]{:S(2)}) collective-permute-start(bf16[2,256,128]{2,1,0:T(8,128)(2,1)S(1)} %shard_map.96), channel_id=1, source_target_pairs={{0,224},{1,225},{2,226},{3,227},{4,228},{5,229},{6,230},{7,231},{8... | collective-permute-start | bytes 393224 | tf_op jit(solution)/shard_map/ppermute | solution.py:33
  42.6 12.9 %collective-permute-start.12 = (bf16[2,256,128]{2,1,0:T(8,128)(2,1)S(1)}, bf16[2,256,128]{2,1,0:T(8,128)(2,1)S(1)}, u32[]{:S(2)}, u32[]{:S(2)}) collective-permute-start(bf16[2,256,128]{2,1,0:T(8,128)(2,1)S(1)} %shard_map.96), channel_id=1, source_target_pairs={{0,64},{1,65},{2,66},{3,67},{4,68},{5,69},{6,70},{7,71},{8,72},{9,... | collective-permute-start | bytes 393224 | tf_op jit(solution)/shard_map/ppermute | solution.py:33
  48.9 1.2 copy-start
  50.1 29.0 %collective-permute-start.1 = (bf16[128,4096]{1,0:T(8,128)(2,1)S(1)}, bf16[128,4096]{1,0:T(8,128)(2,1)S(1)}, u32[]{:S(2)}, u32[]{:S(2)}) collective-permute-start(bf16[128,4096]{1,0:T(8,128)(2,1)S(1)} %fusion.5.refs_0_), channel_id=1, source_target_pairs={{0,1},{1,2},{2,3},{3,0},{4,5},{5,6},{6,7},{7,4},{8,9},{9,10},{10,1... | collective-permute-start | bytes 3145736 | tf_op jit(solution)/shard_map/ppermute | solution.py:33
  52.3 27.0 %collective-permute-start.2 = (bf16[128,4096]{1,0:T(8,128)(2,1)S(1)}, bf16[128,4096]{1,0:T(8,128)(2,1)S(1)}, u32[]{:S(2)}, u32[]{:S(2)}) collective-permute-start(bf16[128,4096]{1,0:T(8,128)(2,1)S(1)} %fusion.5.refs_0_), channel_id=1, source_target_pairs={{0,3},{1,0},{2,1},{3,2},{4,7},{5,4},{6,5},{7,6},{8,11},{9,8},{10,9... | collective-permute-start | bytes 3145736 | tf_op jit(solution)/shard_map/ppermute | solution.py:33
  54.1 47.0 %collective-permute-start.3 = (bf16[128,4096]{1,0:T(8,128)(2,1)S(1)}, bf16[128,4096]{1,0:T(8,128)(2,1)}, u32[]{:S(2)}, u32[]{:S(2)}) collective-permute-start(bf16[128,4096]{1,0:T(8,128)(2,1)S(1)} %fusion.5.refs_0_), channel_id=1, source_target_pairs={{0,2},{1,3},{2,0},{3,1},{4,6},{5,7},{6,4},{7,5},{8,10},{9,11},{10,... | collective-permute-start | bytes 3145736 | tf_op jit(solution)/shard_map/ppermute | solution.py:33
  56.2 13.9 %collective-permute-start.13 = (bf16[8,256,128]{2,1,0:T(8,128)(2,1)}, bf16[8,256,128]{2,1,0:T(8,128)(2,1)}, u32[]{:S(2)}, u32[]{:S(2)}) collective-permute-start(bf16[8,256,128]{2,1,0:T(8,128)(2,1)} %bitcast.15), channel_id=1, source_target_pairs={{0,4},{1,5},{2,6},{3,7},{4,16},{5,17},{6,18},{7,19},{8,12},{9,13},... | collective-permute-start | bytes 1572872 | tf_op jit(solution)/shard_map/ppermute | solution.py:33
  56.2 21.8 %collective-permute-start.14 = (bf16[8,256,128]{2,1,0:T(8,128)(2,1)}, bf16[8,256,128]{2,1,0:T(8,128)(2,1)}, u32[]{:S(2)}, u32[]{:S(2)}) collective-permute-start(bf16[8,256,128]{2,1,0:T(8,128)(2,1)} %bitcast.15), channel_id=1, source_target_pairs={{0,20},{1,21},{2,22},{3,23},{4,0},{5,1},{6,2},{7,3},{8,28},{9,29},... | collective-permute-start | bytes 1572872 | tf_op jit(solution)/shard_map/ppermute | solution.py:33
  70.1 33.7 %collective-permute-start.15 = (bf16[8,256,128]{2,1,0:T(8,128)(2,1)}, bf16[8,256,128]{2,1,0:T(8,128)(2,1)S(1)}, u32[]{:S(2)}, u32[]{:S(2)}) collective-permute-start(bf16[8,256,128]{2,1,0:T(8,128)(2,1)} %bitcast.15), channel_id=1, source_target_pairs={{0,16},{1,17},{2,18},{3,19},{4,20},{5,21},{6,22},{7,23},{8,24},{9,... | collective-permute-start | bytes 1572872 | tf_op jit(solution)/shard_map/ppermute | solution.py:33
  78.1 26.6 %collective-permute-start.4 = (bf16[128,4096]{1,0:T(8,128)(2,1)S(1)}, bf16[128,4096]{1,0:T(8,128)(2,1)S(1)}, u32[]{:S(2)}, u32[]{:S(2)}) collective-permute-start(bf16[128,4096]{1,0:T(8,128)(2,1)S(1)} %fusion.5.refs_0_), channel_id=1, source_target_pairs={{0,8},{1,9},{2,10},{3,11},{4,12},{5,13},{6,14},{7,15},{8,0},{9,1},... | collective-permute-start | bytes 3145736 | tf_op jit(solution)/shard_map/ppermute | solution.py:33
  79.2 25.6 %collective-permute-start.5 = (bf16[128,4096]{1,0:T(8,128)(2,1)S(1)}, bf16[128,4096]{1,0:T(8,128)(2,1)S(1)}, u32[]{:S(2)}, u32[]{:S(2)}) collective-permute-start(bf16[128,4096]{1,0:T(8,128)(2,1)S(1)} %collective-permute-done.1.refs_1_), channel_id=1, source_target_pairs={{0,8},{1,9},{2,10},{3,11},{4,12},{5,13},{6,14},{7,15},{8,0},{9,1},... | collective-permute-start | bytes 3145736 | tf_op jit(solution)/shard_map/ppermute | solution.py:33
  79.3 25.5 %collective-permute-start.6 = (bf16[128,4096]{1,0:T(8,128)(2,1)S(1)}, bf16[128,4096]{1,0:T(8,128)(2,1)S(1)}, u32[]{:S(2)}, u32[]{:S(2)}) collective-permute-start(bf16[128,4096]{1,0:T(8,128)(2,1)S(1)} %collective-permute-done.2.refs_2_), channel_id=1, source_target_pairs={{0,8},{1,9},{2,10},{3,11},{4,12},{5,13},{6,14},{7,15},{8,0},{9,1},... | collective-permute-start | bytes 3145736 | tf_op jit(solution)/shard_map/ppermute | solution.py:33
  101.1 3.6 %collective-permute-start.7 = (bf16[128,4096]{1,0:T(8,128)(2,1)}, bf16[128,4096]{1,0:T(8,128)(2,1)S(1)}, u32[]{:S(2)}, u32[]{:S(2)}) collective-permute-start(bf16[128,4096]{1,0:T(8,128)(2,1)} %collective-permute-done.3.refs_3_), channel_id=1, source_target_pairs={{0,8},{1,9},{2,10},{3,11},{4,12},{5,13},{6,14},{7,15},{8,0},{9,1},... | collective-permute-start | bytes 3145736 | tf_op jit(solution)/shard_map/ppermute | solution.py:33
  104.7 33.9 %collective-permute-start.17 = (bf16[8,4,256,128]{3,2,1,0:T(8,128)(2,1)}, bf16[8,4,256,128]{3,2,1,0:T(8,128)(2,1)}, u32[]{:S(2)}, u32[]{:S(2)}) collective-permute-start(bf16[8,4,256,128]{3,2,1,0:T(8,128)(2,1)} %bitcast_dynamic-update-slice_fusion.2.refs_9_), channel_id=1, source_target_pairs={{0,8},{1,9},{2,10},{3,11},{4,12},{5,13},{6,14},{7,15},{8,0},{9,1},... | collective-permute-start | bytes 6291464 | tf_op jit(solution)/shard_map/ppermute | solution.py:33
  104.8 1.0 copy-start.6
  105.8 1.0 copy-start.10
  106.8 1.0 copy-start.11
  107.8 1.0 copy-start.12
  108.8 1.0 copy-start.13
  109.7 1.0 copy-start.14
  110.8 1.0 copy-start.15
  137.7 2.3 collective-permute-start.16
  140.0 1.0 copy-start.16
  145.8 14.4 %collective-permute-start.18 = (bf16[64,4096]{1,0:T(8,128)(2,1)S(1)}, bf16[64,4096]{1,0:T(8,128)(2,1)S(1)}, u32[]{:S(2)}, u32[]{:S(2)}) collective-permute-start(bf16[64,4096]{1,0:T(8,128)(2,1)S(1)} %get-tuple-element.35.refs_0_), channel_id=1, source_target_pairs={{0,1},{1,2},{2,3},{3,0},{4,5},{5,6},{6,7},{7,4},{8,9},{9,10},{10,1... | collective-permute-start | bytes 1572872 | tf_op jit(solution)/shard_map/ppermute | solution.py:33
  146.3 13.9 %collective-permute-start.19 = (bf16[64,4096]{1,0:T(8,128)(2,1)S(1)}, bf16[64,4096]{1,0:T(8,128)(2,1)S(1)}, u32[]{:S(2)}, u32[]{:S(2)}) collective-permute-start(bf16[64,4096]{1,0:T(8,128)(2,1)S(1)} %get-tuple-element.39), channel_id=1, source_target_pairs={{0,3},{1,0},{2,1},{3,2},{4,7},{5,4},{6,5},{7,6},{8,11},{9,8},{10,9... | collective-permute-start | bytes 1572872 | tf_op jit(solution)/shard_map/ppermute | solution.py:33
  148.5 22.9 %collective-permute-start.21 = (bf16[64,4096]{1,0:T(8,128)(2,1)}, bf16[64,4096]{1,0:T(8,128)(2,1)S(1)}, u32[]{:S(2)}, u32[]{:S(2)}) collective-permute-start(bf16[64,4096]{1,0:T(8,128)(2,1)} %get-tuple-element.41), channel_id=1, source_target_pairs={{0,1},{1,2},{2,3},{3,0},{4,5},{5,6},{6,7},{7,4},{8,9},{9,10},{10,1... | collective-permute-start | bytes 1572872 | tf_op jit(solution)/shard_map/ppermute | solution.py:33
  148.5 22.9 %collective-permute-start.22 = (bf16[64,4096]{1,0:T(8,128)(2,1)}, bf16[64,4096]{1,0:T(8,128)(2,1)S(1)}, u32[]{:S(2)}, u32[]{:S(2)}) collective-permute-start(bf16[64,4096]{1,0:T(8,128)(2,1)} %get-tuple-element.42), channel_id=1, source_target_pairs={{0,3},{1,0},{2,1},{3,2},{4,7},{5,4},{6,5},{7,6},{8,11},{9,8},{10,9... | collective-permute-start | bytes 1572872 | tf_op jit(solution)/shard_map/ppermute | solution.py:33
  160.2 1.2 copy-start.4
  161.4 1.2 copy-start.5
  162.8 35.7 %collective-permute-start.20 = (bf16[64,4096]{1,0:T(8,128)(2,1)S(1)}, bf16[64,4096]{1,0:T(8,128)(2,1)S(1)}, u32[]{:S(2)}, u32[]{:S(2)}) collective-permute-start(bf16[64,4096]{1,0:T(8,128)(2,1)S(1)} %get-tuple-element.40), channel_id=1, source_target_pairs={{0,1},{1,2},{2,3},{3,0},{4,5},{5,6},{6,7},{7,4},{8,9},{9,10},{10,1... | collective-permute-start | bytes 1572872 | tf_op jit(solution)/shard_map/ppermute | solution.py:33
  162.9 35.6 %collective-permute-start.23 = (bf16[64,4096]{1,0:T(8,128)(2,1)S(1)}, bf16[64,4096]{1,0:T(8,128)(2,1)S(1)}, u32[]{:S(2)}, u32[]{:S(2)}) collective-permute-start(bf16[64,4096]{1,0:T(8,128)(2,1)S(1)} %get-tuple-element.43), channel_id=1, source_target_pairs={{0,3},{1,0},{2,1},{3,2},{4,7},{5,4},{6,5},{7,6},{8,11},{9,8},{10,9... | collective-permute-start | bytes 1572872 | tf_op jit(solution)/shard_map/ppermute | solution.py:33
  171.3 0.8 copy-start.7
  172.1 0.9 copy-start.17
  173.0 25.4 %copy-start.1 = (bf16[128,4096]{1,0:T(8,128)(2,1)S(1)}, bf16[128,4096]{1,0:T(8,128)(2,1)}, u32[]{:S(2)}) copy-start(bf16[128,4096]{1,0:T(8,128)(2,1)} %copy-done) | copy-start | bytes 3145732
  173.0 25.4 %copy-start.2 = (f32[128,4096]{1,0:T(8,128)S(1)}, f32[128,4096]{1,0:T(8,128)}, u32[]{:S(2)}) copy-start(f32[128,4096]{1,0:T(8,128)} %get-tuple-element.36.own) | copy-start | bytes 6291460
  180.6 5.5 %collective-permute-start.28 = (bf16[128,512]{1,0:T(8,128)(2,1)S(1)}, bf16[128,512]{1,0:T(8,128)(2,1)S(1)}, u32[]{:S(2)}, u32[]{:S(2)}) collective-permute-start(bf16[128,512]{1,0:T(8,128)(2,1)S(1)} %get-tuple-element.47), channel_id=1, source_target_pairs={{0,2},{1,3},{2,0},{3,1},{4,6},{5,7},{6,4},{7,5},{8,10},{9,11},{10,... | collective-permute-start | bytes 393224 | tf_op jit(solution)/shard_map/ppermute | solution.py:33
  181.9 6.0 %collective-permute-start.27 = (bf16[128,512]{1,0:T(8,128)(2,1)S(1)}, bf16[128,512]{1,0:T(8,128)(2,1)S(1)}, u32[]{:S(2)}, u32[]{:S(2)}) collective-permute-start(bf16[128,512]{1,0:T(8,128)(2,1)S(1)} %get-tuple-element.46), channel_id=1, source_target_pairs={{0,1},{1,2},{2,3},{3,0},{4,5},{5,6},{6,7},{7,4},{8,9},{9,10},{10,1... | collective-permute-start | bytes 393224 | tf_op jit(solution)/shard_map/ppermute | solution.py:33
  183.7 4.3 %collective-permute-start.26 = (bf16[128,512]{1,0:T(8,128)(2,1)S(1)}, bf16[128,512]{1,0:T(8,128)(2,1)S(1)}, u32[]{:S(2)}, u32[]{:S(2)}) collective-permute-start(bf16[128,512]{1,0:T(8,128)(2,1)S(1)} %get-tuple-element.45), channel_id=1, source_target_pairs={{0,3},{1,0},{2,1},{3,2},{4,7},{5,4},{6,5},{7,6},{8,11},{9,8},{10,9... | collective-permute-start | bytes 393224 | tf_op jit(solution)/shard_map/ppermute | solution.py:33
  188.0 7.8 %collective-permute-start.29 = (bf16[128,512]{1,0:T(8,128)(2,1)S(1)}, bf16[128,512]{1,0:T(8,128)(2,1)S(1)}, u32[]{:S(2)}, u32[]{:S(2)}) collective-permute-start(bf16[128,512]{1,0:T(8,128)(2,1)S(1)} %add_convert_fusion.refs_0_), channel_id=1, source_target_pairs={{0,128},{1,129},{2,130},{3,131},{4,132},{5,133},{6,134},{7,135},{8... | collective-permute-start | bytes 393224 | tf_op jit(solution)/shard_map/ppermute | solution.py:33
  195.8 13.9 %collective-permute-start.30 = (bf16[128,512]{1,0:T(8,128)(2,1)S(1)}, bf16[128,512]{1,0:T(8,128)(2,1)S(1)}, u32[]{:S(2)}, u32[]{:S(2)}) collective-permute-start(bf16[128,512]{1,0:T(8,128)(2,1)S(1)} %collective-permute-done.29), channel_id=1, source_target_pairs={{0,1},{1,2},{2,3},{3,0},{4,5},{5,6},{6,7},{7,4},{8,9},{9,10},{10,1... | collective-permute-start | bytes 393224 | tf_op jit(solution)/shard_map/ppermute | solution.py:33
  196.3 13.5 %collective-permute-start.31 = (bf16[128,512]{1,0:T(8,128)(2,1)S(1)}, bf16[128,512]{1,0:T(8,128)(2,1)S(1)}, u32[]{:S(2)}, u32[]{:S(2)}) collective-permute-start(bf16[128,512]{1,0:T(8,128)(2,1)S(1)} %collective-permute-done.29), channel_id=1, source_target_pairs={{0,3},{1,0},{2,1},{3,2},{4,7},{5,4},{6,5},{7,6},{8,11},{9,8},{10,9... | collective-permute-start | bytes 393224 | tf_op jit(solution)/shard_map/ppermute | solution.py:33
  198.5 1.0 copy-start.8
  199.5 17.5 %copy-start.3 = (bf16[512,1536]{1,0:T(8,128)(2,1)S(1)}, bf16[512,1536]{1,0:T(8,128)(2,1)}, u32[]{:S(2)}) copy-start(bf16[512,1536]{1,0:T(8,128)(2,1)} %refs_1_.1) | copy-start | bytes 4718596
  199.5 17.5 %copy-start.9 = (bf16[512,512]{1,0:T(8,128)(2,1)S(1)}, bf16[512,512]{1,0:T(8,128)(2,1)}, u32[]{:S(2)}) copy-start(bf16[512,512]{1,0:T(8,128)(2,1)} %refs_2_.1) | copy-start | bytes 1572868
  200.6 27.0 %collective-permute-start.24 = (bf16[128,4096]{1,0:T(8,128)(2,1)S(1)}, bf16[128,4096]{1,0:T(8,128)(2,1)S(1)}, u32[]{:S(2)}, u32[]{:S(2)}) collective-permute-start(bf16[128,4096]{1,0:T(8,128)(2,1)S(1)} %shard_map.101), channel_id=1, source_target_pairs={{0,0},{1,1},{2,2},{3,3},{4,8},{5,9},{6,10},{7,11},{8,4},{9,5},{10,... | collective-permute-start | bytes 3145736 | tf_op jit(solution)/shard_map/ppermute | solution.py:33
  209.6 5.4 %collective-permute-start.32 = (bf16[128,512]{1,0:T(8,128)(2,1)S(1)}, bf16[128,512]{1,0:T(8,128)(2,1)S(1)}, u32[]{:S(2)}, u32[]{:S(2)}) collective-permute-start(bf16[128,512]{1,0:T(8,128)(2,1)S(1)} %collective-permute-done.29), channel_id=1, source_target_pairs={{0,2},{1,3},{2,0},{3,1},{4,6},{5,7},{6,4},{7,5},{8,10},{9,11},{10,... | collective-permute-start | bytes 393224 | tf_op jit(solution)/shard_map/ppermute | solution.py:33
  215.0 2.0 collective-permute-start.33
  221.2 6.3 %collective-permute-start.34 = (bf16[128,512]{1,0:T(8,128)(2,1)S(1)}, bf16[128,512]{1,0:T(8,128)(2,1)S(1)}, u32[]{:S(2)}, u32[]{:S(2)}) collective-permute-start(bf16[128,512]{1,0:T(8,128)(2,1)S(1)} %shard_map.104), channel_id=1, source_target_pairs={{0,0},{1,1},{2,2},{3,3},{4,8},{5,9},{6,10},{7,11},{8,4},{9,5},{10,... | collective-permute-start | bytes 393224 | tf_op jit(solution)/shard_map/ppermute | solution.py:33
Sparse Core Ops, SparseCore 0:
  19.7 101.5 all-gather.2
  123.1 39.4 all-gather.4

commit v4 on v3

--- a/solution.py
+++ b/solution.py
@@ -74,19 +74,6 @@
     return whole.reshape((8,) + block.shape)
 
 
-def along_x_parts(block):
-    return [block] + [moved(block, along_x(k)) for k in DISTANCES]
-
-
-def gathered_x(block, x, axis):
-    whole = jnp.zeros(block.shape[:axis] + (4,) + block.shape[axis:], block.dtype)
-    for k, part in zip((0,) + DISTANCES, along_x_parts(block)):
-        at = [0] * whole.ndim
-        at[axis] = (x - k) % 4
-        whole = lax.dynamic_update_slice(whole, jnp.expand_dims(part, axis), at)
-    return whole
-
-
 def layer_norm(rows_in, norm_gain, norm_bias):
     values = rows_in.astype(jnp.float32)
     center = jnp.mean(values, axis=-1, keepdims=True)
@@ -155,11 +142,11 @@
     )
 
 
-PARTS = 4
+PARTS = 2
 
 
 def attention_kernel(*refs):
-    *pieces, weight, _, own, other, held, held_weight, total, projected, sems = refs
+    *pieces, weight, own, other, held, held_weight, total, projected, sems = refs
     depth = held.shape[1] // PARTS
     block = weight.shape[3]
     copies = []
@@ -219,7 +206,7 @@
                 )
 
 
-def attention(pieces, weight, earlier):
+def attention(pieces, weight):
     count = sum(piece.shape[0] for piece in pieces)
     depth = pieces[0].shape[1]
     block = weight.shape[3]
@@ -231,7 +218,7 @@
         60,
         flops=2 * count * depth * columns,
         moved_bytes=2 * depth * (count + columns),
-        in_specs=[pl.BlockSpec(memory_space=pltpu.HBM)] * (len(pieces) + 2),
+        in_specs=[pl.BlockSpec(memory_space=pltpu.HBM)] * (len(pieces) + 1),
         out_specs=(pl.BlockSpec(memory_space=pltpu.VMEM),) * 2,
         scratch_shapes=[
             pltpu.VMEM((count, depth), jnp.bfloat16),
@@ -240,19 +227,19 @@
             pltpu.VMEM((count, columns), jnp.bfloat16),
             pltpu.SemaphoreType.DMA((PARTS, len(pieces) + 6)),
         ],
-    )(*pieces, weight, earlier)
-
-
-def out_matrix(weight, other_weight):
-    planes, xs, halves = weight.shape[:3]
-    return jnp.concatenate(
-        [
-            jnp.concatenate([w[p, x, h] for p in range(planes) for x in range(xs)], axis=1)
-            for w in (weight, other_weight)
-            for h in range(halves)
-        ],
-        axis=0,
-    )
+    )(*pieces, weight)
+
+
+def place_weights(matrix, place, parts, others):
+    planes, _, block, wide = parts[0].shape
+    for i, side in enumerate((parts, others)):
+        for k, part in zip((0,) + DISTANCES, side):
+            for plane in range(planes):
+                at = (plane * 4 + (place[0] - k + 4) % 4) * wide
+                columns = pl.ds(pl.multiple_of(at, wide), wide)
+                for half in range(2):
+                    first = (2 * i + half) * block
+                    matrix[first : first + block, columns] = part[plane, half]
 
 
 def match_matrix(weight):
@@ -261,50 +248,57 @@
     return jnp.concatenate(blocks, axis=0)
 
 
-def send_kernel(skipped, picked, mine, theirs, weight, other_weight, *refs):
-    outs = refs[skipped:]
+def terms_kernel(skipped, picked, place, mine, theirs, *refs):
+    parts, others, outs, matrix = refs[:4], refs[4:8], refs[8 + skipped : -1], refs[-1]
+    place_weights(matrix, place, parts, others)
     both = [
         jnp.concatenate([mine[at : at + many, :], theirs[at : at + many, :]], axis=1)
-        for at, many in picked
+        for spans, _ in picked
+        for at, many in spans
     ]
-    products = dot(jnp.concatenate(both, axis=0), out_matrix(weight, other_weight))
+    products = dot(jnp.concatenate(both, axis=0), matrix[...])
     at = 0
     for out in outs:
         out[...] = products[at : at + out.shape[0]].astype(out.dtype)
         at += out.shape[0]
 
 
-def weight_part(weight):
-    return pl.BlockSpec((2,) + weight.shape[1:], lambda i: (i, 0, 0, 0, 0))
-
-
-def terms(mine, theirs, weight, other_weight, picked, dtype, earlier=()):
+def terms(x, mine, theirs, parts, picked, earlier=()):
+    counts = [sum(many for _, many in spans) for spans, _ in picked]
     earlier = list(earlier)
-    planes, xs, _, _, wide = weight.shape
-    columns = 2 * xs * wide
+    planes, halves, block, wide = parts[0].shape
+    columns = 2 * 4 * wide
     whole = pl.BlockSpec(mine.shape, lambda i: (0, 0))
-    return local(
-        functools.partial(send_kernel, len(earlier), picked),
-        tuple(jax.ShapeDtypeStruct((many, planes * xs * wide), dtype) for _, many in picked),
-        52,
+    part = pl.BlockSpec((2, halves, block, wide), lambda i: (i, 0, 0, 0))
+    return local(
+        functools.partial(terms_kernel, len(earlier), picked),
+        tuple(
+            jax.ShapeDtypeStruct((many, planes * 4 * wide), kind)
+            for many, (_, kind) in zip(counts, picked)
+        ),
+        24,
         flops=2_000_000_000,
         moved_bytes=8_000_000,
         grid=(planes // 2,),
-        in_specs=[whole, whole, weight_part(weight), weight_part(other_weight)]
+        in_specs=[pl.BlockSpec(memory_space=pltpu.SMEM), whole, whole]
+        + [part] * 8
         + [pl.BlockSpec(memory_space=pltpu.HBM)] * len(earlier),
-        out_specs=tuple(pl.BlockSpec((many, columns), lambda i: (0, i)) for _, many in picked),
-    )(mine, theirs, weight, other_weight, *earlier)
-
-
-def descriptor_kernel(tokens, mine, theirs, weight, other_weight, match_weight, _, __, *rest):
+        out_specs=tuple(pl.BlockSpec((many, columns), lambda i: (0, i)) for many in counts),
+        scratch_shapes=[pltpu.VMEM((4 * block, columns), jnp.bfloat16)],
+    )(x.astype(jnp.int32).reshape(1), mine, theirs, *parts, *earlier)
+
+
+def descriptor_kernel(tokens, own, down, down_high, up_low, up, match_weight, *rest):
     *sums, total = rest
+    mid = up_low.shape[0]
+    others = [down[mid:, :], down_high[...], up_low[...], up[...], down[:mid, :]]
     step = pl.program_id(0)
     rows = tokens.shape[0]
-    both = jnp.concatenate([mine[...], theirs[...]], axis=1)
-    products = dot(both, out_matrix(weight, other_weight))
-    with_tokens = products[:rows] + tokens[...].astype(jnp.float32)
-    rounded = jnp.concatenate([with_tokens, products[rows:]], axis=0).astype(jnp.bfloat16)
-    product = dot(rounded, match_matrix(match_weight))
+    with_tokens = (own[...] + tokens[...].astype(jnp.float32)).astype(jnp.bfloat16)
+    product = dot(
+        jnp.concatenate([with_tokens] + others, axis=0),
+        match_matrix(match_weight),
+    )
 
     @pl.when(step == 0)
     def _():
@@ -320,11 +314,12 @@
             out[...] = total[i * rows : (i + 1) * rows].astype(out.dtype)
 
 
-def descriptor_terms(tokens, mine, theirs, weight, other_weight, match_weight, *earlier):
-    planes, xs, _, _, wide = weight.shape
-    rows = tokens.shape[0]
+def descriptor_terms(tokens, own, down, down_high, up_low, up, match_weight):
+    rows, depth = tokens.shape
     width = match_weight.shape[-1]
-    whole = pl.BlockSpec(mine.shape, lambda i: (0, 0))
+    columns = 1024
+    full = pl.BlockSpec((rows, columns), lambda i: (0, i))
+    half = pl.BlockSpec((rows // 2, columns), lambda i: (0, i))
     square = pl.BlockSpec((rows, width), lambda i: (0, 0))
     f32, bf16 = jnp.float32, jnp.bfloat16
     return local(
@@ -334,38 +329,45 @@
         52,
         flops=4_000_000_000,
         moved_bytes=12_000_000,
-        grid=(planes // 2,),
-        in_specs=[
-            pl.BlockSpec((rows, 2 * xs * wide), lambda i: (0, i)),
-            whole,
-            whole,
-            weight_part(weight),
-            weight_part(other_weight),
-            weight_part(match_weight),
-        ]
-        + [pl.BlockSpec(memory_space=pltpu.HBM)] * len(earlier),
+        grid=(depth // columns,),
+        in_specs=[full, full, full, half, half, full]
+        + [pl.BlockSpec((2,) + match_weight.shape[1:], lambda i: (i, 0, 0, 0, 0))],
         out_specs=(square,) * 4,
         scratch_shapes=[pltpu.VMEM((4 * rows, width), f32)],
-    )(tokens, mine, theirs, weight, other_weight, match_weight, *earlier)
-
-
-def added_kernel(a, b, c, d, first, second):
-    first[...] = (a[...] + b[...].astype(jnp.float32)).astype(first.dtype)
-    second[...] = (c[...] + d[...].astype(jnp.float32)).astype(second.dtype)
-
-
-def added(a, b, c, d):
-    return local(added_kernel, (jax.ShapeDtypeStruct(a.shape, b.dtype),) * 2, 20)(a, b, c, d)
-
-
-def features_kernel(tokens, own, low_a, high_a, low_b, high_b, features):
+    )(tokens, own, down, down_high, up_low, up, match_weight)
+
+
+def added_kernel(a, b, c, d, _, first, second):
+    first[...] = (a[...].astype(jnp.float32) + b[...].astype(jnp.float32)).astype(first.dtype)
+    second[...] = (c[...].astype(jnp.float32) + d[...].astype(jnp.float32)).astype(second.dtype)
+
+
+def added(a, b, c, d, earlier):
+    rows, depth = a.shape
+    columns = 1024
+    part = pl.BlockSpec((rows, columns), lambda i: (0, i))
+    return local(
+        added_kernel,
+        (jax.ShapeDtypeStruct(a.shape, b.dtype),) * 2,
+        20,
+        grid=(depth // columns,),
+        in_specs=[part, pl.BlockSpec((rows, columns), lambda i: (1, i)), part, part]
+        + [pl.BlockSpec(memory_space=pltpu.HBM)],
+        out_specs=(part,) * 2,
+    )(a, b, c, d, earlier)
+
+
+def features_kernel(tokens, own, up_low, up, down, down_high, features):
+    mid = up_low.shape[0]
     summed = own[...]
-    summed = summed + jnp.concatenate([low_a[...], high_a[...]], axis=0).astype(jnp.float32)
-    summed = summed + jnp.concatenate([low_b[...], high_b[...]], axis=0).astype(jnp.float32)
+    from_below = [up_low[...], up[:mid, :]]
+    from_above = [down[mid:, :], down_high[...]]
+    summed = summed + jnp.concatenate(from_below, axis=0).astype(jnp.float32)
+    summed = summed + jnp.concatenate(from_above, axis=0).astype(jnp.float32)
     features[...] = (tokens[...].astype(jnp.float32) + summed).astype(jnp.bfloat16)
 
 
-def features_of(tokens, own, halves):
+def features_of(tokens, own, up_low, up, down, down_high):
     rows, depth = tokens.shape
     columns = 1024
     whole = pl.BlockSpec((rows, columns), lambda i: (0, i))
@@ -375,9 +377,9 @@
         jax.ShapeDtypeStruct((rows, depth), jnp.bfloat16),
         20,
         grid=(depth // columns,),
-        in_specs=[whole, whole] + [half] * 4,
+        in_specs=[whole, whole, half, whole, whole, half],
         out_specs=whole,
-    )(tokens, own, *halves)
+    )(tokens, own, up_low, up, down, down_high)
 
 
 def matcher_kernel(*refs):
@@ -452,31 +454,36 @@
 
     tokens = swapped_roles(tokens)
     normed = layer_norm(tokens, norm_gain, norm_bias)
-    out_own = gathered_x(gathered_z(packed[split:], z), x, 1)
-    out_other = moved(out_own, other_core)
+    out_z = gathered_z(packed[split:], z)
     pieces = [normed] + [moved(normed, along_y(k)) for k in DISTANCES]
+    *received, out_z = together(*pieces[1:], out_z)
+    pieces = pieces[:1] + received
     pieces += [moved(piece, other_core) for piece in pieces]
+    out_z = out_z.reshape(8, 2, block, wide)
     pieces = together(*pieces, flops=WAIT)
-    mine, theirs = attention(pieces, weights, out_own)
-
-    shape = (8, 4, 2, block, wide)
-    both = (mine, moved(theirs, other_core), out_own.reshape(shape), out_other.reshape(shape))
-    far_low, far_high, up_high, down_low = terms(
-        *both, [(3 * rows, mid), (3 * rows + mid, mid), (2 * rows + mid, mid), (rows, mid)], bf16
+    parts = [out_z] + [moved(out_z, along_x(k)) for k in DISTANCES]
+    others = [moved(out_z, other_core)]
+    mine, theirs = attention(pieces, weights)
+    mine, *parts[1:] = together(mine, *parts[1:])
+    others += [moved(part, other_core) for part in parts[1:]]
+
+    both = (x, mine, moved(theirs, other_core), parts + others)
+    up, down = terms(
+        *both,
+        [([(2 * rows + mid, rows)], bf16), ([(3 * rows + mid, mid), (rows, mid)], bf16)],
     )
     own, down_high, up_low = terms(
-        *both, [(0, rows), (rows + mid, mid), (2 * rows, mid)], f32, [far_low]
-    )
-    far_low, far_high = moved(far_low, along_y(1)), moved(far_high, along_y(-1))
-    up_high, down_low = moved(up_high, along_y(1)), moved(down_low, along_y(-1))
-    up_low, down_high = added(up_low, far_low, down_high, far_high)
+        *both, [([(0, rows)], f32), ([(rows + mid, mid)], bf16), ([(2 * rows, mid)], bf16)], [up]
+    )
+    sums = descriptor_terms(tokens, own, down, down_high, up_low, up, match_all)
+    up, down = moved(up, along_y(1)), moved(down, along_y(-1))
+    sums_there = [moved(part, along_y(k)) for part, k in zip(sums[1:], (-1, 1, 2))]
+    descriptor = sums[0] + sum(part.astype(f32) for part in sums_there)
+    descriptor = descriptor.astype(bf16)
+    up_low, down_high = added(up_low, up, down_high, down, descriptor)
     up_low, down_high = moved(up_low, along_y(1)), moved(down_high, along_y(-1))
-    sums = descriptor_terms(tokens, *both, match_all, up_high, down_low)
-    features = features_of(tokens, own, (up_low, up_high, down_low, down_high))
-
-    received = [moved(part, along_y(k)) for part, k in zip(sums[1:], (-1, 1, 2))]
-    descriptor = sums[0] + sum(part.astype(f32) for part in received)
-    descriptor = descriptor.astype(bf16)
+    features = features_of(tokens, own, up_low, up, down, down_high)
+
     partner = moved(descriptor, along_z(4))
     quarter = jnp.concatenate([partner] + [moved(partner, along_y(k)) for k in DISTANCES], axis=0)
     pieces = [quarter, moved(quarter, other_core)]

time: 237 us -> 240 us (1.013)
  waiting for transfers between devices: 68.5 us -> 102 us
  starting transfers between devices: 80.7 us -> 58.7 us
  local copies, waits for them, and re-layouts: 27.1 us -> 21.7 us
    ppermute x35 -> x36, starting transfers between devices: 80.7 us -> 58.6 us  [moved(): return lax.ppermute(block, AXES, route)]
    ppermute x35 -> x36, waiting for transfers between devices: 58.9 us -> 74.7 us  [moved(): return lax.ppermute(block, AXES, route)]
    all_gather x1, waiting for transfers between devices: 9.55 us -> 24.7 us  [per_device(): lax.all_gather(packed[:split], ('z', 'xh', 'xl'), axis=0, tiled=True)]
    dynamic_update_slice x4 -> x0, local copies, waits for them, and re-layouts: 6.66 us -> none  [gathered_x(): whole = lax.dynamic_update_slice(whole, jnp.expand_dims(part, axis), at)]
    unnamed x49 -> x65, local copies, waits for them, and re-layouts: 16.9 us -> 20.7 us
    dynamic_update_slice x4, other arithmetic: 2.71 us -> 0.19 us  [gathered_z(): whole = lax.dynamic_update_slice(whole, low[:, None], (0, owner % 4) + rest)]
    all_gather x1, waiting for transfers between devices: 0.01 us -> 2.48 us  [per_device(): match_all = lax.all_gather(match_pair, ('z', 'core'), axis=0, tiled=True)]
  transfers between devices with their start and end apart: 37 -> 38, of which waited for: 16 -> 20; matrix products, arithmetic and copies ran while one was open for 6% -> 1% of each run, Pallas kernels for 17% -> 16%
where the time goes in v4:
time: 240 us; the launch traced here: 239 us
  waiting for transfers between devices  102 us (42%)
  starting transfers between devices  58.7 us (24%)
  Pallas kernels  38.2 us (16%)
  local copies, waits for them, and re-layouts  21.7 us (9%)
  between operations  14.5 us (6%)
  other arithmetic  4.06 us (2%)
    ppermute x36, waiting for transfers between devices, moved(): return lax.ppermute(block, AXES, route)  74.7 us
    ppermute x36, starting transfers between devices, moved(): return lax.ppermute(block, AXES, route)  58.6 us
    all_gather x1, waiting for transfers between devices, per_device(): lax.all_gather(packed[:split], ('z', 'xh', 'xl'), axis=0, tiled=True)  24.7 us
    unnamed x65, local copies, waits for them, and re-layouts  20.7 us
    pallas_call x1, Pallas kernels, attention(): local(attention_kernel, (result, result), 60, flops=2 * count * depth * c...  16.5 us
    pallas_call x2, Pallas kernels, terms(): local(functools.partial(terms_kernel, len(earlier), picked), tuple((jax.S...  9.88 us
    pallas_call x1, Pallas kernels, descriptor_terms(): local(descriptor_kernel, (jax.ShapeDtypeStruct((rows, width), f32),) + (j...  5.95 us
  transfers between devices with their start and end apart: 38, of which 20 were waited for; matrix products, arithmetic and copies ran while one was open for 1% of the time, Pallas kernels for 16%

profile of v4, /device:TPU:1, one launch (start us, length us, event | category | flops | bytes accessed | tf_op | source)
XLA Modules:
  0.0 239.1 jit_solution(7989415783675254142)
XLA Ops:
  7.2 1.0 copy.67.refs_0_
  8.2 1.1 copy.33
  9.5 0.9 pad_maximum_fusion
  10.4 4.5 %collective-permute-start.4 = (bf16[1024,128]{1,0:T(8,128)(2,1)S(1)}, bf16[1024,128]{1,0:T(8,128)(2,1)S(1)}, u32[]{:S(2)}, u32[]{:S(2)}) collective-permute-start(bf16[1024,128]{1,0:T(8,128)(2,1)S(1)} %pad_maximum_fusion), channel_id=1, source_target_pairs={{0,0},{1,1},{2,2},{3,3},{4,8},{5,9},{6,10},{7,11},{8,4},{9,5},{10,... | collective-permute-start | bytes 786440 | tf_op jit(solution)/shard_map/ppermute | solution.py:33
  14.9 4.0 %collective-permute-done.4.refs_1_ = bf16[1024,128]{1,0:T(8,128)(2,1)S(1)} collective-permute-done((bf16[1024,128]{1,0:T(8,128)(2,1)S(1)}, bf16[1024,128]{1,0:T(8,128)(2,1)S(1)}, u32[]{:S(2)}, u32[]{:S(2)}) %collective-permute-start.4) | collective-permute-done | bytes 262176 | tf_op jit(solution)/shard_map/ppermute | solution.py:33
  19.8 6.1 %collective-permute-done.23 = bf16[128,512]{1,0:T(8,128)(2,1)S(1)} collective-permute-done((bf16[128,512]{1,0:T(8,128)(2,1)S(1)}, bf16[128,512]{1,0:T(8,128)(2,1)S(1)}, u32[]{:S(2)}, u32[]{:S(2)}) %collective-permute-start.23) | collective-permute-done | bytes 131104 | tf_op jit(solution)/shard_map/ppermute | solution.py:33
  26.7 2.5 %collective-permute-start = (bf16[128,4096]{1,0:T(8,128)(2,1)S(1)}, bf16[128,4096]{1,0:T(8,128)(2,1)S(1)}, u32[]{:S(2)}, u32[]{:S(2)}) collective-permute-start(bf16[128,4096]{1,0:T(8,128)(2,1)S(1)} %copy-done.28), channel_id=1, source_target_pairs={{0,0},{1,1},{2,2},{3,3},{4,8},{5,9},{6,10},{7,11},{8,4},{9,5},{10,... | collective-permute-start | bytes 3145736 | tf_op jit(solution)/shard_map/ppermute | solution.py:33
  29.2 7.0 %collective-permute-start.5 = (bf16[256,128]{1,0:T(8,128)(2,1)S(1)}, bf16[256,128]{1,0:T(8,128)(2,1)S(1)}, u32[]{:S(2)}, u32[]{:S(2)}) collective-permute-start(bf16[256,128]{1,0:T(8,128)(2,1)S(1)} %get-tuple-element.61), channel_id=1, source_target_pairs={{0,128},{1,129},{2,130},{3,131},{4,132},{5,133},{6,134},{7,135},{8... | collective-permute-start | bytes 196616 | tf_op jit(solution)/shard_map/ppermute | solution.py:33
  36.2 9.1 %collective-permute-done.tokens = bf16[128,4096]{1,0:T(8,128)(2,1)S(1)} collective-permute-done((bf16[128,4096]{1,0:T(8,128)(2,1)S(1)}, bf16[128,4096]{1,0:T(8,128)(2,1)S(1)}, u32[]{:S(2)}, u32[]{:S(2)}) %collective-permute-start) | collective-permute-done | bytes 1048608 | tf_op jit(solution)/shard_map/ppermute | solution.py:33
  46.1 1.5 fusion.5.refs_0_
  47.6 1.3 collective-permute-start.1
  48.9 1.4 collective-permute-start.2
  50.3 1.6 collective-permute-start.3
  52.0 1.7 collective-permute-start.6
  53.7 4.6 %collective-permute-start.7 = (bf16[2,256,128]{2,1,0:T(8,128)(2,1)S(1)}, bf16[2,256,128]{2,1,0:T(8,128)(2,1)S(1)}, u32[]{:S(2)}, u32[]{:S(2)}) collective-permute-start(bf16[2,256,128]{2,1,0:T(8,128)(2,1)S(1)} %shard_map.95), channel_id=1, source_target_pairs={{0,224},{1,225},{2,226},{3,227},{4,228},{5,229},{6,230},{7,231},{8... | collective-permute-start | bytes 393224 | tf_op jit(solution)/shard_map/ppermute | solution.py:33
  58.4 3.0 %collective-permute-done.6 = bf16[2,256,128]{2,1,0:T(8,128)(2,1)S(1)} collective-permute-done((bf16[2,256,128]{2,1,0:T(8,128)(2,1)S(1)}, bf16[2,256,128]{2,1,0:T(8,128)(2,1)S(1)}, u32[]{:S(2)}, u32[]{:S(2)}) %collective-permute-start.6) | collective-permute-done | bytes 131104 | tf_op jit(solution)/shard_map/ppermute | solution.py:33
  61.5 6.2 %collective-permute-done.8 = bf16[2,256,128]{2,1,0:T(8,128)(2,1)S(1)} collective-permute-done((bf16[2,256,128]{2,1,0:T(8,128)(2,1)S(1)}, bf16[2,256,128]{2,1,0:T(8,128)(2,1)S(1)}, u32[]{:S(2)}, u32[]{:S(2)}) %collective-permute-start.8) | collective-permute-done | bytes 131104 | tf_op jit(solution)/shard_map/ppermute | solution.py:33
  67.9 5.2 %collective-permute-done.1.refs_0_ = bf16[128,4096]{1,0:T(8,128)(2,1)S(1)} collective-permute-done((bf16[128,4096]{1,0:T(8,128)(2,1)}, bf16[128,4096]{1,0:T(8,128)(2,1)S(1)}, u32[]{:S(2)}, u32[]{:S(2)}) %collective-permute-start.1) | collective-permute-done | bytes 1048608 | tf_op jit(solution)/shard_map/ppermute | solution.py:33
  73.1 1.3 collective-permute-done.2.refs_1_
  74.4 14.1 %collective-permute-done.3.refs_2_ = bf16[128,4096]{1,0:T(8,128)(2,1)} collective-permute-done((bf16[128,4096]{1,0:T(8,128)(2,1)}, bf16[128,4096]{1,0:T(8,128)(2,1)}, u32[]{:S(2)}, u32[]{:S(2)}) %collective-permute-start.3) | collective-permute-done | bytes 1048608 | tf_op jit(solution)/shard_map/ppermute | solution.py:33
  89.0 2.7 %collective-permute-start.14 = (bf16[8,2,128,128]{3,2,1,0:T(8,128)(2,1)S(1)}, bf16[8,2,128,128]{3,2,1,0:T(8,128)(2,1)}, u32[]{:S(2)}, u32[]{:S(2)}) collective-permute-start(bf16[8,2,128,128]{3,2,1,0:T(8,128)(2,1)S(1)} %bitcast.38), channel_id=1, source_target_pairs={{0,20},{1,21},{2,22},{3,23},{4,0},{5,1},{6,2},{7,3},{8,28},{9,29},... | collective-permute-start | bytes 1572872 | tf_op jit(solution)/shard_map/ppermute | solution.py:33
  92.1 2.1 collective-permute-done.11.refs_6_
  94.4 1.0 copy-done.5
  95.4 1.0 copy-done.6
  96.5 1.0 copy-done.16
  97.4 1.0 copy-done.17
  98.4 1.0 copy-done.18
  99.4 1.0 copy-done.19
  100.4 24.7 %all-gather.3.cloned.1.call-done = bf16[24576,128]{1,0:T(8,128)(2,1)} async-done(((bf16[768,128]{1,0:T(8,128)(2,1)}), bf16[24576,128]{1,0:T(8,128)(2,1)}) %all-gather.3.cloned.1.call-update) | async-done | bytes 6291472 | tf_op jit(solution)/shard_map/all_gather | solution.py:442
  125.1 16.5 %shard_map.98 = (bf16[512,256]{1,0:T(8,128)(2,1)}, bf16[512,256]{1,0:T(8,128)(2,1)}) custom-call(bf16[128,4096]{1,0:T(8,128)(2,1)} %get-tuple-element.34.refs_0_, bf16[128,4096]{1,0:T(8,128)(2,1)} %copy-done.5, bf16[128,4096]{1,0:T(8,128)(2,1)} %copy-done.6, bf16[128,4096]{1,0:T(8,128)(2,1)} %get-tuple-element.37.refs_3_, bf16[128,4096]{1,0:T(8,128)(2,1)} %copy-done.16, ...), custom_call_target="tpu_custom_call" | custom-call | flops 6442450944 | bytes 14680064 | tf_op jit(solution)/shard_map/pallas_call | solution.py:215
  141.6 0.9 copy-done.12
  143.3 1.3 collective-permute-start.18
  145.1 3.4 %collective-permute-done.16.theirs = bf16[512,256]{1,0:T(8,128)(2,1)S(1)} collective-permute-done((bf16[512,256]{1,0:T(8,128)(2,1)}, bf16[512,256]{1,0:T(8,128)(2,1)S(1)}, u32[]{:S(2)}, u32[]{:S(2)}) %collective-permute-start.16) | collective-permute-done | bytes 262176 | tf_op jit(solution)/shard_map/ppermute | solution.py:33
  148.5 1.1 copy-done.14
  149.7 5.3 %shard_map.100 = (bf16[128,4096]{1,0:T(8,128)(2,1)}, bf16[128,4096]{1,0:T(8,128)(2,1)}) custom-call(s32[1]{0:T(128)} %bitcast.place, bf16[512,256]{1,0:T(8,128)(2,1)S(1)} %copy-done.14, bf16[512,256]{1,0:T(8,128)(2,1)S(1)} %collective-permute-done.16.theirs, bf16[8,2,128,128]{3,2,1,0:T(8,128)(2,1)S(1)} %bitcast.41, ...), custom_call_target="tpu_custom_call" | custom-call | flops 2000000000 | bytes 8000000 | tf_op jit(solution)/shard_map/pallas_call | solution.py:273
  155.1 1.1 collective-permute-start.21
  156.2 2.0 collective-permute-start.22
  158.2 1.1 copy-done.21
  159.3 1.1 copy-done.23
  160.3 1.0 copy-done.25
  161.4 4.5 %shard_map.101 = (f32[128,4096]{1,0:T(8,128)S(1)}, bf16[64,4096]{1,0:T(8,128)(2,1)S(1)}, bf16[64,4096]{1,0:T(8,128)(2,1)S(1)}) custom-call(s32[1]{0:T(128)} %bitcast.place, bf16[512,256]{1,0:T(8,128)(2,1)S(1)} %copy-done.15, bf16[512,256]{1,0:T(8,128)(2,1)S(1)} %collective-permute-done.16.theirs, bf16[8,2,128,128]{3,2,1,0:T(8,128)(2,1)S(1)} %bitcast.42, ...), custom_call_target="tpu_custom_call" | custom-call | flops 2000000000 | bytes 8000000 | tf_op jit(solution)/shard_map/pallas_call | solution.py:273
  165.9 1.3 copy-done.2
  168.1 0.8 copy-done.9
  168.9 2.5 %all-gather.5.cloned.1.call-done = bf16[4096,512]{1,0:T(8,128)(2,1)} async-done(((bf16[256,512]{1,0:T(8,128)(2,1)}), bf16[4096,512]{1,0:T(8,128)(2,1)}) %all-gather.5.cloned.1.call-update) | async-done | bytes 4194320 | tf_op jit(solution)/shard_map/all_gather | solution.py:452
  171.4 1.0 copy-done.8
  172.4 1.0 copy-done.10
  173.5 5.9 %shard_map.103 = (f32[128,512]{1,0:T(8,128)S(1)}, bf16[128,512]{1,0:T(8,128)(2,1)S(1)}, bf16[128,512]{1,0:T(8,128)(2,1)S(1)}, bf16[128,512]{1,0:T(8,128)(2,1)S(1)}) custom-call(bf16[128,4096]{1,0:T(8,128)(2,1)} %copy-done, f32[128,4096]{1,0:T(8,128)} %copy-done.2, bf16[128,4096]{1,0:T(8,128)(2,1)} %get-tuple-element.53.down, bf16[64,4096]{1,0:T(8,128)(2,1)S(1)} %copy-done.8, ...), custom_call_target="tpu_custom_call" | custom-call | flops 4000000000 | bytes 12000000 | tf_op jit(solution)/shard_map/pallas_call | solution.py:325
  179.4 2.7 %collective-permute-start.24 = (bf16[128,512]{1,0:T(8,128)(2,1)S(1)}, bf16[128,512]{1,0:T(8,128)(2,1)S(1)}, u32[]{:S(2)}, u32[]{:S(2)}) collective-permute-start(bf16[128,512]{1,0:T(8,128)(2,1)S(1)} %get-tuple-element.55), channel_id=1, source_target_pairs={{0,3},{1,0},{2,1},{3,2},{4,7},{5,4},{6,5},{7,6},{8,11},{9,8},{10,9... | collective-permute-start | bytes 393224 | tf_op jit(solution)/shard_map/ppermute | solution.py:33
  182.1 1.8 collective-permute-start.26
  183.9 1.6 collective-permute-done.24
  185.5 3.2 %collective-permute-done.25 = bf16[128,512]{1,0:T(8,128)(2,1)S(1)} collective-permute-done((bf16[128,512]{1,0:T(8,128)(2,1)S(1)}, bf16[128,512]{1,0:T(8,128)(2,1)S(1)}, u32[]{:S(2)}, u32[]{:S(2)}) %collective-permute-start.25) | collective-permute-done | bytes 131104 | tf_op jit(solution)/shard_map/ppermute | solution.py:33
  188.7 1.1 collective-permute-done.26
  190.7 2.5 %collective-permute-start.28 = (bf16[64,4096]{1,0:T(8,128)(2,1)S(1)}, bf16[64,4096]{1,0:T(8,128)(2,1)S(1)}, u32[]{:S(2)}, u32[]{:S(2)}) collective-permute-start(bf16[64,4096]{1,0:T(8,128)(2,1)S(1)} %get-tuple-element.59), channel_id=1, source_target_pairs={{0,3},{1,0},{2,1},{3,2},{4,7},{5,4},{6,5},{7,6},{8,11},{9,8},{10,9... | collective-permute-start | bytes 1572872 | tf_op jit(solution)/shard_map/ppermute | solution.py:33
  193.2 4.1 %collective-permute-start.30 = (bf16[128,512]{1,0:T(8,128)(2,1)S(1)}, bf16[128,512]{1,0:T(8,128)(2,1)S(1)}, u32[]{:S(2)}, u32[]{:S(2)}) collective-permute-start(bf16[128,512]{1,0:T(8,128)(2,1)S(1)} %add_convert_fusion._.refs_0_), channel_id=1, source_target_pairs={{0,128},{1,129},{2,130},{3,131},{4,132},{5,133},{6,134},{7,135},{8... | collective-permute-start | bytes 393224 | tf_op jit(solution)/shard_map/ppermute | solution.py:33
  197.3 3.7 %collective-permute-done.30 = bf16[128,512]{1,0:T(8,128)(2,1)S(1)} collective-permute-done((bf16[128,512]{1,0:T(8,128)(2,1)S(1)}, bf16[128,512]{1,0:T(8,128)(2,1)S(1)}, u32[]{:S(2)}, u32[]{:S(2)}) %collective-permute-start.30) | collective-permute-done | bytes 131104 | tf_op jit(solution)/shard_map/ppermute | solution.py:33
  201.0 2.7 %collective-permute-start.32 = (bf16[128,512]{1,0:T(8,128)(2,1)S(1)}, bf16[128,512]{1,0:T(8,128)(2,1)S(1)}, u32[]{:S(2)}, u32[]{:S(2)}) collective-permute-start(bf16[128,512]{1,0:T(8,128)(2,1)S(1)} %collective-permute-done.30), channel_id=1, source_target_pairs={{0,3},{1,0},{2,1},{3,2},{4,7},{5,4},{6,5},{7,6},{8,11},{9,8},{10,9... | collective-permute-start | bytes 393224 | tf_op jit(solution)/shard_map/ppermute | solution.py:33
  203.7 1.1 shard_map.105
  204.9 7.8 %collective-permute-start.29 = (bf16[128,4096]{1,0:T(8,128)(2,1)S(1)}, bf16[128,4096]{1,0:T(8,128)(2,1)S(1)}, u32[]{:S(2)}, u32[]{:S(2)}) collective-permute-start(bf16[128,4096]{1,0:T(8,128)(2,1)S(1)} %shard_map.105), channel_id=1, source_target_pairs={{0,0},{1,1},{2,2},{3,3},{4,8},{5,9},{6,10},{7,11},{8,4},{9,5},{10,... | collective-permute-start | bytes 3145736 | tf_op jit(solution)/shard_map/ppermute | solution.py:33
  212.8 5.3 %collective-permute-done.33 = bf16[128,512]{1,0:T(8,128)(2,1)S(1)} collective-permute-done((bf16[128,512]{1,0:T(8,128)(2,1)S(1)}, bf16[128,512]{1,0:T(8,128)(2,1)S(1)}, u32[]{:S(2)}, u32[]{:S(2)}) %collective-permute-start.33) | collective-permute-done | bytes 131104 | tf_op jit(solution)/shard_map/ppermute | solution.py:33
  218.2 1.9 collective-permute-done.34.refs_4_
  220.1 4.2 %shard_map.106 = bf16[128,512]{1,0:T(8,128)(2,1)S(1)} custom-call(bf16[128,512]{1,0:T(8,128)(2,1)S(1)} %add_convert_fusion._.refs_0_, bf16[512,1536]{1,0:T(8,128)(2,1)S(1)} %copy-done.4, bf16[512,512]{1,0:T(8,128)(2,1)S(1)} %copy-done.11, bf16[512,512]{1,0:T(8,128)(2,1)S(1)} %constant_dynamic-update-slice_fusion.refs_3_, ...), custom_call_target="tpu_custom_call" | custom-call | tf_op jit(solution)/shard_map/pallas_call | solution.py:416
  224.3 3.1 %collective-permute-start.35 = (bf16[128,512]{1,0:T(8,128)(2,1)S(1)}, bf16[128,512]{1,0:T(8,128)(2,1)S(1)}, u32[]{:S(2)}, u32[]{:S(2)}) collective-permute-start(bf16[128,512]{1,0:T(8,128)(2,1)S(1)} %shard_map.106), channel_id=1, source_target_pairs={{0,0},{1,1},{2,2},{3,3},{4,8},{5,9},{6,10},{7,11},{8,4},{9,5},{10,... | collective-permute-start | bytes 393224 | tf_op jit(solution)/shard_map/ppermute | solution.py:33
  227.4 3.2 %collective-permute-done.35 = bf16[128,512]{1,0:T(8,128)(2,1)S(1)} collective-permute-done((bf16[128,512]{1,0:T(8,128)(2,1)S(1)}, bf16[128,512]{1,0:T(8,128)(2,1)S(1)}, u32[]{:S(2)}, u32[]{:S(2)}) %collective-permute-start.35) | collective-permute-done | bytes 131104 | tf_op jit(solution)/shard_map/ppermute | solution.py:33
  230.6 1.0 copy.68
  (109 shorter events, 7.9 us)
Async XLA Ops:
  7.2 19.6 %copy-start.28 = (bf16[128,4096]{1,0:T(8,128)(2,1)S(1)}, bf16[128,4096]{1,0:T(8,128)(2,1)}, u32[]{:S(2)}) copy-start(bf16[128,4096]{1,0:T(8,128)(2,1)} %param.8) | copy-start | bytes 3145732
  7.2 117.9 %all-gather.3.cloned.1.call-start = ((), (), s32[]{:S(2)}) async-start(), calls=%async_computation | async-start | bytes 6488064 | tf_op jit(solution)/shard_map/all_gather | solution.py:442
  10.3 35.7 %copy-start.26 = (f32[4096]{0:T(1024)S(1)}, f32[4096]{0:T(1024)}, u32[]{:S(2)}) copy-start(f32[4096]{0:T(1024)} %param.10) | copy-start | bytes 49156
  10.3 35.7 %copy-start.27 = (f32[4096]{0:T(1024)S(1)}, f32[4096]{0:T(1024)}, u32[]{:S(2)}) copy-start(f32[4096]{0:T(1024)} %param.9) | copy-start | bytes 49156
  10.4 8.6 %collective-permute-start.4 = (bf16[1024,128]{1,0:T(8,128)(2,1)S(1)}, bf16[1024,128]{1,0:T(8,128)(2,1)S(1)}, u32[]{:S(2)}, u32[]{:S(2)}) collective-permute-start(bf16[1024,128]{1,0:T(8,128)(2,1)S(1)} %pad_maximum_fusion), channel_id=1, source_target_pairs={{0,0},{1,1},{2,2},{3,3},{4,8},{5,9},{6,10},{7,11},{8,4},{9,5},{10,... | collective-permute-start | bytes 786440 | tf_op jit(solution)/shard_map/ppermute | solution.py:33
  19.6 151.7 %all-gather.5.cloned.1.call-start = ((), (), s32[]{:S(2)}) async-start(), calls=%async_computation.1 | async-start | bytes 4456448 | tf_op jit(solution)/shard_map/all_gather | solution.py:452
  19.7 6.2 %collective-permute-start.23 = (bf16[128,512]{1,0:T(8,128)(2,1)S(1)}, bf16[128,512]{1,0:T(8,128)(2,1)S(1)}, u32[]{:S(2)}, u32[]{:S(2)}) collective-permute-start(bf16[128,512]{1,0:T(8,128)(2,1)S(1)} %shard_map.102), channel_id=1, source_target_pairs={{0,20},{1,21},{2,22},{3,23},{4,16},{5,17},{6,18},{7,19},{8,28},{9,... | collective-permute-start | bytes 393224 | tf_op jit(solution)/shard_map/ppermute | solution.py:33
  26.7 18.6 %collective-permute-start = (bf16[128,4096]{1,0:T(8,128)(2,1)S(1)}, bf16[128,4096]{1,0:T(8,128)(2,1)S(1)}, u32[]{:S(2)}, u32[]{:S(2)}) collective-permute-start(bf16[128,4096]{1,0:T(8,128)(2,1)S(1)} %copy-done.28), channel_id=1, source_target_pairs={{0,0},{1,1},{2,2},{3,3},{4,8},{5,9},{6,10},{7,11},{8,4},{9,5},{10,... | collective-permute-start | bytes 3145736 | tf_op jit(solution)/shard_map/ppermute | solution.py:33
  29.2 22.7 %collective-permute-start.5 = (bf16[256,128]{1,0:T(8,128)(2,1)S(1)}, bf16[256,128]{1,0:T(8,128)(2,1)S(1)}, u32[]{:S(2)}, u32[]{:S(2)}) collective-permute-start(bf16[256,128]{1,0:T(8,128)(2,1)S(1)} %get-tuple-element.61), channel_id=1, source_target_pairs={{0,128},{1,129},{2,130},{3,131},{4,132},{5,133},{6,134},{7,135},{8... | collective-permute-start | bytes 196616 | tf_op jit(solution)/shard_map/ppermute | solution.py:33
  45.4 2.2 copy-start
  47.6 25.5 %collective-permute-start.1 = (bf16[128,4096]{1,0:T(8,128)(2,1)}, bf16[128,4096]{1,0:T(8,128)(2,1)S(1)}, u32[]{:S(2)}, u32[]{:S(2)}) collective-permute-start(bf16[128,4096]{1,0:T(8,128)(2,1)} %fusion.5.refs_0_), channel_id=1, source_target_pairs={{0,1},{1,2},{2,3},{3,0},{4,5},{5,6},{6,7},{7,4},{8,9},{9,10},{10,1... | collective-permute-start | bytes 3145736 | tf_op jit(solution)/shard_map/ppermute | solution.py:33
  48.9 25.6 %collective-permute-start.2 = (bf16[128,4096]{1,0:T(8,128)(2,1)}, bf16[128,4096]{1,0:T(8,128)(2,1)S(1)}, u32[]{:S(2)}, u32[]{:S(2)}) collective-permute-start(bf16[128,4096]{1,0:T(8,128)(2,1)} %fusion.5.refs_0_), channel_id=1, source_target_pairs={{0,3},{1,0},{2,1},{3,2},{4,7},{5,4},{6,5},{7,6},{8,11},{9,8},{10,9... | collective-permute-start | bytes 3145736 | tf_op jit(solution)/shard_map/ppermute | solution.py:33
  50.3 38.2 %collective-permute-start.3 = (bf16[128,4096]{1,0:T(8,128)(2,1)}, bf16[128,4096]{1,0:T(8,128)(2,1)}, u32[]{:S(2)}, u32[]{:S(2)}) collective-permute-start(bf16[128,4096]{1,0:T(8,128)(2,1)} %fusion.5.refs_0_), channel_id=1, source_target_pairs={{0,2},{1,3},{2,0},{3,1},{4,6},{5,7},{6,4},{7,5},{8,10},{9,11},{10,... | collective-permute-start | bytes 3145736 | tf_op jit(solution)/shard_map/ppermute | solution.py:33
  52.0 9.4 %collective-permute-start.6 = (bf16[2,256,128]{2,1,0:T(8,128)(2,1)S(1)}, bf16[2,256,128]{2,1,0:T(8,128)(2,1)S(1)}, u32[]{:S(2)}, u32[]{:S(2)}) collective-permute-start(bf16[2,256,128]{2,1,0:T(8,128)(2,1)S(1)} %shard_map.95), channel_id=1, source_target_pairs={{0,32},{1,33},{2,34},{3,35},{4,36},{5,37},{6,38},{7,39},{8,40},{9,... | collective-permute-start | bytes 393224 | tf_op jit(solution)/shard_map/ppermute | solution.py:33
  53.7 7.7 %collective-permute-start.7 = (bf16[2,256,128]{2,1,0:T(8,128)(2,1)S(1)}, bf16[2,256,128]{2,1,0:T(8,128)(2,1)S(1)}, u32[]{:S(2)}, u32[]{:S(2)}) collective-permute-start(bf16[2,256,128]{2,1,0:T(8,128)(2,1)S(1)} %shard_map.95), channel_id=1, source_target_pairs={{0,224},{1,225},{2,226},{3,227},{4,228},{5,229},{6,230},{7,231},{8... | collective-permute-start | bytes 393224 | tf_op jit(solution)/shard_map/ppermute | solution.py:33
  61.4 6.3 %collective-permute-start.8 = (bf16[2,256,128]{2,1,0:T(8,128)(2,1)S(1)}, bf16[2,256,128]{2,1,0:T(8,128)(2,1)S(1)}, u32[]{:S(2)}, u32[]{:S(2)}) collective-permute-start(bf16[2,256,128]{2,1,0:T(8,128)(2,1)S(1)} %shard_map.95), channel_id=1, source_target_pairs={{0,64},{1,65},{2,66},{3,67},{4,68},{5,69},{6,70},{7,71},{8,72},{9,... | collective-permute-start | bytes 393224 | tf_op jit(solution)/shard_map/ppermute | solution.py:33
  67.8 21.3 %collective-permute-start.9 = (bf16[128,4096]{1,0:T(8,128)(2,1)}, bf16[128,4096]{1,0:T(8,128)(2,1)S(1)}, u32[]{:S(2)}, u32[]{:S(2)}) collective-permute-start(bf16[128,4096]{1,0:T(8,128)(2,1)} %fusion.5.refs_0_), channel_id=1, source_target_pairs={{0,8},{1,9},{2,10},{3,11},{4,12},{5,13},{6,14},{7,15},{8,0},{9,1},... | collective-permute-start | bytes 3145736 | tf_op jit(solution)/shard_map/ppermute | solution.py:33
  88.5 3.2 %collective-permute-start.10 = (bf16[128,4096]{1,0:T(8,128)(2,1)S(1)}, bf16[128,4096]{1,0:T(8,128)(2,1)S(1)}, u32[]{:S(2)}, u32[]{:S(2)}) collective-permute-start(bf16[128,4096]{1,0:T(8,128)(2,1)S(1)} %get-tuple-element.31.refs_1_), channel_id=1, source_target_pairs={{0,8},{1,9},{2,10},{3,11},{4,12},{5,13},{6,14},{7,15},{8,0},{9,1},... | collective-permute-start | bytes 3145736 | tf_op jit(solution)/shard_map/ppermute | solution.py:33
  88.5 5.7 %collective-permute-start.11 = (bf16[128,4096]{1,0:T(8,128)(2,1)S(1)}, bf16[128,4096]{1,0:T(8,128)(2,1)S(1)}, u32[]{:S(2)}, u32[]{:S(2)}) collective-permute-start(bf16[128,4096]{1,0:T(8,128)(2,1)S(1)} %get-tuple-element.32.refs_2_), channel_id=1, source_target_pairs={{0,8},{1,9},{2,10},{3,11},{4,12},{5,13},{6,14},{7,15},{8,0},{9,1},... | collective-permute-start | bytes 3145736 | tf_op jit(solution)/shard_map/ppermute | solution.py:33
  89.0 5.4 %collective-permute-start.12 = (bf16[128,4096]{1,0:T(8,128)(2,1)}, bf16[128,4096]{1,0:T(8,128)(2,1)S(1)}, u32[]{:S(2)}, u32[]{:S(2)}) collective-permute-start(bf16[128,4096]{1,0:T(8,128)(2,1)} %get-tuple-element.33.refs_3_), channel_id=1, source_target_pairs={{0,8},{1,9},{2,10},{3,11},{4,12},{5,13},{6,14},{7,15},{8,0},{9,1},... | collective-permute-start | bytes 3145736 | tf_op jit(solution)/shard_map/ppermute | solution.py:33
  89.0 52.5 %collective-permute-start.13 = (bf16[8,2,128,128]{3,2,1,0:T(8,128)(2,1)S(1)}, bf16[8,2,128,128]{3,2,1,0:T(8,128)(2,1)S(1)}, u32[]{:S(2)}, u32[]{:S(2)}) collective-permute-start(bf16[8,2,128,128]{3,2,1,0:T(8,128)(2,1)S(1)} %bitcast.37), channel_id=1, source_target_pairs={{0,4},{1,5},{2,6},{3,7},{4,16},{5,17},{6,18},{7,19},{8,12},{9,13},... | collective-permute-start | bytes 1572872 | tf_op jit(solution)/shard_map/ppermute | solution.py:33
  89.0 52.6 %collective-permute-start.14 = (bf16[8,2,128,128]{3,2,1,0:T(8,128)(2,1)S(1)}, bf16[8,2,128,128]{3,2,1,0:T(8,128)(2,1)}, u32[]{:S(2)}, u32[]{:S(2)}) collective-permute-start(bf16[8,2,128,128]{3,2,1,0:T(8,128)(2,1)S(1)} %bitcast.38), channel_id=1, source_target_pairs={{0,20},{1,21},{2,22},{3,23},{4,0},{5,1},{6,2},{7,3},{8,28},{9,29},... | collective-permute-start | bytes 1572872 | tf_op jit(solution)/shard_map/ppermute | solution.py:33
  91.7 49.9 %collective-permute-start.15 = (bf16[8,2,128,128]{3,2,1,0:T(8,128)(2,1)S(1)}, bf16[8,2,128,128]{3,2,1,0:T(8,128)(2,1)}, u32[]{:S(2)}, u32[]{:S(2)}) collective-permute-start(bf16[8,2,128,128]{3,2,1,0:T(8,128)(2,1)S(1)} %bitcast.39), channel_id=1, source_target_pairs={{0,16},{1,17},{2,18},{3,19},{4,20},{5,21},{6,22},{7,23},{8,24},{9,... | collective-permute-start | bytes 1572872 | tf_op jit(solution)/shard_map/ppermute | solution.py:33
  94.2 50.9 %collective-permute-start.17 = (bf16[8,2,128,128]{3,2,1,0:T(8,128)(2,1)S(1)}, bf16[8,2,128,128]{3,2,1,0:T(8,128)(2,1)}, u32[]{:S(2)}, u32[]{:S(2)}) collective-permute-start(bf16[8,2,128,128]{3,2,1,0:T(8,128)(2,1)S(1)} %bitcast.40), channel_id=1, source_target_pairs={{0,8},{1,9},{2,10},{3,11},{4,12},{5,13},{6,14},{7,15},{8,0},{9,1},... | collective-permute-start | bytes 1572872 | tf_op jit(solution)/shard_map/ppermute | solution.py:33
  94.4 1.0 copy-start.5
  95.4 1.1 copy-start.6
  96.5 1.0 copy-start.16
  97.4 1.0 copy-start.17
  98.4 1.0 copy-start.18
  99.4 1.0 copy-start.19
  141.6 1.0 copy-start.12
  143.3 5.2 %collective-permute-start.18 = (bf16[8,2,128,128]{3,2,1,0:T(8,128)(2,1)S(1)}, bf16[8,2,128,128]{3,2,1,0:T(8,128)(2,1)S(1)}, u32[]{:S(2)}, u32[]{:S(2)}) collective-permute-start(bf16[8,2,128,128]{3,2,1,0:T(8,128)(2,1)S(1)} %get-tuple-element.46.refs_1_), channel_id=1, source_target_pairs={{0,8},{1,9},{2,10},{3,11},{4,12},{5,13},{6,14},{7,15},{8,0},{9,1},... | collective-permute-start | bytes 1572872 | tf_op jit(solution)/shard_map/ppermute | solution.py:33
  144.6 3.9 %collective-permute-start.19 = (bf16[8,2,128,128]{3,2,1,0:T(8,128)(2,1)}, bf16[8,2,128,128]{3,2,1,0:T(8,128)(2,1)S(1)}, u32[]{:S(2)}, u32[]{:S(2)}) collective-permute-start(bf16[8,2,128,128]{3,2,1,0:T(8,128)(2,1)} %get-tuple-element.47.refs_2_), channel_id=1, source_target_pairs={{0,8},{1,9},{2,10},{3,11},{4,12},{5,13},{6,14},{7,15},{8,0},{9,1},... | collective-permute-start | bytes 1572872 | tf_op jit(solution)/shard_map/ppermute | solution.py:33
  144.6 3.9 %collective-permute-start.20 = (bf16[8,2,128,128]{3,2,1,0:T(8,128)(2,1)}, bf16[8,2,128,128]{3,2,1,0:T(8,128)(2,1)S(1)}, u32[]{:S(2)}, u32[]{:S(2)}) collective-permute-start(bf16[8,2,128,128]{3,2,1,0:T(8,128)(2,1)} %get-tuple-element.48.refs_3_), channel_id=1, source_target_pairs={{0,8},{1,9},{2,10},{3,11},{4,12},{5,13},{6,14},{7,15},{8,0},{9,1},... | collective-permute-start | bytes 1572872 | tf_op jit(solution)/shard_map/ppermute | solution.py:33
  145.1 3.4 %collective-permute-start.16 = (bf16[512,256]{1,0:T(8,128)(2,1)}, bf16[512,256]{1,0:T(8,128)(2,1)S(1)}, u32[]{:S(2)}, u32[]{:S(2)}) collective-permute-start(bf16[512,256]{1,0:T(8,128)(2,1)} %get-tuple-element.45), channel_id=1, source_target_pairs={{0,8},{1,9},{2,10},{3,11},{4,12},{5,13},{6,14},{7,15},{8,0},{9,1},... | collective-permute-start | bytes 786440 | tf_op jit(solution)/shard_map/ppermute | solution.py:33
  148.5 6.5 %copy-start.20 = (bf16[8,2,128,128]{3,2,1,0:T(8,128)(2,1)}, bf16[8,2,128,128]{3,2,1,0:T(8,128)(2,1)S(1)}, u32[]{:S(2)}) copy-start(bf16[8,2,128,128]{3,2,1,0:T(8,128)(2,1)S(1)} %collective-permute-done.18.refs_5_) | copy-start | bytes 1572868
  148.5 6.5 %copy-start.22 = (bf16[8,2,128,128]{3,2,1,0:T(8,128)(2,1)}, bf16[8,2,128,128]{3,2,1,0:T(8,128)(2,1)S(1)}, u32[]{:S(2)}) copy-start(bf16[8,2,128,128]{3,2,1,0:T(8,128)(2,1)S(1)} %collective-permute-done.19.refs_6_) | copy-start | bytes 1572868
  148.5 6.5 %copy-start.24 = (bf16[8,2,128,128]{3,2,1,0:T(8,128)(2,1)}, bf16[8,2,128,128]{3,2,1,0:T(8,128)(2,1)S(1)}, u32[]{:S(2)}) copy-start(bf16[8,2,128,128]{3,2,1,0:T(8,128)(2,1)S(1)} %collective-permute-done.20.refs_7_) | copy-start | bytes 1572868
  148.5 1.2 copy-start.14
  149.7 8.5 %copy-start.15 = (bf16[512,256]{1,0:T(8,128)(2,1)S(1)}, bf16[512,256]{1,0:T(8,128)(2,1)}, u32[]{:S(2)}) copy-start(bf16[512,256]{1,0:T(8,128)(2,1)} %copy-done.13) | copy-start | bytes 786436
  155.1 34.8 %collective-permute-start.21 = (bf16[128,4096]{1,0:T(8,128)(2,1)}, bf16[128,4096]{1,0:T(8,128)(2,1)S(1)}, u32[]{:S(2)}, u32[]{:S(2)}) collective-permute-start(bf16[128,4096]{1,0:T(8,128)(2,1)} %get-tuple-element.49.refs_8_.up), channel_id=1, source_target_pairs={{0,1},{1,2},{2,3},{3,0},{4,5},{5,6},{6,7},{7,4},{8,9},{9,10},{10,1... | collective-permute-start | bytes 3145736 | tf_op jit(solution)/shard_map/ppermute | solution.py:33
  156.2 33.7 %collective-permute-start.22 = (bf16[128,4096]{1,0:T(8,128)(2,1)}, bf16[128,4096]{1,0:T(8,128)(2,1)S(1)}, u32[]{:S(2)}, u32[]{:S(2)}) collective-permute-start(bf16[128,4096]{1,0:T(8,128)(2,1)} %get-tuple-element.53.down), channel_id=1, source_target_pairs={{0,3},{1,0},{2,1},{3,2},{4,7},{5,4},{6,5},{7,6},{8,11},{9,8},{10,9... | collective-permute-start | bytes 3145736 | tf_op jit(solution)/shard_map/ppermute | solution.py:33
  158.2 1.1 copy-start.21
  159.3 1.1 copy-start.23
  160.3 1.1 copy-start.25
  165.9 1.3 copy-start.2
  171.4 1.0 copy-start.8
  172.4 1.0 copy-start.10
  179.4 24.3 %copy-start.1 = (bf16[128,4096]{1,0:T(8,128)(2,1)S(1)}, bf16[128,4096]{1,0:T(8,128)(2,1)}, u32[]{:S(2)}) copy-start(bf16[128,4096]{1,0:T(8,128)(2,1)} %copy-done) | copy-start | bytes 3145732
  179.4 24.3 %copy-start.3 = (f32[128,4096]{1,0:T(8,128)S(1)}, f32[128,4096]{1,0:T(8,128)}, u32[]{:S(2)}) copy-start(f32[128,4096]{1,0:T(8,128)} %copy-done.2) | copy-start | bytes 6291460
  179.4 6.1 %collective-permute-start.24 = (bf16[128,512]{1,0:T(8,128)(2,1)S(1)}, bf16[128,512]{1,0:T(8,128)(2,1)S(1)}, u32[]{:S(2)}, u32[]{:S(2)}) collective-permute-start(bf16[128,512]{1,0:T(8,128)(2,1)S(1)} %get-tuple-element.55), channel_id=1, source_target_pairs={{0,3},{1,0},{2,1},{3,2},{4,7},{5,4},{6,5},{7,6},{8,11},{9,8},{10,9... | collective-permute-start | bytes 393224 | tf_op jit(solution)/shard_map/ppermute | solution.py:33
  182.1 6.6 %collective-permute-start.25 = (bf16[128,512]{1,0:T(8,128)(2,1)S(1)}, bf16[128,512]{1,0:T(8,128)(2,1)S(1)}, u32[]{:S(2)}, u32[]{:S(2)}) collective-permute-start(bf16[128,512]{1,0:T(8,128)(2,1)S(1)} %get-tuple-element.56), channel_id=1, source_target_pairs={{0,1},{1,2},{2,3},{3,0},{4,5},{5,6},{6,7},{7,4},{8,9},{9,10},{10,1... | collective-permute-start | bytes 393224 | tf_op jit(solution)/shard_map/ppermute | solution.py:33
  182.1 7.7 %collective-permute-start.26 = (bf16[128,512]{1,0:T(8,128)(2,1)S(1)}, bf16[128,512]{1,0:T(8,128)(2,1)S(1)}, u32[]{:S(2)}, u32[]{:S(2)}) collective-permute-start(bf16[128,512]{1,0:T(8,128)(2,1)S(1)} %get-tuple-element.57), channel_id=1, source_target_pairs={{0,2},{1,3},{2,0},{3,1},{4,6},{5,7},{6,4},{7,5},{8,10},{9,11},{10,... | collective-permute-start | bytes 393224 | tf_op jit(solution)/shard_map/ppermute | solution.py:33
  190.4 13.3 %collective-permute-start.27 = (bf16[64,4096]{1,0:T(8,128)(2,1)S(1)}, bf16[64,4096]{1,0:T(8,128)(2,1)S(1)}, u32[]{:S(2)}, u32[]{:S(2)}) collective-permute-start(bf16[64,4096]{1,0:T(8,128)(2,1)S(1)} %get-tuple-element.58), channel_id=1, source_target_pairs={{0,1},{1,2},{2,3},{3,0},{4,5},{5,6},{6,7},{7,4},{8,9},{9,10},{10,1... | collective-permute-start | bytes 1572872 | tf_op jit(solution)/shard_map/ppermute | solution.py:33
  190.7 29.4 %copy-start.11 = (bf16[512,512]{1,0:T(8,128)(2,1)S(1)}, bf16[512,512]{1,0:T(8,128)(2,1)}, u32[]{:S(2)}) copy-start(bf16[512,512]{1,0:T(8,128)(2,1)} %refs_2_.1) | copy-start | bytes 1572868
  190.7 13.0 %collective-permute-start.28 = (bf16[64,4096]{1,0:T(8,128)(2,1)S(1)}, bf16[64,4096]{1,0:T(8,128)(2,1)S(1)}, u32[]{:S(2)}, u32[]{:S(2)}) collective-permute-start(bf16[64,4096]{1,0:T(8,128)(2,1)S(1)} %get-tuple-element.59), channel_id=1, source_target_pairs={{0,3},{1,0},{2,1},{3,2},{4,7},{5,4},{6,5},{7,6},{8,11},{9,8},{10,9... | collective-permute-start | bytes 1572872 | tf_op jit(solution)/shard_map/ppermute | solution.py:33
  193.2 7.8 %collective-permute-start.30 = (bf16[128,512]{1,0:T(8,128)(2,1)S(1)}, bf16[128,512]{1,0:T(8,128)(2,1)S(1)}, u32[]{:S(2)}, u32[]{:S(2)}) collective-permute-start(bf16[128,512]{1,0:T(8,128)(2,1)S(1)} %add_convert_fusion._.refs_0_), channel_id=1, source_target_pairs={{0,128},{1,129},{2,130},{3,131},{4,132},{5,133},{6,134},{7,135},{8... | collective-permute-start | bytes 393224 | tf_op jit(solution)/shard_map/ppermute | solution.py:33
  201.0 11.7 %collective-permute-start.31 = (bf16[128,512]{1,0:T(8,128)(2,1)S(1)}, bf16[128,512]{1,0:T(8,128)(2,1)S(1)}, u32[]{:S(2)}, u32[]{:S(2)}) collective-permute-start(bf16[128,512]{1,0:T(8,128)(2,1)S(1)} %collective-permute-done.30), channel_id=1, source_target_pairs={{0,1},{1,2},{2,3},{3,0},{4,5},{5,6},{6,7},{7,4},{8,9},{9,10},{10,1... | collective-permute-start | bytes 393224 | tf_op jit(solution)/shard_map/ppermute | solution.py:33
  201.0 11.8 %collective-permute-start.32 = (bf16[128,512]{1,0:T(8,128)(2,1)S(1)}, bf16[128,512]{1,0:T(8,128)(2,1)S(1)}, u32[]{:S(2)}, u32[]{:S(2)}) collective-permute-start(bf16[128,512]{1,0:T(8,128)(2,1)S(1)} %collective-permute-done.30), channel_id=1, source_target_pairs={{0,3},{1,0},{2,1},{3,2},{4,7},{5,4},{6,5},{7,6},{8,11},{9,8},{10,9... | collective-permute-start | bytes 393224 | tf_op jit(solution)/shard_map/ppermute | solution.py:33
  203.7 16.4 %copy-start.4 = (bf16[512,1536]{1,0:T(8,128)(2,1)S(1)}, bf16[512,1536]{1,0:T(8,128)(2,1)}, u32[]{:S(2)}) copy-start(bf16[512,1536]{1,0:T(8,128)(2,1)} %refs_1_.1) | copy-start | bytes 4718596
  204.9 25.7 %collective-permute-start.29 = (bf16[128,4096]{1,0:T(8,128)(2,1)S(1)}, bf16[128,4096]{1,0:T(8,128)(2,1)S(1)}, u32[]{:S(2)}, u32[]{:S(2)}) collective-permute-start(bf16[128,4096]{1,0:T(8,128)(2,1)S(1)} %shard_map.105), channel_id=1, source_target_pairs={{0,0},{1,1},{2,2},{3,3},{4,8},{5,9},{6,10},{7,11},{8,4},{9,5},{10,... | collective-permute-start | bytes 3145736 | tf_op jit(solution)/shard_map/ppermute | solution.py:33
  212.7 5.4 %collective-permute-start.33 = (bf16[128,512]{1,0:T(8,128)(2,1)S(1)}, bf16[128,512]{1,0:T(8,128)(2,1)S(1)}, u32[]{:S(2)}, u32[]{:S(2)}) collective-permute-start(bf16[128,512]{1,0:T(8,128)(2,1)S(1)} %collective-permute-done.30), channel_id=1, source_target_pairs={{0,2},{1,3},{2,0},{3,1},{4,6},{5,7},{6,4},{7,5},{8,10},{9,11},{10,... | collective-permute-start | bytes 393224 | tf_op jit(solution)/shard_map/ppermute | solution.py:33
  218.1 2.0 collective-permute-start.34
  224.3 6.3 %collective-permute-start.35 = (bf16[128,512]{1,0:T(8,128)(2,1)S(1)}, bf16[128,512]{1,0:T(8,128)(2,1)S(1)}, u32[]{:S(2)}, u32[]{:S(2)}) collective-permute-start(bf16[128,512]{1,0:T(8,128)(2,1)S(1)} %shard_map.106), channel_id=1, source_target_pairs={{0,0},{1,1},{2,2},{3,3},{4,8},{5,9},{6,10},{7,11},{8,4},{9,5},{10,... | collective-permute-start | bytes 393224 | tf_op jit(solution)/shard_map/ppermute | solution.py:33
  (3 other events, 2.3 us)
Sparse Core Ops, SparseCore 0:
  19.8 105.2 all-gather.2
  126.9 44.4 all-gather.4

commit v5 on v4

--- a/solution.py
+++ b/solution.py
@@ -74,6 +74,15 @@
     return whole.reshape((8,) + block.shape)
 
 
+def gathered_x(block, x, axis):
+    whole = jnp.zeros(block.shape[:axis] + (4,) + block.shape[axis:], block.dtype)
+    for k, part in [(0, block)] + [(k, moved(block, along_x(k))) for k in DISTANCES]:
+        at = [0] * whole.ndim
+        at[axis] = (x - k) % 4
+        whole = lax.dynamic_update_slice(whole, jnp.expand_dims(part, axis), at)
+    return whole
+
+
 def layer_norm(rows_in, norm_gain, norm_bias):
     values = rows_in.astype(jnp.float32)
     center = jnp.mean(values, axis=-1, keepdims=True)
@@ -146,7 +155,7 @@
 
 
 def attention_kernel(*refs):
-    *pieces, weight, own, other, held, held_weight, total, projected, sems = refs
+    *pieces, weight, _, own, other, held, held_weight, total, projected, sems = refs
     depth = held.shape[1] // PARTS
     block = weight.shape[3]
     copies = []
@@ -206,7 +215,7 @@
                 )
 
 
-def attention(pieces, weight):
+def attention(pieces, weight, earlier):
     count = sum(piece.shape[0] for piece in pieces)
     depth = pieces[0].shape[1]
     block = weight.shape[3]
@@ -218,7 +227,7 @@
         60,
         flops=2 * count * depth * columns,
         moved_bytes=2 * depth * (count + columns),
-        in_specs=[pl.BlockSpec(memory_space=pltpu.HBM)] * (len(pieces) + 1),
+        in_specs=[pl.BlockSpec(memory_space=pltpu.HBM)] * (len(pieces) + 2),
         out_specs=(pl.BlockSpec(memory_space=pltpu.VMEM),) * 2,
         scratch_shapes=[
             pltpu.VMEM((count, depth), jnp.bfloat16),
@@ -227,19 +236,19 @@
             pltpu.VMEM((count, columns), jnp.bfloat16),
             pltpu.SemaphoreType.DMA((PARTS, len(pieces) + 6)),
         ],
-    )(*pieces, weight)
-
-
-def place_weights(matrix, place, parts, others):
-    planes, _, block, wide = parts[0].shape
-    for i, side in enumerate((parts, others)):
-        for k, part in zip((0,) + DISTANCES, side):
-            for plane in range(planes):
-                at = (plane * 4 + (place[0] - k + 4) % 4) * wide
-                columns = pl.ds(pl.multiple_of(at, wide), wide)
-                for half in range(2):
-                    first = (2 * i + half) * block
-                    matrix[first : first + block, columns] = part[plane, half]
+    )(*pieces, weight, earlier)
+
+
+def out_matrix(weight, other_weight):
+    planes, xs, halves = weight.shape[:3]
+    return jnp.concatenate(
+        [
+            jnp.concatenate([w[p, x, h] for p in range(planes) for x in range(xs)], axis=1)
+            for w in (weight, other_weight)
+            for h in range(halves)
+        ],
+        axis=0,
+    )
 
 
 def match_matrix(weight):
@@ -248,44 +257,41 @@
     return jnp.concatenate(blocks, axis=0)
 
 
-def terms_kernel(skipped, picked, place, mine, theirs, *refs):
-    parts, others, outs, matrix = refs[:4], refs[4:8], refs[8 + skipped : -1], refs[-1]
-    place_weights(matrix, place, parts, others)
+def terms_kernel(skipped, picked, mine, theirs, weight, other_weight, *refs):
+    outs = refs[skipped:]
     both = [
         jnp.concatenate([mine[at : at + many, :], theirs[at : at + many, :]], axis=1)
         for spans, _ in picked
         for at, many in spans
     ]
-    products = dot(jnp.concatenate(both, axis=0), matrix[...])
+    products = dot(jnp.concatenate(both, axis=0), out_matrix(weight, other_weight))
     at = 0
     for out in outs:
         out[...] = products[at : at + out.shape[0]].astype(out.dtype)
         at += out.shape[0]
 
 
-def terms(x, mine, theirs, parts, picked, earlier=()):
+def terms(mine, theirs, weight, other_weight, picked, earlier=()):
     counts = [sum(many for _, many in spans) for spans, _ in picked]
     earlier = list(earlier)
-    planes, halves, block, wide = parts[0].shape
-    columns = 2 * 4 * wide
+    planes, xs, _, _, wide = weight.shape
+    columns = 2 * xs * wide
     whole = pl.BlockSpec(mine.shape, lambda i: (0, 0))
-    part = pl.BlockSpec((2, halves, block, wide), lambda i: (i, 0, 0, 0))
+    part = pl.BlockSpec((2,) + weight.shape[1:], lambda i: (i, 0, 0, 0, 0))
     return local(
         functools.partial(terms_kernel, len(earlier), picked),
         tuple(
-            jax.ShapeDtypeStruct((many, planes * 4 * wide), kind)
+            jax.ShapeDtypeStruct((many, planes * xs * wide), kind)
             for many, (_, kind) in zip(counts, picked)
         ),
         24,
         flops=2_000_000_000,
         moved_bytes=8_000_000,
         grid=(planes // 2,),
-        in_specs=[pl.BlockSpec(memory_space=pltpu.SMEM), whole, whole]
-        + [part] * 8
+        in_specs=[whole, whole, part, part]
         + [pl.BlockSpec(memory_space=pltpu.HBM)] * len(earlier),
         out_specs=tuple(pl.BlockSpec((many, columns), lambda i: (0, i)) for many in counts),
-        scratch_shapes=[pltpu.VMEM((4 * block, columns), jnp.bfloat16)],
-    )(x.astype(jnp.int32).reshape(1), mine, theirs, *parts, *earlier)
+    )(mine, theirs, weight, other_weight, *earlier)
 
 
 def descriptor_kernel(tokens, own, down, down_high, up_low, up, match_weight, *rest):
@@ -439,10 +445,19 @@
     packed = qkv_weight.reshape(block, -1, wide).transpose(1, 0, 2).reshape(-1, wide)
     packed = swapped_roles(jnp.concatenate([packed, out_weight], axis=0))
     split = packed.shape[0] - out_weight.shape[0]
-    weights = lax.all_gather(packed[:split], ("z", "xh", "xl"), axis=0, tiled=True)
+    weights = lax.all_gather(gathered_x(packed[:split], x, 0), "z", axis=0, tiled=True)
     weights = weights.reshape(8, 4, split // block, block, wide)
 
-    match_weight = after(match_weight, packed)
+    tokens = swapped_roles(tokens)
+    normed = layer_norm(tokens, norm_gain, norm_bias)
+    out_own = gathered_x(gathered_z(packed[split:], z), x, 1)
+    out_other = moved(out_own, other_core)
+    pieces = [normed] + [moved(normed, along_y(k)) for k in DISTANCES]
+    pieces += [moved(piece, other_core) for piece in pieces]
+    pieces = together(*pieces, flops=WAIT)
+    mine, theirs = attention(pieces, weights, out_own)
+
+    match_weight = after(match_weight, normed)
     other_half = moved(match_weight, lambda p: {"xh": 1 - p["xh"], "xl": 1 - p["xl"]})
     match_pair = jnp.where(
         lax.axis_index("xh") == 0,
@@ -452,22 +467,8 @@
     match_all = lax.all_gather(match_pair, ("z", "core"), axis=0, tiled=True)
     match_all = match_all.reshape(8, 2, 2, match_weight.shape[0], width)
 
-    tokens = swapped_roles(tokens)
-    normed = layer_norm(tokens, norm_gain, norm_bias)
-    out_z = gathered_z(packed[split:], z)
-    pieces = [normed] + [moved(normed, along_y(k)) for k in DISTANCES]
-    *received, out_z = together(*pieces[1:], out_z)
-    pieces = pieces[:1] + received
-    pieces += [moved(piece, other_core) for piece in pieces]
-    out_z = out_z.reshape(8, 2, block, wide)
-    pieces = together(*pieces, flops=WAIT)
-    parts = [out_z] + [moved(out_z, along_x(k)) for k in DISTANCES]
-    others = [moved(out_z, other_core)]
-    mine, theirs = attention(pieces, weights)
-    mine, *parts[1:] = together(mine, *parts[1:])
-    others += [moved(part, other_core) for part in parts[1:]]
-
-    both = (x, mine, moved(theirs, other_core), parts + others)
+    shape = (8, 4, 2, block, wide)
+    both = (mine, moved(theirs, other_core), out_own.reshape(shape), out_other.reshape(shape))
     up, down = terms(
         *both,
         [([(2 * rows + mid, rows)], bf16), ([(3 * rows + mid, mid), (rows, mid)], bf16)],

time: 240 us -> 248 us (1.033)
  starting transfers between devices: 58.7 us -> 90.9 us
  waiting for transfers between devices: 102 us -> 80.5 us
    ppermute x36, starting transfers between devices: 58.6 us -> 90.8 us  [moved(): return lax.ppermute(block, AXES, route)]
    all_gather x1, waiting for transfers between devices: 24.7 us -> 0.01 us  [per_device(): lax.all_gather(gathered_x(packed[:split], x, 0), 'z', axis=0, tiled=True)]
    unnamed x65 -> x45, local copies, waits for them, and re-layouts: 20.7 us -> 14.8 us
    ppermute x36, waiting for transfers between devices: 74.7 us -> 80.4 us  [moved(): return lax.ppermute(block, AXES, route)]
    dynamic_update_slice x0 -> x8, local copies, waits for them, and re-layouts: none -> 3.79 us  [gathered_x(): whole = lax.dynamic_update_slice(whole, jnp.expand_dims(part, axis), at)]
  transfers between devices with their start and end apart: 38 -> 38, of which waited for: 20 -> 19; matrix products, arithmetic and copies ran while one was open for 1% -> 3% of each run, Pallas kernels for 16% -> 15%
where the time goes in v5:
time: 248 us; the launch traced here: 247 us
  starting transfers between devices  90.9 us (37%)
  waiting for transfers between devices  80.5 us (32%)
  Pallas kernels  37.3 us (15%)
  local copies, waits for them, and re-layouts  20.8 us (8%)
  between operations  14.5 us (6%)
  other arithmetic  3.14 us (1%)
    ppermute x36, starting transfers between devices, moved(): return lax.ppermute(block, AXES, route)  90.8 us
    ppermute x36, waiting for transfers between devices, moved(): return lax.ppermute(block, AXES, route)  80.4 us
    pallas_call x1, Pallas kernels, attention(): local(attention_kernel, (result, result), 60, flops=2 * count * depth * c...  16.6 us
    unnamed x45, local copies, waits for them, and re-layouts  14.8 us
    pallas_call x2, Pallas kernels, terms(): local(functools.partial(terms_kernel, len(earlier), picked), tuple((jax.S...  8.87 us
    pallas_call x1, Pallas kernels, descriptor_terms(): local(descriptor_kernel, (jax.ShapeDtypeStruct((rows, width), f32),) + (j...  5.95 us
  transfers between devices with their start and end apart: 38, of which 19 were waited for; matrix products, arithmetic and copies ran while one was open for 3% of the time, Pallas kernels for 15%

profile of v5, /device:TPU:1, one launch (start us, length us, event | category | flops | bytes accessed | tf_op | source)
XLA Modules:
  0.0 247.1 jit_solution(7794812192378292956)
XLA Ops:
  7.2 0.9 copy.71.refs_0_
  8.1 1.1 copy.35
  9.4 0.9 pad_maximum_fusion
  10.3 4.5 %collective-permute-start.8 = (bf16[1024,128]{1,0:T(8,128)(2,1)S(1)}, bf16[1024,128]{1,0:T(8,128)(2,1)S(1)}, u32[]{:S(2)}, u32[]{:S(2)}) collective-permute-start(bf16[1024,128]{1,0:T(8,128)(2,1)S(1)} %pad_maximum_fusion), channel_id=1, source_target_pairs={{0,0},{1,1},{2,2},{3,3},{4,8},{5,9},{6,10},{7,11},{8,4},{9,5},{10,... | collective-permute-start | bytes 786440 | tf_op jit(solution)/shard_map/ppermute | solution.py:33
  14.9 4.0 %collective-permute-done.8 = bf16[1024,128]{1,0:T(8,128)(2,1)S(1)} collective-permute-done((bf16[1024,128]{1,0:T(8,128)(2,1)S(1)}, bf16[1024,128]{1,0:T(8,128)(2,1)S(1)}, u32[]{:S(2)}, u32[]{:S(2)}) %collective-permute-start.8) | collective-permute-done | bytes 262176 | tf_op jit(solution)/shard_map/ppermute | solution.py:33
  19.0 2.7 %collective-permute-start.10 = (bf16[768,128]{1,0:T(8,128)(2,1)S(1)}, bf16[768,128]{1,0:T(8,128)(2,1)S(1)}, u32[]{:S(2)}, u32[]{:S(2)}) collective-permute-start(bf16[768,128]{1,0:T(8,128)(2,1)S(1)} %slice.8), channel_id=1, source_target_pairs={{0,20},{1,21},{2,22},{3,23},{4,0},{5,1},{6,2},{7,3},{8,28},{9,29},... | collective-permute-start | bytes 589832 | tf_op jit(solution)/shard_map/ppermute | solution.py:33
  21.7 1.5 collective-permute-start.11
  23.3 3.9 %collective-permute-done.9 = bf16[768,128]{1,0:T(8,128)(2,1)S(1)} collective-permute-done((bf16[768,128]{1,0:T(8,128)(2,1)S(1)}, bf16[768,128]{1,0:T(8,128)(2,1)S(1)}, u32[]{:S(2)}, u32[]{:S(2)}) %collective-permute-start.9) | collective-permute-done | bytes 196640 | tf_op jit(solution)/shard_map/ppermute | solution.py:33
  27.3 2.8 %collective-permute-done.11 = bf16[768,128]{1,0:T(8,128)(2,1)S(1)} collective-permute-done((bf16[768,128]{1,0:T(8,128)(2,1)S(1)}, bf16[768,128]{1,0:T(8,128)(2,1)S(1)}, u32[]{:S(2)}, u32[]{:S(2)}) %collective-permute-start.11) | collective-permute-done | bytes 196640 | tf_op jit(solution)/shard_map/ppermute | solution.py:33
  31.1 4.7 %collective-permute-start = (bf16[128,4096]{1,0:T(8,128)(2,1)S(1)}, bf16[128,4096]{1,0:T(8,128)(2,1)S(1)}, u32[]{:S(2)}, u32[]{:S(2)}) collective-permute-start(bf16[128,4096]{1,0:T(8,128)(2,1)S(1)} %copy-done.18), channel_id=1, source_target_pairs={{0,0},{1,1},{2,2},{3,3},{4,8},{5,9},{6,10},{7,11},{8,4},{9,5},{10,... | collective-permute-start | bytes 3145736 | tf_op jit(solution)/shard_map/ppermute | solution.py:33
  35.8 12.5 %collective-permute-done.tokens = bf16[128,4096]{1,0:T(8,128)(2,1)S(1)} collective-permute-done((bf16[128,4096]{1,0:T(8,128)(2,1)S(1)}, bf16[128,4096]{1,0:T(8,128)(2,1)S(1)}, u32[]{:S(2)}, u32[]{:S(2)}) %collective-permute-start) | collective-permute-done | bytes 1048608 | tf_op jit(solution)/shard_map/ppermute | solution.py:33
  49.5 6.0 %collective-permute-done.23 = bf16[128,512]{1,0:T(8,128)(2,1)S(1)} collective-permute-done((bf16[128,512]{1,0:T(8,128)(2,1)S(1)}, bf16[128,512]{1,0:T(8,128)(2,1)S(1)}, u32[]{:S(2)}, u32[]{:S(2)}) %collective-permute-start.23) | collective-permute-done | bytes 131104 | tf_op jit(solution)/shard_map/ppermute | solution.py:33
  56.3 7.9 %collective-permute-start.12 = (bf16[256,128]{1,0:T(8,128)(2,1)S(1)}, bf16[256,128]{1,0:T(8,128)(2,1)S(1)}, u32[]{:S(2)}, u32[]{:S(2)}) collective-permute-start(bf16[256,128]{1,0:T(8,128)(2,1)S(1)} %get-tuple-element.45), channel_id=1, source_target_pairs={{0,128},{1,129},{2,130},{3,131},{4,132},{5,133},{6,134},{7,135},{8... | collective-permute-start | bytes 196616 | tf_op jit(solution)/shard_map/ppermute | solution.py:33
  64.2 3.7 %collective-permute-done.12 = bf16[256,128]{1,0:T(8,128)(2,1)S(1)} collective-permute-done((bf16[256,128]{1,0:T(8,128)(2,1)S(1)}, bf16[256,128]{1,0:T(8,128)(2,1)S(1)}, u32[]{:S(2)}, u32[]{:S(2)}) %collective-permute-start.12) | collective-permute-done | bytes 65568 | tf_op jit(solution)/shard_map/ppermute | solution.py:33
  68.8 4.4 %collective-permute-start.14 = (bf16[2,256,128]{2,1,0:T(8,128)(2,1)S(1)}, bf16[2,256,128]{2,1,0:T(8,128)(2,1)S(1)}, u32[]{:S(2)}, u32[]{:S(2)}) collective-permute-start(bf16[2,256,128]{2,1,0:T(8,128)(2,1)S(1)} %shard_map.96), channel_id=1, source_target_pairs={{0,224},{1,225},{2,226},{3,227},{4,228},{5,229},{6,230},{7,231},{8... | collective-permute-start | bytes 393224 | tf_op jit(solution)/shard_map/ppermute | solution.py:33
  73.3 6.3 %collective-permute-done.13 = bf16[2,256,128]{2,1,0:T(8,128)(2,1)S(1)} collective-permute-done((bf16[2,256,128]{2,1,0:T(8,128)(2,1)S(1)}, bf16[2,256,128]{2,1,0:T(8,128)(2,1)S(1)}, u32[]{:S(2)}, u32[]{:S(2)}) %collective-permute-start.13) | collective-permute-done | bytes 131104 | tf_op jit(solution)/shard_map/ppermute | solution.py:33
  79.7 1.4 collective-permute-start.1
  81.1 1.5 collective-permute-start.2
  82.6 1.6 collective-permute-start.3
  84.2 2.0 collective-permute-done.15
  86.3 2.7 %collective-permute-start.17 = (bf16[8,256,128]{2,1,0:T(8,128)(2,1)S(1)}, bf16[8,256,128]{2,1,0:T(8,128)(2,1)S(1)}, u32[]{:S(2)}, u32[]{:S(2)}) collective-permute-start(bf16[8,256,128]{2,1,0:T(8,128)(2,1)S(1)} %bitcast.56), channel_id=1, source_target_pairs={{0,20},{1,21},{2,22},{3,23},{4,0},{5,1},{6,2},{7,3},{8,28},{9,29},... | collective-permute-start | bytes 1572872 | tf_op jit(solution)/shard_map/ppermute | solution.py:33
  89.0 10.2 %collective-permute-done.16 = bf16[8,256,128]{2,1,0:T(8,128)(2,1)S(1)} collective-permute-done((bf16[8,256,128]{2,1,0:T(8,128)(2,1)S(1)}, bf16[8,256,128]{2,1,0:T(8,128)(2,1)S(1)}, u32[]{:S(2)}, u32[]{:S(2)}) %collective-permute-start.16) | collective-permute-done | bytes 524320 | tf_op jit(solution)/shard_map/ppermute | solution.py:33
  99.9 1.8 broadcast_in_dim.51
  101.7 0.9 constant_dynamic-update-slice_fusion.4
  102.6 0.9 bitcast_dynamic-update-slice_fusion.1
  103.5 8.9 %collective-permute-start.4 = (bf16[128,4096]{1,0:T(8,128)(2,1)S(1)}, bf16[128,4096]{1,0:T(8,128)(2,1)S(1)}, u32[]{:S(2)}, u32[]{:S(2)}) collective-permute-start(bf16[128,4096]{1,0:T(8,128)(2,1)S(1)} %fusion.5.refs_0_.refs_1_), channel_id=1, source_target_pairs={{0,8},{1,9},{2,10},{3,11},{4,12},{5,13},{6,14},{7,15},{8,0},{9,1},... | collective-permute-start | bytes 3145736 | tf_op jit(solution)/shard_map/ppermute | solution.py:33
  112.4 16.1 %collective-permute-start.6 = (bf16[128,4096]{1,0:T(8,128)(2,1)S(1)}, bf16[128,4096]{1,0:T(8,128)(2,1)S(1)}, u32[]{:S(2)}, u32[]{:S(2)}) collective-permute-start(bf16[128,4096]{1,0:T(8,128)(2,1)S(1)} %collective-permute-done.2.refs_2_), channel_id=1, source_target_pairs={{0,8},{1,9},{2,10},{3,11},{4,12},{5,13},{6,14},{7,15},{8,0},{9,1},... | collective-permute-start | bytes 3145736 | tf_op jit(solution)/shard_map/ppermute | solution.py:33
  128.5 1.8 collective-permute-start.7
  130.3 0.9 bitcast_dynamic-update-slice_fusion
  131.2 0.9 bitcast_dynamic-update-slice_fusion.2.refs_9_
  132.6 1.0 copy-done.2
  133.7 1.0 copy-done.7
  134.7 1.0 copy-done.8
  135.7 1.0 copy-done.9
  136.7 1.0 copy-done.10
  137.7 1.0 copy-done.11
  138.6 1.0 copy-done.12
  139.6 1.0 copy-done.13
  140.6 16.6 %shard_map.97 = (bf16[512,256]{1,0:T(8,128)(2,1)}, bf16[512,256]{1,0:T(8,128)(2,1)}) custom-call(bf16[128,4096]{1,0:T(8,128)(2,1)} %copy-done.2, bf16[128,4096]{1,0:T(8,128)(2,1)} %copy-done.7, bf16[128,4096]{1,0:T(8,128)(2,1)} %copy-done.8, bf16[128,4096]{1,0:T(8,128)(2,1)} %copy-done.9, bf16[128,4096]{1,0:T(8,128)(2,1)} %copy-done.10, ...), custom_call_target="tpu_custom_call" | custom-call | flops 6442450944 | bytes 14680064 | tf_op jit(solution)/shard_map/pallas_call | solution.py:224
  157.7 1.4 collective-permute-done.19.theirs
  159.1 0.9 copy-done.14
  160.0 4.9 %shard_map.98 = (bf16[128,4096]{1,0:T(8,128)(2,1)}, bf16[128,4096]{1,0:T(8,128)(2,1)}) custom-call(bf16[512,256]{1,0:T(8,128)(2,1)S(1)} %copy-done.14, bf16[512,256]{1,0:T(8,128)(2,1)S(1)} %collective-permute-done.19.theirs, bf16[8,4,2,128,128]{4,3,2,1,0:T(8,128)(2,1)} %bitcast.25.weight, bf16[8,4,2,128,128]{4,3,2,1,0:T(8,128)(2,1)} %bitcast.26.other_weight), custom_call_target="tpu_custom_call" | custom-call | flops 2000000000 | bytes 8000000 | tf_op jit(solution)/shard_map/pallas_call | solution.py:281
  165.7 2.6 %collective-permute-start.22 = (bf16[128,4096]{1,0:T(8,128)(2,1)}, bf16[128,4096]{1,0:T(8,128)(2,1)S(1)}, u32[]{:S(2)}, u32[]{:S(2)}) collective-permute-start(bf16[128,4096]{1,0:T(8,128)(2,1)} %get-tuple-element.37.down), channel_id=1, source_target_pairs={{0,3},{1,0},{2,1},{3,2},{4,7},{5,4},{6,5},{7,6},{8,11},{9,8},{10,9... | collective-permute-start | bytes 3145736 | tf_op jit(solution)/shard_map/ppermute | solution.py:33
  168.3 3.9 %shard_map.99 = (f32[128,4096]{1,0:T(8,128)S(1)}, bf16[64,4096]{1,0:T(8,128)(2,1)S(1)}, bf16[64,4096]{1,0:T(8,128)(2,1)S(1)}) custom-call(bf16[512,256]{1,0:T(8,128)(2,1)S(1)} %copy-done.14, bf16[512,256]{1,0:T(8,128)(2,1)S(1)} %collective-permute-done.19.theirs, bf16[8,4,2,128,128]{4,3,2,1,0:T(8,128)(2,1)} %bitcast.25.weight, ...), custom_call_target="tpu_custom_call" | custom-call | flops 2000000000 | bytes 8000000 | tf_op jit(solution)/shard_map/pallas_call | solution.py:281
  172.2 1.3 copy-done.3
  173.6 6.0 %shard_map.101 = (f32[128,512]{1,0:T(8,128)S(1)}, bf16[128,512]{1,0:T(8,128)(2,1)S(1)}, bf16[128,512]{1,0:T(8,128)(2,1)S(1)}, bf16[128,512]{1,0:T(8,128)(2,1)S(1)}) custom-call(bf16[128,4096]{1,0:T(8,128)(2,1)} %copy-done, f32[128,4096]{1,0:T(8,128)} %copy-done.3, bf16[128,4096]{1,0:T(8,128)(2,1)} %get-tuple-element.37.down, ...), custom_call_target="tpu_custom_call" | custom-call | flops 4000000000 | bytes 12000000 | tf_op jit(solution)/shard_map/pallas_call | solution.py:331
  179.6 3.7 %collective-permute-start.26 = (bf16[128,512]{1,0:T(8,128)(2,1)S(1)}, bf16[128,512]{1,0:T(8,128)(2,1)S(1)}, u32[]{:S(2)}, u32[]{:S(2)}) collective-permute-start(bf16[128,512]{1,0:T(8,128)(2,1)S(1)} %get-tuple-element.41), channel_id=1, source_target_pairs={{0,2},{1,3},{2,0},{3,1},{4,6},{5,7},{6,4},{7,5},{8,10},{9,11},{10,... | collective-permute-start | bytes 393224 | tf_op jit(solution)/shard_map/ppermute | solution.py:33
  183.3 2.7 %collective-permute-start.24 = (bf16[128,512]{1,0:T(8,128)(2,1)S(1)}, bf16[128,512]{1,0:T(8,128)(2,1)S(1)}, u32[]{:S(2)}, u32[]{:S(2)}) collective-permute-start(bf16[128,512]{1,0:T(8,128)(2,1)S(1)} %get-tuple-element.39), channel_id=1, source_target_pairs={{0,3},{1,0},{2,1},{3,2},{4,7},{5,4},{6,5},{7,6},{8,11},{9,8},{10,9... | collective-permute-start | bytes 393224 | tf_op jit(solution)/shard_map/ppermute | solution.py:33
  186.0 10.6 %collective-permute-done.26 = bf16[128,512]{1,0:T(8,128)(2,1)S(1)} collective-permute-done((bf16[128,512]{1,0:T(8,128)(2,1)S(1)}, bf16[128,512]{1,0:T(8,128)(2,1)S(1)}, u32[]{:S(2)}, u32[]{:S(2)}) %collective-permute-start.26) | collective-permute-done | bytes 131104 | tf_op jit(solution)/shard_map/ppermute | solution.py:33
  197.1 1.6 collective-permute-done.24
  199.4 1.2 collective-permute-start.27
  200.6 1.6 collective-permute-start.28
  202.2 4.3 %collective-permute-start.30 = (bf16[128,512]{1,0:T(8,128)(2,1)S(1)}, bf16[128,512]{1,0:T(8,128)(2,1)S(1)}, u32[]{:S(2)}, u32[]{:S(2)}) collective-permute-start(bf16[128,512]{1,0:T(8,128)(2,1)S(1)} %add_convert_fusion._.refs_0_), channel_id=1, source_target_pairs={{0,128},{1,129},{2,130},{3,131},{4,132},{5,133},{6,134},{7,135},{8... | collective-permute-start | bytes 393224 | tf_op jit(solution)/shard_map/ppermute | solution.py:33
  206.4 3.5 %collective-permute-done.30 = bf16[128,512]{1,0:T(8,128)(2,1)S(1)} collective-permute-done((bf16[128,512]{1,0:T(8,128)(2,1)S(1)}, bf16[128,512]{1,0:T(8,128)(2,1)S(1)}, u32[]{:S(2)}, u32[]{:S(2)}) %collective-permute-start.30) | collective-permute-done | bytes 131104 | tf_op jit(solution)/shard_map/ppermute | solution.py:33
  210.0 2.7 %collective-permute-start.32 = (bf16[128,512]{1,0:T(8,128)(2,1)S(1)}, bf16[128,512]{1,0:T(8,128)(2,1)S(1)}, u32[]{:S(2)}, u32[]{:S(2)}) collective-permute-start(bf16[128,512]{1,0:T(8,128)(2,1)S(1)} %collective-permute-done.30), channel_id=1, source_target_pairs={{0,3},{1,0},{2,1},{3,2},{4,7},{5,4},{6,5},{7,6},{8,11},{9,8},{10,9... | collective-permute-start | bytes 393224 | tf_op jit(solution)/shard_map/ppermute | solution.py:33
  212.9 1.1 shard_map.103
  214.1 4.1 %collective-permute-start.29 = (bf16[128,4096]{1,0:T(8,128)(2,1)S(1)}, bf16[128,4096]{1,0:T(8,128)(2,1)S(1)}, u32[]{:S(2)}, u32[]{:S(2)}) collective-permute-start(bf16[128,4096]{1,0:T(8,128)(2,1)S(1)} %shard_map.103), channel_id=1, source_target_pairs={{0,0},{1,1},{2,2},{3,3},{4,8},{5,9},{6,10},{7,11},{8,4},{9,5},{10,... | collective-permute-start | bytes 3145736 | tf_op jit(solution)/shard_map/ppermute | solution.py:33
  218.9 4.6 %collective-permute-done.33 = bf16[128,512]{1,0:T(8,128)(2,1)S(1)} collective-permute-done((bf16[128,512]{1,0:T(8,128)(2,1)S(1)}, bf16[128,512]{1,0:T(8,128)(2,1)S(1)}, u32[]{:S(2)}, u32[]{:S(2)}) %collective-permute-start.33) | collective-permute-done | bytes 131104 | tf_op jit(solution)/shard_map/ppermute | solution.py:33
  223.6 3.0 %collective-permute-start.34 = (bf16[512,512]{1,0:T(8,128)(2,1)S(1)}, bf16[512,512]{1,0:T(8,128)(2,1)S(1)}, u32[]{:S(2)}, u32[]{:S(2)}) collective-permute-start(bf16[512,512]{1,0:T(8,128)(2,1)S(1)} %constant_dynamic-update-slice_fusion.refs_3_), channel_id=1, source_target_pairs={{0,8},{1,9},{2,10},{3,11},{4,12},{5,13},{6,14},{7,15},{8,0},{9,1},... | collective-permute-start | bytes 1572872 | tf_op jit(solution)/shard_map/ppermute | solution.py:33
  226.6 1.5 collective-permute-done.34.refs_4_
  228.1 4.2 %shard_map.104 = bf16[128,512]{1,0:T(8,128)(2,1)S(1)} custom-call(bf16[128,512]{1,0:T(8,128)(2,1)S(1)} %add_convert_fusion._.refs_0_, bf16[512,1536]{1,0:T(8,128)(2,1)S(1)} %copy-done.5, bf16[512,512]{1,0:T(8,128)(2,1)S(1)} %copy-done.6, bf16[512,512]{1,0:T(8,128)(2,1)S(1)} %constant_dynamic-update-slice_fusion.refs_3_, ...), custom_call_target="tpu_custom_call" | custom-call | tf_op jit(solution)/shard_map/pallas_call | solution.py:422
  232.3 1.9 collective-permute-start.35
  234.2 4.4 %collective-permute-done.35 = bf16[128,512]{1,0:T(8,128)(2,1)S(1)} collective-permute-done((bf16[128,512]{1,0:T(8,128)(2,1)S(1)}, bf16[128,512]{1,0:T(8,128)(2,1)S(1)}, u32[]{:S(2)}, u32[]{:S(2)}) %collective-permute-start.35) | collective-permute-done | bytes 131104 | tf_op jit(solution)/shard_map/ppermute | solution.py:33
  238.6 1.0 copy.72
  (97 shorter events, 10.1 us)
Async XLA Ops:
  7.2 133.5 %all-gather.3.cloned.1.call-start = ((), (), s32[]{:S(2)}) async-start(), calls=%async_computation | async-start | bytes 7077888 | tf_op jit(solution)/shard_map/all_gather | solution.py:448
  9.4 21.7 %copy-start.18 = (bf16[128,4096]{1,0:T(8,128)(2,1)S(1)}, bf16[128,4096]{1,0:T(8,128)(2,1)}, u32[]{:S(2)}) copy-start(bf16[128,4096]{1,0:T(8,128)(2,1)} %param.8) | copy-start | bytes 3145732
  10.3 8.6 %collective-permute-start.8 = (bf16[1024,128]{1,0:T(8,128)(2,1)S(1)}, bf16[1024,128]{1,0:T(8,128)(2,1)S(1)}, u32[]{:S(2)}, u32[]{:S(2)}) collective-permute-start(bf16[1024,128]{1,0:T(8,128)(2,1)S(1)} %pad_maximum_fusion), channel_id=1, source_target_pairs={{0,0},{1,1},{2,2},{3,3},{4,8},{5,9},{6,10},{7,11},{8,4},{9,5},{10,... | collective-permute-start | bytes 786440 | tf_op jit(solution)/shard_map/ppermute | solution.py:33
  18.9 8.3 %collective-permute-start.9 = (bf16[768,128]{1,0:T(8,128)(2,1)S(1)}, bf16[768,128]{1,0:T(8,128)(2,1)S(1)}, u32[]{:S(2)}, u32[]{:S(2)}) collective-permute-start(bf16[768,128]{1,0:T(8,128)(2,1)S(1)} %slice.8), channel_id=1, source_target_pairs={{0,4},{1,5},{2,6},{3,7},{4,16},{5,17},{6,18},{7,19},{8,12},{9,13},... | collective-permute-start | bytes 589832 | tf_op jit(solution)/shard_map/ppermute | solution.py:33
  19.0 8.3 %collective-permute-start.10 = (bf16[768,128]{1,0:T(8,128)(2,1)S(1)}, bf16[768,128]{1,0:T(8,128)(2,1)S(1)}, u32[]{:S(2)}, u32[]{:S(2)}) collective-permute-start(bf16[768,128]{1,0:T(8,128)(2,1)S(1)} %slice.8), channel_id=1, source_target_pairs={{0,20},{1,21},{2,22},{3,23},{4,0},{5,1},{6,2},{7,3},{8,28},{9,29},... | collective-permute-start | bytes 589832 | tf_op jit(solution)/shard_map/ppermute | solution.py:33
  21.7 8.4 %collective-permute-start.11 = (bf16[768,128]{1,0:T(8,128)(2,1)S(1)}, bf16[768,128]{1,0:T(8,128)(2,1)S(1)}, u32[]{:S(2)}, u32[]{:S(2)}) collective-permute-start(bf16[768,128]{1,0:T(8,128)(2,1)S(1)} %slice.8), channel_id=1, source_target_pairs={{0,16},{1,17},{2,18},{3,19},{4,20},{5,21},{6,22},{7,23},{8,24},{9,... | collective-permute-start | bytes 589832 | tf_op jit(solution)/shard_map/ppermute | solution.py:33
  23.3 25.6 %copy-start.16 = (f32[4096]{0:T(1024)S(1)}, f32[4096]{0:T(1024)}, u32[]{:S(2)}) copy-start(f32[4096]{0:T(1024)} %param.10) | copy-start | bytes 49156
  23.3 25.6 %copy-start.17 = (f32[4096]{0:T(1024)S(1)}, f32[4096]{0:T(1024)}, u32[]{:S(2)}) copy-start(f32[4096]{0:T(1024)} %param.9) | copy-start | bytes 49156
  30.1 0.9 copy-start.15
  31.0 142.6 %all-gather.5.cloned.1.call-start = ((), (), s32[]{:S(2)}) async-start(), calls=%async_computation.1 | async-start | bytes 4456448 | tf_op jit(solution)/shard_map/all_gather | solution.py:467
  31.1 17.1 %collective-permute-start = (bf16[128,4096]{1,0:T(8,128)(2,1)S(1)}, bf16[128,4096]{1,0:T(8,128)(2,1)S(1)}, u32[]{:S(2)}, u32[]{:S(2)}) collective-permute-start(bf16[128,4096]{1,0:T(8,128)(2,1)S(1)} %copy-done.18), channel_id=1, source_target_pairs={{0,0},{1,1},{2,2},{3,3},{4,8},{5,9},{6,10},{7,11},{8,4},{9,5},{10,... | collective-permute-start | bytes 3145736 | tf_op jit(solution)/shard_map/ppermute | solution.py:33
  48.2 1.2 copy-start
  49.4 6.1 %collective-permute-start.23 = (bf16[128,512]{1,0:T(8,128)(2,1)S(1)}, bf16[128,512]{1,0:T(8,128)(2,1)S(1)}, u32[]{:S(2)}, u32[]{:S(2)}) collective-permute-start(bf16[128,512]{1,0:T(8,128)(2,1)S(1)} %shard_map.100), channel_id=1, source_target_pairs={{0,20},{1,21},{2,22},{3,23},{4,16},{5,17},{6,18},{7,19},{8,28},{9,... | collective-permute-start | bytes 393224 | tf_op jit(solution)/shard_map/ppermute | solution.py:33
  56.3 11.6 %collective-permute-start.12 = (bf16[256,128]{1,0:T(8,128)(2,1)S(1)}, bf16[256,128]{1,0:T(8,128)(2,1)S(1)}, u32[]{:S(2)}, u32[]{:S(2)}) collective-permute-start(bf16[256,128]{1,0:T(8,128)(2,1)S(1)} %get-tuple-element.45), channel_id=1, source_target_pairs={{0,128},{1,129},{2,130},{3,131},{4,132},{5,133},{6,134},{7,135},{8... | collective-permute-start | bytes 196616 | tf_op jit(solution)/shard_map/ppermute | solution.py:33
  68.0 11.6 %collective-permute-start.13 = (bf16[2,256,128]{2,1,0:T(8,128)(2,1)S(1)}, bf16[2,256,128]{2,1,0:T(8,128)(2,1)S(1)}, u32[]{:S(2)}, u32[]{:S(2)}) collective-permute-start(bf16[2,256,128]{2,1,0:T(8,128)(2,1)S(1)} %shard_map.96), channel_id=1, source_target_pairs={{0,32},{1,33},{2,34},{3,35},{4,36},{5,37},{6,38},{7,39},{8,40},{9,... | collective-permute-start | bytes 393224 | tf_op jit(solution)/shard_map/ppermute | solution.py:33
  68.8 10.9 %collective-permute-start.14 = (bf16[2,256,128]{2,1,0:T(8,128)(2,1)S(1)}, bf16[2,256,128]{2,1,0:T(8,128)(2,1)S(1)}, u32[]{:S(2)}, u32[]{:S(2)}) collective-permute-start(bf16[2,256,128]{2,1,0:T(8,128)(2,1)S(1)} %shard_map.96), channel_id=1, source_target_pairs={{0,224},{1,225},{2,226},{3,227},{4,228},{5,229},{6,230},{7,231},{8... | collective-permute-start | bytes 393224 | tf_op jit(solution)/shard_map/ppermute | solution.py:33
  73.1 13.1 %collective-permute-start.15 = (bf16[2,256,128]{2,1,0:T(8,128)(2,1)S(1)}, bf16[2,256,128]{2,1,0:T(8,128)(2,1)S(1)}, u32[]{:S(2)}, u32[]{:S(2)}) collective-permute-start(bf16[2,256,128]{2,1,0:T(8,128)(2,1)S(1)} %shard_map.96), channel_id=1, source_target_pairs={{0,64},{1,65},{2,66},{3,67},{4,68},{5,69},{6,70},{7,71},{8,72},{9,... | collective-permute-start | bytes 393224 | tf_op jit(solution)/shard_map/ppermute | solution.py:33
  79.7 32.7 %collective-permute-start.1 = (bf16[128,4096]{1,0:T(8,128)(2,1)S(1)}, bf16[128,4096]{1,0:T(8,128)(2,1)S(1)}, u32[]{:S(2)}, u32[]{:S(2)}) collective-permute-start(bf16[128,4096]{1,0:T(8,128)(2,1)S(1)} %fusion.5.refs_0_.refs_1_), channel_id=1, source_target_pairs={{0,1},{1,2},{2,3},{3,0},{4,5},{5,6},{6,7},{7,4},{8,9},{9,10},{10,1... | collective-permute-start | bytes 3145736 | tf_op jit(solution)/shard_map/ppermute | solution.py:33
  81.1 31.3 %collective-permute-start.2 = (bf16[128,4096]{1,0:T(8,128)(2,1)S(1)}, bf16[128,4096]{1,0:T(8,128)(2,1)S(1)}, u32[]{:S(2)}, u32[]{:S(2)}) collective-permute-start(bf16[128,4096]{1,0:T(8,128)(2,1)S(1)} %fusion.5.refs_0_.refs_1_), channel_id=1, source_target_pairs={{0,3},{1,0},{2,1},{3,2},{4,7},{5,4},{6,5},{7,6},{8,11},{9,8},{10,9... | collective-permute-start | bytes 3145736 | tf_op jit(solution)/shard_map/ppermute | solution.py:33
  82.6 45.9 %collective-permute-start.3 = (bf16[128,4096]{1,0:T(8,128)(2,1)S(1)}, bf16[128,4096]{1,0:T(8,128)(2,1)S(1)}, u32[]{:S(2)}, u32[]{:S(2)}) collective-permute-start(bf16[128,4096]{1,0:T(8,128)(2,1)S(1)} %fusion.5.refs_0_.refs_1_), channel_id=1, source_target_pairs={{0,2},{1,3},{2,0},{3,1},{4,6},{5,7},{6,4},{7,5},{8,10},{9,11},{10,... | collective-permute-start | bytes 3145736 | tf_op jit(solution)/shard_map/ppermute | solution.py:33
  86.2 13.0 %collective-permute-start.16 = (bf16[8,256,128]{2,1,0:T(8,128)(2,1)S(1)}, bf16[8,256,128]{2,1,0:T(8,128)(2,1)S(1)}, u32[]{:S(2)}, u32[]{:S(2)}) collective-permute-start(bf16[8,256,128]{2,1,0:T(8,128)(2,1)S(1)} %bitcast.55), channel_id=1, source_target_pairs={{0,4},{1,5},{2,6},{3,7},{4,16},{5,17},{6,18},{7,19},{8,12},{9,13},... | collective-permute-start | bytes 1572872 | tf_op jit(solution)/shard_map/ppermute | solution.py:33
  86.3 17.2 %collective-permute-start.17 = (bf16[8,256,128]{2,1,0:T(8,128)(2,1)S(1)}, bf16[8,256,128]{2,1,0:T(8,128)(2,1)S(1)}, u32[]{:S(2)}, u32[]{:S(2)}) collective-permute-start(bf16[8,256,128]{2,1,0:T(8,128)(2,1)S(1)} %bitcast.56), channel_id=1, source_target_pairs={{0,20},{1,21},{2,22},{3,23},{4,0},{5,1},{6,2},{7,3},{8,28},{9,29},... | collective-permute-start | bytes 1572872 | tf_op jit(solution)/shard_map/ppermute | solution.py:33
  99.2 32.0 %collective-permute-start.18 = (bf16[8,256,128]{2,1,0:T(8,128)(2,1)S(1)}, bf16[8,256,128]{2,1,0:T(8,128)(2,1)S(1)}, u32[]{:S(2)}, u32[]{:S(2)}) collective-permute-start(bf16[8,256,128]{2,1,0:T(8,128)(2,1)S(1)} %bitcast.57), channel_id=1, source_target_pairs={{0,16},{1,17},{2,18},{3,19},{4,20},{5,21},{6,22},{7,23},{8,24},{9,... | collective-permute-start | bytes 1572872 | tf_op jit(solution)/shard_map/ppermute | solution.py:33
  103.5 28.6 %collective-permute-start.4 = (bf16[128,4096]{1,0:T(8,128)(2,1)S(1)}, bf16[128,4096]{1,0:T(8,128)(2,1)S(1)}, u32[]{:S(2)}, u32[]{:S(2)}) collective-permute-start(bf16[128,4096]{1,0:T(8,128)(2,1)S(1)} %fusion.5.refs_0_.refs_1_), channel_id=1, source_target_pairs={{0,8},{1,9},{2,10},{3,11},{4,12},{5,13},{6,14},{7,15},{8,0},{9,1},... | collective-permute-start | bytes 3145736 | tf_op jit(solution)/shard_map/ppermute | solution.py:33
  112.4 19.8 %collective-permute-start.5 = (bf16[128,4096]{1,0:T(8,128)(2,1)S(1)}, bf16[128,4096]{1,0:T(8,128)(2,1)S(1)}, u32[]{:S(2)}, u32[]{:S(2)}) collective-permute-start(bf16[128,4096]{1,0:T(8,128)(2,1)S(1)} %collective-permute-done.1.refs_1_), channel_id=1, source_target_pairs={{0,8},{1,9},{2,10},{3,11},{4,12},{5,13},{6,14},{7,15},{8,0},{9,1},... | collective-permute-start | bytes 3145736 | tf_op jit(solution)/shard_map/ppermute | solution.py:33
  112.4 19.8 %collective-permute-start.6 = (bf16[128,4096]{1,0:T(8,128)(2,1)S(1)}, bf16[128,4096]{1,0:T(8,128)(2,1)S(1)}, u32[]{:S(2)}, u32[]{:S(2)}) collective-permute-start(bf16[128,4096]{1,0:T(8,128)(2,1)S(1)} %collective-permute-done.2.refs_2_), channel_id=1, source_target_pairs={{0,8},{1,9},{2,10},{3,11},{4,12},{5,13},{6,14},{7,15},{8,0},{9,1},... | collective-permute-start | bytes 3145736 | tf_op jit(solution)/shard_map/ppermute | solution.py:33
  128.5 4.2 %collective-permute-start.7 = (bf16[128,4096]{1,0:T(8,128)(2,1)S(1)}, bf16[128,4096]{1,0:T(8,128)(2,1)S(1)}, u32[]{:S(2)}, u32[]{:S(2)}) collective-permute-start(bf16[128,4096]{1,0:T(8,128)(2,1)S(1)} %collective-permute-done.3.refs_3_), channel_id=1, source_target_pairs={{0,8},{1,9},{2,10},{3,11},{4,12},{5,13},{6,14},{7,15},{8,0},{9,1},... | collective-permute-start | bytes 3145736 | tf_op jit(solution)/shard_map/ppermute | solution.py:33
  132.1 25.6 %collective-permute-start.20 = (bf16[8,4,256,128]{3,2,1,0:T(8,128)(2,1)}, bf16[8,4,256,128]{3,2,1,0:T(8,128)(2,1)}, u32[]{:S(2)}, u32[]{:S(2)}) collective-permute-start(bf16[8,4,256,128]{3,2,1,0:T(8,128)(2,1)} %bitcast_dynamic-update-slice_fusion.2.refs_9_), channel_id=1, source_target_pairs={{0,8},{1,9},{2,10},{3,11},{4,12},{5,13},{6,14},{7,15},{8,0},{9,1},... | collective-permute-start | bytes 6291464 | tf_op jit(solution)/shard_map/ppermute | solution.py:33
  132.6 1.0 copy-start.2
  133.7 1.0 copy-start.7
  134.6 1.0 copy-start.8
  135.7 1.0 copy-start.9
  136.7 1.0 copy-start.10
  137.7 1.0 copy-start.11
  138.6 1.0 copy-start.12
  139.6 1.0 copy-start.13
  157.3 1.8 collective-permute-start.19
  159.1 1.0 copy-start.14
  165.0 33.8 %collective-permute-start.21 = (bf16[128,4096]{1,0:T(8,128)(2,1)}, bf16[128,4096]{1,0:T(8,128)(2,1)S(1)}, u32[]{:S(2)}, u32[]{:S(2)}) collective-permute-start(bf16[128,4096]{1,0:T(8,128)(2,1)} %get-tuple-element.33.refs_0_.up), channel_id=1, source_target_pairs={{0,1},{1,2},{2,3},{3,0},{4,5},{5,6},{6,7},{7,4},{8,9},{9,10},{10,1... | collective-permute-start | bytes 3145736 | tf_op jit(solution)/shard_map/ppermute | solution.py:33
  165.7 33.1 %collective-permute-start.22 = (bf16[128,4096]{1,0:T(8,128)(2,1)}, bf16[128,4096]{1,0:T(8,128)(2,1)S(1)}, u32[]{:S(2)}, u32[]{:S(2)}) collective-permute-start(bf16[128,4096]{1,0:T(8,128)(2,1)} %get-tuple-element.37.down), channel_id=1, source_target_pairs={{0,3},{1,0},{2,1},{3,2},{4,7},{5,4},{6,5},{7,6},{8,11},{9,8},{10,9... | collective-permute-start | bytes 3145736 | tf_op jit(solution)/shard_map/ppermute | solution.py:33
  172.2 1.4 copy-start.3
  179.6 33.4 %copy-start.1 = (bf16[128,4096]{1,0:T(8,128)(2,1)S(1)}, bf16[128,4096]{1,0:T(8,128)(2,1)}, u32[]{:S(2)}) copy-start(bf16[128,4096]{1,0:T(8,128)(2,1)} %copy-done) | copy-start | bytes 3145732
  179.6 33.4 %copy-start.4 = (f32[128,4096]{1,0:T(8,128)S(1)}, f32[128,4096]{1,0:T(8,128)}, u32[]{:S(2)}) copy-start(f32[128,4096]{1,0:T(8,128)} %copy-done.3) | copy-start | bytes 6291460
  179.6 17.0 %collective-permute-start.26 = (bf16[128,512]{1,0:T(8,128)(2,1)S(1)}, bf16[128,512]{1,0:T(8,128)(2,1)S(1)}, u32[]{:S(2)}, u32[]{:S(2)}) collective-permute-start(bf16[128,512]{1,0:T(8,128)(2,1)S(1)} %get-tuple-element.41), channel_id=1, source_target_pairs={{0,2},{1,3},{2,0},{3,1},{4,6},{5,7},{6,4},{7,5},{8,10},{9,11},{10,... | collective-permute-start | bytes 393224 | tf_op jit(solution)/shard_map/ppermute | solution.py:33
  183.3 13.8 %collective-permute-start.25 = (bf16[128,512]{1,0:T(8,128)(2,1)S(1)}, bf16[128,512]{1,0:T(8,128)(2,1)S(1)}, u32[]{:S(2)}, u32[]{:S(2)}) collective-permute-start(bf16[128,512]{1,0:T(8,128)(2,1)S(1)} %get-tuple-element.40), channel_id=1, source_target_pairs={{0,1},{1,2},{2,3},{3,0},{4,5},{5,6},{6,7},{7,4},{8,9},{9,10},{10,1... | collective-permute-start | bytes 393224 | tf_op jit(solution)/shard_map/ppermute | solution.py:33
  183.3 15.4 %collective-permute-start.24 = (bf16[128,512]{1,0:T(8,128)(2,1)S(1)}, bf16[128,512]{1,0:T(8,128)(2,1)S(1)}, u32[]{:S(2)}, u32[]{:S(2)}) collective-permute-start(bf16[128,512]{1,0:T(8,128)(2,1)S(1)} %get-tuple-element.39), channel_id=1, source_target_pairs={{0,3},{1,0},{2,1},{3,2},{4,7},{5,4},{6,5},{7,6},{8,11},{9,8},{10,9... | collective-permute-start | bytes 393224 | tf_op jit(solution)/shard_map/ppermute | solution.py:33
  199.4 13.5 %collective-permute-start.27 = (bf16[64,4096]{1,0:T(8,128)(2,1)S(1)}, bf16[64,4096]{1,0:T(8,128)(2,1)S(1)}, u32[]{:S(2)}, u32[]{:S(2)}) collective-permute-start(bf16[64,4096]{1,0:T(8,128)(2,1)S(1)} %get-tuple-element.42), channel_id=1, source_target_pairs={{0,1},{1,2},{2,3},{3,0},{4,5},{5,6},{6,7},{7,4},{8,9},{9,10},{10,1... | collective-permute-start | bytes 1572872 | tf_op jit(solution)/shard_map/ppermute | solution.py:33
  200.6 27.5 %copy-start.6 = (bf16[512,512]{1,0:T(8,128)(2,1)S(1)}, bf16[512,512]{1,0:T(8,128)(2,1)}, u32[]{:S(2)}) copy-start(bf16[512,512]{1,0:T(8,128)(2,1)} %refs_2_.1) | copy-start | bytes 1572868
  200.6 12.4 %collective-permute-start.28 = (bf16[64,4096]{1,0:T(8,128)(2,1)S(1)}, bf16[64,4096]{1,0:T(8,128)(2,1)S(1)}, u32[]{:S(2)}, u32[]{:S(2)}) collective-permute-start(bf16[64,4096]{1,0:T(8,128)(2,1)S(1)} %get-tuple-element.43), channel_id=1, source_target_pairs={{0,3},{1,0},{2,1},{3,2},{4,7},{5,4},{6,5},{7,6},{8,11},{9,8},{10,9... | collective-permute-start | bytes 1572872 | tf_op jit(solution)/shard_map/ppermute | solution.py:33
  202.2 7.8 %collective-permute-start.30 = (bf16[128,512]{1,0:T(8,128)(2,1)S(1)}, bf16[128,512]{1,0:T(8,128)(2,1)S(1)}, u32[]{:S(2)}, u32[]{:S(2)}) collective-permute-start(bf16[128,512]{1,0:T(8,128)(2,1)S(1)} %add_convert_fusion._.refs_0_), channel_id=1, source_target_pairs={{0,128},{1,129},{2,130},{3,131},{4,132},{5,133},{6,134},{7,135},{8... | collective-permute-start | bytes 393224 | tf_op jit(solution)/shard_map/ppermute | solution.py:33
  210.0 8.9 %collective-permute-start.31 = (bf16[128,512]{1,0:T(8,128)(2,1)S(1)}, bf16[128,512]{1,0:T(8,128)(2,1)S(1)}, u32[]{:S(2)}, u32[]{:S(2)}) collective-permute-start(bf16[128,512]{1,0:T(8,128)(2,1)S(1)} %collective-permute-done.30), channel_id=1, source_target_pairs={{0,1},{1,2},{2,3},{3,0},{4,5},{5,6},{6,7},{7,4},{8,9},{9,10},{10,1... | collective-permute-start | bytes 393224 | tf_op jit(solution)/shard_map/ppermute | solution.py:33
  210.0 8.9 %collective-permute-start.32 = (bf16[128,512]{1,0:T(8,128)(2,1)S(1)}, bf16[128,512]{1,0:T(8,128)(2,1)S(1)}, u32[]{:S(2)}, u32[]{:S(2)}) collective-permute-start(bf16[128,512]{1,0:T(8,128)(2,1)S(1)} %collective-permute-done.30), channel_id=1, source_target_pairs={{0,3},{1,0},{2,1},{3,2},{4,7},{5,4},{6,5},{7,6},{8,11},{9,8},{10,9... | collective-permute-start | bytes 393224 | tf_op jit(solution)/shard_map/ppermute | solution.py:33
  212.9 15.2 %copy-start.5 = (bf16[512,1536]{1,0:T(8,128)(2,1)S(1)}, bf16[512,1536]{1,0:T(8,128)(2,1)}, u32[]{:S(2)}) copy-start(bf16[512,1536]{1,0:T(8,128)(2,1)} %refs_1_.1) | copy-start | bytes 4718596
  214.1 24.5 %collective-permute-start.29 = (bf16[128,4096]{1,0:T(8,128)(2,1)S(1)}, bf16[128,4096]{1,0:T(8,128)(2,1)S(1)}, u32[]{:S(2)}, u32[]{:S(2)}) collective-permute-start(bf16[128,4096]{1,0:T(8,128)(2,1)S(1)} %shard_map.103), channel_id=1, source_target_pairs={{0,0},{1,1},{2,2},{3,3},{4,8},{5,9},{6,10},{7,11},{8,4},{9,5},{10,... | collective-permute-start | bytes 3145736 | tf_op jit(solution)/shard_map/ppermute | solution.py:33
  218.2 5.4 %collective-permute-start.33 = (bf16[128,512]{1,0:T(8,128)(2,1)S(1)}, bf16[128,512]{1,0:T(8,128)(2,1)S(1)}, u32[]{:S(2)}, u32[]{:S(2)}) collective-permute-start(bf16[128,512]{1,0:T(8,128)(2,1)S(1)} %collective-permute-done.30), channel_id=1, source_target_pairs={{0,2},{1,3},{2,0},{3,1},{4,6},{5,7},{6,4},{7,5},{8,10},{9,11},{10,... | collective-permute-start | bytes 393224 | tf_op jit(solution)/shard_map/ppermute | solution.py:33
  223.6 4.5 %collective-permute-start.34 = (bf16[512,512]{1,0:T(8,128)(2,1)S(1)}, bf16[512,512]{1,0:T(8,128)(2,1)S(1)}, u32[]{:S(2)}, u32[]{:S(2)}) collective-permute-start(bf16[512,512]{1,0:T(8,128)(2,1)S(1)} %constant_dynamic-update-slice_fusion.refs_3_), channel_id=1, source_target_pairs={{0,8},{1,9},{2,10},{3,11},{4,12},{5,13},{6,14},{7,15},{8,0},{9,1},... | collective-permute-start | bytes 1572872 | tf_op jit(solution)/shard_map/ppermute | solution.py:33
  232.3 6.3 %collective-permute-start.35 = (bf16[128,512]{1,0:T(8,128)(2,1)S(1)}, bf16[128,512]{1,0:T(8,128)(2,1)S(1)}, u32[]{:S(2)}, u32[]{:S(2)}) collective-permute-start(bf16[128,512]{1,0:T(8,128)(2,1)S(1)} %shard_map.104), channel_id=1, source_target_pairs={{0,0},{1,1},{2,2},{3,3},{4,8},{5,9},{6,10},{7,11},{8,4},{9,5},{10,... | collective-permute-start | bytes 393224 | tf_op jit(solution)/shard_map/ppermute | solution.py:33
Sparse Core Ops, SparseCore 0:
  31.1 86.8 all-gather.2
  119.8 41.1 all-gather.4

commit v6 on v5

--- a/solution.py
+++ b/solution.py
@@ -13,7 +13,7 @@
 HEAD_DIM = 128
 MATCH_HEADS = 8
 DISTANCES = (1, -1, 2)
-WAIT = 6_000_000_000
+WAIT = 23_000_000_000
 LOG2_E = math.log2(math.e)
 AXES = ("z", "xh", "core", "xl", "y")
 SIZES = (8, 2, 2, 2, 4)
@@ -49,6 +49,14 @@
     def target(p):
         x = (p["xh"] * 2 + p["xl"] + k) % 4
         return {"xh": x // 2, "xl": x % 2}
+
+    return target
+
+
+def swapped_along_x(k):
+    def target(p):
+        p = {**p, "core": p["xl"], "xl": p["core"]}
+        return {**p, **along_x(k)(p)}
 
     return target
 
@@ -443,21 +451,26 @@
 
     block, wide = qkv_weight.shape[0], out_weight.shape[1]
     packed = qkv_weight.reshape(block, -1, wide).transpose(1, 0, 2).reshape(-1, wide)
-    packed = swapped_roles(jnp.concatenate([packed, out_weight], axis=0))
-    split = packed.shape[0] - out_weight.shape[0]
-    weights = lax.all_gather(gathered_x(packed[:split], x, 0), "z", axis=0, tiled=True)
+    split = packed.shape[0]
+    by_x = jnp.zeros((4, split, wide), bf16)
+    for k in (0,) + DISTANCES:
+        part = moved(packed, swapped_along_x(k))
+        by_x = lax.dynamic_update_slice(by_x, part[None], ((x - k) % 4, 0, 0))
+    weights = lax.all_gather(by_x, "z", axis=0, tiled=True)
+    out_weight = swapped_roles(out_weight)
     weights = weights.reshape(8, 4, split // block, block, wide)
 
     tokens = swapped_roles(tokens)
     normed = layer_norm(tokens, norm_gain, norm_bias)
-    out_own = gathered_x(gathered_z(packed[split:], z), x, 1)
+    out_own = gathered_x(gathered_z(after(out_weight, normed), z), x, 1)
     out_other = moved(out_own, other_core)
     pieces = [normed] + [moved(normed, along_y(k)) for k in DISTANCES]
+    received = pieces[3]
     pieces += [moved(piece, other_core) for piece in pieces]
     pieces = together(*pieces, flops=WAIT)
     mine, theirs = attention(pieces, weights, out_own)
 
-    match_weight = after(match_weight, normed)
+    match_weight = after(match_weight, received)
     other_half = moved(match_weight, lambda p: {"xh": 1 - p["xh"], "xl": 1 - p["xl"]})
     match_pair = jnp.where(
         lax.axis_index("xh") == 0,

time: 248 us -> 246 us (level)
  starting transfers between devices: 90.9 us -> 61.1 us
  waiting for transfers between devices: 80.5 us -> 110 us
    ppermute x36 -> x37, starting transfers between devices: 90.8 us -> 61 us  [moved(): return lax.ppermute(block, AXES, route)]
    ppermute x36 -> x37, waiting for transfers between devices: 80.4 us -> 110 us  [moved(): return lax.ppermute(block, AXES, route)]
    unnamed x45 -> x47, local copies, waits for them, and re-layouts: 14.8 us -> 14.9 us
  transfers between devices with their start and end apart: 38 -> 39, of which waited for: 19 -> 20; matrix products, arithmetic and copies ran while one was open for 3% -> 3% of each run, Pallas kernels for 15% -> 15%
where the time goes in v6:
time: 246 us
  waiting for transfers between devices  110 us (45%)
  starting transfers between devices  61.1 us (25%)
  Pallas kernels  37.3 us (15%)
  local copies, waits for them, and re-layouts  20.7 us (8%)
  between operations  14.5 us (6%)
    ppermute x37, waiting for transfers between devices, moved(): return lax.ppermute(block, AXES, route)  110 us
    ppermute x37, starting transfers between devices, moved(): return lax.ppermute(block, AXES, route)  61 us
    pallas_call x1, Pallas kernels, attention(): local(attention_kernel, (result, result), 60, flops=2 * count * depth * c...  16.6 us
    unnamed x47, local copies, waits for them, and re-layouts  14.9 us
    pallas_call x2, Pallas kernels, terms(): local(functools.partial(terms_kernel, len(earlier), picked), tuple((jax.S...  8.91 us
    pallas_call x1, Pallas kernels, descriptor_terms(): local(descriptor_kernel, (jax.ShapeDtypeStruct((rows, width), f32),) + (j...  5.95 us
  transfers between devices with their start and end apart: 39, of which 20 were waited for; matrix products, arithmetic and copies ran while one was open for 3% of the time, Pallas kernels for 15%

profile of v6, /device:TPU:1, one launch (start us, length us, event | category | flops | bytes accessed | tf_op | source)
XLA Modules:
  0.0 245.8 jit_solution(17135089684383777138)
XLA Ops:
  7.2 0.9 copy.80.refs_0_
  8.1 1.2 copy.43
  9.5 4.5 %collective-permute-start.8 = (bf16[768,128]{1,0:T(8,128)(2,1)S(1)}, bf16[768,128]{1,0:T(8,128)(2,1)S(1)}, u32[]{:S(2)}, u32[]{:S(2)}) collective-permute-start(bf16[768,128]{1,0:T(8,128)(2,1)S(1)} %bitcast.60), channel_id=1, source_target_pairs={{0,0},{1,1},{2,2},{3,3},{4,8},{5,9},{6,10},{7,11},{8,4},{9,5},{10,... | collective-permute-start | bytes 589832 | tf_op jit(solution)/shard_map/ppermute | solution.py:33
  14.5 4.4 %collective-permute-start.11 = (bf16[768,128]{1,0:T(8,128)(2,1)S(1)}, bf16[768,128]{1,0:T(8,128)(2,1)S(1)}, u32[]{:S(2)}, u32[]{:S(2)}) collective-permute-start(bf16[768,128]{1,0:T(8,128)(2,1)S(1)} %bitcast.63), channel_id=1, source_target_pairs={{0,16},{1,17},{2,18},{3,19},{4,24},{5,25},{6,26},{7,27},{8,20},{9,... | collective-permute-start | bytes 589832 | tf_op jit(solution)/shard_map/ppermute | solution.py:33
  19.1 3.2 %collective-permute-done.9 = bf16[768,128]{1,0:T(8,128)(2,1)S(1)} collective-permute-done((bf16[768,128]{1,0:T(8,128)(2,1)S(1)}, bf16[768,128]{1,0:T(8,128)(2,1)S(1)}, u32[]{:S(2)}, u32[]{:S(2)}) %collective-permute-start.9) | collective-permute-done | bytes 196640 | tf_op jit(solution)/shard_map/ppermute | solution.py:33
  22.4 4.1 %collective-permute-done.11 = bf16[768,128]{1,0:T(8,128)(2,1)S(1)} collective-permute-done((bf16[768,128]{1,0:T(8,128)(2,1)S(1)}, bf16[768,128]{1,0:T(8,128)(2,1)S(1)}, u32[]{:S(2)}, u32[]{:S(2)}) %collective-permute-start.11) | collective-permute-done | bytes 196640 | tf_op jit(solution)/shard_map/ppermute | solution.py:33
  27.4 2.5 %collective-permute-start = (bf16[128,4096]{1,0:T(8,128)(2,1)S(1)}, bf16[128,4096]{1,0:T(8,128)(2,1)S(1)}, u32[]{:S(2)}, u32[]{:S(2)}) collective-permute-start(bf16[128,4096]{1,0:T(8,128)(2,1)S(1)} %copy-done.18), channel_id=1, source_target_pairs={{0,0},{1,1},{2,2},{3,3},{4,8},{5,9},{6,10},{7,11},{8,4},{9,5},{10,... | collective-permute-start | bytes 3145736 | tf_op jit(solution)/shard_map/ppermute | solution.py:33
  29.9 14.0 %collective-permute-done.tokens = bf16[128,4096]{1,0:T(8,128)(2,1)S(1)} collective-permute-done((bf16[128,4096]{1,0:T(8,128)(2,1)S(1)}, bf16[128,4096]{1,0:T(8,128)(2,1)S(1)}, u32[]{:S(2)}, u32[]{:S(2)}) %collective-permute-start) | collective-permute-done | bytes 1048608 | tf_op jit(solution)/shard_map/ppermute | solution.py:33
  45.2 3.0 %collective-permute-start.3 = (bf16[128,4096]{1,0:T(8,128)(2,1)S(1)}, bf16[128,4096]{1,0:T(8,128)(2,1)S(1)}, u32[]{:S(2)}, u32[]{:S(2)}) collective-permute-start(bf16[128,4096]{1,0:T(8,128)(2,1)S(1)} %fusion.5.refs_0_.refs_1_), channel_id=1, source_target_pairs={{0,2},{1,3},{2,0},{3,1},{4,6},{5,7},{6,4},{7,5},{8,10},{9,11},{10,... | collective-permute-start | bytes 3145736 | tf_op jit(solution)/shard_map/ppermute | solution.py:33
  48.2 12.3 %collective-permute-done.3.refs_3_.refs_1_ = bf16[128,4096]{1,0:T(8,128)(2,1)S(1)} collective-permute-done((bf16[128,4096]{1,0:T(8,128)(2,1)S(1)}, bf16[128,4096]{1,0:T(8,128)(2,1)S(1)}, u32[]{:S(2)}, u32[]{:S(2)}) %collective-permute-start.3) | collective-permute-done | bytes 1048608 | tf_op jit(solution)/shard_map/ppermute | solution.py:33
  60.4 6.1 %collective-permute-done.24 = bf16[128,512]{1,0:T(8,128)(2,1)S(1)} collective-permute-done((bf16[128,512]{1,0:T(8,128)(2,1)S(1)}, bf16[128,512]{1,0:T(8,128)(2,1)S(1)}, u32[]{:S(2)}, u32[]{:S(2)}) %collective-permute-start.24) | collective-permute-done | bytes 131104 | tf_op jit(solution)/shard_map/ppermute | solution.py:33
  67.3 2.1 collective-permute-start.12
  69.4 3.9 %collective-permute-done.12.refs_0_ = bf16[256,128]{1,0:T(8,128)(2,1)S(1)} collective-permute-done((bf16[256,128]{1,0:T(8,128)(2,1)S(1)}, bf16[256,128]{1,0:T(8,128)(2,1)S(1)}, u32[]{:S(2)}, u32[]{:S(2)}) %collective-permute-start.12) | collective-permute-done | bytes 65568 | tf_op jit(solution)/shard_map/ppermute | solution.py:33
  73.3 6.9 %collective-permute-start.13 = (bf16[256,128]{1,0:T(8,128)(2,1)S(1)}, bf16[256,128]{1,0:T(8,128)(2,1)S(1)}, u32[]{:S(2)}, u32[]{:S(2)}) collective-permute-start(bf16[256,128]{1,0:T(8,128)(2,1)S(1)} %shard_map.96), channel_id=1, source_target_pairs={{0,128},{1,129},{2,130},{3,131},{4,132},{5,133},{6,134},{7,135},{8... | collective-permute-start | bytes 196616 | tf_op jit(solution)/shard_map/ppermute | solution.py:33
  80.2 2.1 collective-permute-start.1
  83.0 0.9 collective-permute-done.13
  84.1 3.7 %collective-permute-start.15 = (bf16[2,256,128]{2,1,0:T(8,128)(2,1)S(1)}, bf16[2,256,128]{2,1,0:T(8,128)(2,1)S(1)}, u32[]{:S(2)}, u32[]{:S(2)}) collective-permute-start(bf16[2,256,128]{2,1,0:T(8,128)(2,1)S(1)} %shard_map.97), channel_id=1, source_target_pairs={{0,224},{1,225},{2,226},{3,227},{4,228},{5,229},{6,230},{7,231},{8... | collective-permute-start | bytes 393224 | tf_op jit(solution)/shard_map/ppermute | solution.py:33
  87.9 6.2 %collective-permute-done.14 = bf16[2,256,128]{2,1,0:T(8,128)(2,1)S(1)} collective-permute-done((bf16[2,256,128]{2,1,0:T(8,128)(2,1)S(1)}, bf16[2,256,128]{2,1,0:T(8,128)(2,1)S(1)}, u32[]{:S(2)}, u32[]{:S(2)}) %collective-permute-start.14) | collective-permute-done | bytes 131104 | tf_op jit(solution)/shard_map/ppermute | solution.py:33
  95.0 5.2 %collective-permute-done.16 = bf16[2,256,128]{2,1,0:T(8,128)(2,1)S(1)} collective-permute-done((bf16[2,256,128]{2,1,0:T(8,128)(2,1)S(1)}, bf16[2,256,128]{2,1,0:T(8,128)(2,1)S(1)}, u32[]{:S(2)}, u32[]{:S(2)}) %collective-permute-start.16) | collective-permute-done | bytes 131104 | tf_op jit(solution)/shard_map/ppermute | solution.py:33
  100.3 2.7 %collective-permute-start.18 = (bf16[8,256,128]{2,1,0:T(8,128)(2,1)S(1)}, bf16[8,256,128]{2,1,0:T(8,128)(2,1)S(1)}, u32[]{:S(2)}, u32[]{:S(2)}) collective-permute-start(bf16[8,256,128]{2,1,0:T(8,128)(2,1)S(1)} %bitcast.56), channel_id=1, source_target_pairs={{0,20},{1,21},{2,22},{3,23},{4,0},{5,1},{6,2},{7,3},{8,28},{9,29},... | collective-permute-start | bytes 1572872 | tf_op jit(solution)/shard_map/ppermute | solution.py:33
  103.0 1.7 collective-permute-start.4
  105.2 8.7 %collective-permute-done.17 = bf16[8,256,128]{2,1,0:T(8,128)(2,1)S(1)} collective-permute-done((bf16[8,256,128]{2,1,0:T(8,128)(2,1)S(1)}, bf16[8,256,128]{2,1,0:T(8,128)(2,1)S(1)}, u32[]{:S(2)}, u32[]{:S(2)}) %collective-permute-start.17) | collective-permute-done | bytes 524320 | tf_op jit(solution)/shard_map/ppermute | solution.py:33
  113.9 1.9 collective-permute-start.7
  115.9 1.8 broadcast_in_dim.51
  117.6 0.9 constant_dynamic-update-slice_fusion.4
  118.5 0.9 bitcast_dynamic-update-slice_fusion.1
  119.4 0.9 bitcast_dynamic-update-slice_fusion
  120.3 10.6 %collective-permute-done.19 = bf16[8,256,128]{2,1,0:T(8,128)(2,1)S(1)} collective-permute-done((bf16[8,256,128]{2,1,0:T(8,128)(2,1)S(1)}, bf16[8,256,128]{2,1,0:T(8,128)(2,1)S(1)}, u32[]{:S(2)}, u32[]{:S(2)}) %collective-permute-start.19) | collective-permute-done | bytes 524320 | tf_op jit(solution)/shard_map/ppermute | solution.py:33
  132.6 1.0 copy-done.2
  133.6 1.0 copy-done.6
  134.6 1.0 copy-done.8
  135.6 1.0 copy-done.9
  136.6 1.0 copy-done.10
  137.6 1.0 copy-done.11
  138.6 1.0 copy-done.12
  139.6 1.0 copy-done.13
  140.6 16.6 %shard_map.98 = (bf16[512,256]{1,0:T(8,128)(2,1)}, bf16[512,256]{1,0:T(8,128)(2,1)}) custom-call(bf16[128,4096]{1,0:T(8,128)(2,1)} %copy-done.2, bf16[128,4096]{1,0:T(8,128)(2,1)} %copy-done.8, bf16[128,4096]{1,0:T(8,128)(2,1)} %copy-done.9, bf16[128,4096]{1,0:T(8,128)(2,1)} %copy-done.6, bf16[128,4096]{1,0:T(8,128)(2,1)} %copy-done.10, ...), custom_call_target="tpu_custom_call" | custom-call | flops 6442450944 | bytes 14680064 | tf_op jit(solution)/shard_map/pallas_call | solution.py:232
  157.3 1.7 collective-permute-done.20.theirs
  159.0 0.9 copy-done.14
  160.0 5.0 %shard_map.99 = (bf16[128,4096]{1,0:T(8,128)(2,1)}, bf16[128,4096]{1,0:T(8,128)(2,1)}) custom-call(bf16[512,256]{1,0:T(8,128)(2,1)S(1)} %copy-done.14, bf16[512,256]{1,0:T(8,128)(2,1)S(1)} %collective-permute-done.20.theirs, bf16[8,4,2,128,128]{4,3,2,1,0:T(8,128)(2,1)} %bitcast.25.weight, bf16[8,4,2,128,128]{4,3,2,1,0:T(8,128)(2,1)} %bitcast.26.other_weight), custom_call_target="tpu_custom_call" | custom-call | flops 2000000000 | bytes 8000000 | tf_op jit(solution)/shard_map/pallas_call | solution.py:289
  165.0 1.8 collective-permute-start.22
  166.7 1.0 collective-permute-start.23
  167.7 3.9 %shard_map.100 = (f32[128,4096]{1,0:T(8,128)S(1)}, bf16[64,4096]{1,0:T(8,128)(2,1)S(1)}, bf16[64,4096]{1,0:T(8,128)(2,1)S(1)}) custom-call(bf16[512,256]{1,0:T(8,128)(2,1)S(1)} %copy-done.14, bf16[512,256]{1,0:T(8,128)(2,1)S(1)} %collective-permute-done.20.theirs, bf16[8,4,2,128,128]{4,3,2,1,0:T(8,128)(2,1)} %bitcast.25.weight, ...), custom_call_target="tpu_custom_call" | custom-call | flops 2000000000 | bytes 8000000 | tf_op jit(solution)/shard_map/pallas_call | solution.py:289
  171.7 1.3 copy-done.3
  173.0 5.9 %shard_map.102 = (f32[128,512]{1,0:T(8,128)S(1)}, bf16[128,512]{1,0:T(8,128)(2,1)S(1)}, bf16[128,512]{1,0:T(8,128)(2,1)S(1)}, bf16[128,512]{1,0:T(8,128)(2,1)S(1)}) custom-call(bf16[128,4096]{1,0:T(8,128)(2,1)} %copy-done, f32[128,4096]{1,0:T(8,128)} %copy-done.3, bf16[128,4096]{1,0:T(8,128)(2,1)} %get-tuple-element.37.down, ...), custom_call_target="tpu_custom_call" | custom-call | flops 4000000000 | bytes 12000000 | tf_op jit(solution)/shard_map/pallas_call | solution.py:339
  179.0 2.4 collective-permute-start.27
  181.5 2.7 %collective-permute-start.25 = (bf16[128,512]{1,0:T(8,128)(2,1)S(1)}, bf16[128,512]{1,0:T(8,128)(2,1)S(1)}, u32[]{:S(2)}, u32[]{:S(2)}) collective-permute-start(bf16[128,512]{1,0:T(8,128)(2,1)S(1)} %get-tuple-element.39), channel_id=1, source_target_pairs={{0,3},{1,0},{2,1},{3,2},{4,7},{5,4},{6,5},{7,6},{8,11},{9,8},{10,9... | collective-permute-start | bytes 393224 | tf_op jit(solution)/shard_map/ppermute | solution.py:33
  184.1 11.0 %collective-permute-done.27 = bf16[128,512]{1,0:T(8,128)(2,1)S(1)} collective-permute-done((bf16[128,512]{1,0:T(8,128)(2,1)S(1)}, bf16[128,512]{1,0:T(8,128)(2,1)S(1)}, u32[]{:S(2)}, u32[]{:S(2)}) %collective-permute-start.27) | collective-permute-done | bytes 131104 | tf_op jit(solution)/shard_map/ppermute | solution.py:33
  195.1 1.7 collective-permute-done.26
  197.6 1.3 collective-permute-start.28
  198.9 1.4 collective-permute-start.29
  200.3 1.6 collective-permute-start.31
  202.0 8.1 %collective-permute-done.31 = bf16[128,512]{1,0:T(8,128)(2,1)S(1)} collective-permute-done((bf16[128,512]{1,0:T(8,128)(2,1)S(1)}, bf16[128,512]{1,0:T(8,128)(2,1)S(1)}, u32[]{:S(2)}, u32[]{:S(2)}) %collective-permute-start.31) | collective-permute-done | bytes 131104 | tf_op jit(solution)/shard_map/ppermute | solution.py:33
  210.1 2.7 %collective-permute-start.33 = (bf16[128,512]{1,0:T(8,128)(2,1)S(1)}, bf16[128,512]{1,0:T(8,128)(2,1)S(1)}, u32[]{:S(2)}, u32[]{:S(2)}) collective-permute-start(bf16[128,512]{1,0:T(8,128)(2,1)S(1)} %collective-permute-done.31), channel_id=1, source_target_pairs={{0,3},{1,0},{2,1},{3,2},{4,7},{5,4},{6,5},{7,6},{8,11},{9,8},{10,9... | collective-permute-start | bytes 393224 | tf_op jit(solution)/shard_map/ppermute | solution.py:33
  212.8 1.1 shard_map.104
  213.9 3.8 %collective-permute-start.30 = (bf16[128,4096]{1,0:T(8,128)(2,1)S(1)}, bf16[128,4096]{1,0:T(8,128)(2,1)S(1)}, u32[]{:S(2)}, u32[]{:S(2)}) collective-permute-start(bf16[128,4096]{1,0:T(8,128)(2,1)S(1)} %shard_map.104), channel_id=1, source_target_pairs={{0,0},{1,1},{2,2},{3,3},{4,8},{5,9},{6,10},{7,11},{8,4},{9,5},{10,... | collective-permute-start | bytes 3145736 | tf_op jit(solution)/shard_map/ppermute | solution.py:33
  217.7 0.9 collective-permute-start.34
  218.7 5.3 %collective-permute-done.34 = bf16[128,512]{1,0:T(8,128)(2,1)S(1)} collective-permute-done((bf16[128,512]{1,0:T(8,128)(2,1)S(1)}, bf16[128,512]{1,0:T(8,128)(2,1)S(1)}, u32[]{:S(2)}, u32[]{:S(2)}) %collective-permute-start.34) | collective-permute-done | bytes 131104 | tf_op jit(solution)/shard_map/ppermute | solution.py:33
  224.0 1.3 collective-permute-start.35
  225.3 1.5 collective-permute-done.35.refs_4_
  226.8 4.2 %shard_map.105 = bf16[128,512]{1,0:T(8,128)(2,1)S(1)} custom-call(bf16[128,512]{1,0:T(8,128)(2,1)S(1)} %add_convert_fusion._.refs_0_, bf16[512,1536]{1,0:T(8,128)(2,1)S(1)} %copy-done.5, bf16[512,512]{1,0:T(8,128)(2,1)S(1)} %copy-done.7, bf16[512,512]{1,0:T(8,128)(2,1)S(1)} %constant_dynamic-update-slice_fusion.refs_3_, ...), custom_call_target="tpu_custom_call" | custom-call | tf_op jit(solution)/shard_map/pallas_call | solution.py:430
  231.0 1.9 collective-permute-start.36
  233.0 4.4 %collective-permute-done.36 = bf16[128,512]{1,0:T(8,128)(2,1)S(1)} collective-permute-done((bf16[128,512]{1,0:T(8,128)(2,1)S(1)}, bf16[128,512]{1,0:T(8,128)(2,1)S(1)}, u32[]{:S(2)}, u32[]{:S(2)}) %collective-permute-start.36) | collective-permute-done | bytes 131104 | tf_op jit(solution)/shard_map/ppermute | solution.py:33
  237.3 1.0 copy.81
  (99 shorter events, 9.7 us)
Async XLA Ops:
  7.2 133.4 %all-gather.3.cloned.1.call-start = ((), (), s32[]{:S(2)}) async-start(), calls=%async_computation | async-start | bytes 7077888 | tf_op jit(solution)/shard_map/all_gather | solution.py:459
  8.1 19.3 %copy-start.18 = (bf16[128,4096]{1,0:T(8,128)(2,1)S(1)}, bf16[128,4096]{1,0:T(8,128)(2,1)}, u32[]{:S(2)}) copy-start(bf16[128,4096]{1,0:T(8,128)(2,1)} %param.8) | copy-start | bytes 3145732
  9.5 9.4 %collective-permute-start.8 = (bf16[768,128]{1,0:T(8,128)(2,1)S(1)}, bf16[768,128]{1,0:T(8,128)(2,1)S(1)}, u32[]{:S(2)}, u32[]{:S(2)}) collective-permute-start(bf16[768,128]{1,0:T(8,128)(2,1)S(1)} %bitcast.60), channel_id=1, source_target_pairs={{0,0},{1,1},{2,2},{3,3},{4,8},{5,9},{6,10},{7,11},{8,4},{9,5},{10,... | collective-permute-start | bytes 589832 | tf_op jit(solution)/shard_map/ppermute | solution.py:33
  14.0 8.3 %collective-permute-start.9 = (bf16[768,128]{1,0:T(8,128)(2,1)S(1)}, bf16[768,128]{1,0:T(8,128)(2,1)S(1)}, u32[]{:S(2)}, u32[]{:S(2)}) collective-permute-start(bf16[768,128]{1,0:T(8,128)(2,1)S(1)} %bitcast.61), channel_id=1, source_target_pairs={{0,4},{1,5},{2,6},{3,7},{4,12},{5,13},{6,14},{7,15},{8,16},{9,17},... | collective-permute-start | bytes 589832 | tf_op jit(solution)/shard_map/ppermute | solution.py:33
  14.4 8.0 %collective-permute-start.10 = (bf16[768,128]{1,0:T(8,128)(2,1)S(1)}, bf16[768,128]{1,0:T(8,128)(2,1)S(1)}, u32[]{:S(2)}, u32[]{:S(2)}) collective-permute-start(bf16[768,128]{1,0:T(8,128)(2,1)S(1)} %bitcast.62), channel_id=1, source_target_pairs={{0,20},{1,21},{2,22},{3,23},{4,28},{5,29},{6,30},{7,31},{8,0},{9,1... | collective-permute-start | bytes 589832 | tf_op jit(solution)/shard_map/ppermute | solution.py:33
  14.5 12.0 %collective-permute-start.11 = (bf16[768,128]{1,0:T(8,128)(2,1)S(1)}, bf16[768,128]{1,0:T(8,128)(2,1)S(1)}, u32[]{:S(2)}, u32[]{:S(2)}) collective-permute-start(bf16[768,128]{1,0:T(8,128)(2,1)S(1)} %bitcast.63), channel_id=1, source_target_pairs={{0,16},{1,17},{2,18},{3,19},{4,24},{5,25},{6,26},{7,27},{8,20},{9,... | collective-permute-start | bytes 589832 | tf_op jit(solution)/shard_map/ppermute | solution.py:33
  19.0 25.6 %copy-start.16 = (f32[4096]{0:T(1024)S(1)}, f32[4096]{0:T(1024)}, u32[]{:S(2)}) copy-start(f32[4096]{0:T(1024)} %param.10) | copy-start | bytes 49156
  19.0 25.6 %copy-start.17 = (f32[4096]{0:T(1024)S(1)}, f32[4096]{0:T(1024)}, u32[]{:S(2)}) copy-start(f32[4096]{0:T(1024)} %param.9) | copy-start | bytes 49156
  26.5 0.9 copy-start.15
  27.4 145.7 %all-gather.5.cloned.1.call-start = ((), (), s32[]{:S(2)}) async-start(), calls=%async_computation.1 | async-start | bytes 4456448 | tf_op jit(solution)/shard_map/all_gather | solution.py:480
  27.4 16.5 %collective-permute-start = (bf16[128,4096]{1,0:T(8,128)(2,1)S(1)}, bf16[128,4096]{1,0:T(8,128)(2,1)S(1)}, u32[]{:S(2)}, u32[]{:S(2)}) collective-permute-start(bf16[128,4096]{1,0:T(8,128)(2,1)S(1)} %copy-done.18), channel_id=1, source_target_pairs={{0,0},{1,1},{2,2},{3,3},{4,8},{5,9},{6,10},{7,11},{8,4},{9,5},{10,... | collective-permute-start | bytes 3145736 | tf_op jit(solution)/shard_map/ppermute | solution.py:33
  44.0 1.2 copy-start
  44.6 22.7 %copy-start.19 = (bf16[256,128]{1,0:T(8,128)(2,1)S(1)}, bf16[256,128]{1,0:T(8,128)(2,1)}, u32[]{:S(2)}) copy-start(bf16[256,128]{1,0:T(8,128)(2,1)} %param.12) | copy-start | bytes 196612
  45.2 15.3 %collective-permute-start.3 = (bf16[128,4096]{1,0:T(8,128)(2,1)S(1)}, bf16[128,4096]{1,0:T(8,128)(2,1)S(1)}, u32[]{:S(2)}, u32[]{:S(2)}) collective-permute-start(bf16[128,4096]{1,0:T(8,128)(2,1)S(1)} %fusion.5.refs_0_.refs_1_), channel_id=1, source_target_pairs={{0,2},{1,3},{2,0},{3,1},{4,6},{5,7},{6,4},{7,5},{8,10},{9,11},{10,... | collective-permute-start | bytes 3145736 | tf_op jit(solution)/shard_map/ppermute | solution.py:33
  60.4 6.1 %collective-permute-start.24 = (bf16[128,512]{1,0:T(8,128)(2,1)S(1)}, bf16[128,512]{1,0:T(8,128)(2,1)S(1)}, u32[]{:S(2)}, u32[]{:S(2)}) collective-permute-start(bf16[128,512]{1,0:T(8,128)(2,1)S(1)} %shard_map.101), channel_id=1, source_target_pairs={{0,20},{1,21},{2,22},{3,23},{4,16},{5,17},{6,18},{7,19},{8,28},{9,... | collective-permute-start | bytes 393224 | tf_op jit(solution)/shard_map/ppermute | solution.py:33
  67.3 6.0 %collective-permute-start.12 = (bf16[256,128]{1,0:T(8,128)(2,1)S(1)}, bf16[256,128]{1,0:T(8,128)(2,1)S(1)}, u32[]{:S(2)}, u32[]{:S(2)}) collective-permute-start(bf16[256,128]{1,0:T(8,128)(2,1)S(1)} %copy-done.19), channel_id=1, source_target_pairs={{0,0},{1,1},{2,2},{3,3},{4,8},{5,9},{6,10},{7,11},{8,4},{9,5},{10,... | collective-permute-start | bytes 196616 | tf_op jit(solution)/shard_map/ppermute | solution.py:33
  73.3 10.6 %collective-permute-start.13 = (bf16[256,128]{1,0:T(8,128)(2,1)S(1)}, bf16[256,128]{1,0:T(8,128)(2,1)S(1)}, u32[]{:S(2)}, u32[]{:S(2)}) collective-permute-start(bf16[256,128]{1,0:T(8,128)(2,1)S(1)} %shard_map.96), channel_id=1, source_target_pairs={{0,128},{1,129},{2,130},{3,131},{4,132},{5,133},{6,134},{7,135},{8... | collective-permute-start | bytes 196616 | tf_op jit(solution)/shard_map/ppermute | solution.py:33
  80.2 24.4 %collective-permute-start.1 = (bf16[128,4096]{1,0:T(8,128)(2,1)S(1)}, bf16[128,4096]{1,0:T(8,128)(2,1)S(1)}, u32[]{:S(2)}, u32[]{:S(2)}) collective-permute-start(bf16[128,4096]{1,0:T(8,128)(2,1)S(1)} %fusion.5.refs_0_.refs_1_), channel_id=1, source_target_pairs={{0,1},{1,2},{2,3},{3,0},{4,5},{5,6},{6,7},{7,4},{8,9},{9,10},{10,1... | collective-permute-start | bytes 3145736 | tf_op jit(solution)/shard_map/ppermute | solution.py:33
  82.3 22.4 %collective-permute-start.2 = (bf16[128,4096]{1,0:T(8,128)(2,1)S(1)}, bf16[128,4096]{1,0:T(8,128)(2,1)S(1)}, u32[]{:S(2)}, u32[]{:S(2)}) collective-permute-start(bf16[128,4096]{1,0:T(8,128)(2,1)S(1)} %fusion.5.refs_0_.refs_1_), channel_id=1, source_target_pairs={{0,3},{1,0},{2,1},{3,2},{4,7},{5,4},{6,5},{7,6},{8,11},{9,8},{10,9... | collective-permute-start | bytes 3145736 | tf_op jit(solution)/shard_map/ppermute | solution.py:33
  83.9 10.2 %collective-permute-start.14 = (bf16[2,256,128]{2,1,0:T(8,128)(2,1)S(1)}, bf16[2,256,128]{2,1,0:T(8,128)(2,1)S(1)}, u32[]{:S(2)}, u32[]{:S(2)}) collective-permute-start(bf16[2,256,128]{2,1,0:T(8,128)(2,1)S(1)} %shard_map.97), channel_id=1, source_target_pairs={{0,32},{1,33},{2,34},{3,35},{4,36},{5,37},{6,38},{7,39},{8,40},{9,... | collective-permute-start | bytes 393224 | tf_op jit(solution)/shard_map/ppermute | solution.py:33
  84.1 10.8 %collective-permute-start.15 = (bf16[2,256,128]{2,1,0:T(8,128)(2,1)S(1)}, bf16[2,256,128]{2,1,0:T(8,128)(2,1)S(1)}, u32[]{:S(2)}, u32[]{:S(2)}) collective-permute-start(bf16[2,256,128]{2,1,0:T(8,128)(2,1)S(1)} %shard_map.97), channel_id=1, source_target_pairs={{0,224},{1,225},{2,226},{3,227},{4,228},{5,229},{6,230},{7,231},{8... | collective-permute-start | bytes 393224 | tf_op jit(solution)/shard_map/ppermute | solution.py:33
  87.8 12.4 %collective-permute-start.16 = (bf16[2,256,128]{2,1,0:T(8,128)(2,1)S(1)}, bf16[2,256,128]{2,1,0:T(8,128)(2,1)S(1)}, u32[]{:S(2)}, u32[]{:S(2)}) collective-permute-start(bf16[2,256,128]{2,1,0:T(8,128)(2,1)S(1)} %shard_map.97), channel_id=1, source_target_pairs={{0,64},{1,65},{2,66},{3,67},{4,68},{5,69},{6,70},{7,71},{8,72},{9,... | collective-permute-start | bytes 393224 | tf_op jit(solution)/shard_map/ppermute | solution.py:33
  100.2 13.7 %collective-permute-start.17 = (bf16[8,256,128]{2,1,0:T(8,128)(2,1)S(1)}, bf16[8,256,128]{2,1,0:T(8,128)(2,1)S(1)}, u32[]{:S(2)}, u32[]{:S(2)}) collective-permute-start(bf16[8,256,128]{2,1,0:T(8,128)(2,1)S(1)} %bitcast.55), channel_id=1, source_target_pairs={{0,4},{1,5},{2,6},{3,7},{4,16},{5,17},{6,18},{7,19},{8,12},{9,13},... | collective-permute-start | bytes 1572872 | tf_op jit(solution)/shard_map/ppermute | solution.py:33
  100.3 15.5 %collective-permute-start.18 = (bf16[8,256,128]{2,1,0:T(8,128)(2,1)S(1)}, bf16[8,256,128]{2,1,0:T(8,128)(2,1)S(1)}, u32[]{:S(2)}, u32[]{:S(2)}) collective-permute-start(bf16[8,256,128]{2,1,0:T(8,128)(2,1)S(1)} %bitcast.56), channel_id=1, source_target_pairs={{0,20},{1,21},{2,22},{3,23},{4,0},{5,1},{6,2},{7,3},{8,28},{9,29},... | collective-permute-start | bytes 1572872 | tf_op jit(solution)/shard_map/ppermute | solution.py:33
  103.0 29.6 %collective-permute-start.4 = (bf16[128,4096]{1,0:T(8,128)(2,1)S(1)}, bf16[128,4096]{1,0:T(8,128)(2,1)S(1)}, u32[]{:S(2)}, u32[]{:S(2)}) collective-permute-start(bf16[128,4096]{1,0:T(8,128)(2,1)S(1)} %fusion.5.refs_0_.refs_1_), channel_id=1, source_target_pairs={{0,8},{1,9},{2,10},{3,11},{4,12},{5,13},{6,14},{7,15},{8,0},{9,1},... | collective-permute-start | bytes 3145736 | tf_op jit(solution)/shard_map/ppermute | solution.py:33
  104.7 27.9 %collective-permute-start.5 = (bf16[128,4096]{1,0:T(8,128)(2,1)S(1)}, bf16[128,4096]{1,0:T(8,128)(2,1)S(1)}, u32[]{:S(2)}, u32[]{:S(2)}) collective-permute-start(bf16[128,4096]{1,0:T(8,128)(2,1)S(1)} %collective-permute-done.1.refs_1_), channel_id=1, source_target_pairs={{0,8},{1,9},{2,10},{3,11},{4,12},{5,13},{6,14},{7,15},{8,0},{9,1},... | collective-permute-start | bytes 3145736 | tf_op jit(solution)/shard_map/ppermute | solution.py:33
  104.7 27.9 %collective-permute-start.6 = (bf16[128,4096]{1,0:T(8,128)(2,1)S(1)}, bf16[128,4096]{1,0:T(8,128)(2,1)S(1)}, u32[]{:S(2)}, u32[]{:S(2)}) collective-permute-start(bf16[128,4096]{1,0:T(8,128)(2,1)S(1)} %collective-permute-done.2.refs_2_), channel_id=1, source_target_pairs={{0,8},{1,9},{2,10},{3,11},{4,12},{5,13},{6,14},{7,15},{8,0},{9,1},... | collective-permute-start | bytes 3145736 | tf_op jit(solution)/shard_map/ppermute | solution.py:33
  113.9 18.7 %collective-permute-start.7 = (bf16[128,4096]{1,0:T(8,128)(2,1)S(1)}, bf16[128,4096]{1,0:T(8,128)(2,1)S(1)}, u32[]{:S(2)}, u32[]{:S(2)}) collective-permute-start(bf16[128,4096]{1,0:T(8,128)(2,1)S(1)} %collective-permute-done.3.refs_3_.refs_1_), channel_id=1, source_target_pairs={{0,8},{1,9},{2,10},{3,11},{4,12},{5,13},{6,14},{7,15},{8,0},{9,1},... | collective-permute-start | bytes 3145736 | tf_op jit(solution)/shard_map/ppermute | solution.py:33
  115.9 15.1 %collective-permute-start.19 = (bf16[8,256,128]{2,1,0:T(8,128)(2,1)S(1)}, bf16[8,256,128]{2,1,0:T(8,128)(2,1)S(1)}, u32[]{:S(2)}, u32[]{:S(2)}) collective-permute-start(bf16[8,256,128]{2,1,0:T(8,128)(2,1)S(1)} %bitcast.57), channel_id=1, source_target_pairs={{0,16},{1,17},{2,18},{3,19},{4,20},{5,21},{6,22},{7,23},{8,24},{9,... | collective-permute-start | bytes 1572872 | tf_op jit(solution)/shard_map/ppermute | solution.py:33
  131.8 25.5 %collective-permute-start.21 = (bf16[8,4,256,128]{3,2,1,0:T(8,128)(2,1)}, bf16[8,4,256,128]{3,2,1,0:T(8,128)(2,1)}, u32[]{:S(2)}, u32[]{:S(2)}) collective-permute-start(bf16[8,4,256,128]{3,2,1,0:T(8,128)(2,1)} %bitcast_dynamic-update-slice_fusion.2.refs_9_), channel_id=1, source_target_pairs={{0,8},{1,9},{2,10},{3,11},{4,12},{5,13},{6,14},{7,15},{8,0},{9,1},... | collective-permute-start | bytes 6291464 | tf_op jit(solution)/shard_map/ppermute | solution.py:33
  132.6 1.0 copy-start.2
  133.6 1.0 copy-start.6
  134.6 1.0 copy-start.8
  135.6 1.0 copy-start.9
  136.6 1.0 copy-start.10
  137.6 1.0 copy-start.11
  138.6 1.0 copy-start.12
  139.6 1.0 copy-start.13
  157.2 1.8 collective-permute-start.20
  159.0 1.0 copy-start.14
  165.0 32.0 %collective-permute-start.22 = (bf16[128,4096]{1,0:T(8,128)(2,1)}, bf16[128,4096]{1,0:T(8,128)(2,1)S(1)}, u32[]{:S(2)}, u32[]{:S(2)}) collective-permute-start(bf16[128,4096]{1,0:T(8,128)(2,1)} %get-tuple-element.33.refs_0_.up), channel_id=1, source_target_pairs={{0,1},{1,2},{2,3},{3,0},{4,5},{5,6},{6,7},{7,4},{8,9},{9,10},{10,1... | collective-permute-start | bytes 3145736 | tf_op jit(solution)/shard_map/ppermute | solution.py:33
  166.7 30.3 %collective-permute-start.23 = (bf16[128,4096]{1,0:T(8,128)(2,1)}, bf16[128,4096]{1,0:T(8,128)(2,1)S(1)}, u32[]{:S(2)}, u32[]{:S(2)}) collective-permute-start(bf16[128,4096]{1,0:T(8,128)(2,1)} %get-tuple-element.37.down), channel_id=1, source_target_pairs={{0,3},{1,0},{2,1},{3,2},{4,7},{5,4},{6,5},{7,6},{8,11},{9,8},{10,9... | collective-permute-start | bytes 3145736 | tf_op jit(solution)/shard_map/ppermute | solution.py:33
  171.7 1.4 copy-start.3
  179.0 33.7 %copy-start.1 = (bf16[128,4096]{1,0:T(8,128)(2,1)S(1)}, bf16[128,4096]{1,0:T(8,128)(2,1)}, u32[]{:S(2)}) copy-start(bf16[128,4096]{1,0:T(8,128)(2,1)} %copy-done) | copy-start | bytes 3145732
  179.0 33.7 %copy-start.4 = (f32[128,4096]{1,0:T(8,128)S(1)}, f32[128,4096]{1,0:T(8,128)}, u32[]{:S(2)}) copy-start(f32[128,4096]{1,0:T(8,128)} %copy-done.3) | copy-start | bytes 6291460
  179.0 16.1 %collective-permute-start.27 = (bf16[128,512]{1,0:T(8,128)(2,1)S(1)}, bf16[128,512]{1,0:T(8,128)(2,1)S(1)}, u32[]{:S(2)}, u32[]{:S(2)}) collective-permute-start(bf16[128,512]{1,0:T(8,128)(2,1)S(1)} %get-tuple-element.41), channel_id=1, source_target_pairs={{0,2},{1,3},{2,0},{3,1},{4,6},{5,7},{6,4},{7,5},{8,10},{9,11},{10,... | collective-permute-start | bytes 393224 | tf_op jit(solution)/shard_map/ppermute | solution.py:33
  181.5 15.3 %collective-permute-start.26 = (bf16[128,512]{1,0:T(8,128)(2,1)S(1)}, bf16[128,512]{1,0:T(8,128)(2,1)S(1)}, u32[]{:S(2)}, u32[]{:S(2)}) collective-permute-start(bf16[128,512]{1,0:T(8,128)(2,1)S(1)} %get-tuple-element.40), channel_id=1, source_target_pairs={{0,1},{1,2},{2,3},{3,0},{4,5},{5,6},{6,7},{7,4},{8,9},{9,10},{10,1... | collective-permute-start | bytes 393224 | tf_op jit(solution)/shard_map/ppermute | solution.py:33
  181.5 15.5 %collective-permute-start.25 = (bf16[128,512]{1,0:T(8,128)(2,1)S(1)}, bf16[128,512]{1,0:T(8,128)(2,1)S(1)}, u32[]{:S(2)}, u32[]{:S(2)}) collective-permute-start(bf16[128,512]{1,0:T(8,128)(2,1)S(1)} %get-tuple-element.39), channel_id=1, source_target_pairs={{0,3},{1,0},{2,1},{3,2},{4,7},{5,4},{6,5},{7,6},{8,11},{9,8},{10,9... | collective-permute-start | bytes 393224 | tf_op jit(solution)/shard_map/ppermute | solution.py:33
  197.6 15.1 %collective-permute-start.28 = (bf16[64,4096]{1,0:T(8,128)(2,1)S(1)}, bf16[64,4096]{1,0:T(8,128)(2,1)S(1)}, u32[]{:S(2)}, u32[]{:S(2)}) collective-permute-start(bf16[64,4096]{1,0:T(8,128)(2,1)S(1)} %get-tuple-element.42), channel_id=1, source_target_pairs={{0,1},{1,2},{2,3},{3,0},{4,5},{5,6},{6,7},{7,4},{8,9},{9,10},{10,1... | collective-permute-start | bytes 1572872 | tf_op jit(solution)/shard_map/ppermute | solution.py:33
  198.9 27.9 %copy-start.7 = (bf16[512,512]{1,0:T(8,128)(2,1)S(1)}, bf16[512,512]{1,0:T(8,128)(2,1)}, u32[]{:S(2)}) copy-start(bf16[512,512]{1,0:T(8,128)(2,1)} %refs_2_.1) | copy-start | bytes 1572868
  198.9 13.8 %collective-permute-start.29 = (bf16[64,4096]{1,0:T(8,128)(2,1)S(1)}, bf16[64,4096]{1,0:T(8,128)(2,1)S(1)}, u32[]{:S(2)}, u32[]{:S(2)}) collective-permute-start(bf16[64,4096]{1,0:T(8,128)(2,1)S(1)} %get-tuple-element.43), channel_id=1, source_target_pairs={{0,3},{1,0},{2,1},{3,2},{4,7},{5,4},{6,5},{7,6},{8,11},{9,8},{10,9... | collective-permute-start | bytes 1572872 | tf_op jit(solution)/shard_map/ppermute | solution.py:33
  200.3 9.7 %collective-permute-start.31 = (bf16[128,512]{1,0:T(8,128)(2,1)S(1)}, bf16[128,512]{1,0:T(8,128)(2,1)S(1)}, u32[]{:S(2)}, u32[]{:S(2)}) collective-permute-start(bf16[128,512]{1,0:T(8,128)(2,1)S(1)} %add_convert_fusion._.refs_0_), channel_id=1, source_target_pairs={{0,128},{1,129},{2,130},{3,131},{4,132},{5,133},{6,134},{7,135},{8... | collective-permute-start | bytes 393224 | tf_op jit(solution)/shard_map/ppermute | solution.py:33
  210.0 8.6 %collective-permute-start.32 = (bf16[128,512]{1,0:T(8,128)(2,1)S(1)}, bf16[128,512]{1,0:T(8,128)(2,1)S(1)}, u32[]{:S(2)}, u32[]{:S(2)}) collective-permute-start(bf16[128,512]{1,0:T(8,128)(2,1)S(1)} %collective-permute-done.31), channel_id=1, source_target_pairs={{0,1},{1,2},{2,3},{3,0},{4,5},{5,6},{6,7},{7,4},{8,9},{9,10},{10,1... | collective-permute-start | bytes 393224 | tf_op jit(solution)/shard_map/ppermute | solution.py:33
  210.1 8.6 %collective-permute-start.33 = (bf16[128,512]{1,0:T(8,128)(2,1)S(1)}, bf16[128,512]{1,0:T(8,128)(2,1)S(1)}, u32[]{:S(2)}, u32[]{:S(2)}) collective-permute-start(bf16[128,512]{1,0:T(8,128)(2,1)S(1)} %collective-permute-done.31), channel_id=1, source_target_pairs={{0,3},{1,0},{2,1},{3,2},{4,7},{5,4},{6,5},{7,6},{8,11},{9,8},{10,9... | collective-permute-start | bytes 393224 | tf_op jit(solution)/shard_map/ppermute | solution.py:33
  212.7 14.1 %copy-start.5 = (bf16[512,1536]{1,0:T(8,128)(2,1)S(1)}, bf16[512,1536]{1,0:T(8,128)(2,1)}, u32[]{:S(2)}) copy-start(bf16[512,1536]{1,0:T(8,128)(2,1)} %refs_1_.1) | copy-start | bytes 4718596
  213.9 23.4 %collective-permute-start.30 = (bf16[128,4096]{1,0:T(8,128)(2,1)S(1)}, bf16[128,4096]{1,0:T(8,128)(2,1)S(1)}, u32[]{:S(2)}, u32[]{:S(2)}) collective-permute-start(bf16[128,4096]{1,0:T(8,128)(2,1)S(1)} %shard_map.104), channel_id=1, source_target_pairs={{0,0},{1,1},{2,2},{3,3},{4,8},{5,9},{6,10},{7,11},{8,4},{9,5},{10,... | collective-permute-start | bytes 3145736 | tf_op jit(solution)/shard_map/ppermute | solution.py:33
  217.7 6.3 %collective-permute-start.34 = (bf16[128,512]{1,0:T(8,128)(2,1)S(1)}, bf16[128,512]{1,0:T(8,128)(2,1)S(1)}, u32[]{:S(2)}, u32[]{:S(2)}) collective-permute-start(bf16[128,512]{1,0:T(8,128)(2,1)S(1)} %collective-permute-done.31), channel_id=1, source_target_pairs={{0,2},{1,3},{2,0},{3,1},{4,6},{5,7},{6,4},{7,5},{8,10},{9,11},{10,... | collective-permute-start | bytes 393224 | tf_op jit(solution)/shard_map/ppermute | solution.py:33
  224.0 2.8 %collective-permute-start.35 = (bf16[512,512]{1,0:T(8,128)(2,1)S(1)}, bf16[512,512]{1,0:T(8,128)(2,1)S(1)}, u32[]{:S(2)}, u32[]{:S(2)}) collective-permute-start(bf16[512,512]{1,0:T(8,128)(2,1)S(1)} %constant_dynamic-update-slice_fusion.refs_3_), channel_id=1, source_target_pairs={{0,8},{1,9},{2,10},{3,11},{4,12},{5,13},{6,14},{7,15},{8,0},{9,1},... | collective-permute-start | bytes 1572872 | tf_op jit(solution)/shard_map/ppermute | solution.py:33
  231.0 6.3 %collective-permute-start.36 = (bf16[128,512]{1,0:T(8,128)(2,1)S(1)}, bf16[128,512]{1,0:T(8,128)(2,1)S(1)}, u32[]{:S(2)}, u32[]{:S(2)}) collective-permute-start(bf16[128,512]{1,0:T(8,128)(2,1)S(1)} %shard_map.105), channel_id=1, source_target_pairs={{0,0},{1,1},{2,2},{3,3},{4,8},{5,9},{6,10},{7,11},{8,4},{9,5},{10,... | collective-permute-start | bytes 393224 | tf_op jit(solution)/shard_map/ppermute | solution.py:33
Sparse Core Ops, SparseCore 0:
  27.5 85.0 all-gather.2
  114.4 41.1 all-gather.4

commit v7 on v6

--- a/solution.py
+++ b/solution.py
@@ -462,15 +462,15 @@
 
     tokens = swapped_roles(tokens)
     normed = layer_norm(tokens, norm_gain, norm_bias)
-    out_own = gathered_x(gathered_z(after(out_weight, normed), z), x, 1)
+    pieces = [normed] + [moved(normed, along_y(k)) for k in DISTANCES]
+    *pieces[1:], out_z = together(*pieces[1:], gathered_z(out_weight, z))
+    pieces += [moved(piece, other_core) for piece in pieces]
+    out_own = gathered_x(out_z, x, 1)
     out_other = moved(out_own, other_core)
-    pieces = [normed] + [moved(normed, along_y(k)) for k in DISTANCES]
-    received = pieces[3]
-    pieces += [moved(piece, other_core) for piece in pieces]
     pieces = together(*pieces, flops=WAIT)
     mine, theirs = attention(pieces, weights, out_own)
 
-    match_weight = after(match_weight, received)
+    match_weight = after(match_weight, pieces[0])
     other_half = moved(match_weight, lambda p: {"xh": 1 - p["xh"], "xl": 1 - p["xl"]})
     match_pair = jnp.where(
         lax.axis_index("xh") == 0,

time: 246 us -> 240 us (0.976)
  starting transfers between devices: 61.1 us -> 57.5 us
    ppermute x37, starting transfers between devices: 61 us -> 57.4 us  [moved(): return lax.ppermute(block, AXES, route)]
where the time goes in v7:
time: 240 us
  waiting for transfers between devices  111 us (46%)
  starting transfers between devices  57.5 us (24%)
  Pallas kernels  36.7 us (15%)
  local copies, waits for them, and re-layouts  18.6 us (8%)
  between operations  14.4 us (6%)
    ppermute x37, waiting for transfers between devices, moved(): return lax.ppermute(block, AXES, route)  110 us
    ppermute x37, starting transfers between devices, moved(): return lax.ppermute(block, AXES, route)  57.4 us
    pallas_call x1, Pallas kernels, attention(): local(attention_kernel, (result, result), 60, flops=2 * count * depth * c...  16.6 us
    unnamed x47, local copies, waits for them, and re-layouts  12.5 us
    pallas_call x2, Pallas kernels, terms(): local(functools.partial(terms_kernel, len(earlier), picked), tuple((jax.S...  8.24 us
    pallas_call x1, Pallas kernels, descriptor_terms(): local(descriptor_kernel, (jax.ShapeDtypeStruct((rows, width), f32),) + (j...  5.95 us
  transfers between devices with their start and end apart: 39, of which 20 were waited for; matrix products, arithmetic and copies ran while one was open for 3% of the time, Pallas kernels for 15%

profile of v7, /device:TPU:1, one launch (start us, length us, event | category | flops | bytes accessed | tf_op | source)
XLA Modules:
  0.0 240.0 jit_solution(15566440986341383064)
XLA Ops:
  7.2 0.9 copy.78.refs_0_
  8.1 1.1 copy.44
  9.4 4.5 %collective-permute-start.13 = (bf16[768,128]{1,0:T(8,128)(2,1)S(1)}, bf16[768,128]{1,0:T(8,128)(2,1)S(1)}, u32[]{:S(2)}, u32[]{:S(2)}) collective-permute-start(bf16[768,128]{1,0:T(8,128)(2,1)S(1)} %bitcast.55), channel_id=1, source_target_pairs={{0,0},{1,1},{2,2},{3,3},{4,8},{5,9},{6,10},{7,11},{8,4},{9,5},{10,... | collective-permute-start | bytes 589832 | tf_op jit(solution)/shard_map/ppermute | solution.py:33
  14.4 4.4 %collective-permute-start.16 = (bf16[768,128]{1,0:T(8,128)(2,1)S(1)}, bf16[768,128]{1,0:T(8,128)(2,1)S(1)}, u32[]{:S(2)}, u32[]{:S(2)}) collective-permute-start(bf16[768,128]{1,0:T(8,128)(2,1)S(1)} %bitcast.58), channel_id=1, source_target_pairs={{0,16},{1,17},{2,18},{3,19},{4,24},{5,25},{6,26},{7,27},{8,20},{9,... | collective-permute-start | bytes 589832 | tf_op jit(solution)/shard_map/ppermute | solution.py:33
  19.0 3.2 %collective-permute-done.14 = bf16[768,128]{1,0:T(8,128)(2,1)S(1)} collective-permute-done((bf16[768,128]{1,0:T(8,128)(2,1)S(1)}, bf16[768,128]{1,0:T(8,128)(2,1)S(1)}, u32[]{:S(2)}, u32[]{:S(2)}) %collective-permute-start.14) | collective-permute-done | bytes 196640 | tf_op jit(solution)/shard_map/ppermute | solution.py:33
  22.3 4.1 %collective-permute-done.16 = bf16[768,128]{1,0:T(8,128)(2,1)S(1)} collective-permute-done((bf16[768,128]{1,0:T(8,128)(2,1)S(1)}, bf16[768,128]{1,0:T(8,128)(2,1)S(1)}, u32[]{:S(2)}, u32[]{:S(2)}) %collective-permute-start.16) | collective-permute-done | bytes 196640 | tf_op jit(solution)/shard_map/ppermute | solution.py:33
  26.4 0.9 copy-done.16
  27.4 2.5 %collective-permute-start = (bf16[128,4096]{1,0:T(8,128)(2,1)}, bf16[128,4096]{1,0:T(8,128)(2,1)S(1)}, u32[]{:S(2)}, u32[]{:S(2)}) collective-permute-start(bf16[128,4096]{1,0:T(8,128)(2,1)} %param.8), channel_id=1, source_target_pairs={{0,0},{1,1},{2,2},{3,3},{4,8},{5,9},{6,10},{7,11},{8,4},{9,5},{10,... | collective-permute-start | bytes 3145736 | tf_op jit(solution)/shard_map/ppermute | solution.py:33
  29.9 3.1 %collective-permute-start.4 = (bf16[256,128]{1,0:T(8,128)(2,1)S(1)}, bf16[256,128]{1,0:T(8,128)(2,1)S(1)}, u32[]{:S(2)}, u32[]{:S(2)}) collective-permute-start(bf16[256,128]{1,0:T(8,128)(2,1)S(1)} %copy-done.19), channel_id=1, source_target_pairs={{0,0},{1,1},{2,2},{3,3},{4,8},{5,9},{6,10},{7,11},{8,4},{9,5},{10,... | collective-permute-start | bytes 196616 | tf_op jit(solution)/shard_map/ppermute | solution.py:33
  33.0 11.8 %collective-permute-done.4 = bf16[256,128]{1,0:T(8,128)(2,1)S(1)} collective-permute-done((bf16[256,128]{1,0:T(8,128)(2,1)S(1)}, bf16[256,128]{1,0:T(8,128)(2,1)S(1)}, u32[]{:S(2)}, u32[]{:S(2)}) %collective-permute-start.4) | collective-permute-done | bytes 65568 | tf_op jit(solution)/shard_map/ppermute | solution.py:33
  44.8 6.9 %collective-permute-start.5 = (bf16[256,128]{1,0:T(8,128)(2,1)S(1)}, bf16[256,128]{1,0:T(8,128)(2,1)S(1)}, u32[]{:S(2)}, u32[]{:S(2)}) collective-permute-start(bf16[256,128]{1,0:T(8,128)(2,1)S(1)} %collective-permute-done.4), channel_id=1, source_target_pairs={{0,128},{1,129},{2,130},{3,131},{4,132},{5,133},{6,134},{7,135},{8... | collective-permute-start | bytes 196616 | tf_op jit(solution)/shard_map/ppermute | solution.py:33
  52.9 1.4 collective-permute-start.1
  54.3 1.5 collective-permute-start.2
  55.8 1.6 collective-permute-start.3
  57.4 0.8 collective-permute-start.6
  58.2 1.9 collective-permute-start.7
  60.3 5.8 %collective-permute-done.6 = bf16[2,256,128]{2,1,0:T(8,128)(2,1)S(1)} collective-permute-done((bf16[2,256,128]{2,1,0:T(8,128)(2,1)S(1)}, bf16[2,256,128]{2,1,0:T(8,128)(2,1)S(1)}, u32[]{:S(2)}, u32[]{:S(2)}) %collective-permute-start.6) | collective-permute-done | bytes 131104 | tf_op jit(solution)/shard_map/ppermute | solution.py:33
  66.2 9.0 %collective-permute-done.8 = bf16[2,256,128]{2,1,0:T(8,128)(2,1)S(1)} collective-permute-done((bf16[2,256,128]{2,1,0:T(8,128)(2,1)S(1)}, bf16[2,256,128]{2,1,0:T(8,128)(2,1)S(1)}, u32[]{:S(2)}, u32[]{:S(2)}) %collective-permute-start.8) | collective-permute-done | bytes 131104 | tf_op jit(solution)/shard_map/ppermute | solution.py:33
  75.3 2.8 %collective-permute-done.1.refs_0_ = bf16[128,4096]{1,0:T(8,128)(2,1)S(1)} collective-permute-done((bf16[128,4096]{1,0:T(8,128)(2,1)S(1)}, bf16[128,4096]{1,0:T(8,128)(2,1)S(1)}, u32[]{:S(2)}, u32[]{:S(2)}) %collective-permute-start.1) | collective-permute-done | bytes 1048608 | tf_op jit(solution)/shard_map/ppermute | solution.py:33
  78.1 10.9 %collective-permute-done.3.refs_2_ = bf16[128,4096]{1,0:T(8,128)(2,1)} collective-permute-done((bf16[128,4096]{1,0:T(8,128)(2,1)S(1)}, bf16[128,4096]{1,0:T(8,128)(2,1)}, u32[]{:S(2)}, u32[]{:S(2)}) %collective-permute-start.3) | collective-permute-done | bytes 1048608 | tf_op jit(solution)/shard_map/ppermute | solution.py:33
  89.5 3.6 %collective-permute-done.10.refs_5_ = bf16[128,4096]{1,0:T(8,128)(2,1)S(1)} collective-permute-done((bf16[128,4096]{1,0:T(8,128)(2,1)S(1)}, bf16[128,4096]{1,0:T(8,128)(2,1)S(1)}, u32[]{:S(2)}, u32[]{:S(2)}) %collective-permute-start.10) | collective-permute-done | bytes 1048608 | tf_op jit(solution)/shard_map/ppermute | solution.py:33
  93.4 1.5 collective-permute-done.12.refs_7_
  94.9 1.0 copy-done.10
  95.9 1.0 copy-done.11
  96.9 1.0 copy-done.12
  97.9 1.0 copy-done.13
  98.9 6.3 %collective-permute-done.24 = bf16[128,512]{1,0:T(8,128)(2,1)S(1)} collective-permute-done((bf16[128,512]{1,0:T(8,128)(2,1)S(1)}, bf16[128,512]{1,0:T(8,128)(2,1)S(1)}, u32[]{:S(2)}, u32[]{:S(2)}) %collective-permute-start.24) | collective-permute-done | bytes 131104 | tf_op jit(solution)/shard_map/ppermute | solution.py:33
  105.2 0.8 maximum_select_fusion
  106.1 2.7 %collective-permute-start.18 = (bf16[8,256,128]{2,1,0:T(8,128)(2,1)S(1)}, bf16[8,256,128]{2,1,0:T(8,128)(2,1)S(1)}, u32[]{:S(2)}, u32[]{:S(2)}) collective-permute-start(bf16[8,256,128]{2,1,0:T(8,128)(2,1)S(1)} %get-tuple-element.38), channel_id=1, source_target_pairs={{0,20},{1,21},{2,22},{3,23},{4,0},{5,1},{6,2},{7,3},{8,28},{9,29},... | collective-permute-start | bytes 1572872 | tf_op jit(solution)/shard_map/ppermute | solution.py:33
  108.7 1.9 broadcast_in_dim.59
  110.6 0.9 bitcast_dynamic-update-slice_fusion.3
  111.6 9.2 %collective-permute-done.17 = bf16[8,256,128]{2,1,0:T(8,128)(2,1)S(1)} collective-permute-done((bf16[8,256,128]{2,1,0:T(8,128)(2,1)S(1)}, bf16[8,256,128]{2,1,0:T(8,128)(2,1)S(1)}, u32[]{:S(2)}, u32[]{:S(2)}) %collective-permute-start.17) | collective-permute-done | bytes 524320 | tf_op jit(solution)/shard_map/ppermute | solution.py:33
  120.8 1.0 bitcast_dynamic-update-slice_fusion.2
  121.8 0.9 bitcast_dynamic-update-slice_fusion.1
  122.7 7.4 %collective-permute-done.19 = bf16[8,256,128]{2,1,0:T(8,128)(2,1)S(1)} collective-permute-done((bf16[8,256,128]{2,1,0:T(8,128)(2,1)S(1)}, bf16[8,256,128]{2,1,0:T(8,128)(2,1)S(1)}, u32[]{:S(2)}, u32[]{:S(2)}) %collective-permute-start.19) | collective-permute-done | bytes 524320 | tf_op jit(solution)/shard_map/ppermute | solution.py:33
  130.2 0.9 bitcast_dynamic-update-slice_fusion.refs_9_
  131.1 4.6 %collective-permute-start.21 = (bf16[8,4,256,128]{3,2,1,0:T(8,128)(2,1)}, bf16[8,4,256,128]{3,2,1,0:T(8,128)(2,1)S(1)}, u32[]{:S(2)}, u32[]{:S(2)}) collective-permute-start(bf16[8,4,256,128]{3,2,1,0:T(8,128)(2,1)} %bitcast_dynamic-update-slice_fusion.refs_9_), channel_id=1, source_target_pairs={{0,8},{1,9},{2,10},{3,11},{4,12},{5,13},{6,14},{7,15},{8,0},{9,1},... | collective-permute-start | bytes 6291464 | tf_op jit(solution)/shard_map/ppermute | solution.py:33
  135.7 16.6 %shard_map.98 = (bf16[512,256]{1,0:T(8,128)(2,1)}, bf16[512,256]{1,0:T(8,128)(2,1)}) custom-call(bf16[128,4096]{1,0:T(8,128)(2,1)} %copy-done.2, bf16[128,4096]{1,0:T(8,128)(2,1)} %copy-done.6, bf16[128,4096]{1,0:T(8,128)(2,1)} %get-tuple-element.32.refs_2_, bf16[128,4096]{1,0:T(8,128)(2,1)} %get-tuple-element.33.refs_3_, bf16[128,4096]{1,0:T(8,128)(2,1)} %copy-done.10, ...), custom_call_target="tpu_custom_call" | custom-call | flops 6442450944 | bytes 14680064 | tf_op jit(solution)/shard_map/pallas_call | solution.py:232
  152.4 1.7 collective-permute-done.20.theirs
  154.1 0.9 copy-done.14
  155.1 4.6 %shard_map.99 = (bf16[128,4096]{1,0:T(8,128)(2,1)}, bf16[128,4096]{1,0:T(8,128)(2,1)}) custom-call(bf16[512,256]{1,0:T(8,128)(2,1)S(1)} %copy-done.14, bf16[512,256]{1,0:T(8,128)(2,1)S(1)} %collective-permute-done.20.theirs, bf16[8,4,2,128,128]{4,3,2,1,0:T(8,128)(2,1)} %bitcast.23.weight, bf16[8,4,2,128,128]{4,3,2,1,0:T(8,128)(2,1)S(1)} %bitcast.52), custom_call_target="tpu_custom_call" | custom-call | flops 2000000000 | bytes 8000000 | tf_op jit(solution)/shard_map/pallas_call | solution.py:289
  159.7 1.4 collective-permute-start.22
  161.2 1.3 collective-permute-start.23
  162.4 1.6 copy-done.9
  164.0 3.6 %shard_map.100 = (f32[128,4096]{1,0:T(8,128)S(1)}, bf16[64,4096]{1,0:T(8,128)(2,1)S(1)}, bf16[64,4096]{1,0:T(8,128)(2,1)S(1)}) custom-call(bf16[512,256]{1,0:T(8,128)(2,1)S(1)} %copy-done.15, bf16[512,256]{1,0:T(8,128)(2,1)S(1)} %collective-permute-done.20.theirs, bf16[8,4,2,128,128]{4,3,2,1,0:T(8,128)(2,1)} %bitcast.23.weight, ...), custom_call_target="tpu_custom_call" | custom-call | flops 2000000000 | bytes 8000000 | tf_op jit(solution)/shard_map/pallas_call | solution.py:289
  167.6 1.3 copy-done.3
  169.0 5.9 %shard_map.102 = (f32[128,512]{1,0:T(8,128)S(1)}, bf16[128,512]{1,0:T(8,128)(2,1)S(1)}, bf16[128,512]{1,0:T(8,128)(2,1)S(1)}, bf16[128,512]{1,0:T(8,128)(2,1)S(1)}) custom-call(bf16[128,4096]{1,0:T(8,128)(2,1)} %copy-done, f32[128,4096]{1,0:T(8,128)} %copy-done.3, bf16[128,4096]{1,0:T(8,128)(2,1)} %get-tuple-element.45.down, ...), custom_call_target="tpu_custom_call" | custom-call | flops 4000000000 | bytes 12000000 | tf_op jit(solution)/shard_map/pallas_call | solution.py:339
  174.9 0.9 collective-permute-start.27
  176.6 1.9 collective-permute-start.25
  178.5 10.6 %collective-permute-done.27 = bf16[128,512]{1,0:T(8,128)(2,1)S(1)} collective-permute-done((bf16[128,512]{1,0:T(8,128)(2,1)S(1)}, bf16[128,512]{1,0:T(8,128)(2,1)S(1)}, u32[]{:S(2)}, u32[]{:S(2)}) %collective-permute-start.27) | collective-permute-done | bytes 131104 | tf_op jit(solution)/shard_map/ppermute | solution.py:33
  189.1 2.3 collective-permute-done.26
  192.4 2.4 collective-permute-start.29
  194.8 8.5 %collective-permute-done.31 = bf16[128,512]{1,0:T(8,128)(2,1)S(1)} collective-permute-done((bf16[128,512]{1,0:T(8,128)(2,1)S(1)}, bf16[128,512]{1,0:T(8,128)(2,1)S(1)}, u32[]{:S(2)}, u32[]{:S(2)}) %collective-permute-start.31) | collective-permute-done | bytes 131104 | tf_op jit(solution)/shard_map/ppermute | solution.py:33
  203.3 2.7 %collective-permute-start.33 = (bf16[128,512]{1,0:T(8,128)(2,1)S(1)}, bf16[128,512]{1,0:T(8,128)(2,1)S(1)}, u32[]{:S(2)}, u32[]{:S(2)}) collective-permute-start(bf16[128,512]{1,0:T(8,128)(2,1)S(1)} %collective-permute-done.31), channel_id=1, source_target_pairs={{0,3},{1,0},{2,1},{3,2},{4,7},{5,4},{6,5},{7,6},{8,11},{9,8},{10,9... | collective-permute-start | bytes 393224 | tf_op jit(solution)/shard_map/ppermute | solution.py:33
  206.0 1.1 shard_map.104
  207.1 4.7 %collective-permute-start.30 = (bf16[128,4096]{1,0:T(8,128)(2,1)S(1)}, bf16[128,4096]{1,0:T(8,128)(2,1)S(1)}, u32[]{:S(2)}, u32[]{:S(2)}) collective-permute-start(bf16[128,4096]{1,0:T(8,128)(2,1)S(1)} %shard_map.104), channel_id=1, source_target_pairs={{0,0},{1,1},{2,2},{3,3},{4,8},{5,9},{6,10},{7,11},{8,4},{9,5},{10,... | collective-permute-start | bytes 3145736 | tf_op jit(solution)/shard_map/ppermute | solution.py:33
  211.9 1.0 collective-permute-start.34
  212.9 5.6 %collective-permute-done.34 = bf16[128,512]{1,0:T(8,128)(2,1)S(1)} collective-permute-done((bf16[128,512]{1,0:T(8,128)(2,1)S(1)}, bf16[128,512]{1,0:T(8,128)(2,1)S(1)}, u32[]{:S(2)}, u32[]{:S(2)}) %collective-permute-start.34) | collective-permute-done | bytes 131104 | tf_op jit(solution)/shard_map/ppermute | solution.py:33
  218.5 1.0 collective-permute-start.35
  219.5 1.5 collective-permute-done.35.refs_4_
  221.0 4.2 %shard_map.105 = bf16[128,512]{1,0:T(8,128)(2,1)S(1)} custom-call(bf16[128,512]{1,0:T(8,128)(2,1)S(1)} %add_convert_fusion._.refs_0_, bf16[512,1536]{1,0:T(8,128)(2,1)S(1)} %copy-done.5, bf16[512,512]{1,0:T(8,128)(2,1)S(1)} %copy-done.7, bf16[512,512]{1,0:T(8,128)(2,1)S(1)} %constant_dynamic-update-slice_fusion.refs_3_, ...), custom_call_target="tpu_custom_call" | custom-call | tf_op jit(solution)/shard_map/pallas_call | solution.py:430
  225.2 1.9 collective-permute-start.36
  227.2 4.4 %collective-permute-done.36 = bf16[128,512]{1,0:T(8,128)(2,1)S(1)} collective-permute-done((bf16[128,512]{1,0:T(8,128)(2,1)S(1)}, bf16[128,512]{1,0:T(8,128)(2,1)S(1)}, u32[]{:S(2)}, u32[]{:S(2)}) %collective-permute-start.36) | collective-permute-done | bytes 131104 | tf_op jit(solution)/shard_map/ppermute | solution.py:33
  231.5 1.0 copy.79
  (99 shorter events, 6.0 us)
Async XLA Ops:
  7.2 128.5 %all-gather.3.cloned.1.call-start = ((), (), s32[]{:S(2)}) async-start(), calls=%async_computation | async-start | bytes 7077888 | tf_op jit(solution)/shard_map/all_gather | solution.py:459
  8.1 21.8 %copy-start.19 = (bf16[256,128]{1,0:T(8,128)(2,1)S(1)}, bf16[256,128]{1,0:T(8,128)(2,1)}, u32[]{:S(2)}) copy-start(bf16[256,128]{1,0:T(8,128)(2,1)} %param.12) | copy-start | bytes 196612
  9.4 9.4 %collective-permute-start.13 = (bf16[768,128]{1,0:T(8,128)(2,1)S(1)}, bf16[768,128]{1,0:T(8,128)(2,1)S(1)}, u32[]{:S(2)}, u32[]{:S(2)}) collective-permute-start(bf16[768,128]{1,0:T(8,128)(2,1)S(1)} %bitcast.55), channel_id=1, source_target_pairs={{0,0},{1,1},{2,2},{3,3},{4,8},{5,9},{6,10},{7,11},{8,4},{9,5},{10,... | collective-permute-start | bytes 589832 | tf_op jit(solution)/shard_map/ppermute | solution.py:33
  13.9 8.3 %collective-permute-start.14 = (bf16[768,128]{1,0:T(8,128)(2,1)S(1)}, bf16[768,128]{1,0:T(8,128)(2,1)S(1)}, u32[]{:S(2)}, u32[]{:S(2)}) collective-permute-start(bf16[768,128]{1,0:T(8,128)(2,1)S(1)} %bitcast.56), channel_id=1, source_target_pairs={{0,4},{1,5},{2,6},{3,7},{4,12},{5,13},{6,14},{7,15},{8,16},{9,17},... | collective-permute-start | bytes 589832 | tf_op jit(solution)/shard_map/ppermute | solution.py:33
  14.3 8.0 %collective-permute-start.15 = (bf16[768,128]{1,0:T(8,128)(2,1)S(1)}, bf16[768,128]{1,0:T(8,128)(2,1)S(1)}, u32[]{:S(2)}, u32[]{:S(2)}) collective-permute-start(bf16[768,128]{1,0:T(8,128)(2,1)S(1)} %bitcast.57), channel_id=1, source_target_pairs={{0,20},{1,21},{2,22},{3,23},{4,28},{5,29},{6,30},{7,31},{8,0},{9,1... | collective-permute-start | bytes 589832 | tf_op jit(solution)/shard_map/ppermute | solution.py:33
  14.4 12.0 %collective-permute-start.16 = (bf16[768,128]{1,0:T(8,128)(2,1)S(1)}, bf16[768,128]{1,0:T(8,128)(2,1)S(1)}, u32[]{:S(2)}, u32[]{:S(2)}) collective-permute-start(bf16[768,128]{1,0:T(8,128)(2,1)S(1)} %bitcast.58), channel_id=1, source_target_pairs={{0,16},{1,17},{2,18},{3,19},{4,24},{5,25},{6,26},{7,27},{8,20},{9,... | collective-permute-start | bytes 589832 | tf_op jit(solution)/shard_map/ppermute | solution.py:33
  19.0 33.4 %copy-start.17 = (f32[4096]{0:T(1024)S(1)}, f32[4096]{0:T(1024)}, u32[]{:S(2)}) copy-start(f32[4096]{0:T(1024)} %param.10) | copy-start | bytes 49156
  19.0 33.4 %copy-start.18 = (f32[4096]{0:T(1024)S(1)}, f32[4096]{0:T(1024)}, u32[]{:S(2)}) copy-start(f32[4096]{0:T(1024)} %param.9) | copy-start | bytes 49156
  26.4 0.9 copy-start.16
  27.3 141.6 %all-gather.5.cloned.1.call-start = ((), (), s32[]{:S(2)}) async-start(), calls=%async_computation.1 | async-start | bytes 4456448 | tf_op jit(solution)/shard_map/all_gather | solution.py:480
  27.4 24.3 %collective-permute-start = (bf16[128,4096]{1,0:T(8,128)(2,1)}, bf16[128,4096]{1,0:T(8,128)(2,1)S(1)}, u32[]{:S(2)}, u32[]{:S(2)}) collective-permute-start(bf16[128,4096]{1,0:T(8,128)(2,1)} %param.8), channel_id=1, source_target_pairs={{0,0},{1,1},{2,2},{3,3},{4,8},{5,9},{6,10},{7,11},{8,4},{9,5},{10,... | collective-permute-start | bytes 3145736 | tf_op jit(solution)/shard_map/ppermute | solution.py:33
  29.9 14.9 %collective-permute-start.4 = (bf16[256,128]{1,0:T(8,128)(2,1)S(1)}, bf16[256,128]{1,0:T(8,128)(2,1)S(1)}, u32[]{:S(2)}, u32[]{:S(2)}) collective-permute-start(bf16[256,128]{1,0:T(8,128)(2,1)S(1)} %copy-done.19), channel_id=1, source_target_pairs={{0,0},{1,1},{2,2},{3,3},{4,8},{5,9},{6,10},{7,11},{8,4},{9,5},{10,... | collective-permute-start | bytes 196616 | tf_op jit(solution)/shard_map/ppermute | solution.py:33
  44.8 12.6 %collective-permute-start.5 = (bf16[256,128]{1,0:T(8,128)(2,1)S(1)}, bf16[256,128]{1,0:T(8,128)(2,1)S(1)}, u32[]{:S(2)}, u32[]{:S(2)}) collective-permute-start(bf16[256,128]{1,0:T(8,128)(2,1)S(1)} %collective-permute-done.4), channel_id=1, source_target_pairs={{0,128},{1,129},{2,130},{3,131},{4,132},{5,133},{6,134},{7,135},{8... | collective-permute-start | bytes 196616 | tf_op jit(solution)/shard_map/ppermute | solution.py:33
  51.7 1.2 copy-start
  52.9 25.1 %collective-permute-start.1 = (bf16[128,4096]{1,0:T(8,128)(2,1)S(1)}, bf16[128,4096]{1,0:T(8,128)(2,1)S(1)}, u32[]{:S(2)}, u32[]{:S(2)}) collective-permute-start(bf16[128,4096]{1,0:T(8,128)(2,1)S(1)} %fusion.5.refs_0_), channel_id=1, source_target_pairs={{0,1},{1,2},{2,3},{3,0},{4,5},{5,6},{6,7},{7,4},{8,9},{9,10},{10,1... | collective-permute-start | bytes 3145736 | tf_op jit(solution)/shard_map/ppermute | solution.py:33
  54.3 23.8 %collective-permute-start.2 = (bf16[128,4096]{1,0:T(8,128)(2,1)S(1)}, bf16[128,4096]{1,0:T(8,128)(2,1)}, u32[]{:S(2)}, u32[]{:S(2)}) collective-permute-start(bf16[128,4096]{1,0:T(8,128)(2,1)S(1)} %fusion.5.refs_0_), channel_id=1, source_target_pairs={{0,3},{1,0},{2,1},{3,2},{4,7},{5,4},{6,5},{7,6},{8,11},{9,8},{10,9... | collective-permute-start | bytes 3145736 | tf_op jit(solution)/shard_map/ppermute | solution.py:33
  55.8 33.2 %collective-permute-start.3 = (bf16[128,4096]{1,0:T(8,128)(2,1)S(1)}, bf16[128,4096]{1,0:T(8,128)(2,1)}, u32[]{:S(2)}, u32[]{:S(2)}) collective-permute-start(bf16[128,4096]{1,0:T(8,128)(2,1)S(1)} %fusion.5.refs_0_), channel_id=1, source_target_pairs={{0,2},{1,3},{2,0},{3,1},{4,6},{5,7},{6,4},{7,5},{8,10},{9,11},{10,... | collective-permute-start | bytes 3145736 | tf_op jit(solution)/shard_map/ppermute | solution.py:33
  57.4 8.6 %collective-permute-start.6 = (bf16[2,256,128]{2,1,0:T(8,128)(2,1)S(1)}, bf16[2,256,128]{2,1,0:T(8,128)(2,1)S(1)}, u32[]{:S(2)}, u32[]{:S(2)}) collective-permute-start(bf16[2,256,128]{2,1,0:T(8,128)(2,1)S(1)} %shard_map.95), channel_id=1, source_target_pairs={{0,32},{1,33},{2,34},{3,35},{4,36},{5,37},{6,38},{7,39},{8,40},{9,... | collective-permute-start | bytes 393224 | tf_op jit(solution)/shard_map/ppermute | solution.py:33
  58.2 7.9 %collective-permute-start.7 = (bf16[2,256,128]{2,1,0:T(8,128)(2,1)S(1)}, bf16[2,256,128]{2,1,0:T(8,128)(2,1)S(1)}, u32[]{:S(2)}, u32[]{:S(2)}) collective-permute-start(bf16[2,256,128]{2,1,0:T(8,128)(2,1)S(1)} %shard_map.95), channel_id=1, source_target_pairs={{0,224},{1,225},{2,226},{3,227},{4,228},{5,229},{6,230},{7,231},{8... | collective-permute-start | bytes 393224 | tf_op jit(solution)/shard_map/ppermute | solution.py:33
  66.1 9.1 %collective-permute-start.8 = (bf16[2,256,128]{2,1,0:T(8,128)(2,1)S(1)}, bf16[2,256,128]{2,1,0:T(8,128)(2,1)S(1)}, u32[]{:S(2)}, u32[]{:S(2)}) collective-permute-start(bf16[2,256,128]{2,1,0:T(8,128)(2,1)S(1)} %shard_map.95), channel_id=1, source_target_pairs={{0,64},{1,65},{2,66},{3,67},{4,68},{5,69},{6,70},{7,71},{8,72},{9,... | collective-permute-start | bytes 393224 | tf_op jit(solution)/shard_map/ppermute | solution.py:33
  75.2 14.3 %collective-permute-start.9 = (bf16[128,4096]{1,0:T(8,128)(2,1)S(1)}, bf16[128,4096]{1,0:T(8,128)(2,1)S(1)}, u32[]{:S(2)}, u32[]{:S(2)}) collective-permute-start(bf16[128,4096]{1,0:T(8,128)(2,1)S(1)} %fusion.5.refs_0_), channel_id=1, source_target_pairs={{0,8},{1,9},{2,10},{3,11},{4,12},{5,13},{6,14},{7,15},{8,0},{9,1},... | collective-permute-start | bytes 3145736 | tf_op jit(solution)/shard_map/ppermute | solution.py:33
  89.0 4.1 %collective-permute-start.10 = (bf16[128,4096]{1,0:T(8,128)(2,1)S(1)}, bf16[128,4096]{1,0:T(8,128)(2,1)S(1)}, u32[]{:S(2)}, u32[]{:S(2)}) collective-permute-start(bf16[128,4096]{1,0:T(8,128)(2,1)S(1)} %get-tuple-element.27.refs_1_), channel_id=1, source_target_pairs={{0,8},{1,9},{2,10},{3,11},{4,12},{5,13},{6,14},{7,15},{8,0},{9,1},... | collective-permute-start | bytes 3145736 | tf_op jit(solution)/shard_map/ppermute | solution.py:33
  89.0 4.4 %collective-permute-start.11 = (bf16[128,4096]{1,0:T(8,128)(2,1)}, bf16[128,4096]{1,0:T(8,128)(2,1)S(1)}, u32[]{:S(2)}, u32[]{:S(2)}) collective-permute-start(bf16[128,4096]{1,0:T(8,128)(2,1)} %get-tuple-element.28.refs_2_), channel_id=1, source_target_pairs={{0,8},{1,9},{2,10},{3,11},{4,12},{5,13},{6,14},{7,15},{8,0},{9,1},... | collective-permute-start | bytes 3145736 | tf_op jit(solution)/shard_map/ppermute | solution.py:33
  89.5 5.4 %collective-permute-start.12 = (bf16[128,4096]{1,0:T(8,128)(2,1)}, bf16[128,4096]{1,0:T(8,128)(2,1)S(1)}, u32[]{:S(2)}, u32[]{:S(2)}) collective-permute-start(bf16[128,4096]{1,0:T(8,128)(2,1)} %get-tuple-element.29.refs_3_), channel_id=1, source_target_pairs={{0,8},{1,9},{2,10},{3,11},{4,12},{5,13},{6,14},{7,15},{8,0},{9,1},... | collective-permute-start | bytes 3145736 | tf_op jit(solution)/shard_map/ppermute | solution.py:33
  94.9 1.0 copy-start.10
  95.9 1.0 copy-start.11
  96.9 1.0 copy-start.12
  97.9 1.0 copy-start.13
  98.9 11.7 %copy-start.2 = (bf16[128,4096]{1,0:T(8,128)(2,1)}, bf16[128,4096]{1,0:T(8,128)(2,1)S(1)}, u32[]{:S(2)}) copy-start(bf16[128,4096]{1,0:T(8,128)(2,1)S(1)} %get-tuple-element.30.refs_0_.refs_1_) | copy-start | bytes 3145732
  98.9 11.7 %copy-start.6 = (bf16[128,4096]{1,0:T(8,128)(2,1)}, bf16[128,4096]{1,0:T(8,128)(2,1)S(1)}, u32[]{:S(2)}) copy-start(bf16[128,4096]{1,0:T(8,128)(2,1)S(1)} %get-tuple-element.31.refs_1_) | copy-start | bytes 3145732
  98.9 6.3 %collective-permute-start.24 = (bf16[128,512]{1,0:T(8,128)(2,1)S(1)}, bf16[128,512]{1,0:T(8,128)(2,1)S(1)}, u32[]{:S(2)}, u32[]{:S(2)}) collective-permute-start(bf16[128,512]{1,0:T(8,128)(2,1)S(1)} %shard_map.101), channel_id=1, source_target_pairs={{0,20},{1,21},{2,22},{3,23},{4,16},{5,17},{6,18},{7,19},{8,28},{9,... | collective-permute-start | bytes 393224 | tf_op jit(solution)/shard_map/ppermute | solution.py:33
  106.0 14.8 %collective-permute-start.17 = (bf16[8,256,128]{2,1,0:T(8,128)(2,1)S(1)}, bf16[8,256,128]{2,1,0:T(8,128)(2,1)S(1)}, u32[]{:S(2)}, u32[]{:S(2)}) collective-permute-start(bf16[8,256,128]{2,1,0:T(8,128)(2,1)S(1)} %get-tuple-element.38), channel_id=1, source_target_pairs={{0,4},{1,5},{2,6},{3,7},{4,16},{5,17},{6,18},{7,19},{8,12},{9,13},... | collective-permute-start | bytes 1572872 | tf_op jit(solution)/shard_map/ppermute | solution.py:33
  106.1 15.7 %collective-permute-start.18 = (bf16[8,256,128]{2,1,0:T(8,128)(2,1)S(1)}, bf16[8,256,128]{2,1,0:T(8,128)(2,1)S(1)}, u32[]{:S(2)}, u32[]{:S(2)}) collective-permute-start(bf16[8,256,128]{2,1,0:T(8,128)(2,1)S(1)} %get-tuple-element.38), channel_id=1, source_target_pairs={{0,20},{1,21},{2,22},{3,23},{4,0},{5,1},{6,2},{7,3},{8,28},{9,29},... | collective-permute-start | bytes 1572872 | tf_op jit(solution)/shard_map/ppermute | solution.py:33
  108.7 21.4 %collective-permute-start.19 = (bf16[8,256,128]{2,1,0:T(8,128)(2,1)S(1)}, bf16[8,256,128]{2,1,0:T(8,128)(2,1)S(1)}, u32[]{:S(2)}, u32[]{:S(2)}) collective-permute-start(bf16[8,256,128]{2,1,0:T(8,128)(2,1)S(1)} %get-tuple-element.38), channel_id=1, source_target_pairs={{0,16},{1,17},{2,18},{3,19},{4,20},{5,21},{6,22},{7,23},{8,24},{9,... | collective-permute-start | bytes 1572872 | tf_op jit(solution)/shard_map/ppermute | solution.py:33
  131.1 21.3 %collective-permute-start.21 = (bf16[8,4,256,128]{3,2,1,0:T(8,128)(2,1)}, bf16[8,4,256,128]{3,2,1,0:T(8,128)(2,1)S(1)}, u32[]{:S(2)}, u32[]{:S(2)}) collective-permute-start(bf16[8,4,256,128]{3,2,1,0:T(8,128)(2,1)} %bitcast_dynamic-update-slice_fusion.refs_9_), channel_id=1, source_target_pairs={{0,8},{1,9},{2,10},{3,11},{4,12},{5,13},{6,14},{7,15},{8,0},{9,1},... | collective-permute-start | bytes 6291464 | tf_op jit(solution)/shard_map/ppermute | solution.py:33
  152.3 1.8 collective-permute-start.20
  152.4 7.3 %copy-start.8 = (bf16[8,4,256,128]{3,2,1,0:T(8,128)(2,1)}, bf16[8,4,256,128]{3,2,1,0:T(8,128)(2,1)S(1)}, u32[]{:S(2)}) copy-start(bf16[8,4,256,128]{3,2,1,0:T(8,128)(2,1)S(1)} %collective-permute-done.21) | copy-start | bytes 6291460
  154.1 1.0 copy-start.14
  155.1 7.3 %copy-start.15 = (bf16[512,256]{1,0:T(8,128)(2,1)S(1)}, bf16[512,256]{1,0:T(8,128)(2,1)}, u32[]{:S(2)}) copy-start(bf16[512,256]{1,0:T(8,128)(2,1)} %get-tuple-element.39.mine) | copy-start | bytes 786436
  159.7 31.7 %collective-permute-start.22 = (bf16[128,4096]{1,0:T(8,128)(2,1)}, bf16[128,4096]{1,0:T(8,128)(2,1)S(1)}, u32[]{:S(2)}, u32[]{:S(2)}) collective-permute-start(bf16[128,4096]{1,0:T(8,128)(2,1)} %get-tuple-element.41.refs_0_.up), channel_id=1, source_target_pairs={{0,1},{1,2},{2,3},{3,0},{4,5},{5,6},{6,7},{7,4},{8,9},{9,10},{10,1... | collective-permute-start | bytes 3145736 | tf_op jit(solution)/shard_map/ppermute | solution.py:33
  161.2 30.3 %collective-permute-start.23 = (bf16[128,4096]{1,0:T(8,128)(2,1)}, bf16[128,4096]{1,0:T(8,128)(2,1)S(1)}, u32[]{:S(2)}, u32[]{:S(2)}) collective-permute-start(bf16[128,4096]{1,0:T(8,128)(2,1)} %get-tuple-element.45.down), channel_id=1, source_target_pairs={{0,3},{1,0},{2,1},{3,2},{4,7},{5,4},{6,5},{7,6},{8,11},{9,8},{10,9... | collective-permute-start | bytes 3145736 | tf_op jit(solution)/shard_map/ppermute | solution.py:33
  162.4 1.6 copy-start.9
  167.6 1.3 copy-start.3
  174.9 31.1 %copy-start.1 = (bf16[128,4096]{1,0:T(8,128)(2,1)S(1)}, bf16[128,4096]{1,0:T(8,128)(2,1)}, u32[]{:S(2)}) copy-start(bf16[128,4096]{1,0:T(8,128)(2,1)} %copy-done) | copy-start | bytes 3145732
  174.9 31.1 %copy-start.4 = (f32[128,4096]{1,0:T(8,128)S(1)}, f32[128,4096]{1,0:T(8,128)}, u32[]{:S(2)}) copy-start(f32[128,4096]{1,0:T(8,128)} %copy-done.3) | copy-start | bytes 6291460
  174.9 14.2 %collective-permute-start.27 = (bf16[128,512]{1,0:T(8,128)(2,1)S(1)}, bf16[128,512]{1,0:T(8,128)(2,1)S(1)}, u32[]{:S(2)}, u32[]{:S(2)}) collective-permute-start(bf16[128,512]{1,0:T(8,128)(2,1)S(1)} %get-tuple-element.49), channel_id=1, source_target_pairs={{0,2},{1,3},{2,0},{3,1},{4,6},{5,7},{6,4},{7,5},{8,10},{9,11},{10,... | collective-permute-start | bytes 393224 | tf_op jit(solution)/shard_map/ppermute | solution.py:33
  175.9 15.5 %collective-permute-start.26 = (bf16[128,512]{1,0:T(8,128)(2,1)S(1)}, bf16[128,512]{1,0:T(8,128)(2,1)S(1)}, u32[]{:S(2)}, u32[]{:S(2)}) collective-permute-start(bf16[128,512]{1,0:T(8,128)(2,1)S(1)} %get-tuple-element.48), channel_id=1, source_target_pairs={{0,1},{1,2},{2,3},{3,0},{4,5},{5,6},{6,7},{7,4},{8,9},{9,10},{10,1... | collective-permute-start | bytes 393224 | tf_op jit(solution)/shard_map/ppermute | solution.py:33
  176.6 14.8 %collective-permute-start.25 = (bf16[128,512]{1,0:T(8,128)(2,1)S(1)}, bf16[128,512]{1,0:T(8,128)(2,1)S(1)}, u32[]{:S(2)}, u32[]{:S(2)}) collective-permute-start(bf16[128,512]{1,0:T(8,128)(2,1)S(1)} %get-tuple-element.47), channel_id=1, source_target_pairs={{0,3},{1,0},{2,1},{3,2},{4,7},{5,4},{6,5},{7,6},{8,11},{9,8},{10,9... | collective-permute-start | bytes 393224 | tf_op jit(solution)/shard_map/ppermute | solution.py:33
  192.1 13.9 %collective-permute-start.28 = (bf16[64,4096]{1,0:T(8,128)(2,1)S(1)}, bf16[64,4096]{1,0:T(8,128)(2,1)S(1)}, u32[]{:S(2)}, u32[]{:S(2)}) collective-permute-start(bf16[64,4096]{1,0:T(8,128)(2,1)S(1)} %get-tuple-element.50), channel_id=1, source_target_pairs={{0,1},{1,2},{2,3},{3,0},{4,5},{5,6},{6,7},{7,4},{8,9},{9,10},{10,1... | collective-permute-start | bytes 1572872 | tf_op jit(solution)/shard_map/ppermute | solution.py:33
  192.4 28.6 %copy-start.7 = (bf16[512,512]{1,0:T(8,128)(2,1)S(1)}, bf16[512,512]{1,0:T(8,128)(2,1)}, u32[]{:S(2)}) copy-start(bf16[512,512]{1,0:T(8,128)(2,1)} %refs_2_.1) | copy-start | bytes 1572868
  192.4 13.6 %collective-permute-start.29 = (bf16[64,4096]{1,0:T(8,128)(2,1)S(1)}, bf16[64,4096]{1,0:T(8,128)(2,1)S(1)}, u32[]{:S(2)}, u32[]{:S(2)}) collective-permute-start(bf16[64,4096]{1,0:T(8,128)(2,1)S(1)} %get-tuple-element.51), channel_id=1, source_target_pairs={{0,3},{1,0},{2,1},{3,2},{4,7},{5,4},{6,5},{7,6},{8,11},{9,8},{10,9... | collective-permute-start | bytes 1572872 | tf_op jit(solution)/shard_map/ppermute | solution.py:33
  194.8 8.5 %collective-permute-start.31 = (bf16[128,512]{1,0:T(8,128)(2,1)S(1)}, bf16[128,512]{1,0:T(8,128)(2,1)S(1)}, u32[]{:S(2)}, u32[]{:S(2)}) collective-permute-start(bf16[128,512]{1,0:T(8,128)(2,1)S(1)} %add_convert_fusion._.refs_0_), channel_id=1, source_target_pairs={{0,128},{1,129},{2,130},{3,131},{4,132},{5,133},{6,134},{7,135},{8... | collective-permute-start | bytes 393224 | tf_op jit(solution)/shard_map/ppermute | solution.py:33
  203.3 9.6 %collective-permute-start.32 = (bf16[128,512]{1,0:T(8,128)(2,1)S(1)}, bf16[128,512]{1,0:T(8,128)(2,1)S(1)}, u32[]{:S(2)}, u32[]{:S(2)}) collective-permute-start(bf16[128,512]{1,0:T(8,128)(2,1)S(1)} %collective-permute-done.31), channel_id=1, source_target_pairs={{0,1},{1,2},{2,3},{3,0},{4,5},{5,6},{6,7},{7,4},{8,9},{9,10},{10,1... | collective-permute-start | bytes 393224 | tf_op jit(solution)/shard_map/ppermute | solution.py:33
  203.3 9.6 %collective-permute-start.33 = (bf16[128,512]{1,0:T(8,128)(2,1)S(1)}, bf16[128,512]{1,0:T(8,128)(2,1)S(1)}, u32[]{:S(2)}, u32[]{:S(2)}) collective-permute-start(bf16[128,512]{1,0:T(8,128)(2,1)S(1)} %collective-permute-done.31), channel_id=1, source_target_pairs={{0,3},{1,0},{2,1},{3,2},{4,7},{5,4},{6,5},{7,6},{8,11},{9,8},{10,9... | collective-permute-start | bytes 393224 | tf_op jit(solution)/shard_map/ppermute | solution.py:33
  206.0 15.0 %copy-start.5 = (bf16[512,1536]{1,0:T(8,128)(2,1)S(1)}, bf16[512,1536]{1,0:T(8,128)(2,1)}, u32[]{:S(2)}) copy-start(bf16[512,1536]{1,0:T(8,128)(2,1)} %refs_1_.1) | copy-start | bytes 4718596
  207.1 24.4 %collective-permute-start.30 = (bf16[128,4096]{1,0:T(8,128)(2,1)S(1)}, bf16[128,4096]{1,0:T(8,128)(2,1)S(1)}, u32[]{:S(2)}, u32[]{:S(2)}) collective-permute-start(bf16[128,4096]{1,0:T(8,128)(2,1)S(1)} %shard_map.104), channel_id=1, source_target_pairs={{0,0},{1,1},{2,2},{3,3},{4,8},{5,9},{6,10},{7,11},{8,4},{9,5},{10,... | collective-permute-start | bytes 3145736 | tf_op jit(solution)/shard_map/ppermute | solution.py:33
  211.9 6.6 %collective-permute-start.34 = (bf16[128,512]{1,0:T(8,128)(2,1)S(1)}, bf16[128,512]{1,0:T(8,128)(2,1)S(1)}, u32[]{:S(2)}, u32[]{:S(2)}) collective-permute-start(bf16[128,512]{1,0:T(8,128)(2,1)S(1)} %collective-permute-done.31), channel_id=1, source_target_pairs={{0,2},{1,3},{2,0},{3,1},{4,6},{5,7},{6,4},{7,5},{8,10},{9,11},{10,... | collective-permute-start | bytes 393224 | tf_op jit(solution)/shard_map/ppermute | solution.py:33
  218.5 2.5 %collective-permute-start.35 = (bf16[512,512]{1,0:T(8,128)(2,1)S(1)}, bf16[512,512]{1,0:T(8,128)(2,1)S(1)}, u32[]{:S(2)}, u32[]{:S(2)}) collective-permute-start(bf16[512,512]{1,0:T(8,128)(2,1)S(1)} %constant_dynamic-update-slice_fusion.refs_3_), channel_id=1, source_target_pairs={{0,8},{1,9},{2,10},{3,11},{4,12},{5,13},{6,14},{7,15},{8,0},{9,1},... | collective-permute-start | bytes 1572872 | tf_op jit(solution)/shard_map/ppermute | solution.py:33
  225.2 6.3 %collective-permute-start.36 = (bf16[128,512]{1,0:T(8,128)(2,1)S(1)}, bf16[128,512]{1,0:T(8,128)(2,1)S(1)}, u32[]{:S(2)}, u32[]{:S(2)}) collective-permute-start(bf16[128,512]{1,0:T(8,128)(2,1)S(1)} %shard_map.105), channel_id=1, source_target_pairs={{0,0},{1,1},{2,2},{3,3},{4,8},{5,9},{6,10},{7,11},{8,4},{9,5},{10,... | collective-permute-start | bytes 393224 | tf_op jit(solution)/shard_map/ppermute | solution.py:33
Sparse Core Ops, SparseCore 0:
  27.5 83.6 all-gather.2
  113.0 41.2 all-gather.4

commit v8 on v7

--- a/solution.py
+++ b/solution.py
@@ -82,15 +82,6 @@
     return whole.reshape((8,) + block.shape)
 
 
-def gathered_x(block, x, axis):
-    whole = jnp.zeros(block.shape[:axis] + (4,) + block.shape[axis:], block.dtype)
-    for k, part in [(0, block)] + [(k, moved(block, along_x(k))) for k in DISTANCES]:
-        at = [0] * whole.ndim
-        at[axis] = (x - k) % 4
-        whole = lax.dynamic_update_slice(whole, jnp.expand_dims(part, axis), at)
-    return whole
-
-
 def layer_norm(rows_in, norm_gain, norm_bias):
     values = rows_in.astype(jnp.float32)
     center = jnp.mean(values, axis=-1, keepdims=True)
@@ -163,7 +154,7 @@
 
 
 def attention_kernel(*refs):
-    *pieces, weight, _, own, other, held, held_weight, total, projected, sems = refs
+    *pieces, weight, own, other, held, held_weight, total, projected, sems = refs
     depth = held.shape[1] // PARTS
     block = weight.shape[3]
     copies = []
@@ -223,7 +214,7 @@
                 )
 
 
-def attention(pieces, weight, earlier):
+def attention(pieces, weight):
     count = sum(piece.shape[0] for piece in pieces)
     depth = pieces[0].shape[1]
     block = weight.shape[3]
@@ -235,7 +226,7 @@
         60,
         flops=2 * count * depth * columns,
         moved_bytes=2 * depth * (count + columns),
-        in_specs=[pl.BlockSpec(memory_space=pltpu.HBM)] * (len(pieces) + 2),
+        in_specs=[pl.BlockSpec(memory_space=pltpu.HBM)] * (len(pieces) + 1),
         out_specs=(pl.BlockSpec(memory_space=pltpu.VMEM),) * 2,
         scratch_shapes=[
             pltpu.VMEM((count, depth), jnp.bfloat16),
@@ -244,7 +235,7 @@
             pltpu.VMEM((count, columns), jnp.bfloat16),
             pltpu.SemaphoreType.DMA((PARTS, len(pieces) + 6)),
         ],
-    )(*pieces, weight, earlier)
+    )(*pieces, weight)
 
 
 def out_matrix(weight, other_weight):
@@ -465,10 +456,15 @@
     pieces = [normed] + [moved(normed, along_y(k)) for k in DISTANCES]
     *pieces[1:], out_z = together(*pieces[1:], gathered_z(out_weight, z))
     pieces += [moved(piece, other_core) for piece in pieces]
-    out_own = gathered_x(out_z, x, 1)
+    out_parts = [moved(out_z, along_x(k)) for k in DISTANCES]
+    out_own = jnp.zeros((8, 4) + out_z.shape[1:], bf16)
+    out_own = lax.dynamic_update_slice(out_own, out_z[:, None], (0, x, 0, 0))
+    pieces = together(*pieces, flops=WAIT)
+    mine, theirs = attention(pieces, weights)
+    mine, *out_parts = together(mine, *out_parts)
+    for k, part in zip(DISTANCES, out_parts):
+        out_own = lax.dynamic_update_slice(out_own, part[:, None], (0, (x - k) % 4, 0, 0))
     out_other = moved(out_own, other_core)
-    pieces = together(*pieces, flops=WAIT)
-    mine, theirs = attention(pieces, weights, out_own)
 
     match_weight = after(match_weight, pieces[0])
     other_half = moved(match_weight, lambda p: {"xh": 1 - p["xh"], "xl": 1 - p["xl"]})

time: 240 us -> 227 us (0.946)
  waiting for transfers between devices: 111 us -> 98 us
    ppermute x37, waiting for transfers between devices: 110 us -> 98 us  [moved(): return lax.ppermute(block, AXES, route)]
  transfers between devices with their start and end apart: 39 -> 39, of which waited for: 20 -> 20; matrix products, arithmetic and copies ran while one was open for 3% -> 4% of each run, Pallas kernels for 15% -> 16%
where the time goes in v8:
time: 227 us; the launch traced here: 226 us
  waiting for transfers between devices  98 us (43%)
  starting transfers between devices  57.1 us (25%)
  Pallas kernels  36.5 us (16%)
  local copies, waits for them, and re-layouts  17.8 us (8%)
  between operations  14.4 us (6%)
    ppermute x37, waiting for transfers between devices, moved(): return lax.ppermute(block, AXES, route)  98 us
    ppermute x37, starting transfers between devices, moved(): return lax.ppermute(block, AXES, route)  57.1 us
    pallas_call x1, Pallas kernels, attention(): local(attention_kernel, (result, result), 60, flops=2 * count * depth * c...  16.5 us
    unnamed x47, local copies, waits for them, and re-layouts  11.9 us
    pallas_call x2, Pallas kernels, terms(): local(functools.partial(terms_kernel, len(earlier), picked), tuple((jax.S...  8.19 us
    pallas_call x1, Pallas kernels, descriptor_terms(): local(descriptor_kernel, (jax.ShapeDtypeStruct((rows, width), f32),) + (j...  5.95 us
  transfers between devices with their start and end apart: 39, of which 20 were waited for; matrix products, arithmetic and copies ran while one was open for 4% of the time, Pallas kernels for 16%

profile of v8, /device:TPU:1, one launch (start us, length us, event | category | flops | bytes accessed | tf_op | source)
XLA Modules:
  0.0 226.1 jit_solution(14624140911536576332)
XLA Ops:
  7.2 0.9 copy.102.refs_0_
  8.1 1.1 copy.60
  9.4 4.5 %collective-permute-start.13 = (bf16[768,128]{1,0:T(8,128)(2,1)S(1)}, bf16[768,128]{1,0:T(8,128)(2,1)S(1)}, u32[]{:S(2)}, u32[]{:S(2)}) collective-permute-start(bf16[768,128]{1,0:T(8,128)(2,1)S(1)} %bitcast.63), channel_id=1, source_target_pairs={{0,0},{1,1},{2,2},{3,3},{4,8},{5,9},{6,10},{7,11},{8,4},{9,5},{10,... | collective-permute-start | bytes 589832 | tf_op jit(solution)/shard_map/ppermute | solution.py:33
  14.4 4.4 %collective-permute-start.16 = (bf16[768,128]{1,0:T(8,128)(2,1)S(1)}, bf16[768,128]{1,0:T(8,128)(2,1)S(1)}, u32[]{:S(2)}, u32[]{:S(2)}) collective-permute-start(bf16[768,128]{1,0:T(8,128)(2,1)S(1)} %bitcast.66), channel_id=1, source_target_pairs={{0,16},{1,17},{2,18},{3,19},{4,24},{5,25},{6,26},{7,27},{8,20},{9,... | collective-permute-start | bytes 589832 | tf_op jit(solution)/shard_map/ppermute | solution.py:33
  19.0 3.2 %collective-permute-done.14 = bf16[768,128]{1,0:T(8,128)(2,1)S(1)} collective-permute-done((bf16[768,128]{1,0:T(8,128)(2,1)S(1)}, bf16[768,128]{1,0:T(8,128)(2,1)S(1)}, u32[]{:S(2)}, u32[]{:S(2)}) %collective-permute-start.14) | collective-permute-done | bytes 196640 | tf_op jit(solution)/shard_map/ppermute | solution.py:33
  22.3 4.1 %collective-permute-done.16 = bf16[768,128]{1,0:T(8,128)(2,1)S(1)} collective-permute-done((bf16[768,128]{1,0:T(8,128)(2,1)S(1)}, bf16[768,128]{1,0:T(8,128)(2,1)S(1)}, u32[]{:S(2)}, u32[]{:S(2)}) %collective-permute-start.16) | collective-permute-done | bytes 196640 | tf_op jit(solution)/shard_map/ppermute | solution.py:33
  26.4 0.9 copy-done.15
  27.4 2.5 %collective-permute-start = (bf16[128,4096]{1,0:T(8,128)(2,1)}, bf16[128,4096]{1,0:T(8,128)(2,1)S(1)}, u32[]{:S(2)}, u32[]{:S(2)}) collective-permute-start(bf16[128,4096]{1,0:T(8,128)(2,1)} %param.8), channel_id=1, source_target_pairs={{0,0},{1,1},{2,2},{3,3},{4,8},{5,9},{6,10},{7,11},{8,4},{9,5},{10,... | collective-permute-start | bytes 3145736 | tf_op jit(solution)/shard_map/ppermute | solution.py:33
  29.9 3.1 %collective-permute-start.4 = (bf16[256,128]{1,0:T(8,128)(2,1)S(1)}, bf16[256,128]{1,0:T(8,128)(2,1)S(1)}, u32[]{:S(2)}, u32[]{:S(2)}) collective-permute-start(bf16[256,128]{1,0:T(8,128)(2,1)S(1)} %copy-done.19), channel_id=1, source_target_pairs={{0,0},{1,1},{2,2},{3,3},{4,8},{5,9},{6,10},{7,11},{8,4},{9,5},{10,... | collective-permute-start | bytes 196616 | tf_op jit(solution)/shard_map/ppermute | solution.py:33
  33.0 11.8 %collective-permute-done.4 = bf16[256,128]{1,0:T(8,128)(2,1)S(1)} collective-permute-done((bf16[256,128]{1,0:T(8,128)(2,1)S(1)}, bf16[256,128]{1,0:T(8,128)(2,1)S(1)}, u32[]{:S(2)}, u32[]{:S(2)}) %collective-permute-start.4) | collective-permute-done | bytes 65568 | tf_op jit(solution)/shard_map/ppermute | solution.py:33
  44.8 6.9 %collective-permute-start.5 = (bf16[256,128]{1,0:T(8,128)(2,1)S(1)}, bf16[256,128]{1,0:T(8,128)(2,1)S(1)}, u32[]{:S(2)}, u32[]{:S(2)}) collective-permute-start(bf16[256,128]{1,0:T(8,128)(2,1)S(1)} %collective-permute-done.4), channel_id=1, source_target_pairs={{0,128},{1,129},{2,130},{3,131},{4,132},{5,133},{6,134},{7,135},{8... | collective-permute-start | bytes 196616 | tf_op jit(solution)/shard_map/ppermute | solution.py:33
  52.9 1.4 collective-permute-start.1
  54.3 1.5 collective-permute-start.2
  55.8 1.6 collective-permute-start.3
  57.4 0.8 collective-permute-start.6
  58.2 1.9 collective-permute-start.7
  60.3 5.8 %collective-permute-done.6 = bf16[2,256,128]{2,1,0:T(8,128)(2,1)S(1)} collective-permute-done((bf16[2,256,128]{2,1,0:T(8,128)(2,1)S(1)}, bf16[2,256,128]{2,1,0:T(8,128)(2,1)S(1)}, u32[]{:S(2)}, u32[]{:S(2)}) %collective-permute-start.6) | collective-permute-done | bytes 131104 | tf_op jit(solution)/shard_map/ppermute | solution.py:33
  66.2 9.0 %collective-permute-done.8 = bf16[2,256,128]{2,1,0:T(8,128)(2,1)S(1)} collective-permute-done((bf16[2,256,128]{2,1,0:T(8,128)(2,1)S(1)}, bf16[2,256,128]{2,1,0:T(8,128)(2,1)S(1)}, u32[]{:S(2)}, u32[]{:S(2)}) %collective-permute-start.8) | collective-permute-done | bytes 131104 | tf_op jit(solution)/shard_map/ppermute | solution.py:33
  75.3 2.8 %collective-permute-done.1.refs_0_ = bf16[128,4096]{1,0:T(8,128)(2,1)S(1)} collective-permute-done((bf16[128,4096]{1,0:T(8,128)(2,1)S(1)}, bf16[128,4096]{1,0:T(8,128)(2,1)S(1)}, u32[]{:S(2)}, u32[]{:S(2)}) %collective-permute-start.1) | collective-permute-done | bytes 1048608 | tf_op jit(solution)/shard_map/ppermute | solution.py:33
  78.1 10.9 %collective-permute-done.3.refs_2_ = bf16[128,4096]{1,0:T(8,128)(2,1)} collective-permute-done((bf16[128,4096]{1,0:T(8,128)(2,1)S(1)}, bf16[128,4096]{1,0:T(8,128)(2,1)}, u32[]{:S(2)}, u32[]{:S(2)}) %collective-permute-start.3) | collective-permute-done | bytes 1048608 | tf_op jit(solution)/shard_map/ppermute | solution.py:33
  89.5 3.6 %collective-permute-done.10.refs_5_ = bf16[128,4096]{1,0:T(8,128)(2,1)S(1)} collective-permute-done((bf16[128,4096]{1,0:T(8,128)(2,1)S(1)}, bf16[128,4096]{1,0:T(8,128)(2,1)S(1)}, u32[]{:S(2)}, u32[]{:S(2)}) %collective-permute-start.10) | collective-permute-done | bytes 1048608 | tf_op jit(solution)/shard_map/ppermute | solution.py:33
  93.4 1.5 collective-permute-done.12.refs_7_
  94.9 1.0 copy-done.11
  95.9 1.0 copy-done.12
  96.9 1.0 copy-done.13
  97.9 1.0 copy-done.14
  98.9 6.3 %collective-permute-done.24 = bf16[128,512]{1,0:T(8,128)(2,1)S(1)} collective-permute-done((bf16[128,512]{1,0:T(8,128)(2,1)S(1)}, bf16[128,512]{1,0:T(8,128)(2,1)S(1)}, u32[]{:S(2)}, u32[]{:S(2)}) %collective-permute-start.24) | collective-permute-done | bytes 131104 | tf_op jit(solution)/shard_map/ppermute | solution.py:33
  105.2 0.8 maximum_select_fusion
  106.1 2.7 %collective-permute-start.18 = (bf16[8,256,128]{2,1,0:T(8,128)(2,1)S(1)}, bf16[8,256,128]{2,1,0:T(8,128)(2,1)S(1)}, u32[]{:S(2)}, u32[]{:S(2)}) collective-permute-start(bf16[8,256,128]{2,1,0:T(8,128)(2,1)S(1)} %get-tuple-element.43), channel_id=1, source_target_pairs={{0,20},{1,21},{2,22},{3,23},{4,0},{5,1},{6,2},{7,3},{8,28},{9,29},... | collective-permute-start | bytes 1572872 | tf_op jit(solution)/shard_map/ppermute | solution.py:33
  108.7 1.9 broadcast_in_dim.59
  110.6 0.9 bitcast_dynamic-update-slice_fusion.3
  111.5 16.5 %shard_map.98 = (bf16[512,256]{1,0:T(8,128)(2,1)}, bf16[512,256]{1,0:T(8,128)(2,1)}) custom-call(bf16[128,4096]{1,0:T(8,128)(2,1)} %copy-done.2, bf16[128,4096]{1,0:T(8,128)(2,1)} %copy-done.6, bf16[128,4096]{1,0:T(8,128)(2,1)} %get-tuple-element.36.refs_2_, bf16[128,4096]{1,0:T(8,128)(2,1)} %get-tuple-element.37.refs_3_, bf16[128,4096]{1,0:T(8,128)(2,1)} %copy-done.11, ...), custom_call_target="tpu_custom_call" | custom-call | flops 6442450944 | bytes 14680064 | tf_op jit(solution)/shard_map/pallas_call | solution.py:223
  128.0 2.1 collective-permute-done.19.refs_3_
  130.2 0.9 copy-done.8
  131.1 0.9 bitcast_dynamic-update-slice_fusion.2
  132.0 0.9 bitcast_dynamic-update-slice_fusion.1
  132.9 0.9 bitcast_dynamic-update-slice_fusion
  133.8 2.7 %collective-permute-start.21 = (bf16[8,4,256,128]{3,2,1,0:T(8,128)(2,1)}, bf16[8,4,256,128]{3,2,1,0:T(8,128)(2,1)S(1)}, u32[]{:S(2)}, u32[]{:S(2)}) collective-permute-start(bf16[8,4,256,128]{3,2,1,0:T(8,128)(2,1)} %bitcast_dynamic-update-slice_fusion), channel_id=1, source_target_pairs={{0,8},{1,9},{2,10},{3,11},{4,12},{5,13},{6,14},{7,15},{8,0},{9,1},... | collective-permute-start | bytes 6291464 | tf_op jit(solution)/shard_map/ppermute | solution.py:33
  136.5 4.4 %collective-permute-done.20.theirs = bf16[512,256]{1,0:T(8,128)(2,1)S(1)} collective-permute-done((bf16[512,256]{1,0:T(8,128)(2,1)S(1)}, bf16[512,256]{1,0:T(8,128)(2,1)S(1)}, u32[]{:S(2)}, u32[]{:S(2)}) %collective-permute-start.20) | collective-permute-done | bytes 262176 | tf_op jit(solution)/shard_map/ppermute | solution.py:33
  141.0 4.6 %shard_map.100 = (bf16[128,4096]{1,0:T(8,128)(2,1)}, bf16[128,4096]{1,0:T(8,128)(2,1)}) custom-call(bf16[512,256]{1,0:T(8,128)(2,1)S(1)} %get-tuple-element.44.mine, bf16[512,256]{1,0:T(8,128)(2,1)S(1)} %collective-permute-done.20.theirs, bf16[8,4,2,128,128]{4,3,2,1,0:T(8,128)(2,1)} %bitcast.27.weight, bf16[8,4,2,128,128]{4,3,2,1,0:T(8,128)(2,1)S(1)} %bitcast.60), custom_call_target="tpu_custom_call" | custom-call | flops 2000000000 | bytes 8000000 | tf_op jit(solution)/shard_map/pallas_call | solution.py:280
  145.6 1.5 collective-permute-start.22
  147.1 1.2 collective-permute-start.23
  148.3 0.9 copy-done.10
  149.2 3.6 %shard_map.101 = (f32[128,4096]{1,0:T(8,128)S(1)}, bf16[64,4096]{1,0:T(8,128)(2,1)S(1)}, bf16[64,4096]{1,0:T(8,128)(2,1)S(1)}) custom-call(bf16[512,256]{1,0:T(8,128)(2,1)S(1)} %copy-done.10, bf16[512,256]{1,0:T(8,128)(2,1)S(1)} %collective-permute-done.20.theirs, bf16[8,4,2,128,128]{4,3,2,1,0:T(8,128)(2,1)} %bitcast.27.weight, ...), custom_call_target="tpu_custom_call" | custom-call | flops 2000000000 | bytes 8000000 | tf_op jit(solution)/shard_map/pallas_call | solution.py:280
  152.8 1.3 copy-done.3
  154.2 5.9 %shard_map.103 = (f32[128,512]{1,0:T(8,128)S(1)}, bf16[128,512]{1,0:T(8,128)(2,1)S(1)}, bf16[128,512]{1,0:T(8,128)(2,1)S(1)}, bf16[128,512]{1,0:T(8,128)(2,1)S(1)}) custom-call(bf16[128,4096]{1,0:T(8,128)(2,1)} %copy-done, f32[128,4096]{1,0:T(8,128)} %copy-done.3, bf16[128,4096]{1,0:T(8,128)(2,1)} %get-tuple-element.53.down, ...), custom_call_target="tpu_custom_call" | custom-call | flops 4000000000 | bytes 12000000 | tf_op jit(solution)/shard_map/pallas_call | solution.py:330
  160.2 2.7 %collective-permute-start.25 = (bf16[128,512]{1,0:T(8,128)(2,1)S(1)}, bf16[128,512]{1,0:T(8,128)(2,1)S(1)}, u32[]{:S(2)}, u32[]{:S(2)}) collective-permute-start(bf16[128,512]{1,0:T(8,128)(2,1)S(1)} %get-tuple-element.55), channel_id=1, source_target_pairs={{0,3},{1,0},{2,1},{3,2},{4,7},{5,4},{6,5},{7,6},{8,11},{9,8},{10,9... | collective-permute-start | bytes 393224 | tf_op jit(solution)/shard_map/ppermute | solution.py:33
  162.9 1.7 collective-permute-start.27
  164.6 9.5 %collective-permute-done.25 = bf16[128,512]{1,0:T(8,128)(2,1)S(1)} collective-permute-done((bf16[128,512]{1,0:T(8,128)(2,1)S(1)}, bf16[128,512]{1,0:T(8,128)(2,1)S(1)}, u32[]{:S(2)}, u32[]{:S(2)}) %collective-permute-start.25) | collective-permute-done | bytes 131104 | tf_op jit(solution)/shard_map/ppermute | solution.py:33
  174.2 3.3 %collective-permute-done.27 = bf16[128,512]{1,0:T(8,128)(2,1)S(1)} collective-permute-done((bf16[128,512]{1,0:T(8,128)(2,1)S(1)}, bf16[128,512]{1,0:T(8,128)(2,1)S(1)}, u32[]{:S(2)}, u32[]{:S(2)}) %collective-permute-start.27) | collective-permute-done | bytes 131104 | tf_op jit(solution)/shard_map/ppermute | solution.py:33
  177.6 0.6 shard_map.104
  178.2 0.6 collective-permute-start.28
  178.8 2.1 collective-permute-start.29
  180.9 8.5 %collective-permute-done.31 = bf16[128,512]{1,0:T(8,128)(2,1)S(1)} collective-permute-done((bf16[128,512]{1,0:T(8,128)(2,1)S(1)}, bf16[128,512]{1,0:T(8,128)(2,1)S(1)}, u32[]{:S(2)}, u32[]{:S(2)}) %collective-permute-start.31) | collective-permute-done | bytes 131104 | tf_op jit(solution)/shard_map/ppermute | solution.py:33
  189.4 2.7 %collective-permute-start.33 = (bf16[128,512]{1,0:T(8,128)(2,1)S(1)}, bf16[128,512]{1,0:T(8,128)(2,1)S(1)}, u32[]{:S(2)}, u32[]{:S(2)}) collective-permute-start(bf16[128,512]{1,0:T(8,128)(2,1)S(1)} %collective-permute-done.31), channel_id=1, source_target_pairs={{0,3},{1,0},{2,1},{3,2},{4,7},{5,4},{6,5},{7,6},{8,11},{9,8},{10,9... | collective-permute-start | bytes 393224 | tf_op jit(solution)/shard_map/ppermute | solution.py:33
  192.1 1.1 shard_map.105
  193.2 6.3 %collective-permute-start.30 = (bf16[128,4096]{1,0:T(8,128)(2,1)S(1)}, bf16[128,4096]{1,0:T(8,128)(2,1)S(1)}, u32[]{:S(2)}, u32[]{:S(2)}) collective-permute-start(bf16[128,4096]{1,0:T(8,128)(2,1)S(1)} %shard_map.105), channel_id=1, source_target_pairs={{0,0},{1,1},{2,2},{3,3},{4,8},{5,9},{6,10},{7,11},{8,4},{9,5},{10,... | collective-permute-start | bytes 3145736 | tf_op jit(solution)/shard_map/ppermute | solution.py:33
  199.7 5.4 %collective-permute-done.34 = bf16[128,512]{1,0:T(8,128)(2,1)S(1)} collective-permute-done((bf16[128,512]{1,0:T(8,128)(2,1)S(1)}, bf16[128,512]{1,0:T(8,128)(2,1)S(1)}, u32[]{:S(2)}, u32[]{:S(2)}) %collective-permute-start.34) | collective-permute-done | bytes 131104 | tf_op jit(solution)/shard_map/ppermute | solution.py:33
  205.2 1.9 collective-permute-done.35.refs_4_
  207.1 4.2 %shard_map.106 = bf16[128,512]{1,0:T(8,128)(2,1)S(1)} custom-call(bf16[128,512]{1,0:T(8,128)(2,1)S(1)} %add_convert_fusion._.refs_0_, bf16[512,1536]{1,0:T(8,128)(2,1)S(1)} %copy-done.5, bf16[512,512]{1,0:T(8,128)(2,1)S(1)} %copy-done.7, bf16[512,512]{1,0:T(8,128)(2,1)S(1)} %constant_dynamic-update-slice_fusion.refs_3_, ...), custom_call_target="tpu_custom_call" | custom-call | tf_op jit(solution)/shard_map/pallas_call | solution.py:421
  211.4 2.8 %collective-permute-start.36 = (bf16[128,512]{1,0:T(8,128)(2,1)S(1)}, bf16[128,512]{1,0:T(8,128)(2,1)S(1)}, u32[]{:S(2)}, u32[]{:S(2)}) collective-permute-start(bf16[128,512]{1,0:T(8,128)(2,1)S(1)} %shard_map.106), channel_id=1, source_target_pairs={{0,0},{1,1},{2,2},{3,3},{4,8},{5,9},{6,10},{7,11},{8,4},{9,5},{10,... | collective-permute-start | bytes 393224 | tf_op jit(solution)/shard_map/ppermute | solution.py:33
  214.2 3.4 %collective-permute-done.36 = bf16[128,512]{1,0:T(8,128)(2,1)S(1)} collective-permute-done((bf16[128,512]{1,0:T(8,128)(2,1)S(1)}, bf16[128,512]{1,0:T(8,128)(2,1)S(1)}, u32[]{:S(2)}, u32[]{:S(2)}) %collective-permute-start.36) | collective-permute-done | bytes 131104 | tf_op jit(solution)/shard_map/ppermute | solution.py:33
  217.7 1.0 copy.103
  218.6 0.7 copy.104
  (100 shorter events, 4.0 us)
Async XLA Ops:
  7.2 104.3 %all-gather.3.cloned.1.call-start = ((), (), s32[]{:S(2)}) async-start(), calls=%async_computation | async-start | bytes 7077888 | tf_op jit(solution)/shard_map/all_gather | solution.py:450
  8.1 21.8 %copy-start.19 = (bf16[256,128]{1,0:T(8,128)(2,1)S(1)}, bf16[256,128]{1,0:T(8,128)(2,1)}, u32[]{:S(2)}) copy-start(bf16[256,128]{1,0:T(8,128)(2,1)} %param.12) | copy-start | bytes 196612
  9.4 9.4 %collective-permute-start.13 = (bf16[768,128]{1,0:T(8,128)(2,1)S(1)}, bf16[768,128]{1,0:T(8,128)(2,1)S(1)}, u32[]{:S(2)}, u32[]{:S(2)}) collective-permute-start(bf16[768,128]{1,0:T(8,128)(2,1)S(1)} %bitcast.63), channel_id=1, source_target_pairs={{0,0},{1,1},{2,2},{3,3},{4,8},{5,9},{6,10},{7,11},{8,4},{9,5},{10,... | collective-permute-start | bytes 589832 | tf_op jit(solution)/shard_map/ppermute | solution.py:33
  13.9 8.3 %collective-permute-start.14 = (bf16[768,128]{1,0:T(8,128)(2,1)S(1)}, bf16[768,128]{1,0:T(8,128)(2,1)S(1)}, u32[]{:S(2)}, u32[]{:S(2)}) collective-permute-start(bf16[768,128]{1,0:T(8,128)(2,1)S(1)} %bitcast.64), channel_id=1, source_target_pairs={{0,4},{1,5},{2,6},{3,7},{4,12},{5,13},{6,14},{7,15},{8,16},{9,17},... | collective-permute-start | bytes 589832 | tf_op jit(solution)/shard_map/ppermute | solution.py:33
  14.3 8.0 %collective-permute-start.15 = (bf16[768,128]{1,0:T(8,128)(2,1)S(1)}, bf16[768,128]{1,0:T(8,128)(2,1)S(1)}, u32[]{:S(2)}, u32[]{:S(2)}) collective-permute-start(bf16[768,128]{1,0:T(8,128)(2,1)S(1)} %bitcast.65), channel_id=1, source_target_pairs={{0,20},{1,21},{2,22},{3,23},{4,28},{5,29},{6,30},{7,31},{8,0},{9,1... | collective-permute-start | bytes 589832 | tf_op jit(solution)/shard_map/ppermute | solution.py:33
  14.4 12.0 %collective-permute-start.16 = (bf16[768,128]{1,0:T(8,128)(2,1)S(1)}, bf16[768,128]{1,0:T(8,128)(2,1)S(1)}, u32[]{:S(2)}, u32[]{:S(2)}) collective-permute-start(bf16[768,128]{1,0:T(8,128)(2,1)S(1)} %bitcast.66), channel_id=1, source_target_pairs={{0,16},{1,17},{2,18},{3,19},{4,24},{5,25},{6,26},{7,27},{8,20},{9,... | collective-permute-start | bytes 589832 | tf_op jit(solution)/shard_map/ppermute | solution.py:33
  19.0 33.5 %copy-start.16 = (f32[4096]{0:T(1024)S(1)}, f32[4096]{0:T(1024)}, u32[]{:S(2)}) copy-start(f32[4096]{0:T(1024)} %param.10) | copy-start | bytes 49156
  19.0 33.5 %copy-start.17 = (f32[4096]{0:T(1024)S(1)}, f32[4096]{0:T(1024)}, u32[]{:S(2)}) copy-start(f32[4096]{0:T(1024)} %param.9) | copy-start | bytes 49156
  26.4 0.9 copy-start.15
  27.4 126.8 %all-gather.5.cloned.1.call-start = ((), (), s32[]{:S(2)}) async-start(), calls=%async_computation.1 | async-start | bytes 4456448 | tf_op jit(solution)/shard_map/all_gather | solution.py:476
  27.4 24.3 %collective-permute-start = (bf16[128,4096]{1,0:T(8,128)(2,1)}, bf16[128,4096]{1,0:T(8,128)(2,1)S(1)}, u32[]{:S(2)}, u32[]{:S(2)}) collective-permute-start(bf16[128,4096]{1,0:T(8,128)(2,1)} %param.8), channel_id=1, source_target_pairs={{0,0},{1,1},{2,2},{3,3},{4,8},{5,9},{6,10},{7,11},{8,4},{9,5},{10,... | collective-permute-start | bytes 3145736 | tf_op jit(solution)/shard_map/ppermute | solution.py:33
  29.9 14.9 %collective-permute-start.4 = (bf16[256,128]{1,0:T(8,128)(2,1)S(1)}, bf16[256,128]{1,0:T(8,128)(2,1)S(1)}, u32[]{:S(2)}, u32[]{:S(2)}) collective-permute-start(bf16[256,128]{1,0:T(8,128)(2,1)S(1)} %copy-done.19), channel_id=1, source_target_pairs={{0,0},{1,1},{2,2},{3,3},{4,8},{5,9},{6,10},{7,11},{8,4},{9,5},{10,... | collective-permute-start | bytes 196616 | tf_op jit(solution)/shard_map/ppermute | solution.py:33
  44.8 12.6 %collective-permute-start.5 = (bf16[256,128]{1,0:T(8,128)(2,1)S(1)}, bf16[256,128]{1,0:T(8,128)(2,1)S(1)}, u32[]{:S(2)}, u32[]{:S(2)}) collective-permute-start(bf16[256,128]{1,0:T(8,128)(2,1)S(1)} %collective-permute-done.4), channel_id=1, source_target_pairs={{0,128},{1,129},{2,130},{3,131},{4,132},{5,133},{6,134},{7,135},{8... | collective-permute-start | bytes 196616 | tf_op jit(solution)/shard_map/ppermute | solution.py:33
  51.8 1.2 copy-start
  52.9 25.1 %collective-permute-start.1 = (bf16[128,4096]{1,0:T(8,128)(2,1)S(1)}, bf16[128,4096]{1,0:T(8,128)(2,1)S(1)}, u32[]{:S(2)}, u32[]{:S(2)}) collective-permute-start(bf16[128,4096]{1,0:T(8,128)(2,1)S(1)} %fusion.5.refs_0_), channel_id=1, source_target_pairs={{0,1},{1,2},{2,3},{3,0},{4,5},{5,6},{6,7},{7,4},{8,9},{9,10},{10,1... | collective-permute-start | bytes 3145736 | tf_op jit(solution)/shard_map/ppermute | solution.py:33
  54.3 23.8 %collective-permute-start.2 = (bf16[128,4096]{1,0:T(8,128)(2,1)S(1)}, bf16[128,4096]{1,0:T(8,128)(2,1)}, u32[]{:S(2)}, u32[]{:S(2)}) collective-permute-start(bf16[128,4096]{1,0:T(8,128)(2,1)S(1)} %fusion.5.refs_0_), channel_id=1, source_target_pairs={{0,3},{1,0},{2,1},{3,2},{4,7},{5,4},{6,5},{7,6},{8,11},{9,8},{10,9... | collective-permute-start | bytes 3145736 | tf_op jit(solution)/shard_map/ppermute | solution.py:33
  55.8 33.2 %collective-permute-start.3 = (bf16[128,4096]{1,0:T(8,128)(2,1)S(1)}, bf16[128,4096]{1,0:T(8,128)(2,1)}, u32[]{:S(2)}, u32[]{:S(2)}) collective-permute-start(bf16[128,4096]{1,0:T(8,128)(2,1)S(1)} %fusion.5.refs_0_), channel_id=1, source_target_pairs={{0,2},{1,3},{2,0},{3,1},{4,6},{5,7},{6,4},{7,5},{8,10},{9,11},{10,... | collective-permute-start | bytes 3145736 | tf_op jit(solution)/shard_map/ppermute | solution.py:33
  57.4 8.6 %collective-permute-start.6 = (bf16[2,256,128]{2,1,0:T(8,128)(2,1)S(1)}, bf16[2,256,128]{2,1,0:T(8,128)(2,1)S(1)}, u32[]{:S(2)}, u32[]{:S(2)}) collective-permute-start(bf16[2,256,128]{2,1,0:T(8,128)(2,1)S(1)} %shard_map.95), channel_id=1, source_target_pairs={{0,32},{1,33},{2,34},{3,35},{4,36},{5,37},{6,38},{7,39},{8,40},{9,... | collective-permute-start | bytes 393224 | tf_op jit(solution)/shard_map/ppermute | solution.py:33
  58.2 7.9 %collective-permute-start.7 = (bf16[2,256,128]{2,1,0:T(8,128)(2,1)S(1)}, bf16[2,256,128]{2,1,0:T(8,128)(2,1)S(1)}, u32[]{:S(2)}, u32[]{:S(2)}) collective-permute-start(bf16[2,256,128]{2,1,0:T(8,128)(2,1)S(1)} %shard_map.95), channel_id=1, source_target_pairs={{0,224},{1,225},{2,226},{3,227},{4,228},{5,229},{6,230},{7,231},{8... | collective-permute-start | bytes 393224 | tf_op jit(solution)/shard_map/ppermute | solution.py:33
  66.1 9.1 %collective-permute-start.8 = (bf16[2,256,128]{2,1,0:T(8,128)(2,1)S(1)}, bf16[2,256,128]{2,1,0:T(8,128)(2,1)S(1)}, u32[]{:S(2)}, u32[]{:S(2)}) collective-permute-start(bf16[2,256,128]{2,1,0:T(8,128)(2,1)S(1)} %shard_map.95), channel_id=1, source_target_pairs={{0,64},{1,65},{2,66},{3,67},{4,68},{5,69},{6,70},{7,71},{8,72},{9,... | collective-permute-start | bytes 393224 | tf_op jit(solution)/shard_map/ppermute | solution.py:33
  75.2 14.3 %collective-permute-start.9 = (bf16[128,4096]{1,0:T(8,128)(2,1)S(1)}, bf16[128,4096]{1,0:T(8,128)(2,1)S(1)}, u32[]{:S(2)}, u32[]{:S(2)}) collective-permute-start(bf16[128,4096]{1,0:T(8,128)(2,1)S(1)} %fusion.5.refs_0_), channel_id=1, source_target_pairs={{0,8},{1,9},{2,10},{3,11},{4,12},{5,13},{6,14},{7,15},{8,0},{9,1},... | collective-permute-start | bytes 3145736 | tf_op jit(solution)/shard_map/ppermute | solution.py:33
  89.0 4.1 %collective-permute-start.10 = (bf16[128,4096]{1,0:T(8,128)(2,1)S(1)}, bf16[128,4096]{1,0:T(8,128)(2,1)S(1)}, u32[]{:S(2)}, u32[]{:S(2)}) collective-permute-start(bf16[128,4096]{1,0:T(8,128)(2,1)S(1)} %get-tuple-element.31.refs_1_), channel_id=1, source_target_pairs={{0,8},{1,9},{2,10},{3,11},{4,12},{5,13},{6,14},{7,15},{8,0},{9,1},... | collective-permute-start | bytes 3145736 | tf_op jit(solution)/shard_map/ppermute | solution.py:33
  89.0 4.4 %collective-permute-start.11 = (bf16[128,4096]{1,0:T(8,128)(2,1)}, bf16[128,4096]{1,0:T(8,128)(2,1)S(1)}, u32[]{:S(2)}, u32[]{:S(2)}) collective-permute-start(bf16[128,4096]{1,0:T(8,128)(2,1)} %get-tuple-element.32.refs_2_), channel_id=1, source_target_pairs={{0,8},{1,9},{2,10},{3,11},{4,12},{5,13},{6,14},{7,15},{8,0},{9,1},... | collective-permute-start | bytes 3145736 | tf_op jit(solution)/shard_map/ppermute | solution.py:33
  89.5 5.4 %collective-permute-start.12 = (bf16[128,4096]{1,0:T(8,128)(2,1)}, bf16[128,4096]{1,0:T(8,128)(2,1)S(1)}, u32[]{:S(2)}, u32[]{:S(2)}) collective-permute-start(bf16[128,4096]{1,0:T(8,128)(2,1)} %get-tuple-element.33.refs_3_), channel_id=1, source_target_pairs={{0,8},{1,9},{2,10},{3,11},{4,12},{5,13},{6,14},{7,15},{8,0},{9,1},... | collective-permute-start | bytes 3145736 | tf_op jit(solution)/shard_map/ppermute | solution.py:33
  94.9 1.0 copy-start.11
  95.9 1.0 copy-start.12
  96.9 1.0 copy-start.13
  97.9 1.0 copy-start.14
  98.9 7.1 %copy-start.6 = (bf16[128,4096]{1,0:T(8,128)(2,1)}, bf16[128,4096]{1,0:T(8,128)(2,1)S(1)}, u32[]{:S(2)}) copy-start(bf16[128,4096]{1,0:T(8,128)(2,1)S(1)} %get-tuple-element.35.refs_1_) | copy-start | bytes 3145732
  98.9 11.7 %copy-start.2 = (bf16[128,4096]{1,0:T(8,128)(2,1)}, bf16[128,4096]{1,0:T(8,128)(2,1)S(1)}, u32[]{:S(2)}) copy-start(bf16[128,4096]{1,0:T(8,128)(2,1)S(1)} %get-tuple-element.34.refs_0_.refs_1_) | copy-start | bytes 3145732
  98.9 6.3 %collective-permute-start.24 = (bf16[128,512]{1,0:T(8,128)(2,1)S(1)}, bf16[128,512]{1,0:T(8,128)(2,1)S(1)}, u32[]{:S(2)}, u32[]{:S(2)}) collective-permute-start(bf16[128,512]{1,0:T(8,128)(2,1)S(1)} %shard_map.102), channel_id=1, source_target_pairs={{0,20},{1,21},{2,22},{3,23},{4,16},{5,17},{6,18},{7,19},{8,28},{9,... | collective-permute-start | bytes 393224 | tf_op jit(solution)/shard_map/ppermute | solution.py:33
  106.0 22.0 %collective-permute-start.17 = (bf16[8,256,128]{2,1,0:T(8,128)(2,1)S(1)}, bf16[8,256,128]{2,1,0:T(8,128)(2,1)S(1)}, u32[]{:S(2)}, u32[]{:S(2)}) collective-permute-start(bf16[8,256,128]{2,1,0:T(8,128)(2,1)S(1)} %get-tuple-element.43), channel_id=1, source_target_pairs={{0,4},{1,5},{2,6},{3,7},{4,16},{5,17},{6,18},{7,19},{8,12},{9,13},... | collective-permute-start | bytes 1572872 | tf_op jit(solution)/shard_map/ppermute | solution.py:33
  106.1 22.0 %collective-permute-start.18 = (bf16[8,256,128]{2,1,0:T(8,128)(2,1)S(1)}, bf16[8,256,128]{2,1,0:T(8,128)(2,1)S(1)}, u32[]{:S(2)}, u32[]{:S(2)}) collective-permute-start(bf16[8,256,128]{2,1,0:T(8,128)(2,1)S(1)} %get-tuple-element.43), channel_id=1, source_target_pairs={{0,20},{1,21},{2,22},{3,23},{4,0},{5,1},{6,2},{7,3},{8,28},{9,29},... | collective-permute-start | bytes 1572872 | tf_op jit(solution)/shard_map/ppermute | solution.py:33
  108.7 21.4 %collective-permute-start.19 = (bf16[8,256,128]{2,1,0:T(8,128)(2,1)S(1)}, bf16[8,256,128]{2,1,0:T(8,128)(2,1)S(1)}, u32[]{:S(2)}, u32[]{:S(2)}) collective-permute-start(bf16[8,256,128]{2,1,0:T(8,128)(2,1)S(1)} %get-tuple-element.43), channel_id=1, source_target_pairs={{0,16},{1,17},{2,18},{3,19},{4,20},{5,21},{6,22},{7,23},{8,24},{9,... | collective-permute-start | bytes 1572872 | tf_op jit(solution)/shard_map/ppermute | solution.py:33
  130.2 1.0 copy-start.8
  131.1 5.4 %copy-start.18 = (bf16[512,256]{1,0:T(8,128)(2,1)S(1)}, bf16[512,256]{1,0:T(8,128)(2,1)}, u32[]{:S(2)}) copy-start(bf16[512,256]{1,0:T(8,128)(2,1)} %get-tuple-element.45) | copy-start | bytes 786436
  131.1 14.5 %copy-start.9 = (bf16[512,256]{1,0:T(8,128)(2,1)}, bf16[512,256]{1,0:T(8,128)(2,1)S(1)}, u32[]{:S(2)}) copy-start(bf16[512,256]{1,0:T(8,128)(2,1)S(1)} %get-tuple-element.44.mine) | copy-start | bytes 786436
  133.8 7.2 %collective-permute-start.21 = (bf16[8,4,256,128]{3,2,1,0:T(8,128)(2,1)}, bf16[8,4,256,128]{3,2,1,0:T(8,128)(2,1)S(1)}, u32[]{:S(2)}, u32[]{:S(2)}) collective-permute-start(bf16[8,4,256,128]{3,2,1,0:T(8,128)(2,1)} %bitcast_dynamic-update-slice_fusion), channel_id=1, source_target_pairs={{0,8},{1,9},{2,10},{3,11},{4,12},{5,13},{6,14},{7,15},{8,0},{9,1},... | collective-permute-start | bytes 6291464 | tf_op jit(solution)/shard_map/ppermute | solution.py:33
  136.5 4.4 %collective-permute-start.20 = (bf16[512,256]{1,0:T(8,128)(2,1)S(1)}, bf16[512,256]{1,0:T(8,128)(2,1)S(1)}, u32[]{:S(2)}, u32[]{:S(2)}) collective-permute-start(bf16[512,256]{1,0:T(8,128)(2,1)S(1)} %copy-done.18), channel_id=1, source_target_pairs={{0,8},{1,9},{2,10},{3,11},{4,12},{5,13},{6,14},{7,15},{8,0},{9,1},... | collective-permute-start | bytes 786440 | tf_op jit(solution)/shard_map/ppermute | solution.py:33
  145.6 32.0 %collective-permute-start.22 = (bf16[128,4096]{1,0:T(8,128)(2,1)}, bf16[128,4096]{1,0:T(8,128)(2,1)S(1)}, u32[]{:S(2)}, u32[]{:S(2)}) collective-permute-start(bf16[128,4096]{1,0:T(8,128)(2,1)} %get-tuple-element.49.refs_0_.up), channel_id=1, source_target_pairs={{0,1},{1,2},{2,3},{3,0},{4,5},{5,6},{6,7},{7,4},{8,9},{9,10},{10,1... | collective-permute-start | bytes 3145736 | tf_op jit(solution)/shard_map/ppermute | solution.py:33
  147.1 30.5 %collective-permute-start.23 = (bf16[128,4096]{1,0:T(8,128)(2,1)}, bf16[128,4096]{1,0:T(8,128)(2,1)S(1)}, u32[]{:S(2)}, u32[]{:S(2)}) collective-permute-start(bf16[128,4096]{1,0:T(8,128)(2,1)} %get-tuple-element.53.down), channel_id=1, source_target_pairs={{0,3},{1,0},{2,1},{3,2},{4,7},{5,4},{6,5},{7,6},{8,11},{9,8},{10,9... | collective-permute-start | bytes 3145736 | tf_op jit(solution)/shard_map/ppermute | solution.py:33
  148.3 0.9 copy-start.10
  152.8 1.3 copy-start.3
  160.1 31.9 %copy-start.1 = (bf16[128,4096]{1,0:T(8,128)(2,1)S(1)}, bf16[128,4096]{1,0:T(8,128)(2,1)}, u32[]{:S(2)}) copy-start(bf16[128,4096]{1,0:T(8,128)(2,1)} %copy-done) | copy-start | bytes 3145732
  160.2 31.9 %copy-start.4 = (f32[128,4096]{1,0:T(8,128)S(1)}, f32[128,4096]{1,0:T(8,128)}, u32[]{:S(2)}) copy-start(f32[128,4096]{1,0:T(8,128)} %copy-done.3) | copy-start | bytes 6291460
  160.2 14.0 %collective-permute-start.25 = (bf16[128,512]{1,0:T(8,128)(2,1)S(1)}, bf16[128,512]{1,0:T(8,128)(2,1)S(1)}, u32[]{:S(2)}, u32[]{:S(2)}) collective-permute-start(bf16[128,512]{1,0:T(8,128)(2,1)S(1)} %get-tuple-element.55), channel_id=1, source_target_pairs={{0,3},{1,0},{2,1},{3,2},{4,7},{5,4},{6,5},{7,6},{8,11},{9,8},{10,9... | collective-permute-start | bytes 393224 | tf_op jit(solution)/shard_map/ppermute | solution.py:33
  162.9 11.3 %collective-permute-start.26 = (bf16[128,512]{1,0:T(8,128)(2,1)S(1)}, bf16[128,512]{1,0:T(8,128)(2,1)S(1)}, u32[]{:S(2)}, u32[]{:S(2)}) collective-permute-start(bf16[128,512]{1,0:T(8,128)(2,1)S(1)} %get-tuple-element.56), channel_id=1, source_target_pairs={{0,1},{1,2},{2,3},{3,0},{4,5},{5,6},{6,7},{7,4},{8,9},{9,10},{10,1... | collective-permute-start | bytes 393224 | tf_op jit(solution)/shard_map/ppermute | solution.py:33
  162.9 14.6 %collective-permute-start.27 = (bf16[128,512]{1,0:T(8,128)(2,1)S(1)}, bf16[128,512]{1,0:T(8,128)(2,1)S(1)}, u32[]{:S(2)}, u32[]{:S(2)}) collective-permute-start(bf16[128,512]{1,0:T(8,128)(2,1)S(1)} %get-tuple-element.57), channel_id=1, source_target_pairs={{0,2},{1,3},{2,0},{3,1},{4,6},{5,7},{6,4},{7,5},{8,10},{9,11},{10,... | collective-permute-start | bytes 393224 | tf_op jit(solution)/shard_map/ppermute | solution.py:33
  178.2 13.9 %collective-permute-start.28 = (bf16[64,4096]{1,0:T(8,128)(2,1)S(1)}, bf16[64,4096]{1,0:T(8,128)(2,1)S(1)}, u32[]{:S(2)}, u32[]{:S(2)}) collective-permute-start(bf16[64,4096]{1,0:T(8,128)(2,1)S(1)} %get-tuple-element.58), channel_id=1, source_target_pairs={{0,1},{1,2},{2,3},{3,0},{4,5},{5,6},{6,7},{7,4},{8,9},{9,10},{10,1... | collective-permute-start | bytes 1572872 | tf_op jit(solution)/shard_map/ppermute | solution.py:33
  178.8 28.4 %copy-start.7 = (bf16[512,512]{1,0:T(8,128)(2,1)S(1)}, bf16[512,512]{1,0:T(8,128)(2,1)}, u32[]{:S(2)}) copy-start(bf16[512,512]{1,0:T(8,128)(2,1)} %refs_2_.1) | copy-start | bytes 1572868
  178.8 13.3 %collective-permute-start.29 = (bf16[64,4096]{1,0:T(8,128)(2,1)S(1)}, bf16[64,4096]{1,0:T(8,128)(2,1)S(1)}, u32[]{:S(2)}, u32[]{:S(2)}) collective-permute-start(bf16[64,4096]{1,0:T(8,128)(2,1)S(1)} %get-tuple-element.59), channel_id=1, source_target_pairs={{0,3},{1,0},{2,1},{3,2},{4,7},{5,4},{6,5},{7,6},{8,11},{9,8},{10,9... | collective-permute-start | bytes 1572872 | tf_op jit(solution)/shard_map/ppermute | solution.py:33
  180.9 8.5 %collective-permute-start.31 = (bf16[128,512]{1,0:T(8,128)(2,1)S(1)}, bf16[128,512]{1,0:T(8,128)(2,1)S(1)}, u32[]{:S(2)}, u32[]{:S(2)}) collective-permute-start(bf16[128,512]{1,0:T(8,128)(2,1)S(1)} %add_convert_fusion._.refs_0_), channel_id=1, source_target_pairs={{0,128},{1,129},{2,130},{3,131},{4,132},{5,133},{6,134},{7,135},{8... | collective-permute-start | bytes 393224 | tf_op jit(solution)/shard_map/ppermute | solution.py:33
  189.4 10.3 %collective-permute-start.32 = (bf16[128,512]{1,0:T(8,128)(2,1)S(1)}, bf16[128,512]{1,0:T(8,128)(2,1)S(1)}, u32[]{:S(2)}, u32[]{:S(2)}) collective-permute-start(bf16[128,512]{1,0:T(8,128)(2,1)S(1)} %collective-permute-done.31), channel_id=1, source_target_pairs={{0,1},{1,2},{2,3},{3,0},{4,5},{5,6},{6,7},{7,4},{8,9},{9,10},{10,1... | collective-permute-start | bytes 393224 | tf_op jit(solution)/shard_map/ppermute | solution.py:33
  189.4 10.3 %collective-permute-start.33 = (bf16[128,512]{1,0:T(8,128)(2,1)S(1)}, bf16[128,512]{1,0:T(8,128)(2,1)S(1)}, u32[]{:S(2)}, u32[]{:S(2)}) collective-permute-start(bf16[128,512]{1,0:T(8,128)(2,1)S(1)} %collective-permute-done.31), channel_id=1, source_target_pairs={{0,3},{1,0},{2,1},{3,2},{4,7},{5,4},{6,5},{7,6},{8,11},{9,8},{10,9... | collective-permute-start | bytes 393224 | tf_op jit(solution)/shard_map/ppermute | solution.py:33
  192.1 15.1 %copy-start.5 = (bf16[512,1536]{1,0:T(8,128)(2,1)S(1)}, bf16[512,1536]{1,0:T(8,128)(2,1)}, u32[]{:S(2)}) copy-start(bf16[512,1536]{1,0:T(8,128)(2,1)} %refs_1_.1) | copy-start | bytes 4718596
  193.2 24.4 %collective-permute-start.30 = (bf16[128,4096]{1,0:T(8,128)(2,1)S(1)}, bf16[128,4096]{1,0:T(8,128)(2,1)S(1)}, u32[]{:S(2)}, u32[]{:S(2)}) collective-permute-start(bf16[128,4096]{1,0:T(8,128)(2,1)S(1)} %shard_map.105), channel_id=1, source_target_pairs={{0,0},{1,1},{2,2},{3,3},{4,8},{5,9},{6,10},{7,11},{8,4},{9,5},{10,... | collective-permute-start | bytes 3145736 | tf_op jit(solution)/shard_map/ppermute | solution.py:33
  199.5 5.6 %collective-permute-start.34 = (bf16[128,512]{1,0:T(8,128)(2,1)S(1)}, bf16[128,512]{1,0:T(8,128)(2,1)S(1)}, u32[]{:S(2)}, u32[]{:S(2)}) collective-permute-start(bf16[128,512]{1,0:T(8,128)(2,1)S(1)} %collective-permute-done.31), channel_id=1, source_target_pairs={{0,2},{1,3},{2,0},{3,1},{4,6},{5,7},{6,4},{7,5},{8,10},{9,11},{10,... | collective-permute-start | bytes 393224 | tf_op jit(solution)/shard_map/ppermute | solution.py:33
  205.1 2.0 collective-permute-start.35
  211.4 6.3 %collective-permute-start.36 = (bf16[128,512]{1,0:T(8,128)(2,1)S(1)}, bf16[128,512]{1,0:T(8,128)(2,1)S(1)}, u32[]{:S(2)}, u32[]{:S(2)}) collective-permute-start(bf16[128,512]{1,0:T(8,128)(2,1)S(1)} %shard_map.106), channel_id=1, source_target_pairs={{0,0},{1,1},{2,2},{3,3},{4,8},{5,9},{6,10},{7,11},{8,4},{9,5},{10,... | collective-permute-start | bytes 393224 | tf_op jit(solution)/shard_map/ppermute | solution.py:33
Sparse Core Ops, SparseCore 0:
  27.5 83.6 all-gather.2
  113.0 41.1 all-gather.4

commit v9 on v8

--- a/solution.py
+++ b/solution.py
@@ -177,7 +177,7 @@
         for copy in starting:
             copy.start()
         copies.append(starting)
-    step = 512
+    step = 1024
     for part in range(PARTS):
         for copy in copies[part]:
             copy.wait()
@@ -195,7 +195,7 @@
             else:
                 projected[rows, :] = term.astype(jnp.bfloat16)
 
-    step = 256
+    step = 512
     for head in range(2):
         at = head * 3 * HEAD_DIM
         for half, out in enumerate((own, other)):

time: 227 us -> 241 us (1.062); the launches traced: 226 us -> 237 us
  starting transfers between devices: 57.1 us -> 65.1 us
  waiting for transfers between devices: 98 us -> 101 us
    ppermute x37, starting transfers between devices: 57.1 us -> 65.1 us  [moved(): return lax.ppermute(block, AXES, route)]
    ppermute x37, waiting for transfers between devices: 98 us -> 101 us  [moved(): return lax.ppermute(block, AXES, route)]
  transfers between devices with their start and end apart: 39 -> 39, of which waited for: 20 -> 20; matrix products, arithmetic and copies ran while one was open for 4% -> 3% of each run, Pallas kernels for 16% -> 15%
where the time goes in v9:
time: 241 us; the launch traced here: 237 us
  waiting for transfers between devices  101 us (42%)
  starting transfers between devices  65.1 us (27%)
  Pallas kernels  36 us (15%)
  local copies, waits for them, and re-layouts  17.8 us (7%)
  between operations  14.9 us (6%)
    ppermute x37, waiting for transfers between devices, moved(): return lax.ppermute(block, AXES, route)  101 us
    ppermute x37, starting transfers between devices, moved(): return lax.ppermute(block, AXES, route)  65.1 us
    pallas_call x1, Pallas kernels, attention(): local(attention_kernel, (result, result), 60, flops=2 * count * depth * c...  16 us
    unnamed x47, local copies, waits for them, and re-layouts  11.9 us
    pallas_call x2, Pallas kernels, terms(): local(functools.partial(terms_kernel, len(earlier), picked), tuple((jax.S...  8.17 us
    pallas_call x1, Pallas kernels, descriptor_terms(): local(descriptor_kernel, (jax.ShapeDtypeStruct((rows, width), f32),) + (j...  5.95 us
  transfers between devices with their start and end apart: 39, of which 20 were waited for; matrix products, arithmetic and copies ran while one was open for 3% of the time, Pallas kernels for 15%

profile of v9, /device:TPU:1, one launch (start us, length us, event | category | flops | bytes accessed | tf_op | source)
XLA Modules:
  0.0 236.8 jit_solution(15721914716059052630)
XLA Ops:
  7.2 0.9 copy.102.refs_0_
  8.1 1.1 copy.60
  9.4 4.5 %collective-permute-start.13 = (bf16[768,128]{1,0:T(8,128)(2,1)S(1)}, bf16[768,128]{1,0:T(8,128)(2,1)S(1)}, u32[]{:S(2)}, u32[]{:S(2)}) collective-permute-start(bf16[768,128]{1,0:T(8,128)(2,1)S(1)} %bitcast.63), channel_id=1, source_target_pairs={{0,0},{1,1},{2,2},{3,3},{4,8},{5,9},{6,10},{7,11},{8,4},{9,5},{10,... | collective-permute-start | bytes 589832 | tf_op jit(solution)/shard_map/ppermute | solution.py:33
  14.4 4.4 %collective-permute-start.16 = (bf16[768,128]{1,0:T(8,128)(2,1)S(1)}, bf16[768,128]{1,0:T(8,128)(2,1)S(1)}, u32[]{:S(2)}, u32[]{:S(2)}) collective-permute-start(bf16[768,128]{1,0:T(8,128)(2,1)S(1)} %bitcast.66), channel_id=1, source_target_pairs={{0,16},{1,17},{2,18},{3,19},{4,24},{5,25},{6,26},{7,27},{8,20},{9,... | collective-permute-start | bytes 589832 | tf_op jit(solution)/shard_map/ppermute | solution.py:33
  19.0 3.2 %collective-permute-done.14 = bf16[768,128]{1,0:T(8,128)(2,1)S(1)} collective-permute-done((bf16[768,128]{1,0:T(8,128)(2,1)S(1)}, bf16[768,128]{1,0:T(8,128)(2,1)S(1)}, u32[]{:S(2)}, u32[]{:S(2)}) %collective-permute-start.14) | collective-permute-done | bytes 196640 | tf_op jit(solution)/shard_map/ppermute | solution.py:33
  22.3 4.1 %collective-permute-done.16 = bf16[768,128]{1,0:T(8,128)(2,1)S(1)} collective-permute-done((bf16[768,128]{1,0:T(8,128)(2,1)S(1)}, bf16[768,128]{1,0:T(8,128)(2,1)S(1)}, u32[]{:S(2)}, u32[]{:S(2)}) %collective-permute-start.16) | collective-permute-done | bytes 196640 | tf_op jit(solution)/shard_map/ppermute | solution.py:33
  26.4 0.9 copy-done.15
  27.4 2.5 %collective-permute-start = (bf16[128,4096]{1,0:T(8,128)(2,1)}, bf16[128,4096]{1,0:T(8,128)(2,1)S(1)}, u32[]{:S(2)}, u32[]{:S(2)}) collective-permute-start(bf16[128,4096]{1,0:T(8,128)(2,1)} %param.8), channel_id=1, source_target_pairs={{0,0},{1,1},{2,2},{3,3},{4,8},{5,9},{6,10},{7,11},{8,4},{9,5},{10,... | collective-permute-start | bytes 3145736 | tf_op jit(solution)/shard_map/ppermute | solution.py:33
  29.9 3.1 %collective-permute-start.4 = (bf16[256,128]{1,0:T(8,128)(2,1)S(1)}, bf16[256,128]{1,0:T(8,128)(2,1)S(1)}, u32[]{:S(2)}, u32[]{:S(2)}) collective-permute-start(bf16[256,128]{1,0:T(8,128)(2,1)S(1)} %copy-done.19), channel_id=1, source_target_pairs={{0,0},{1,1},{2,2},{3,3},{4,8},{5,9},{6,10},{7,11},{8,4},{9,5},{10,... | collective-permute-start | bytes 196616 | tf_op jit(solution)/shard_map/ppermute | solution.py:33
  33.0 11.8 %collective-permute-done.4 = bf16[256,128]{1,0:T(8,128)(2,1)S(1)} collective-permute-done((bf16[256,128]{1,0:T(8,128)(2,1)S(1)}, bf16[256,128]{1,0:T(8,128)(2,1)S(1)}, u32[]{:S(2)}, u32[]{:S(2)}) %collective-permute-start.4) | collective-permute-done | bytes 65568 | tf_op jit(solution)/shard_map/ppermute | solution.py:33
  44.8 6.9 %collective-permute-start.5 = (bf16[256,128]{1,0:T(8,128)(2,1)S(1)}, bf16[256,128]{1,0:T(8,128)(2,1)S(1)}, u32[]{:S(2)}, u32[]{:S(2)}) collective-permute-start(bf16[256,128]{1,0:T(8,128)(2,1)S(1)} %collective-permute-done.4), channel_id=1, source_target_pairs={{0,128},{1,129},{2,130},{3,131},{4,132},{5,133},{6,134},{7,135},{8... | collective-permute-start | bytes 196616 | tf_op jit(solution)/shard_map/ppermute | solution.py:33
  52.9 1.4 collective-permute-start.1
  54.3 1.5 collective-permute-start.2
  55.8 1.6 collective-permute-start.3
  57.4 0.8 collective-permute-start.6
  58.2 1.9 collective-permute-start.7
  60.3 5.8 %collective-permute-done.6 = bf16[2,256,128]{2,1,0:T(8,128)(2,1)S(1)} collective-permute-done((bf16[2,256,128]{2,1,0:T(8,128)(2,1)S(1)}, bf16[2,256,128]{2,1,0:T(8,128)(2,1)S(1)}, u32[]{:S(2)}, u32[]{:S(2)}) %collective-permute-start.6) | collective-permute-done | bytes 131104 | tf_op jit(solution)/shard_map/ppermute | solution.py:33
  66.2 9.0 %collective-permute-done.8 = bf16[2,256,128]{2,1,0:T(8,128)(2,1)S(1)} collective-permute-done((bf16[2,256,128]{2,1,0:T(8,128)(2,1)S(1)}, bf16[2,256,128]{2,1,0:T(8,128)(2,1)S(1)}, u32[]{:S(2)}, u32[]{:S(2)}) %collective-permute-start.8) | collective-permute-done | bytes 131104 | tf_op jit(solution)/shard_map/ppermute | solution.py:33
  75.3 2.8 %collective-permute-done.1.refs_0_ = bf16[128,4096]{1,0:T(8,128)(2,1)S(1)} collective-permute-done((bf16[128,4096]{1,0:T(8,128)(2,1)S(1)}, bf16[128,4096]{1,0:T(8,128)(2,1)S(1)}, u32[]{:S(2)}, u32[]{:S(2)}) %collective-permute-start.1) | collective-permute-done | bytes 1048608 | tf_op jit(solution)/shard_map/ppermute | solution.py:33
  78.1 10.9 %collective-permute-done.3.refs_2_ = bf16[128,4096]{1,0:T(8,128)(2,1)} collective-permute-done((bf16[128,4096]{1,0:T(8,128)(2,1)S(1)}, bf16[128,4096]{1,0:T(8,128)(2,1)}, u32[]{:S(2)}, u32[]{:S(2)}) %collective-permute-start.3) | collective-permute-done | bytes 1048608 | tf_op jit(solution)/shard_map/ppermute | solution.py:33
  89.5 3.6 %collective-permute-done.10.refs_5_ = bf16[128,4096]{1,0:T(8,128)(2,1)S(1)} collective-permute-done((bf16[128,4096]{1,0:T(8,128)(2,1)S(1)}, bf16[128,4096]{1,0:T(8,128)(2,1)S(1)}, u32[]{:S(2)}, u32[]{:S(2)}) %collective-permute-start.10) | collective-permute-done | bytes 1048608 | tf_op jit(solution)/shard_map/ppermute | solution.py:33
  93.4 1.5 collective-permute-done.12.refs_7_
  94.9 1.0 copy-done.11
  95.9 1.0 copy-done.12
  96.9 1.0 copy-done.13
  97.9 1.0 copy-done.14
  98.9 9.9 %collective-permute-start.24 = (bf16[128,512]{1,0:T(8,128)(2,1)S(1)}, bf16[128,512]{1,0:T(8,128)(2,1)S(1)}, u32[]{:S(2)}, u32[]{:S(2)}) collective-permute-start(bf16[128,512]{1,0:T(8,128)(2,1)S(1)} %shard_map.102), channel_id=1, source_target_pairs={{0,20},{1,21},{2,22},{3,23},{4,16},{5,17},{6,18},{7,19},{8,28},{9,... | collective-permute-start | bytes 393224 | tf_op jit(solution)/shard_map/ppermute | solution.py:33
  108.9 6.2 %collective-permute-done.24 = bf16[128,512]{1,0:T(8,128)(2,1)S(1)} collective-permute-done((bf16[128,512]{1,0:T(8,128)(2,1)S(1)}, bf16[128,512]{1,0:T(8,128)(2,1)S(1)}, u32[]{:S(2)}, u32[]{:S(2)}) %collective-permute-start.24) | collective-permute-done | bytes 131104 | tf_op jit(solution)/shard_map/ppermute | solution.py:33
  115.0 0.8 maximum_select_fusion
  115.9 2.7 %collective-permute-start.18 = (bf16[8,256,128]{2,1,0:T(8,128)(2,1)S(1)}, bf16[8,256,128]{2,1,0:T(8,128)(2,1)S(1)}, u32[]{:S(2)}, u32[]{:S(2)}) collective-permute-start(bf16[8,256,128]{2,1,0:T(8,128)(2,1)S(1)} %get-tuple-element.43), channel_id=1, source_target_pairs={{0,20},{1,21},{2,22},{3,23},{4,0},{5,1},{6,2},{7,3},{8,28},{9,29},... | collective-permute-start | bytes 1572872 | tf_op jit(solution)/shard_map/ppermute | solution.py:33
  118.6 1.9 broadcast_in_dim.59
  120.5 0.9 bitcast_dynamic-update-slice_fusion.3
  121.3 16.0 %shard_map.98 = (bf16[512,256]{1,0:T(8,128)(2,1)}, bf16[512,256]{1,0:T(8,128)(2,1)}) custom-call(bf16[128,4096]{1,0:T(8,128)(2,1)} %copy-done.2, bf16[128,4096]{1,0:T(8,128)(2,1)} %copy-done.6, bf16[128,4096]{1,0:T(8,128)(2,1)} %get-tuple-element.36.refs_2_, bf16[128,4096]{1,0:T(8,128)(2,1)} %get-tuple-element.37.refs_3_, bf16[128,4096]{1,0:T(8,128)(2,1)} %copy-done.11, ...), custom_call_target="tpu_custom_call" | custom-call | flops 6442450944 | bytes 14680064 | tf_op jit(solution)/shard_map/pallas_call | solution.py:223
  137.3 2.6 %collective-permute-done.19.refs_3_ = bf16[8,256,128]{2,1,0:T(8,128)(2,1)S(1)} collective-permute-done((bf16[8,256,128]{2,1,0:T(8,128)(2,1)S(1)}, bf16[8,256,128]{2,1,0:T(8,128)(2,1)S(1)}, u32[]{:S(2)}, u32[]{:S(2)}) %collective-permute-start.19) | collective-permute-done | bytes 524320 | tf_op jit(solution)/shard_map/ppermute | solution.py:33
  139.9 1.0 copy-done.8
  140.8 0.9 bitcast_dynamic-update-slice_fusion.2
  141.7 0.9 bitcast_dynamic-update-slice_fusion.1
  142.7 0.9 bitcast_dynamic-update-slice_fusion
  143.5 2.8 %collective-permute-start.21 = (bf16[8,4,256,128]{3,2,1,0:T(8,128)(2,1)}, bf16[8,4,256,128]{3,2,1,0:T(8,128)(2,1)S(1)}, u32[]{:S(2)}, u32[]{:S(2)}) collective-permute-start(bf16[8,4,256,128]{3,2,1,0:T(8,128)(2,1)} %bitcast_dynamic-update-slice_fusion), channel_id=1, source_target_pairs={{0,8},{1,9},{2,10},{3,11},{4,12},{5,13},{6,14},{7,15},{8,0},{9,1},... | collective-permute-start | bytes 6291464 | tf_op jit(solution)/shard_map/ppermute | solution.py:33
  146.3 4.4 %collective-permute-done.20.theirs = bf16[512,256]{1,0:T(8,128)(2,1)S(1)} collective-permute-done((bf16[512,256]{1,0:T(8,128)(2,1)S(1)}, bf16[512,256]{1,0:T(8,128)(2,1)S(1)}, u32[]{:S(2)}, u32[]{:S(2)}) %collective-permute-start.20) | collective-permute-done | bytes 262176 | tf_op jit(solution)/shard_map/ppermute | solution.py:33
  150.9 4.6 %shard_map.100 = (bf16[128,4096]{1,0:T(8,128)(2,1)}, bf16[128,4096]{1,0:T(8,128)(2,1)}) custom-call(bf16[512,256]{1,0:T(8,128)(2,1)S(1)} %get-tuple-element.44.mine, bf16[512,256]{1,0:T(8,128)(2,1)S(1)} %collective-permute-done.20.theirs, bf16[8,4,2,128,128]{4,3,2,1,0:T(8,128)(2,1)} %bitcast.27.weight, bf16[8,4,2,128,128]{4,3,2,1,0:T(8,128)(2,1)S(1)} %bitcast.60), custom_call_target="tpu_custom_call" | custom-call | flops 2000000000 | bytes 8000000 | tf_op jit(solution)/shard_map/pallas_call | solution.py:280
  155.5 1.5 collective-permute-start.22
  157.0 1.2 collective-permute-start.23
  158.2 0.9 copy-done.10
  159.1 3.6 %shard_map.101 = (f32[128,4096]{1,0:T(8,128)S(1)}, bf16[64,4096]{1,0:T(8,128)(2,1)S(1)}, bf16[64,4096]{1,0:T(8,128)(2,1)S(1)}) custom-call(bf16[512,256]{1,0:T(8,128)(2,1)S(1)} %copy-done.10, bf16[512,256]{1,0:T(8,128)(2,1)S(1)} %collective-permute-done.20.theirs, bf16[8,4,2,128,128]{4,3,2,1,0:T(8,128)(2,1)} %bitcast.27.weight, ...), custom_call_target="tpu_custom_call" | custom-call | flops 2000000000 | bytes 8000000 | tf_op jit(solution)/shard_map/pallas_call | solution.py:280
  162.7 1.3 copy-done.3
  164.1 5.9 %shard_map.103 = (f32[128,512]{1,0:T(8,128)S(1)}, bf16[128,512]{1,0:T(8,128)(2,1)S(1)}, bf16[128,512]{1,0:T(8,128)(2,1)S(1)}, bf16[128,512]{1,0:T(8,128)(2,1)S(1)}) custom-call(bf16[128,4096]{1,0:T(8,128)(2,1)} %copy-done, f32[128,4096]{1,0:T(8,128)} %copy-done.3, bf16[128,4096]{1,0:T(8,128)(2,1)} %get-tuple-element.53.down, ...), custom_call_target="tpu_custom_call" | custom-call | flops 4000000000 | bytes 12000000 | tf_op jit(solution)/shard_map/pallas_call | solution.py:330
  170.0 0.8 collective-permute-start.25
  170.8 0.8 collective-permute-start.26
  171.6 0.7 collective-permute-start.27
  172.3 11.9 %collective-permute-done.25 = bf16[128,512]{1,0:T(8,128)(2,1)S(1)} collective-permute-done((bf16[128,512]{1,0:T(8,128)(2,1)S(1)}, bf16[128,512]{1,0:T(8,128)(2,1)S(1)}, u32[]{:S(2)}, u32[]{:S(2)}) %collective-permute-start.25) | collective-permute-done | bytes 131104 | tf_op jit(solution)/shard_map/ppermute | solution.py:33
  184.2 3.2 %collective-permute-done.27 = bf16[128,512]{1,0:T(8,128)(2,1)S(1)} collective-permute-done((bf16[128,512]{1,0:T(8,128)(2,1)S(1)}, bf16[128,512]{1,0:T(8,128)(2,1)S(1)}, u32[]{:S(2)}, u32[]{:S(2)}) %collective-permute-start.27) | collective-permute-done | bytes 131104 | tf_op jit(solution)/shard_map/ppermute | solution.py:33
  188.6 2.1 collective-permute-start.29
  190.7 8.5 %collective-permute-done.31 = bf16[128,512]{1,0:T(8,128)(2,1)S(1)} collective-permute-done((bf16[128,512]{1,0:T(8,128)(2,1)S(1)}, bf16[128,512]{1,0:T(8,128)(2,1)S(1)}, u32[]{:S(2)}, u32[]{:S(2)}) %collective-permute-start.31) | collective-permute-done | bytes 131104 | tf_op jit(solution)/shard_map/ppermute | solution.py:33
  199.3 2.7 %collective-permute-start.33 = (bf16[128,512]{1,0:T(8,128)(2,1)S(1)}, bf16[128,512]{1,0:T(8,128)(2,1)S(1)}, u32[]{:S(2)}, u32[]{:S(2)}) collective-permute-start(bf16[128,512]{1,0:T(8,128)(2,1)S(1)} %collective-permute-done.31), channel_id=1, source_target_pairs={{0,3},{1,0},{2,1},{3,2},{4,7},{5,4},{6,5},{7,6},{8,11},{9,8},{10,9... | collective-permute-start | bytes 393224 | tf_op jit(solution)/shard_map/ppermute | solution.py:33
  202.0 1.1 shard_map.105
  203.1 6.3 %collective-permute-start.30 = (bf16[128,4096]{1,0:T(8,128)(2,1)S(1)}, bf16[128,4096]{1,0:T(8,128)(2,1)S(1)}, u32[]{:S(2)}, u32[]{:S(2)}) collective-permute-start(bf16[128,4096]{1,0:T(8,128)(2,1)S(1)} %shard_map.105), channel_id=1, source_target_pairs={{0,0},{1,1},{2,2},{3,3},{4,8},{5,9},{6,10},{7,11},{8,4},{9,5},{10,... | collective-permute-start | bytes 3145736 | tf_op jit(solution)/shard_map/ppermute | solution.py:33
  209.6 5.5 %collective-permute-done.34 = bf16[128,512]{1,0:T(8,128)(2,1)S(1)} collective-permute-done((bf16[128,512]{1,0:T(8,128)(2,1)S(1)}, bf16[128,512]{1,0:T(8,128)(2,1)S(1)}, u32[]{:S(2)}, u32[]{:S(2)}) %collective-permute-start.34) | collective-permute-done | bytes 131104 | tf_op jit(solution)/shard_map/ppermute | solution.py:33
  215.5 1.9 collective-permute-done.35.refs_4_
  217.4 4.2 %shard_map.106 = bf16[128,512]{1,0:T(8,128)(2,1)S(1)} custom-call(bf16[128,512]{1,0:T(8,128)(2,1)S(1)} %add_convert_fusion._.refs_0_, bf16[512,1536]{1,0:T(8,128)(2,1)S(1)} %copy-done.5, bf16[512,512]{1,0:T(8,128)(2,1)S(1)} %copy-done.7, bf16[512,512]{1,0:T(8,128)(2,1)S(1)} %constant_dynamic-update-slice_fusion.refs_3_, ...), custom_call_target="tpu_custom_call" | custom-call | tf_op jit(solution)/shard_map/pallas_call | solution.py:421
  221.6 2.8 %collective-permute-start.36 = (bf16[128,512]{1,0:T(8,128)(2,1)S(1)}, bf16[128,512]{1,0:T(8,128)(2,1)S(1)}, u32[]{:S(2)}, u32[]{:S(2)}) collective-permute-start(bf16[128,512]{1,0:T(8,128)(2,1)S(1)} %shard_map.106), channel_id=1, source_target_pairs={{0,0},{1,1},{2,2},{3,3},{4,8},{5,9},{6,10},{7,11},{8,4},{9,5},{10,... | collective-permute-start | bytes 393224 | tf_op jit(solution)/shard_map/ppermute | solution.py:33
  224.4 3.5 %collective-permute-done.36 = bf16[128,512]{1,0:T(8,128)(2,1)S(1)} collective-permute-done((bf16[128,512]{1,0:T(8,128)(2,1)S(1)}, bf16[128,512]{1,0:T(8,128)(2,1)S(1)}, u32[]{:S(2)}, u32[]{:S(2)}) %collective-permute-start.36) | collective-permute-done | bytes 131104 | tf_op jit(solution)/shard_map/ppermute | solution.py:33
  227.9 1.0 copy.103
  228.9 0.7 copy.104
  (100 shorter events, 5.4 us)
Async XLA Ops:
  7.2 114.2 %all-gather.3.cloned.1.call-start = ((), (), s32[]{:S(2)}) async-start(), calls=%async_computation | async-start | bytes 7077888 | tf_op jit(solution)/shard_map/all_gather | solution.py:450
  8.1 21.8 %copy-start.19 = (bf16[256,128]{1,0:T(8,128)(2,1)S(1)}, bf16[256,128]{1,0:T(8,128)(2,1)}, u32[]{:S(2)}) copy-start(bf16[256,128]{1,0:T(8,128)(2,1)} %param.12) | copy-start | bytes 196612
  9.4 9.4 %collective-permute-start.13 = (bf16[768,128]{1,0:T(8,128)(2,1)S(1)}, bf16[768,128]{1,0:T(8,128)(2,1)S(1)}, u32[]{:S(2)}, u32[]{:S(2)}) collective-permute-start(bf16[768,128]{1,0:T(8,128)(2,1)S(1)} %bitcast.63), channel_id=1, source_target_pairs={{0,0},{1,1},{2,2},{3,3},{4,8},{5,9},{6,10},{7,11},{8,4},{9,5},{10,... | collective-permute-start | bytes 589832 | tf_op jit(solution)/shard_map/ppermute | solution.py:33
  13.9 8.3 %collective-permute-start.14 = (bf16[768,128]{1,0:T(8,128)(2,1)S(1)}, bf16[768,128]{1,0:T(8,128)(2,1)S(1)}, u32[]{:S(2)}, u32[]{:S(2)}) collective-permute-start(bf16[768,128]{1,0:T(8,128)(2,1)S(1)} %bitcast.64), channel_id=1, source_target_pairs={{0,4},{1,5},{2,6},{3,7},{4,12},{5,13},{6,14},{7,15},{8,16},{9,17},... | collective-permute-start | bytes 589832 | tf_op jit(solution)/shard_map/ppermute | solution.py:33
  14.3 8.0 %collective-permute-start.15 = (bf16[768,128]{1,0:T(8,128)(2,1)S(1)}, bf16[768,128]{1,0:T(8,128)(2,1)S(1)}, u32[]{:S(2)}, u32[]{:S(2)}) collective-permute-start(bf16[768,128]{1,0:T(8,128)(2,1)S(1)} %bitcast.65), channel_id=1, source_target_pairs={{0,20},{1,21},{2,22},{3,23},{4,28},{5,29},{6,30},{7,31},{8,0},{9,1... | collective-permute-start | bytes 589832 | tf_op jit(solution)/shard_map/ppermute | solution.py:33
  14.4 12.0 %collective-permute-start.16 = (bf16[768,128]{1,0:T(8,128)(2,1)S(1)}, bf16[768,128]{1,0:T(8,128)(2,1)S(1)}, u32[]{:S(2)}, u32[]{:S(2)}) collective-permute-start(bf16[768,128]{1,0:T(8,128)(2,1)S(1)} %bitcast.66), channel_id=1, source_target_pairs={{0,16},{1,17},{2,18},{3,19},{4,24},{5,25},{6,26},{7,27},{8,20},{9,... | collective-permute-start | bytes 589832 | tf_op jit(solution)/shard_map/ppermute | solution.py:33
  19.0 33.5 %copy-start.16 = (f32[4096]{0:T(1024)S(1)}, f32[4096]{0:T(1024)}, u32[]{:S(2)}) copy-start(f32[4096]{0:T(1024)} %param.10) | copy-start | bytes 49156
  19.0 33.5 %copy-start.17 = (f32[4096]{0:T(1024)S(1)}, f32[4096]{0:T(1024)}, u32[]{:S(2)}) copy-start(f32[4096]{0:T(1024)} %param.9) | copy-start | bytes 49156
  26.4 0.9 copy-start.15
  27.4 136.7 %all-gather.5.cloned.1.call-start = ((), (), s32[]{:S(2)}) async-start(), calls=%async_computation.1 | async-start | bytes 4456448 | tf_op jit(solution)/shard_map/all_gather | solution.py:476
  27.4 24.3 %collective-permute-start = (bf16[128,4096]{1,0:T(8,128)(2,1)}, bf16[128,4096]{1,0:T(8,128)(2,1)S(1)}, u32[]{:S(2)}, u32[]{:S(2)}) collective-permute-start(bf16[128,4096]{1,0:T(8,128)(2,1)} %param.8), channel_id=1, source_target_pairs={{0,0},{1,1},{2,2},{3,3},{4,8},{5,9},{6,10},{7,11},{8,4},{9,5},{10,... | collective-permute-start | bytes 3145736 | tf_op jit(solution)/shard_map/ppermute | solution.py:33
  29.9 14.9 %collective-permute-start.4 = (bf16[256,128]{1,0:T(8,128)(2,1)S(1)}, bf16[256,128]{1,0:T(8,128)(2,1)S(1)}, u32[]{:S(2)}, u32[]{:S(2)}) collective-permute-start(bf16[256,128]{1,0:T(8,128)(2,1)S(1)} %copy-done.19), channel_id=1, source_target_pairs={{0,0},{1,1},{2,2},{3,3},{4,8},{5,9},{6,10},{7,11},{8,4},{9,5},{10,... | collective-permute-start | bytes 196616 | tf_op jit(solution)/shard_map/ppermute | solution.py:33
  44.8 12.6 %collective-permute-start.5 = (bf16[256,128]{1,0:T(8,128)(2,1)S(1)}, bf16[256,128]{1,0:T(8,128)(2,1)S(1)}, u32[]{:S(2)}, u32[]{:S(2)}) collective-permute-start(bf16[256,128]{1,0:T(8,128)(2,1)S(1)} %collective-permute-done.4), channel_id=1, source_target_pairs={{0,128},{1,129},{2,130},{3,131},{4,132},{5,133},{6,134},{7,135},{8... | collective-permute-start | bytes 196616 | tf_op jit(solution)/shard_map/ppermute | solution.py:33
  51.8 1.2 copy-start
  52.9 25.1 %collective-permute-start.1 = (bf16[128,4096]{1,0:T(8,128)(2,1)S(1)}, bf16[128,4096]{1,0:T(8,128)(2,1)S(1)}, u32[]{:S(2)}, u32[]{:S(2)}) collective-permute-start(bf16[128,4096]{1,0:T(8,128)(2,1)S(1)} %fusion.5.refs_0_), channel_id=1, source_target_pairs={{0,1},{1,2},{2,3},{3,0},{4,5},{5,6},{6,7},{7,4},{8,9},{9,10},{10,1... | collective-permute-start | bytes 3145736 | tf_op jit(solution)/shard_map/ppermute | solution.py:33
  54.3 23.8 %collective-permute-start.2 = (bf16[128,4096]{1,0:T(8,128)(2,1)S(1)}, bf16[128,4096]{1,0:T(8,128)(2,1)}, u32[]{:S(2)}, u32[]{:S(2)}) collective-permute-start(bf16[128,4096]{1,0:T(8,128)(2,1)S(1)} %fusion.5.refs_0_), channel_id=1, source_target_pairs={{0,3},{1,0},{2,1},{3,2},{4,7},{5,4},{6,5},{7,6},{8,11},{9,8},{10,9... | collective-permute-start | bytes 3145736 | tf_op jit(solution)/shard_map/ppermute | solution.py:33
  55.8 33.2 %collective-permute-start.3 = (bf16[128,4096]{1,0:T(8,128)(2,1)S(1)}, bf16[128,4096]{1,0:T(8,128)(2,1)}, u32[]{:S(2)}, u32[]{:S(2)}) collective-permute-start(bf16[128,4096]{1,0:T(8,128)(2,1)S(1)} %fusion.5.refs_0_), channel_id=1, source_target_pairs={{0,2},{1,3},{2,0},{3,1},{4,6},{5,7},{6,4},{7,5},{8,10},{9,11},{10,... | collective-permute-start | bytes 3145736 | tf_op jit(solution)/shard_map/ppermute | solution.py:33
  57.4 8.6 %collective-permute-start.6 = (bf16[2,256,128]{2,1,0:T(8,128)(2,1)S(1)}, bf16[2,256,128]{2,1,0:T(8,128)(2,1)S(1)}, u32[]{:S(2)}, u32[]{:S(2)}) collective-permute-start(bf16[2,256,128]{2,1,0:T(8,128)(2,1)S(1)} %shard_map.95), channel_id=1, source_target_pairs={{0,32},{1,33},{2,34},{3,35},{4,36},{5,37},{6,38},{7,39},{8,40},{9,... | collective-permute-start | bytes 393224 | tf_op jit(solution)/shard_map/ppermute | solution.py:33
  58.2 7.9 %collective-permute-start.7 = (bf16[2,256,128]{2,1,0:T(8,128)(2,1)S(1)}, bf16[2,256,128]{2,1,0:T(8,128)(2,1)S(1)}, u32[]{:S(2)}, u32[]{:S(2)}) collective-permute-start(bf16[2,256,128]{2,1,0:T(8,128)(2,1)S(1)} %shard_map.95), channel_id=1, source_target_pairs={{0,224},{1,225},{2,226},{3,227},{4,228},{5,229},{6,230},{7,231},{8... | collective-permute-start | bytes 393224 | tf_op jit(solution)/shard_map/ppermute | solution.py:33
  66.1 9.1 %collective-permute-start.8 = (bf16[2,256,128]{2,1,0:T(8,128)(2,1)S(1)}, bf16[2,256,128]{2,1,0:T(8,128)(2,1)S(1)}, u32[]{:S(2)}, u32[]{:S(2)}) collective-permute-start(bf16[2,256,128]{2,1,0:T(8,128)(2,1)S(1)} %shard_map.95), channel_id=1, source_target_pairs={{0,64},{1,65},{2,66},{3,67},{4,68},{5,69},{6,70},{7,71},{8,72},{9,... | collective-permute-start | bytes 393224 | tf_op jit(solution)/shard_map/ppermute | solution.py:33
  75.2 14.3 %collective-permute-start.9 = (bf16[128,4096]{1,0:T(8,128)(2,1)S(1)}, bf16[128,4096]{1,0:T(8,128)(2,1)S(1)}, u32[]{:S(2)}, u32[]{:S(2)}) collective-permute-start(bf16[128,4096]{1,0:T(8,128)(2,1)S(1)} %fusion.5.refs_0_), channel_id=1, source_target_pairs={{0,8},{1,9},{2,10},{3,11},{4,12},{5,13},{6,14},{7,15},{8,0},{9,1},... | collective-permute-start | bytes 3145736 | tf_op jit(solution)/shard_map/ppermute | solution.py:33
  89.0 4.1 %collective-permute-start.10 = (bf16[128,4096]{1,0:T(8,128)(2,1)S(1)}, bf16[128,4096]{1,0:T(8,128)(2,1)S(1)}, u32[]{:S(2)}, u32[]{:S(2)}) collective-permute-start(bf16[128,4096]{1,0:T(8,128)(2,1)S(1)} %get-tuple-element.31.refs_1_), channel_id=1, source_target_pairs={{0,8},{1,9},{2,10},{3,11},{4,12},{5,13},{6,14},{7,15},{8,0},{9,1},... | collective-permute-start | bytes 3145736 | tf_op jit(solution)/shard_map/ppermute | solution.py:33
  89.0 4.4 %collective-permute-start.11 = (bf16[128,4096]{1,0:T(8,128)(2,1)}, bf16[128,4096]{1,0:T(8,128)(2,1)S(1)}, u32[]{:S(2)}, u32[]{:S(2)}) collective-permute-start(bf16[128,4096]{1,0:T(8,128)(2,1)} %get-tuple-element.32.refs_2_), channel_id=1, source_target_pairs={{0,8},{1,9},{2,10},{3,11},{4,12},{5,13},{6,14},{7,15},{8,0},{9,1},... | collective-permute-start | bytes 3145736 | tf_op jit(solution)/shard_map/ppermute | solution.py:33
  89.5 5.4 %collective-permute-start.12 = (bf16[128,4096]{1,0:T(8,128)(2,1)}, bf16[128,4096]{1,0:T(8,128)(2,1)S(1)}, u32[]{:S(2)}, u32[]{:S(2)}) collective-permute-start(bf16[128,4096]{1,0:T(8,128)(2,1)} %get-tuple-element.33.refs_3_), channel_id=1, source_target_pairs={{0,8},{1,9},{2,10},{3,11},{4,12},{5,13},{6,14},{7,15},{8,0},{9,1},... | collective-permute-start | bytes 3145736 | tf_op jit(solution)/shard_map/ppermute | solution.py:33
  94.9 1.0 copy-start.11
  95.9 1.0 copy-start.12
  96.9 1.0 copy-start.13
  97.9 1.0 copy-start.14
  98.9 16.9 %copy-start.6 = (bf16[128,4096]{1,0:T(8,128)(2,1)}, bf16[128,4096]{1,0:T(8,128)(2,1)S(1)}, u32[]{:S(2)}) copy-start(bf16[128,4096]{1,0:T(8,128)(2,1)S(1)} %get-tuple-element.35.refs_1_) | copy-start | bytes 3145732
  98.9 21.6 %copy-start.2 = (bf16[128,4096]{1,0:T(8,128)(2,1)}, bf16[128,4096]{1,0:T(8,128)(2,1)S(1)}, u32[]{:S(2)}) copy-start(bf16[128,4096]{1,0:T(8,128)(2,1)S(1)} %get-tuple-element.34.refs_0_.refs_1_) | copy-start | bytes 3145732
  98.9 16.1 %collective-permute-start.24 = (bf16[128,512]{1,0:T(8,128)(2,1)S(1)}, bf16[128,512]{1,0:T(8,128)(2,1)S(1)}, u32[]{:S(2)}, u32[]{:S(2)}) collective-permute-start(bf16[128,512]{1,0:T(8,128)(2,1)S(1)} %shard_map.102), channel_id=1, source_target_pairs={{0,20},{1,21},{2,22},{3,23},{4,16},{5,17},{6,18},{7,19},{8,28},{9,... | collective-permute-start | bytes 393224 | tf_op jit(solution)/shard_map/ppermute | solution.py:33
  115.8 21.5 %collective-permute-start.17 = (bf16[8,256,128]{2,1,0:T(8,128)(2,1)S(1)}, bf16[8,256,128]{2,1,0:T(8,128)(2,1)S(1)}, u32[]{:S(2)}, u32[]{:S(2)}) collective-permute-start(bf16[8,256,128]{2,1,0:T(8,128)(2,1)S(1)} %get-tuple-element.43), channel_id=1, source_target_pairs={{0,4},{1,5},{2,6},{3,7},{4,16},{5,17},{6,18},{7,19},{8,12},{9,13},... | collective-permute-start | bytes 1572872 | tf_op jit(solution)/shard_map/ppermute | solution.py:33
  115.9 21.4 %collective-permute-start.18 = (bf16[8,256,128]{2,1,0:T(8,128)(2,1)S(1)}, bf16[8,256,128]{2,1,0:T(8,128)(2,1)S(1)}, u32[]{:S(2)}, u32[]{:S(2)}) collective-permute-start(bf16[8,256,128]{2,1,0:T(8,128)(2,1)S(1)} %get-tuple-element.43), channel_id=1, source_target_pairs={{0,20},{1,21},{2,22},{3,23},{4,0},{5,1},{6,2},{7,3},{8,28},{9,29},... | collective-permute-start | bytes 1572872 | tf_op jit(solution)/shard_map/ppermute | solution.py:33
  118.6 21.3 %collective-permute-start.19 = (bf16[8,256,128]{2,1,0:T(8,128)(2,1)S(1)}, bf16[8,256,128]{2,1,0:T(8,128)(2,1)S(1)}, u32[]{:S(2)}, u32[]{:S(2)}) collective-permute-start(bf16[8,256,128]{2,1,0:T(8,128)(2,1)S(1)} %get-tuple-element.43), channel_id=1, source_target_pairs={{0,16},{1,17},{2,18},{3,19},{4,20},{5,21},{6,22},{7,23},{8,24},{9,... | collective-permute-start | bytes 1572872 | tf_op jit(solution)/shard_map/ppermute | solution.py:33
  139.9 1.0 copy-start.8
  140.8 5.5 %copy-start.18 = (bf16[512,256]{1,0:T(8,128)(2,1)S(1)}, bf16[512,256]{1,0:T(8,128)(2,1)}, u32[]{:S(2)}) copy-start(bf16[512,256]{1,0:T(8,128)(2,1)} %get-tuple-element.45) | copy-start | bytes 786436
  140.8 14.7 %copy-start.9 = (bf16[512,256]{1,0:T(8,128)(2,1)}, bf16[512,256]{1,0:T(8,128)(2,1)S(1)}, u32[]{:S(2)}) copy-start(bf16[512,256]{1,0:T(8,128)(2,1)S(1)} %get-tuple-element.44.mine) | copy-start | bytes 786436
  143.5 7.4 %collective-permute-start.21 = (bf16[8,4,256,128]{3,2,1,0:T(8,128)(2,1)}, bf16[8,4,256,128]{3,2,1,0:T(8,128)(2,1)S(1)}, u32[]{:S(2)}, u32[]{:S(2)}) collective-permute-start(bf16[8,4,256,128]{3,2,1,0:T(8,128)(2,1)} %bitcast_dynamic-update-slice_fusion), channel_id=1, source_target_pairs={{0,8},{1,9},{2,10},{3,11},{4,12},{5,13},{6,14},{7,15},{8,0},{9,1},... | collective-permute-start | bytes 6291464 | tf_op jit(solution)/shard_map/ppermute | solution.py:33
  146.3 4.4 %collective-permute-start.20 = (bf16[512,256]{1,0:T(8,128)(2,1)S(1)}, bf16[512,256]{1,0:T(8,128)(2,1)S(1)}, u32[]{:S(2)}, u32[]{:S(2)}) collective-permute-start(bf16[512,256]{1,0:T(8,128)(2,1)S(1)} %copy-done.18), channel_id=1, source_target_pairs={{0,8},{1,9},{2,10},{3,11},{4,12},{5,13},{6,14},{7,15},{8,0},{9,1},... | collective-permute-start | bytes 786440 | tf_op jit(solution)/shard_map/ppermute | solution.py:33
  155.5 31.9 %collective-permute-start.22 = (bf16[128,4096]{1,0:T(8,128)(2,1)}, bf16[128,4096]{1,0:T(8,128)(2,1)S(1)}, u32[]{:S(2)}, u32[]{:S(2)}) collective-permute-start(bf16[128,4096]{1,0:T(8,128)(2,1)} %get-tuple-element.49.refs_0_.up), channel_id=1, source_target_pairs={{0,1},{1,2},{2,3},{3,0},{4,5},{5,6},{6,7},{7,4},{8,9},{9,10},{10,1... | collective-permute-start | bytes 3145736 | tf_op jit(solution)/shard_map/ppermute | solution.py:33
  157.0 30.4 %collective-permute-start.23 = (bf16[128,4096]{1,0:T(8,128)(2,1)}, bf16[128,4096]{1,0:T(8,128)(2,1)S(1)}, u32[]{:S(2)}, u32[]{:S(2)}) collective-permute-start(bf16[128,4096]{1,0:T(8,128)(2,1)} %get-tuple-element.53.down), channel_id=1, source_target_pairs={{0,3},{1,0},{2,1},{3,2},{4,7},{5,4},{6,5},{7,6},{8,11},{9,8},{10,9... | collective-permute-start | bytes 3145736 | tf_op jit(solution)/shard_map/ppermute | solution.py:33
  158.2 0.9 copy-start.10
  162.7 1.3 copy-start.3
  170.0 31.9 %copy-start.1 = (bf16[128,4096]{1,0:T(8,128)(2,1)S(1)}, bf16[128,4096]{1,0:T(8,128)(2,1)}, u32[]{:S(2)}) copy-start(bf16[128,4096]{1,0:T(8,128)(2,1)} %copy-done) | copy-start | bytes 3145732
  170.0 31.9 %copy-start.4 = (f32[128,4096]{1,0:T(8,128)S(1)}, f32[128,4096]{1,0:T(8,128)}, u32[]{:S(2)}) copy-start(f32[128,4096]{1,0:T(8,128)} %copy-done.3) | copy-start | bytes 6291460
  170.0 14.1 %collective-permute-start.25 = (bf16[128,512]{1,0:T(8,128)(2,1)S(1)}, bf16[128,512]{1,0:T(8,128)(2,1)S(1)}, u32[]{:S(2)}, u32[]{:S(2)}) collective-permute-start(bf16[128,512]{1,0:T(8,128)(2,1)S(1)} %get-tuple-element.55), channel_id=1, source_target_pairs={{0,3},{1,0},{2,1},{3,2},{4,7},{5,4},{6,5},{7,6},{8,11},{9,8},{10,9... | collective-permute-start | bytes 393224 | tf_op jit(solution)/shard_map/ppermute | solution.py:33
  170.8 13.3 %collective-permute-start.26 = (bf16[128,512]{1,0:T(8,128)(2,1)S(1)}, bf16[128,512]{1,0:T(8,128)(2,1)S(1)}, u32[]{:S(2)}, u32[]{:S(2)}) collective-permute-start(bf16[128,512]{1,0:T(8,128)(2,1)S(1)} %get-tuple-element.56), channel_id=1, source_target_pairs={{0,1},{1,2},{2,3},{3,0},{4,5},{5,6},{6,7},{7,4},{8,9},{9,10},{10,1... | collective-permute-start | bytes 393224 | tf_op jit(solution)/shard_map/ppermute | solution.py:33
  171.6 15.7 %collective-permute-start.27 = (bf16[128,512]{1,0:T(8,128)(2,1)S(1)}, bf16[128,512]{1,0:T(8,128)(2,1)S(1)}, u32[]{:S(2)}, u32[]{:S(2)}) collective-permute-start(bf16[128,512]{1,0:T(8,128)(2,1)S(1)} %get-tuple-element.57), channel_id=1, source_target_pairs={{0,2},{1,3},{2,0},{3,1},{4,6},{5,7},{6,4},{7,5},{8,10},{9,11},{10,... | collective-permute-start | bytes 393224 | tf_op jit(solution)/shard_map/ppermute | solution.py:33
  188.0 13.9 %collective-permute-start.28 = (bf16[64,4096]{1,0:T(8,128)(2,1)S(1)}, bf16[64,4096]{1,0:T(8,128)(2,1)S(1)}, u32[]{:S(2)}, u32[]{:S(2)}) collective-permute-start(bf16[64,4096]{1,0:T(8,128)(2,1)S(1)} %get-tuple-element.58), channel_id=1, source_target_pairs={{0,1},{1,2},{2,3},{3,0},{4,5},{5,6},{6,7},{7,4},{8,9},{9,10},{10,1... | collective-permute-start | bytes 1572872 | tf_op jit(solution)/shard_map/ppermute | solution.py:33
  188.6 28.8 %copy-start.7 = (bf16[512,512]{1,0:T(8,128)(2,1)S(1)}, bf16[512,512]{1,0:T(8,128)(2,1)}, u32[]{:S(2)}) copy-start(bf16[512,512]{1,0:T(8,128)(2,1)} %refs_2_.1) | copy-start | bytes 1572868
  188.6 13.3 %collective-permute-start.29 = (bf16[64,4096]{1,0:T(8,128)(2,1)S(1)}, bf16[64,4096]{1,0:T(8,128)(2,1)S(1)}, u32[]{:S(2)}, u32[]{:S(2)}) collective-permute-start(bf16[64,4096]{1,0:T(8,128)(2,1)S(1)} %get-tuple-element.59), channel_id=1, source_target_pairs={{0,3},{1,0},{2,1},{3,2},{4,7},{5,4},{6,5},{7,6},{8,11},{9,8},{10,9... | collective-permute-start | bytes 1572872 | tf_op jit(solution)/shard_map/ppermute | solution.py:33
  190.7 8.5 %collective-permute-start.31 = (bf16[128,512]{1,0:T(8,128)(2,1)S(1)}, bf16[128,512]{1,0:T(8,128)(2,1)S(1)}, u32[]{:S(2)}, u32[]{:S(2)}) collective-permute-start(bf16[128,512]{1,0:T(8,128)(2,1)S(1)} %add_convert_fusion._.refs_0_), channel_id=1, source_target_pairs={{0,128},{1,129},{2,130},{3,131},{4,132},{5,133},{6,134},{7,135},{8... | collective-permute-start | bytes 393224 | tf_op jit(solution)/shard_map/ppermute | solution.py:33
  199.2 10.3 %collective-permute-start.32 = (bf16[128,512]{1,0:T(8,128)(2,1)S(1)}, bf16[128,512]{1,0:T(8,128)(2,1)S(1)}, u32[]{:S(2)}, u32[]{:S(2)}) collective-permute-start(bf16[128,512]{1,0:T(8,128)(2,1)S(1)} %collective-permute-done.31), channel_id=1, source_target_pairs={{0,1},{1,2},{2,3},{3,0},{4,5},{5,6},{6,7},{7,4},{8,9},{9,10},{10,1... | collective-permute-start | bytes 393224 | tf_op jit(solution)/shard_map/ppermute | solution.py:33
  199.3 10.3 %collective-permute-start.33 = (bf16[128,512]{1,0:T(8,128)(2,1)S(1)}, bf16[128,512]{1,0:T(8,128)(2,1)S(1)}, u32[]{:S(2)}, u32[]{:S(2)}) collective-permute-start(bf16[128,512]{1,0:T(8,128)(2,1)S(1)} %collective-permute-done.31), channel_id=1, source_target_pairs={{0,3},{1,0},{2,1},{3,2},{4,7},{5,4},{6,5},{7,6},{8,11},{9,8},{10,9... | collective-permute-start | bytes 393224 | tf_op jit(solution)/shard_map/ppermute | solution.py:33
  201.9 15.4 %copy-start.5 = (bf16[512,1536]{1,0:T(8,128)(2,1)S(1)}, bf16[512,1536]{1,0:T(8,128)(2,1)}, u32[]{:S(2)}) copy-start(bf16[512,1536]{1,0:T(8,128)(2,1)} %refs_1_.1) | copy-start | bytes 4718596
  203.1 24.8 %collective-permute-start.30 = (bf16[128,4096]{1,0:T(8,128)(2,1)S(1)}, bf16[128,4096]{1,0:T(8,128)(2,1)S(1)}, u32[]{:S(2)}, u32[]{:S(2)}) collective-permute-start(bf16[128,4096]{1,0:T(8,128)(2,1)S(1)} %shard_map.105), channel_id=1, source_target_pairs={{0,0},{1,1},{2,2},{3,3},{4,8},{5,9},{6,10},{7,11},{8,4},{9,5},{10,... | collective-permute-start | bytes 3145736 | tf_op jit(solution)/shard_map/ppermute | solution.py:33
  209.4 5.7 %collective-permute-start.34 = (bf16[128,512]{1,0:T(8,128)(2,1)S(1)}, bf16[128,512]{1,0:T(8,128)(2,1)S(1)}, u32[]{:S(2)}, u32[]{:S(2)}) collective-permute-start(bf16[128,512]{1,0:T(8,128)(2,1)S(1)} %collective-permute-done.31), channel_id=1, source_target_pairs={{0,2},{1,3},{2,0},{3,1},{4,6},{5,7},{6,4},{7,5},{8,10},{9,11},{10,... | collective-permute-start | bytes 393224 | tf_op jit(solution)/shard_map/ppermute | solution.py:33
  215.1 2.2 collective-permute-start.35
  221.6 6.3 %collective-permute-start.36 = (bf16[128,512]{1,0:T(8,128)(2,1)S(1)}, bf16[128,512]{1,0:T(8,128)(2,1)S(1)}, u32[]{:S(2)}, u32[]{:S(2)}) collective-permute-start(bf16[128,512]{1,0:T(8,128)(2,1)S(1)} %shard_map.106), channel_id=1, source_target_pairs={{0,0},{1,1},{2,2},{3,3},{4,8},{5,9},{6,10},{7,11},{8,4},{9,5},{10,... | collective-permute-start | bytes 393224 | tf_op jit(solution)/shard_map/ppermute | solution.py:33
Sparse Core Ops, SparseCore 0:
  27.5 83.6 all-gather.2
  115.9 38.4 all-gather.4
